TPU v7x, 32 devices: a whole 2x2x4 slice. The times are simulated.
32 devices in a mesh: tm: 8 (over y, x, core), space: 4 (over z).
Axes of the slice: x: 2, y: 2, z: 4, core: 2. Of those that a mesh axis runs over, the one named last changes fastest.
Arguments:
- sep_block: float32 [8, 1536, 1536], P('tm', 'space'), may hold values from -1 to 10, as said below
- own_couple: bfloat16 [8, 1536, 1536], P('tm', 'space'), may hold values from -0.1875 to 0.1875
- prev_couple: bfloat16 [8, 1536, 1536], P('tm', 'space'), may hold values from -0.1875 to 0.1875
- inner_diag: float32 [8, 1536], P('tm'), may hold values from 0.5 to 4
Outputs:
- reduced_blocks: float32 [8, 1536, 1536], P('tm', 'space')
- left_links: bfloat16 [8, 1536, 1536], P('tm', 'space')
Inputs may be any that keep to these rules, and one draw needn't show every extreme that they name: sep_block is symmetric in its last two dimensions; its diagonal entries lie between 3.5 and 10.
All inputs are finite; a program needn't handle non-finite values.
Results may differ from a plain program's by a relative error of at most 0.0083.
Values may be sent and summed in bfloat16 or wider, within the bound.
No kernel may reach another device: no remote copies, remote signals or barrier semaphores. Data moves between devices by JAX's collectives and lax.ppermute only.
A program may use at most 64 MiB of HBM per device.

v0:
```python
import functools

import jax
import jax.numpy as jnp
from jax import lax
from jax.experimental import pallas as pl
from jax.experimental.pallas import tpu as pltpu
from jax.sharding import PartitionSpec as P

BF16 = jnp.bfloat16
F32 = jnp.float32
EXTRA = 16
WIDTH = 256

ANY = pl.BlockSpec(memory_space=pl.ANY)
SHAPE = jax.ShapeDtypeStruct
FREE = pl.CostEstimate(flops=0, bytes_accessed=0, transcendentals=0)


def after(block, *others):
    def body(*refs):
        del refs

    return pl.pallas_call(
        body,
        out_shape=SHAPE(block.shape, block.dtype),
        in_specs=[ANY] * (1 + len(others)),
        out_specs=ANY,
        input_output_aliases={0: 0},
    )(block, *others)


def scaled_by(matrix, factors):
    return (matrix.astype(F32) * factors.astype(F32)[None, :]).astype(BF16)


def row_scaled_by(matrix, factors):
    return (matrix.astype(F32) * factors.astype(F32)[:, None]).astype(BF16)


def dot_nt(left, right):
    return lax.dot_general(left, right, (((1,), (1,)), ((), ())), preferred_element_type=F32)


def dot_nn(left, right):
    return lax.dot_general(left, right, (((1,), (0,)), ((), ())), preferred_element_type=F32)


def dot_tn(left, right):
    return lax.dot_general(left, right, (((0,), (0,)), ((), ())), preferred_element_type=F32)


def rows_of(scale):
    return jnp.broadcast_to(scale[None, :], (8, scale.shape[0]))


def whole_spec(shape):
    return pl.BlockSpec(shape, lambda j, f: (0,) * len(shape))


def along_spec(count):
    return pl.BlockSpec((count, WIDTH), lambda j, f: (0, j))


def down_spec(count):
    return pl.BlockSpec((WIDTH, count), lambda j, f: (j, 0))


def opening_kernel(flags, own, prev, separator, reciprocal, long):
    rows, order = own.shape
    row_ids = lax.broadcasted_iota(jnp.int32, (rows, order), 0) + flags[1] * rows
    col_ids = lax.broadcasted_iota(jnp.int32, (rows, order), 1)
    on_diagonal = jnp.where(row_ids == col_ids, separator[...], 0.0)
    ones = jnp.ones((8, order), BF16)

    def split(value):
        high = value.astype(BF16)
        return high, (value - high.astype(F32)).astype(BF16)

    def form_diagonal(block):
        wide = block.astype(F32)
        high, low = split((wide * reciprocal[0:1]).astype(BF16).astype(F32) * wide)
        return (dot_nt(ones, high) + dot_nt(ones, low))[0:1]

    def placed(words, count):
        ids = lax.broadcasted_iota(jnp.int32, (EXTRA, count), 0)
        total = jnp.zeros((EXTRA, count), F32)
        for at, word in words.items():
            total = jnp.where(ids == at, word.astype(F32), total)
        return total.astype(BF16)

    long[0:rows, :] = prev[...]
    high, low = split(jnp.sum(on_diagonal, axis=0, keepdims=True))
    long[rows:, :] = placed({0: high, 1: low}, order)
    own_high, own_low = split(form_diagonal(own[...]))
    prev_high, prev_low = split(form_diagonal(prev[...]))
    local = placed({2: own_high, 3: own_low, 4: prev_high, 5: prev_low}, rows)
    long[rows:, 0:rows] = long[rows:, 0:rows] + local


def opening(flags, own, prev, separator, reciprocal):
    rows, order = own.shape
    return pl.pallas_call(
        opening_kernel,
        out_shape=SHAPE((rows + EXTRA, order), BF16),
        grid_spec=pltpu.PrefetchScalarGridSpec(
            num_scalar_prefetch=1,
            grid=(1,),
            in_specs=[whole_spec((rows, order))] * 3 + [whole_spec((8, order))],
            out_specs=whole_spec((rows + EXTRA, order)),
        ),
        compiler_params=pltpu.CompilerParams(vmem_limit_bytes=32 * 1024 * 1024),
        cost_estimate=FREE,
    )(flags, own, prev, separator, reciprocal)


def early_kernel(size, flags, prev_whole, prev_rows, own_rows, separator, plain_rows, *refs):
    sources = refs[: 2 * size - 1]
    link, partial, form, own_out, across, mine, own, sems = refs[2 * size - 1 :]
    rows = separator.shape[0]
    step = pl.program_id(0)
    here = pl.ds(pl.multiple_of(step * WIDTH, WIDTH), WIDTH)

    def copies():
        for spot in range(size):
            for by, source in enumerate(sources):
                distance = (by + 1) // 2 if by % 2 else -(by // 2)
                target = own.at[pl.ds(spot * rows, rows)]
                copy = pltpu.make_async_copy(source.at[pl.ds(0, rows)], target, sems.at[spot])
                yield flags[1] - spot == distance, copy

    @pl.when(step == 0)
    def _():
        for chosen, copy in copies():
            pl.when(chosen)(copy.start)
        for chosen, copy in copies():
            pl.when(chosen)(copy.wait)

    block = own[here, :]
    own_out[...] = block
    link[...] = jnp.where(flags[0] == 1, 0.0, -dot_nt(prev_whole[...], block)).astype(BF16)
    mine[...] = link[pl.ds(pl.multiple_of(flags[1] * rows, rows), rows), :]
    partial[...] = separator[...] - dot_nt(own_rows[...], block)
    prev_block = prev_whole[here, :]
    form[...] = dot_nt(prev_rows[...], prev_block)
    across[...] = jnp.where(flags[0] == 1, 0.0, -dot_nt(plain_rows[...], prev_block)).astype(BF16)


def early_forms(flags, prev_whole, prev_rows, own_rows, separator, plain_rows, sources):
    rows, order = own_rows.shape
    size = order // rows
    return pl.pallas_call(
        functools.partial(early_kernel, size),
        out_shape=[
            SHAPE((order, order), BF16),
            SHAPE((rows, order), F32),
            SHAPE((rows, order), F32),
            SHAPE((order, order), BF16),
            SHAPE((rows, order), BF16),
            SHAPE((rows, order), BF16),
        ],
        grid_spec=pltpu.PrefetchScalarGridSpec(
            num_scalar_prefetch=1,
            grid=(order // WIDTH,),
            in_specs=[
                whole_spec((order, order)),
                whole_spec((rows, order)),
                whole_spec((rows, order)),
                along_spec(rows),
                whole_spec((rows, order)),
            ]
            + [ANY] * len(sources),
            out_specs=[along_spec(order), along_spec(rows), along_spec(rows), down_spec(order), along_spec(rows), along_spec(rows)],
            scratch_shapes=[pltpu.VMEM((order, order), BF16), pltpu.SemaphoreType.DMA((size,))],
        ),
        compiler_params=pltpu.CompilerParams(vmem_limit_bytes=32 * 1024 * 1024),
        cost_estimate=FREE,
    )(flags, prev_whole, prev_rows, own_rows, separator, plain_rows, *sources)


def late_kernel(
    size, flags, reciprocal, prev_rows, plain_rows, mine, own, scale, late_scale, from_below, from_above, far,
    ready, link, corner, across, left_diag, right_diag, raw, scaled, sem,
):
    del ready
    place = flags[1]
    step = pl.program_id(0)
    width = own.shape[0]
    here = pl.ds(pl.multiple_of(step * width, width), width)

    @pl.when(step == 0)
    def _():
        for chosen, source in (
            (place == 0, from_above),
            (place == size - 1, from_below),
            (jnp.logical_and(place != 0, place != size - 1), far),
        ):
            copy = pltpu.make_async_copy(source, raw, sem)
            pl.when(chosen)(copy.start)
            pl.when(chosen)(copy.wait)
        scaled[...] = (raw[...].astype(F32) * reciprocal[0:1]).astype(BF16)
        across[...] = jnp.where(flags[0] == 1, 0.0, -dot_nt(plain_rows[...], scaled[...])).astype(BF16)

    link[:, here] = jnp.where(flags[0] == 1, 0.0, -dot_nt(scaled[...], own[...])).astype(BF16)

    @pl.when(step == pl.num_programs(0) - 1)
    def _():
        late = link[...]
        square = late * late
        keep = jnp.where(flags[2] == 1, 1.0, 0.0)
        ours = mine[...] * scale[0:1]
        corner[...] = (dot_nt(prev_rows[...], scaled[...]) + keep * dot_nt(ours, late)).astype(BF16)
        left_diag[...] = dot_nt(scale[...], square)
        right_diag[...] = dot_nn(late_scale[...], square)


def late_forms(
    flags, reciprocal, prev_rows, plain_rows, mine, own, scale, late_scale, from_below, from_above, far, ready
):
    rows, order = prev_rows.shape
    size = order // rows
    width = 512
    return pl.pallas_call(
        functools.partial(late_kernel, size),
        out_shape=[
            SHAPE((rows, order), BF16),
            SHAPE((rows, rows), BF16),
            SHAPE((rows, rows), BF16),
            SHAPE((8, rows), F32),
            SHAPE((8, order), F32),
        ],
        grid_spec=pltpu.PrefetchScalarGridSpec(
            num_scalar_prefetch=1,
            grid=(order // width,),
            in_specs=[
                whole_spec((8, order)),
                whole_spec((rows, order)),
                whole_spec((rows, order)),
                whole_spec((rows, order)),
                pl.BlockSpec((width, order), lambda j, f: (j, 0)),
                whole_spec((8, order)),
                whole_spec((8, rows)),
                ANY,
                ANY,
                ANY,
                ANY,
            ],
            out_specs=[
                whole_spec((rows, order)),
                whole_spec((rows, rows)),
                whole_spec((rows, rows)),
                whole_spec((8, rows)),
                whole_spec((8, order)),
            ],
            scratch_shapes=[
                pltpu.VMEM((rows, order), BF16),
                pltpu.VMEM((rows, order), BF16),
                pltpu.SemaphoreType.DMA,
            ],
        ),
        compiler_params=pltpu.CompilerParams(vmem_limit_bytes=24 * 1024 * 1024),
    )(
        flags, reciprocal, prev_rows, plain_rows, mine, own, scale, late_scale, from_below, from_above, far,
        ready,
    )


def level_kernel(flags, link, mine, scale, pivot_scale, form, update, left_diag, right_diag):
    part = link[...]
    scaled = mine[...] * scale[0:1]
    keep = jnp.where(flags[2] == 1, 1.0, 0.0)
    update[...] = (form[...] + keep * dot_nt(scaled, part)).astype(BF16)
    square = part * part
    left_diag[...] = dot_nt(scale[...], square)

    @pl.when(pl.program_id(0) == 0)
    def _():
        right_diag[...] = jnp.zeros_like(right_diag)

    right_diag[...] += dot_nn(pivot_scale[...], square)


def level_forms(flags, link, mine, scale, pivot_scale, form):
    rows, order = form.shape
    width = 512
    along = lambda count: pl.BlockSpec((count, width), lambda j, f: (0, j))
    return pl.pallas_call(
        level_kernel,
        out_shape=[SHAPE((rows, order), BF16), SHAPE((8, order), F32), SHAPE((8, order), F32)],
        grid_spec=pltpu.PrefetchScalarGridSpec(
            num_scalar_prefetch=1,
            grid=(order // width,),
            in_specs=[
                pl.BlockSpec((width, order), lambda j, f: (j, 0)),
                whole_spec((rows, order)),
                whole_spec((8, order)),
                along(8),
                along(rows),
            ],
            out_specs=[along(rows), along(8), whole_spec((8, order))],
        ),
        compiler_params=pltpu.CompilerParams(vmem_limit_bytes=24 * 1024 * 1024),
        cost_estimate=FREE,
    )(flags, link, mine, scale, pivot_scale, form)


def on_device(sep_block, own_couple, prev_couple, inner_diag):
    separator = sep_block[0]
    own_rows = own_couple[0]
    prev_rows = prev_couple[0]
    reciprocal = 1.0 / inner_diag[0]
    rows, order = own_rows.shape
    place = lax.axis_index("space")
    size = lax.axis_size("space")
    row_start = place * rows
    partition = lax.axis_index("tm")
    parts = lax.axis_size("tm")

    def between(block, route):
        return lax.ppermute(block, "tm", [(a, b) for a, b in route if 0 <= b < parts])

    even = range(0, parts, 2)
    pivots = range(1, parts, 4)
    everyone = range(parts)

    def one_step(ahead, back, step):
        up = [(j, j + 1) for j in range(step - 1, size - 1)]
        down = [(j, j - 1) for j in range(1, size - step + 1)]
        return lax.ppermute(ahead, "space", up), lax.ppermute(back, "space", down)

    def block_at(arrived, spot):
        block = arrived[0][0]
        for step in range(1, len(arrived)):
            if spot + step < size:
                block = jnp.where(place == spot + step, arrived[step][0], block)
            if spot - step >= 0:
                block = jnp.where(place == spot - step, arrived[step][1], block)
        return block

    own_arrived = [(own_rows, own_rows)]
    own_arrived.append(one_step(own_rows, own_rows, 1))

    is_first = partition == 0
    is_pivot = partition % 2 == 0
    is_receiver = partition % 2 == 1
    is_last = partition % 4 == 3
    flags = jnp.stack([is_first.astype(jnp.int32), place, is_pivot.astype(jnp.int32)])
    prev_long = opening(flags, own_rows, prev_rows, separator, rows_of(reciprocal))
    words = prev_long[rows:]
    prev_long = one_step(prev_long, prev_long, 1)
    prev_arrived = [(prev_rows, prev_rows), tuple(block[:rows] for block in prev_long)]
    words_arrived = [(words, words), tuple(block[rows:] for block in prev_long)]
    own_long = [jnp.concatenate(pair) for pair in zip(own_arrived[1], words_arrived[1])]
    for step in range(2, size):
        prev_arrived.append(one_step(*prev_arrived[-1], step))
        own_long = one_step(*own_long, step)
        own_arrived.append(own_long)
        words_arrived.append(tuple(block[rows:] for block in own_long))

    left_side = place < size // 2
    late_start = jnp.where(left_side, size - 1, 0) * rows
    is_end = jnp.logical_or(place == 0, place == size - 1)
    prev_blocks = [block_at(prev_arrived[:-1], spot) for spot in range(size)]
    zero = jnp.zeros_like(prev_rows)
    prev_blocks[0] = jnp.where(place == size - 1, zero, prev_blocks[0])
    prev_blocks[-1] = jnp.where(place == 0, zero, prev_blocks[-1])
    prev_first = jnp.concatenate(prev_blocks)
    prev_far = jnp.where(left_side, prev_blocks[-1], prev_blocks[0])
    prev_first, prev_far = lax.optimization_barrier((prev_first, prev_far))
    words = [block_at(words_arrived, spot) for spot in range(size)]

    def pair_sum(block, at):
        return block[at].astype(F32) + block[at + 1].astype(F32)

    part_diag = sum(pair_sum(block, 0) for block in words)
    part_diag = part_diag - jnp.concatenate([pair_sum(block, 2)[:rows] for block in words])
    prev_diag = jnp.concatenate([pair_sum(block, 4)[:rows] for block in words])
    diag = part_diag - between(prev_diag, [(p, p - 1) for p in everyone])
    pivot_diag = between(part_diag, [(p, p + 1) for p in even]) - prev_diag
    scale = (1.0 / jnp.maximum(diag, 1.0)).astype(BF16)
    pivot_scale = (1.0 / jnp.maximum(pivot_diag, 1.0)).astype(BF16)

    own_scaled = scaled_by(own_rows, reciprocal)
    sources = [own_rows]
    for up, down in own_arrived[1:]:
        sources += [up, down]
    link, partial, prev_form, own_full, across, mine = early_forms(
        flags, scaled_by(prev_first, reciprocal), prev_rows, own_scaled, separator, own_rows, sources
    )
    scale8, pivot_scale8 = rows_of(scale), rows_of(pivot_scale)
    update, left_diag, right_diag = level_forms(flags, link, mine, scale8, pivot_scale8, prev_form)

    from_below, from_above = prev_arrived[-1]
    late_scale = lax.dynamic_slice_in_dim(pivot_scale, late_start, rows, 0)
    late_scale = jnp.where(is_end, late_scale, jnp.zeros_like(late_scale))
    late, corner, across_late, left_late, right_late = late_forms(
        flags, rows_of(reciprocal), prev_rows, own_rows, mine, own_full, scale8, rows_of(late_scale),
        from_below, from_above, prev_far, right_diag,
    )
    link = lax.dynamic_update_slice_in_dim(link, late, late_start, 0)
    pivot_link = between(link, [(p, p + 1) for p in even])
    update = lax.dynamic_update_slice_in_dim(update, corner, late_start, 1)
    left_diag = lax.dynamic_update_slice_in_dim(left_diag[0], left_late[0], late_start, 0)
    right_diag = right_diag[0] + right_late[0]

    left_diag = between(left_diag, [(p, p - 1) for p in even])
    from_even = between(
        update, [(p, p - 1) for p in range(2, parts, 4)] + [(p, p - 4) for p in range(4, parts, 4)]
    )
    from_odd = between(update, [(p, p - 1) for p in range(1, parts, 2)])
    next_diag = diag - left_diag - right_diag
    next_scale = (1.0 / jnp.maximum(next_diag, 1.0)).astype(BF16)
    pivot_rows = lax.dynamic_slice_in_dim(pivot_link, row_start, rows, 0)
    pivot_rows = lax.optimization_barrier(scaled_by(pivot_rows, pivot_scale))
    next_rows = (-dot_nn(pivot_rows, link)).astype(BF16)
    pivot_rows = between(next_rows, [(p, p + 2) for p in pivots if p != 1])

    left_next = scaled_by(dot_nt(scaled_by(next_rows, next_scale), link), pivot_scale)
    left_next = lax.optimization_barrier(left_next)
    left_next = (-dot_nt(left_next, pivot_link)).astype(BF16)
    from_pivot = between(left_next, [(p, p - 2) for p in pivots])

    next_pivot_scale = between(after(next_scale, left_next), [(p, p + 2) for p in pivots])
    go_on = after(jnp.ones((8, 128), jnp.int32), left_next)[0, 0] == 1
    passed_on = jnp.where(go_on, from_even, jnp.zeros_like(from_even))
    from_far = between(passed_on, [(p - 4, p - 1) for p in range(4, parts, 4)])
    pivot_scale = after(pivot_scale, left_next, pivot_rows)
    across = lax.dynamic_update_slice_in_dim(across, across_late, late_start, 1)
    right = lax.optimization_barrier(scaled_by(across, pivot_scale))
    next_cols = (-dot_nt(right, pivot_link)).astype(BF16)
    both = jnp.concatenate([next_cols, pivot_rows])
    both = lax.optimization_barrier(scaled_by(both, next_pivot_scale))
    both = dot_nn(both, pivot_link) * pivot_scale.astype(F32)[None, :]
    right = jnp.where(is_last, right.astype(F32) - both[:rows], right.astype(F32))
    both = lax.optimization_barrier(jnp.concatenate([right, both[rows:]]).astype(BF16))
    both = lax.optimization_barrier(dot_nn(both, link))
    link_rows = lax.dynamic_slice_in_dim(link, row_start, rows, 0)
    out_link = jnp.where(is_last, both[rows:].astype(BF16), jnp.where(is_receiver, next_rows, link_rows))
    from_even = jnp.where(is_receiver, from_even + from_far, jnp.zeros_like(from_even))
    from_later = (from_even + from_odd).astype(F32) + from_pivot.astype(F32)
    schur = partial - jnp.where(is_receiver, both[:rows], 0.0) - from_later
    return (schur[None], out_link[None])


def solution(mesh):
    placed = (P("tm", "space", None), P("tm", "space", None), P("tm", "space", None), P("tm", None))
    return jax.shard_map(
        on_device,
        mesh=mesh,
        in_specs=placed,
        out_specs=(P("tm", "space", None), P("tm", "space", None)),
        check_vma=False,
    )
```

profile of v0, /device:TPU:7, one launch (start us, length us, event | category | flops | bytes accessed | tf_op | source)
XLA Modules:
  0.0 306.6 jit_solution(5288677869252903714)
XLA Ops:
  0.6 0.7 divide_reduce_fusion
  1.5 1.3 copy-done
  2.7 1.7 copy-done.2
  4.4 3.8 %shard_map.59 = bf16[400,1536]{1,0:T(8,128)(2,1)S(1)} custom-call(s32[3]{0:T(128)S(1)} %pad_add_fusion.flags, bf16[384,1536]{1,0:T(8,128)(2,1)} %bitcast.3.own.plain_rows.refs_0_, bf16[384,1536]{1,0:T(8,128)(2,1)S(1)} %bitcast.29, f32[384,1536]{1,0:T(8,128)S(1)} %bitcast.32, f32[8,1536]{1,0:T(8,128)S(1)} %broadcast_in_dim.22.reciprocal), custom_call_target="tpu_custom_call" | custom-call | tf_op jit(solution)/shard_map/pallas_call | solution.py:103
  8.3 3.3 %collective-permute-start = (bf16[400,1536]{1,0:T(8,128)(2,1)S(1)}, bf16[400,1536]{1,0:T(8,128)(2,1)S(1)}, u32[]{:S(2)}, u32[]{:S(2)}) collective-permute-start(bf16[400,1536]{1,0:T(8,128)(2,1)S(1)} %shard_map.59), channel_id=1, source_target_pairs={{0,1},{1,2},{2,3},{4,5},{5,6},{6,7},{8,9},{9,10},{10,11},{12,13},{... | collective-permute-start | bytes 3686408 | tf_op jit(solution)/shard_map/ppermute | solution.py:329
  11.6 3.2 %collective-permute-start.4 = (bf16[384,1536]{1,0:T(8,128)(2,1)}, bf16[384,1536]{1,0:T(8,128)(2,1)S(1)}, u32[]{:S(2)}, u32[]{:S(2)}) collective-permute-start(bf16[384,1536]{1,0:T(8,128)(2,1)} %bitcast.3.own.plain_rows.refs_0_), channel_id=1, source_target_pairs={{0,1},{1,2},{2,3},{4,5},{5,6},{6,7},{8,9},{9,10},{10,11},{12,13},{... | collective-permute-start | bytes 3538952 | tf_op jit(solution)/shard_map/ppermute | solution.py:329
  14.8 1.3 collective-permute-start.2
  16.1 1.3 collective-permute-start.5
  17.4 19.8 %collective-permute-done = bf16[400,1536]{1,0:T(8,128)(2,1)S(1)} collective-permute-done((bf16[400,1536]{1,0:T(8,128)(2,1)S(1)}, bf16[400,1536]{1,0:T(8,128)(2,1)S(1)}, u32[]{:S(2)}, u32[]{:S(2)}) %collective-permute-start) | collective-permute-done | bytes 1228832 | tf_op jit(solution)/shard_map/ppermute | solution.py:329
  37.2 25.4 %collective-permute-done.4.refs_1_ = bf16[384,1536]{1,0:T(8,128)(2,1)S(1)} collective-permute-done((bf16[384,1536]{1,0:T(8,128)(2,1)}, bf16[384,1536]{1,0:T(8,128)(2,1)S(1)}, u32[]{:S(2)}, u32[]{:S(2)}) %collective-permute-start.4) | collective-permute-done | bytes 1179680 | tf_op jit(solution)/shard_map/ppermute | solution.py:329
  62.5 1.1 pad_maximum_fusion.2
  63.7 1.7 collective-permute-start.6
  65.4 1.3 collective-permute-start.3
  66.7 1.1 slice.234
  67.8 1.7 collective-permute-start.1
  69.5 1.6 multiply_convert_fusion.5.own_rows
  71.2 1.4 collective-permute-start.7
  72.7 0.7 collective-permute-start.8
  73.4 23.1 %collective-permute-done.3 = bf16[384,1536]{1,0:T(8,128)(2,1)} collective-permute-done((bf16[384,1536]{1,0:T(8,128)(2,1)S(1)}, bf16[384,1536]{1,0:T(8,128)(2,1)}, u32[]{:S(2)}, u32[]{:S(2)}) %collective-permute-start.3) | collective-permute-done | bytes 1179680 | tf_op jit(solution)/shard_map/ppermute | solution.py:329
  96.5 1.9 broadcast_select_fusion.1
  98.5 0.4 pad_maximum_fusion
  98.8 1.3 collective-permute-start.13
  100.1 0.7 collective-permute-start.12
  100.9 21.9 %collective-permute-done.7.refs_4_ = bf16[400,1536]{1,0:T(8,128)(2,1)S(1)} collective-permute-done((bf16[400,1536]{1,0:T(8,128)(2,1)S(1)}, bf16[400,1536]{1,0:T(8,128)(2,1)S(1)}, u32[]{:S(2)}, u32[]{:S(2)}) %collective-permute-start.7) | collective-permute-done | bytes 1228832 | tf_op jit(solution)/shard_map/ppermute | solution.py:329
  122.8 1.3 collective-permute-start.9
  124.0 0.9 slice_select_fusion.2
  125.0 49.2 %collective-permute-done.9.refs_6_ = bf16[400,1536]{1,0:T(8,128)(2,1)S(1)} collective-permute-done((bf16[400,1536]{1,0:T(8,128)(2,1)S(1)}, bf16[400,1536]{1,0:T(8,128)(2,1)S(1)}, u32[]{:S(2)}, u32[]{:S(2)}) %collective-permute-start.9) | collective-permute-done | bytes 1228832 | tf_op jit(solution)/shard_map/ppermute | solution.py:329
  174.2 0.8 slice_select_fusion.1
  175.2 4.5 %collective-permute-start.10 = (f32[1536]{0:T(1024)S(1)}, f32[1536]{0:T(1024)S(1)}, u32[]{:S(2)}, u32[]{:S(2)}) collective-permute-start(f32[1536]{0:T(1024)S(1)} %pad_maximum_fusion.4), channel_id=1, source_target_pairs={{4,0},{8,4},{12,8},{16,12},{20,16},{24,20},{28,24},{5,1},{9,5},{13... | collective-permute-start | bytes 18440 | tf_op jit(solution)/shard_map/ppermute | solution.py:320
  179.8 0.7 collective-permute-done.10
  180.5 0.6 divide_convert_fusion.2
  181.2 1.5 collective-permute-start.11
  182.6 3.4 %multiply_convert_fusion.prev_whole = bf16[1536,1536]{1,0:T(8,128)(2,1)} fusion(bf16[1536,1536]{1,0:T(8,128)(2,1)S(1)} %pad_maximum_fusion, f32[1536]{0:T(1024)S(1)} %divide_reduce_fusion), kind=kLoop, calls=%fused_computation | loop fusion | flops 7077888 | bytes 9443328 | tf_op jit(solution)/shard_map/convert_element_type | solution.py:34
  186.0 21.0 %shard_map.60 = (bf16[1536,1536]{1,0:T(8,128)(2,1)}, f32[384,1536]{1,0:T(8,128)S(1)}, f32[384,1536]{1,0:T(8,128)S(1)}, bf16[1536,1536]{1,0:T(8,128)(2,1)}, bf16[...) custom-call(s32[3]{0:T(128)S(1)} %pad_add_fusion.flags, bf16[1536,1536]{1,0:T(8,128)(2,1)} %multiply_convert_fusion.prev_whole, ...), custom_call_target="tpu_custom_call" | custom-call | tf_op jit(solution)/shard_map/pallas_call | solution.py:152
  207.2 7.5 %shard_map.61 = (bf16[384,1536]{1,0:T(8,128)(2,1)S(1)}, f32[8,1536]{1,0:T(8,128)S(1)}, f32[8,1536]{1,0:T(8,128)S(1)}) custom-call(s32[3]{0:T(128)S(1)} %pad_add_fusion.flags, bf16[1536,1536]{1,0:T(8,128)(2,1)} %get-tuple-element.24.link, bf16[384,1536]{1,0:T(8,128)(2,1)S(1)} %get-tuple-element.21.mine, bf16[8,1536]{1,0:T(8,128)(2,1)S(1)} %broadcast_in_dim.23.scale, ...), custom_call_target="tpu_custom_call" | custom-call | tf_op jit(solution)/shard_map/pallas_call | solution.py:287
  214.8 7.2 %shard_map.62 = (bf16[384,1536]{1,0:T(8,128)(2,1)S(1)}, bf16[384,384]{1,0:T(8,128)(2,1)S(1)}, bf16[384,384]{1,0:T(8,128)(2,1)S(1)}, f32[8,384]{1,0:T(8,128)S(1)}, f32[8,1536]{1,0:T(8,128)S(1)}) custom-call(s32[3]{0:T(128)S(1)} %pad_add_fusion.flags, f32[8,1536]{1,0:T(8,128)S(1)} %copy-done.9, bf16[384,1536]{1,0:T(8,128)(2,1)S(1)} %bitcast.31, ...), custom_call_target="tpu_custom_call" | custom-call | tf_op jit(solution)/shard_map/pallas_call | solution.py:223
  222.0 1.2 constant_dynamic-update-slice_fusion.1
  223.2 1.3 collective-permute-start.14
  224.5 1.7 collective-permute-start.18
  226.2 6.8 %collective-permute-start.20 = (bf16[384,1536]{1,0:T(8,128)(2,1)S(1)}, bf16[384,1536]{1,0:T(8,128)(2,1)}, u32[]{:S(2)}, u32[]{:S(2)}) collective-permute-start(bf16[384,1536]{1,0:T(8,128)(2,1)S(1)} %constant_dynamic-update-slice_fusion), channel_id=1, source_target_pairs={{4,0},{12,8},{20,16},{28,24},{5,1},{13,9},{21,17},{29,25},{6,2},{1... | collective-permute-start | bytes 3538952 | tf_op jit(solution)/shard_map/ppermute | solution.py:320
  233.0 0.3 dynamic_update_slice.14
  233.3 0.7 collective-permute-start.15
  234.1 0.6 fusion.35
  234.7 1.5 multiply_convert_fusion.4
  236.1 5.4 %fusion = bf16[384,1536]{1,0:T(8,128)(2,1)} fusion(bf16[384,1536]{1,0:T(8,128)(2,1)S(1)} %multiply_convert_fusion.4, bf16[1536,1536]{1,0:T(8,128)(2,1)} %constant_dynamic-update-slice_fusion.1), kind=kOutput, calls=%fused_computation.9 | convolution fusion | flops 1813118976 | bytes 7077888 | tf_op jit(solution)/shard_map/dot_general | solution.py:46
  241.5 1.5 collective-permute-start.16
  243.0 4.7 %fusion.3 = bf16[384,1536]{1,0:T(8,128)(2,1)S(1)} fusion(bf16[1536,1536]{1,0:T(8,128)(2,1)} %constant_dynamic-update-slice_fusion.1, bf16[384,1536]{1,0:T(8,128)(2,1)} %fusion, f32[1536]{0:T(1024)S(1)} %get-tuple-element.34, f32[1536]{0:T(1024)S(1)} %get-tuple-element.39), kind=kOutput, calls=%fused_computation.12 | convolution fusion | flops 1814888448 | bytes 7090176 | tf_op jit(solution)/shard_map/dot_general | solution.py:42
  247.8 5.4 %fusion.1.refs_1_ = bf16[384,1536]{1,0:T(8,128)(2,1)} fusion(bf16[384,1536]{1,0:T(8,128)(2,1)S(1)} %fusion.3, bf16[1536,1536]{1,0:T(8,128)(2,1)} %collective-permute-done.14), kind=kOutput, calls=%fused_computation.10 | convolution fusion | flops 1813118976 | bytes 7077888 | tf_op jit(solution)/shard_map/dot_general | solution.py:42
  253.2 1.7 collective-permute-start.21
  254.9 1.3 collective-permute-start.17
  256.2 0.6 broadcast_in_dim.28.refs_0_
  256.8 1.2 slice.232
  258.6 2.4 broadcast_select_fusion
  261.0 1.7 collective-permute-start.19
  262.7 16.9 %collective-permute-done.17 = bf16[1536]{0:T(1024)(128)(2,1)S(1)} collective-permute-done((bf16[1536]{0:T(1024)(128)(2,1)}, bf16[1536]{0:T(1024)(128)(2,1)S(1)}, u32[]{:S(2)}, u32[]{:S(2)}) %collective-permute-start.17) | collective-permute-done | bytes 3104 | tf_op jit(solution)/shard_map/ppermute | solution.py:320
  279.6 1.0 copy-done.14
  280.6 0.7 convert_element_type.222
  281.5 4.5 %fusion.2 = bf16[384,1536]{1,0:T(8,128)(2,1)S(1)} fusion(bf16[384,1536]{1,0:T(8,128)(2,1)S(1)} %multiply_convert_fusion.2, bf16[1536,1536]{1,0:T(8,128)(2,1)} %collective-permute-done.14), kind=kOutput, calls=%fused_computation.11 | convolution fusion | flops 1813118976 | bytes 7077888 | tf_op jit(solution)/shard_map/dot_general | solution.py:42
  286.0 0.5 multiply_convert_fusion.1
  286.5 5.7 %convolution_multiply_fusion = f32[768,1536]{1,0:T(8,128)S(1)} fusion(bf16[768,1536]{1,0:T(8,128)(2,1)S(1)} %multiply_convert_fusion.1, bf16[1536,1536]{1,0:T(8,128)(2,1)} %collective-permute-done.14, f32[1536]{0:T(1024)S(1)} %convert_element_type.222), kind=kOutput, calls=%fused_computation.3 | convolution fusion | flops 3625058304 | bytes 11802624 | tf_op jit(solution)/shard_map/dot_general | solution.py:46
  292.3 0.4 fusion.4
  292.9 5.7 %fusion.41 = f32[768,1536]{1,0:T(8,128)S(1)} fusion(bf16[768,1536]{1,0:T(8,128)(2,1)S(1)} %pad_maximum_fusion.1, bf16[1536,1536]{1,0:T(8,128)(2,1)} %constant_dynamic-update-slice_fusion.1), kind=kOutput, calls=%fused_computation.108 | convolution fusion | flops 3623878656 | bytes 11796480 | tf_op jit(solution)/shard_map/dot_general | solution.py:46
  298.6 3.2 %fusion.9 = bf16[1,384,1536]{2,1,0:T(8,128)(2,1)} fusion(f32[768,1536]{1,0:T(8,128)S(1)} %fusion.41, bf16[384,1536]{1,0:T(8,128)(2,1)} %fusion, bf16[1536,1536]{1,0:T(8,128)(2,1)} %constant_dynamic-update-slice_fusion.1, s32[]{:T(128)S(6)} %select_n.234, pred[]{:T(512)S(6)} %eq.32, pred[]{:T(512)S(6)} %eq.31), kind=kLoop, calls=%fused_computation.28 | loop fusion | flops 1179648 | bytes 4718598 | tf_op jit(solution)/shard_map/broadcast_in_dim | solution.py:442
  301.8 4.7 %fusion.7 = f32[1,384,1536]{2,1,0:T(8,128)} fusion(f32[384,1536]{1,0:T(8,128)S(1)} %copy-done.6, f32[768,1536]{1,0:T(8,128)S(1)} %fusion.41, bf16[384,1536]{1,0:T(8,128)(2,1)} %collective-permute-done.21, bf16[384,1536]{1,0:T(8,128)(2,1)} %collective-permute-done.20, bf16[384,1536]{1,0:T(8,128)(2,1)} %collective-permute-done.18, ...), kind=kLoop, calls=%fused_computation.18 | loop fusion | flops 5308416 | bytes 11796481 | tf_op jit(solution)/shard_map/broadcast_in_dim | solution.py:442
  (84 shorter events, 1.5 us)
Async XLA Ops:
  1.5 6.8 %copy-start.8 = (f32[8,1536]{1,0:T(8,128)}, f32[8,1536]{1,0:T(8,128)S(1)}, u32[]{:S(2)}) copy-start(f32[8,1536]{1,0:T(8,128)S(1)} %broadcast_in_dim.22.reciprocal) | copy-start | bytes 147460
  1.5 1.3 copy-start
  2.7 1.7 copy-start.2
  8.3 55.4 %copy-start.7 = (bf16[400,1536]{1,0:T(8,128)(2,1)}, bf16[400,1536]{1,0:T(8,128)(2,1)S(1)}, u32[]{:S(2)}) copy-start(bf16[400,1536]{1,0:T(8,128)(2,1)S(1)} %shard_map.59) | copy-start | bytes 3686404
  8.3 28.9 %collective-permute-start = (bf16[400,1536]{1,0:T(8,128)(2,1)S(1)}, bf16[400,1536]{1,0:T(8,128)(2,1)S(1)}, u32[]{:S(2)}, u32[]{:S(2)}) collective-permute-start(bf16[400,1536]{1,0:T(8,128)(2,1)S(1)} %shard_map.59), channel_id=1, source_target_pairs={{0,1},{1,2},{2,3},{4,5},{5,6},{6,7},{8,9},{9,10},{10,11},{12,13},{... | collective-permute-start | bytes 3686408 | tf_op jit(solution)/shard_map/ppermute | solution.py:329
  11.6 51.0 %collective-permute-start.4 = (bf16[384,1536]{1,0:T(8,128)(2,1)}, bf16[384,1536]{1,0:T(8,128)(2,1)S(1)}, u32[]{:S(2)}, u32[]{:S(2)}) collective-permute-start(bf16[384,1536]{1,0:T(8,128)(2,1)} %bitcast.3.own.plain_rows.refs_0_), channel_id=1, source_target_pairs={{0,1},{1,2},{2,3},{4,5},{5,6},{6,7},{8,9},{9,10},{10,11},{12,13},{... | collective-permute-start | bytes 3538952 | tf_op jit(solution)/shard_map/ppermute | solution.py:329
  14.8 50.6 %collective-permute-start.2 = (bf16[400,1536]{1,0:T(8,128)(2,1)S(1)}, bf16[400,1536]{1,0:T(8,128)(2,1)S(1)}, u32[]{:S(2)}, u32[]{:S(2)}) collective-permute-start(bf16[400,1536]{1,0:T(8,128)(2,1)S(1)} %shard_map.59), channel_id=1, source_target_pairs={{1,0},{2,1},{3,2},{5,4},{6,5},{7,6},{9,8},{10,9},{11,10},{13,12},{... | collective-permute-start | bytes 3686408 | tf_op jit(solution)/shard_map/ppermute | solution.py:329
  16.1 55.1 %collective-permute-start.5 = (bf16[384,1536]{1,0:T(8,128)(2,1)}, bf16[384,1536]{1,0:T(8,128)(2,1)S(1)}, u32[]{:S(2)}, u32[]{:S(2)}) collective-permute-start(bf16[384,1536]{1,0:T(8,128)(2,1)} %bitcast.3.own.plain_rows.refs_0_), channel_id=1, source_target_pairs={{1,0},{2,1},{3,2},{5,4},{6,5},{7,6},{9,8},{10,9},{11,10},{13,12},{... | collective-permute-start | bytes 3538952 | tf_op jit(solution)/shard_map/ppermute | solution.py:329
  37.2 29.6 %copy-start.12 = (bf16[400,1536]{1,0:T(8,128)(2,1)}, bf16[400,1536]{1,0:T(8,128)(2,1)S(1)}, u32[]{:S(2)}) copy-start(bf16[400,1536]{1,0:T(8,128)(2,1)S(1)} %collective-permute-done) | copy-start | bytes 3686404
  63.7 9.0 %collective-permute-start.6 = (bf16[400,1536]{1,0:T(8,128)(2,1)}, bf16[400,1536]{1,0:T(8,128)(2,1)}, u32[]{:S(2)}, u32[]{:S(2)}) collective-permute-start(bf16[400,1536]{1,0:T(8,128)(2,1)} %pad_maximum_fusion.2), channel_id=1, source_target_pairs={{1,2},{2,3},{5,6},{6,7},{9,10},{10,11},{13,14},{14,15},{17,18},{18... | collective-permute-start | bytes 3686408 | tf_op jit(solution)/shard_map/ppermute | solution.py:329
  65.3 2.5 copy-start.10
  65.4 31.1 %collective-permute-start.3 = (bf16[384,1536]{1,0:T(8,128)(2,1)S(1)}, bf16[384,1536]{1,0:T(8,128)(2,1)}, u32[]{:S(2)}, u32[]{:S(2)}) collective-permute-start(bf16[384,1536]{1,0:T(8,128)(2,1)S(1)} %slice.235), channel_id=1, source_target_pairs={{1,0},{2,1},{5,4},{6,5},{9,8},{10,9},{13,12},{14,13},{17,16},{18,1... | collective-permute-start | bytes 3538952 | tf_op jit(solution)/shard_map/ppermute | solution.py:329
  67.8 28.7 %collective-permute-start.1 = (bf16[384,1536]{1,0:T(8,128)(2,1)}, bf16[384,1536]{1,0:T(8,128)(2,1)}, u32[]{:S(2)}, u32[]{:S(2)}) collective-permute-start(bf16[384,1536]{1,0:T(8,128)(2,1)} %slice.234), channel_id=1, source_target_pairs={{1,2},{2,3},{5,6},{6,7},{9,10},{10,11},{13,14},{14,15},{17,18},{18... | collective-permute-start | bytes 3538952 | tf_op jit(solution)/shard_map/ppermute | solution.py:329
  69.5 1.6 slice-start
  69.5 27.0 %copy-start.13 = (bf16[400,1536]{1,0:T(8,128)(2,1)S(1)}, bf16[400,1536]{1,0:T(8,128)(2,1)}, u32[]{:S(2)}) copy-start(bf16[400,1536]{1,0:T(8,128)(2,1)} %copy-done.12) | copy-start | bytes 3686404
  71.1 25.4 %copy-start.1 = (bf16[1,384,1536]{2,1,0:T(8,128)(2,1)S(1)}, bf16[1,384,1536]{2,1,0:T(8,128)(2,1)}, u32[]{:S(2)}) copy-start(bf16[1,384,1536]{2,1,0:T(8,128)(2,1)} %param.6) | copy-start | bytes 3538948
  71.1 25.4 %copy-start.11 = (bf16[400,1536]{1,0:T(8,128)(2,1)S(1)}, bf16[400,1536]{1,0:T(8,128)(2,1)}, u32[]{:S(2)}) copy-start(bf16[400,1536]{1,0:T(8,128)(2,1)} %copy-done.10) | copy-start | bytes 3686404
  71.2 51.5 %collective-permute-start.7 = (bf16[400,1536]{1,0:T(8,128)(2,1)S(1)}, bf16[400,1536]{1,0:T(8,128)(2,1)S(1)}, u32[]{:S(2)}, u32[]{:S(2)}) collective-permute-start(bf16[400,1536]{1,0:T(8,128)(2,1)S(1)} %pad_maximum_fusion.3), channel_id=1, source_target_pairs={{1,0},{2,1},{5,4},{6,5},{9,8},{10,9},{13,12},{14,13},{17,16},{18,1... | collective-permute-start | bytes 3686408 | tf_op jit(solution)/shard_map/ppermute | solution.py:329
  72.7 51.4 %collective-permute-start.8 = (bf16[400,1536]{1,0:T(8,128)(2,1)}, bf16[400,1536]{1,0:T(8,128)(2,1)S(1)}, u32[]{:S(2)}, u32[]{:S(2)}) collective-permute-start(bf16[400,1536]{1,0:T(8,128)(2,1)} %collective-permute-done.6.refs_3_), channel_id=1, source_target_pairs={{2,3},{6,7},{10,11},{14,15},{18,19},{22,23},{26,27},{30,31}} | collective-permute-start | bytes 3686408 | tf_op jit(solution)/shard_map/ppermute | solution.py:329
  98.8 115.9 %collective-permute-start.13 = (bf16[384,1536]{1,0:T(8,128)(2,1)}, bf16[384,1536]{1,0:T(8,128)(2,1)S(1)}, u32[]{:S(2)}, u32[]{:S(2)}) collective-permute-start(bf16[384,1536]{1,0:T(8,128)(2,1)} %collective-permute-done.3), channel_id=1, source_target_pairs={{1,0},{5,4},{9,8},{13,12},{17,16},{21,20},{25,24},{29,28}} | collective-permute-start | bytes 3538952 | tf_op jit(solution)/shard_map/ppermute | solution.py:329
  100.1 114.7 %collective-permute-start.12 = (bf16[384,1536]{1,0:T(8,128)(2,1)}, bf16[384,1536]{1,0:T(8,128)(2,1)S(1)}, u32[]{:S(2)}, u32[]{:S(2)}) collective-permute-start(bf16[384,1536]{1,0:T(8,128)(2,1)} %collective-permute-done.1), channel_id=1, source_target_pairs={{2,3},{6,7},{10,11},{14,15},{18,19},{22,23},{26,27},{30,31}} | collective-permute-start | bytes 3538952 | tf_op jit(solution)/shard_map/ppermute | solution.py:329
  122.8 51.5 %collective-permute-start.9 = (bf16[400,1536]{1,0:T(8,128)(2,1)S(1)}, bf16[400,1536]{1,0:T(8,128)(2,1)S(1)}, u32[]{:S(2)}, u32[]{:S(2)}) collective-permute-start(bf16[400,1536]{1,0:T(8,128)(2,1)S(1)} %collective-permute-done.7.refs_4_), channel_id=1, source_target_pairs={{1,0},{5,4},{9,8},{13,12},{17,16},{21,20},{25,24},{29,28}} | collective-permute-start | bytes 3686408 | tf_op jit(solution)/shard_map/ppermute | solution.py:329
  175.2 5.3 %collective-permute-start.10 = (f32[1536]{0:T(1024)S(1)}, f32[1536]{0:T(1024)S(1)}, u32[]{:S(2)}, u32[]{:S(2)}) collective-permute-start(f32[1536]{0:T(1024)S(1)} %pad_maximum_fusion.4), channel_id=1, source_target_pairs={{4,0},{8,4},{12,8},{16,12},{20,16},{24,20},{28,24},{5,1},{9,5},{13... | collective-permute-start | bytes 18440 | tf_op jit(solution)/shard_map/ppermute | solution.py:320
  181.2 25.9 %collective-permute-start.11 = (f32[1536]{0:T(1024)S(1)}, f32[1536]{0:T(1024)S(1)}, u32[]{:S(2)}, u32[]{:S(2)}) collective-permute-start(f32[1536]{0:T(1024)S(1)} %get-tuple-element.38), channel_id=1, source_target_pairs={{0,4},{8,12},{16,20},{24,28},{1,5},{9,13},{17,21},{25,29},{2,6},{1... | collective-permute-start | bytes 18440 | tf_op jit(solution)/shard_map/ppermute | solution.py:320
  182.6 3.4 %copy-start.3 = (f32[1,384,1536]{2,1,0:T(8,128)S(1)}, f32[1,384,1536]{2,1,0:T(8,128)}, u32[]{:S(2)}) copy-start(f32[1,384,1536]{2,1,0:T(8,128)} %param.4) | copy-start | bytes 7077892
  207.1 7.6 %copy-start.5 = (f32[384,1536]{1,0:T(8,128)}, f32[384,1536]{1,0:T(8,128)S(1)}, u32[]{:S(2)}) copy-start(f32[384,1536]{1,0:T(8,128)S(1)} %get-tuple-element.19) | copy-start | bytes 7077892
  207.1 7.6 %copy-start.16 = (bf16[1536]{0:T(1024)(128)(2,1)}, bf16[1536]{0:T(1024)(128)(2,1)S(1)}, u32[]{:S(2)}) copy-start(bf16[1536]{0:T(1024)(128)(2,1)S(1)} %get-tuple-element.40.refs_0_) | copy-start | bytes 9220
  207.1 7.6 %copy-start.4 = (bf16[1536,1536]{1,0:T(8,128)(2,1)S(1)}, bf16[1536,1536]{1,0:T(8,128)(2,1)}, u32[]{:S(2)}) copy-start(bf16[1536,1536]{1,0:T(8,128)(2,1)} %get-tuple-element.22.own) | copy-start | bytes 14155780
  207.2 7.6 %copy-start.9 = (f32[8,1536]{1,0:T(8,128)S(1)}, f32[8,1536]{1,0:T(8,128)}, u32[]{:S(2)}) copy-start(f32[8,1536]{1,0:T(8,128)} %copy-done.8) | copy-start | bytes 147460
  222.0 12.1 %copy-start.17 = (f32[1536]{0:T(1024)S(1)}, f32[1536]{0:T(1024)}, u32[]{:S(2)}) copy-start(f32[1536]{0:T(1024)} %get-tuple-element.37) | copy-start | bytes 18436
  223.2 11.5 %collective-permute-start.14 = (bf16[1536,1536]{1,0:T(8,128)(2,1)}, bf16[1536,1536]{1,0:T(8,128)(2,1)}, u32[]{:S(2)}, u32[]{:S(2)}) collective-permute-start(bf16[1536,1536]{1,0:T(8,128)(2,1)} %constant_dynamic-update-slice_fusion.1), channel_id=1, source_target_pairs={{0,4},{8,12},{16,20},{24,28},{1,5},{9,13},{17,21},{25,29},{2,6},{1... | collective-permute-start | bytes 14155784 | tf_op jit(solution)/shard_map/ppermute | solution.py:320
  224.5 34.1 %collective-permute-start.18 = (bf16[384,1536]{1,0:T(8,128)(2,1)S(1)}, bf16[384,1536]{1,0:T(8,128)(2,1)}, u32[]{:S(2)}, u32[]{:S(2)}) collective-permute-start(bf16[384,1536]{1,0:T(8,128)(2,1)S(1)} %constant_dynamic-update-slice_fusion), channel_id=1, source_target_pairs={{8,4},{24,20},{16,0},{9,5},{25,21},{17,1},{10,6},{26,22},{18,2},{1... | collective-permute-start | bytes 3538952 | tf_op jit(solution)/shard_map/ppermute | solution.py:320
  226.2 75.6 %collective-permute-start.20 = (bf16[384,1536]{1,0:T(8,128)(2,1)S(1)}, bf16[384,1536]{1,0:T(8,128)(2,1)}, u32[]{:S(2)}, u32[]{:S(2)}) collective-permute-start(bf16[384,1536]{1,0:T(8,128)(2,1)S(1)} %constant_dynamic-update-slice_fusion), channel_id=1, source_target_pairs={{4,0},{12,8},{20,16},{28,24},{5,1},{13,9},{21,17},{29,25},{6,2},{1... | collective-permute-start | bytes 3538952 | tf_op jit(solution)/shard_map/ppermute | solution.py:320
  233.3 0.8 collective-permute-start.15
  241.5 38.1 %collective-permute-start.16 = (bf16[384,1536]{1,0:T(8,128)(2,1)}, bf16[384,1536]{1,0:T(8,128)(2,1)S(1)}, u32[]{:S(2)}, u32[]{:S(2)}) collective-permute-start(bf16[384,1536]{1,0:T(8,128)(2,1)} %fusion), channel_id=1, source_target_pairs={{20,28},{21,29},{22,30},{23,31}} | collective-permute-start | bytes 3538952 | tf_op jit(solution)/shard_map/ppermute | solution.py:320
  253.2 48.7 %collective-permute-start.21 = (bf16[384,1536]{1,0:T(8,128)(2,1)}, bf16[384,1536]{1,0:T(8,128)(2,1)}, u32[]{:S(2)}, u32[]{:S(2)}) collective-permute-start(bf16[384,1536]{1,0:T(8,128)(2,1)} %fusion.1.refs_1_), channel_id=1, source_target_pairs={{20,12},{21,13},{22,14},{23,15}} | collective-permute-start | bytes 3538952 | tf_op jit(solution)/shard_map/ppermute | solution.py:320
  254.9 24.7 %collective-permute-start.17 = (bf16[1536]{0:T(1024)(128)(2,1)}, bf16[1536]{0:T(1024)(128)(2,1)S(1)}, u32[]{:S(2)}, u32[]{:S(2)}) collective-permute-start(bf16[1536]{0:T(1024)(128)(2,1)} %shard_map.64), channel_id=1, source_target_pairs={{4,12},{20,28},{5,13},{21,29},{6,14},{22,30},{7,15},{23,31}} | collective-permute-start | bytes 9224 | tf_op jit(solution)/shard_map/ppermute | solution.py:320
  261.0 40.8 %collective-permute-start.19 = (bf16[384,1536]{1,0:T(8,128)(2,1)}, bf16[384,1536]{1,0:T(8,128)(2,1)}, u32[]{:S(2)}, u32[]{:S(2)}) collective-permute-start(bf16[384,1536]{1,0:T(8,128)(2,1)} %broadcast_select_fusion), channel_id=1, source_target_pairs={{0,12},{1,13},{2,14},{3,15}} | collective-permute-start | bytes 3538952 | tf_op jit(solution)/shard_map/ppermute | solution.py:320
  279.6 1.0 copy-start.14
  281.5 4.5 %copy-start.15 = (bf16[384,1536]{1,0:T(8,128)(2,1)S(1)}, bf16[384,1536]{1,0:T(8,128)(2,1)}, u32[]{:S(2)}) copy-start(bf16[384,1536]{1,0:T(8,128)(2,1)} %copy-done.14) | copy-start | bytes 3538948
  298.6 3.3 %copy-start.6 = (f32[384,1536]{1,0:T(8,128)S(1)}, f32[384,1536]{1,0:T(8,128)}, u32[]{:S(2)}) copy-start(f32[384,1536]{1,0:T(8,128)} %copy-done.5) | copy-start | bytes 7077892
where the time goes:
time: 308 us; the launch traced here: 307 us
  waiting for transfers between devices  157 us (51%)
  starting transfers between devices  41.7 us (14%)
  Pallas kernels  39.5 us (13%)
  matrix products  31.4 us (10%)
  other arithmetic  26.2 us (9%)
  local copies, waits for them, and re-layouts  8.87 us (3%)
    ppermute x12, waiting for transfers between devices, one_step(): return (lax.ppermute(ahead, 'space', up), lax.ppermute(back, 'space', down))  139 us
    ppermute x10, starting transfers between devices, between(): lax.ppermute(block, 'tm', [(a, b) for a, b in route if 0 <= b < parts])  22.5 us
    pallas_call x1, Pallas kernels, early_forms(): pl.pallas_call(functools.partial(early_kernel, size), out_shape=[SHAPE((o...  21 us
    ppermute x12, starting transfers between devices, one_step(): return (lax.ppermute(ahead, 'space', up), lax.ppermute(back, 'space', down))  19.2 us
    ppermute x10, waiting for transfers between devices, between(): lax.ppermute(block, 'tm', [(a, b) for a, b in route if 0 <= b < parts])  17.6 us
    dot_general x3, matrix products, dot_nn(): lax.dot_general(left, right, (((1,), (0,)), ((), ())), preferred_element_...  16.7 us
    dot_general x3, matrix products, dot_nt(): lax.dot_general(left, right, (((1,), (1,)), ((), ())), preferred_element_...  14.6 us
    convert_element_type x9, other arithmetic, scaled_by(): return (matrix.astype(F32) * factors.astype(F32)[None, :]).astype(BF16)  8.39 us
  transfers between devices with their start and end apart: 22, of which 7 were waited for; matrix products, arithmetic and copies ran while one was open for 18% of the time, Pallas kernels for 9%

commit v1 on v0

--- a/solution.py
+++ b/solution.py
@@ -55,7 +55,7 @@
 
 
 def whole_spec(shape):
-    return pl.BlockSpec(shape, lambda j, f: (0,) * len(shape))
+    return pl.BlockSpec(shape, lambda j, f: (0,) * len(shape), pipeline_mode=pl.Buffered(1))
 
 
 def along_spec(count):
@@ -89,7 +89,7 @@
             total = jnp.where(ids == at, word.astype(F32), total)
         return total.astype(BF16)
 
-    long[0:rows, :] = prev[...]
+    long[0:rows, :] = own[...]
     high, low = split(jnp.sum(on_diagonal, axis=0, keepdims=True))
     long[rows:, :] = placed({0: high, 1: low}, order)
     own_high, own_low = split(form_diagonal(own[...]))
@@ -114,9 +114,9 @@
     )(flags, own, prev, separator, reciprocal)
 
 
-def early_kernel(size, flags, prev_whole, prev_rows, own_rows, separator, plain_rows, *refs):
+def early_kernel(size, flags, prev_whole, prev_rows, own_rows, separator, *refs):
     sources = refs[: 2 * size - 1]
-    link, partial, form, own_out, across, mine, own, sems = refs[2 * size - 1 :]
+    link, partial, form, own_out, mine, own, sems = refs[2 * size - 1 :]
     rows = separator.shape[0]
     step = pl.program_id(0)
     here = pl.ds(pl.multiple_of(step * WIDTH, WIDTH), WIDTH)
@@ -141,12 +141,10 @@
     link[...] = jnp.where(flags[0] == 1, 0.0, -dot_nt(prev_whole[...], block)).astype(BF16)
     mine[...] = link[pl.ds(pl.multiple_of(flags[1] * rows, rows), rows), :]
     partial[...] = separator[...] - dot_nt(own_rows[...], block)
-    prev_block = prev_whole[here, :]
-    form[...] = dot_nt(prev_rows[...], prev_block)
-    across[...] = jnp.where(flags[0] == 1, 0.0, -dot_nt(plain_rows[...], prev_block)).astype(BF16)
-
-
-def early_forms(flags, prev_whole, prev_rows, own_rows, separator, plain_rows, sources):
+    form[...] = dot_nt(prev_rows[...], prev_whole[here, :])
+
+
+def early_forms(flags, prev_whole, prev_rows, own_rows, separator, sources):
     rows, order = own_rows.shape
     size = order // rows
     return pl.pallas_call(
@@ -157,7 +155,6 @@
             SHAPE((rows, order), F32),
             SHAPE((order, order), BF16),
             SHAPE((rows, order), BF16),
-            SHAPE((rows, order), BF16),
         ],
         grid_spec=pltpu.PrefetchScalarGridSpec(
             num_scalar_prefetch=1,
@@ -167,15 +164,14 @@
                 whole_spec((rows, order)),
                 whole_spec((rows, order)),
                 along_spec(rows),
-                whole_spec((rows, order)),
             ]
             + [ANY] * len(sources),
-            out_specs=[along_spec(order), along_spec(rows), along_spec(rows), down_spec(order), along_spec(rows), along_spec(rows)],
+            out_specs=[along_spec(order), along_spec(rows), along_spec(rows), down_spec(order), along_spec(rows)],
             scratch_shapes=[pltpu.VMEM((order, order), BF16), pltpu.SemaphoreType.DMA((size,))],
         ),
-        compiler_params=pltpu.CompilerParams(vmem_limit_bytes=32 * 1024 * 1024),
+        compiler_params=pltpu.CompilerParams(vmem_limit_bytes=26 * 1024 * 1024),
         cost_estimate=FREE,
-    )(flags, prev_whole, prev_rows, own_rows, separator, plain_rows, *sources)
+    )(flags, prev_whole, prev_rows, own_rows, separator, *sources)
 
 
 def late_kernel(
@@ -258,7 +254,7 @@
                 pltpu.SemaphoreType.DMA,
             ],
         ),
-        compiler_params=pltpu.CompilerParams(vmem_limit_bytes=24 * 1024 * 1024),
+        compiler_params=pltpu.CompilerParams(vmem_limit_bytes=18 * 1024 * 1024),
     )(
         flags, reciprocal, prev_rows, plain_rows, mine, own, scale, late_scale, from_below, from_above, far,
         ready,
@@ -299,7 +295,7 @@
             ],
             out_specs=[along(rows), along(8), whole_spec((8, order))],
         ),
-        compiler_params=pltpu.CompilerParams(vmem_limit_bytes=24 * 1024 * 1024),
+        compiler_params=pltpu.CompilerParams(vmem_limit_bytes=18 * 1024 * 1024),
         cost_estimate=FREE,
     )(flags, link, mine, scale, pivot_scale, form)
 
@@ -337,25 +333,18 @@
                 block = jnp.where(place == spot - step, arrived[step][1], block)
         return block
 
-    own_arrived = [(own_rows, own_rows)]
-    own_arrived.append(one_step(own_rows, own_rows, 1))
-
     is_first = partition == 0
     is_pivot = partition % 2 == 0
     is_receiver = partition % 2 == 1
     is_last = partition % 4 == 3
     flags = jnp.stack([is_first.astype(jnp.int32), place, is_pivot.astype(jnp.int32)])
-    prev_long = opening(flags, own_rows, prev_rows, separator, rows_of(reciprocal))
-    words = prev_long[rows:]
-    prev_long = one_step(prev_long, prev_long, 1)
-    prev_arrived = [(prev_rows, prev_rows), tuple(block[:rows] for block in prev_long)]
-    words_arrived = [(words, words), tuple(block[rows:] for block in prev_long)]
-    own_long = [jnp.concatenate(pair) for pair in zip(own_arrived[1], words_arrived[1])]
-    for step in range(2, size):
+    own_long = opening(flags, own_rows, prev_rows, separator, rows_of(reciprocal))
+    own_arrived = [(own_long, own_long)]
+    prev_arrived = [(prev_rows, prev_rows)]
+    for step in range(1, size):
+        own_arrived.append(one_step(*own_arrived[-1], step))
         prev_arrived.append(one_step(*prev_arrived[-1], step))
-        own_long = one_step(*own_long, step)
-        own_arrived.append(own_long)
-        words_arrived.append(tuple(block[rows:] for block in own_long))
+    words_arrived = [tuple(block[rows:] for block in pair) for pair in own_arrived]
 
     left_side = place < size // 2
     late_start = jnp.where(left_side, size - 1, 0) * rows
@@ -375,17 +364,19 @@
     part_diag = sum(pair_sum(block, 0) for block in words)
     part_diag = part_diag - jnp.concatenate([pair_sum(block, 2)[:rows] for block in words])
     prev_diag = jnp.concatenate([pair_sum(block, 4)[:rows] for block in words])
+    part_diag, prev_diag = lax.optimization_barrier((part_diag, prev_diag))
     diag = part_diag - between(prev_diag, [(p, p - 1) for p in everyone])
     pivot_diag = between(part_diag, [(p, p + 1) for p in even]) - prev_diag
     scale = (1.0 / jnp.maximum(diag, 1.0)).astype(BF16)
     pivot_scale = (1.0 / jnp.maximum(pivot_diag, 1.0)).astype(BF16)
 
     own_scaled = scaled_by(own_rows, reciprocal)
-    sources = [own_rows]
+    sources = [own_long]
     for up, down in own_arrived[1:]:
         sources += [up, down]
-    link, partial, prev_form, own_full, across, mine = early_forms(
-        flags, scaled_by(prev_first, reciprocal), prev_rows, own_scaled, separator, own_rows, sources
+    prev_first = scaled_by(prev_first, reciprocal)
+    link, partial, prev_form, own_full, mine = early_forms(
+        flags, prev_first, prev_rows, own_scaled, separator, sources
     )
     scale8, pivot_scale8 = rows_of(scale), rows_of(pivot_scale)
     update, left_diag, right_diag = level_forms(flags, link, mine, scale8, pivot_scale8, prev_form)
@@ -407,7 +398,6 @@
     from_even = between(
         update, [(p, p - 1) for p in range(2, parts, 4)] + [(p, p - 4) for p in range(4, parts, 4)]
     )
-    from_odd = between(update, [(p, p - 1) for p in range(1, parts, 2)])
     next_diag = diag - left_diag - right_diag
     next_scale = (1.0 / jnp.maximum(next_diag, 1.0)).astype(BF16)
     pivot_rows = lax.dynamic_slice_in_dim(pivot_link, row_start, rows, 0)
@@ -423,8 +413,13 @@
     next_pivot_scale = between(after(next_scale, left_next), [(p, p + 2) for p in pivots])
     go_on = after(jnp.ones((8, 128), jnp.int32), left_next)[0, 0] == 1
     passed_on = jnp.where(go_on, from_even, jnp.zeros_like(from_even))
+    own_update = jnp.where(go_on, update, jnp.zeros_like(update))
+    from_odd = between(own_update, [(p, p - 1) for p in range(1, parts, 2)])
     from_far = between(passed_on, [(p - 4, p - 1) for p in range(4, parts, 4)])
     pivot_scale = after(pivot_scale, left_next, pivot_rows)
+    across = jnp.where(go_on, own_rows, jnp.zeros_like(own_rows))
+    across = (-dot_nt(across, prev_first)).astype(BF16)
+    across = jnp.where(is_first, jnp.zeros_like(across), across)
     across = lax.dynamic_update_slice_in_dim(across, across_late, late_start, 1)
     right = lax.optimization_barrier(scaled_by(across, pivot_scale))
     next_cols = (-dot_nt(right, pivot_link)).astype(BF16)

time: 308 us -> 275 us (0.89)
  the two profiles are of different devices: /device:TPU:7 before, /device:TPU:24 now
where the time goes in v1:
time: 275 us; the launch traced here: 273 us
  waiting for transfers between devices  117 us (43%)
  starting transfers between devices  44 us (16%)
  Pallas kernels  35.2 us (13%)
  matrix products  34.6 us (13%)
  other arithmetic  28.2 us (10%)
  local copies, waits for them, and re-layouts  12.1 us (4%)
    ppermute x12, waiting for transfers between devices, one_step(): return (lax.ppermute(ahead, 'space', up), lax.ppermute(back, 'space', down))  117 us
    ppermute x10, starting transfers between devices, between(): lax.ppermute(block, 'tm', [(a, b) for a, b in route if 0 <= b < parts])  22.3 us
    ppermute x12, starting transfers between devices, one_step(): return (lax.ppermute(ahead, 'space', up), lax.ppermute(back, 'space', down))  21.8 us
    pallas_call x1, Pallas kernels, early_forms(): pl.pallas_call(functools.partial(early_kernel, size), out_shape=[SHAPE((o...  19.3 us
    dot_general x4, matrix products, dot_nt(): lax.dot_general(left, right, (((1,), (1,)), ((), ())), preferred_element_...  17.9 us
    dot_general x3, matrix products, dot_nn(): lax.dot_general(left, right, (((1,), (0,)), ((), ())), preferred_element_...  16.7 us
    convert_element_type x9, other arithmetic, scaled_by(): return (matrix.astype(F32) * factors.astype(F32)[None, :]).astype(BF16)  10 us
    broadcast_in_dim x2, other arithmetic, on_device(): return (schur[None], out_link[None])  7.27 us
  transfers between devices with their start and end apart: 22, of which 8 were waited for; matrix products, arithmetic and copies ran while one was open for 23% of the time, Pallas kernels for 9%

profile of v1, /device:TPU:24, one launch (start us, length us, event | category | flops | bytes accessed | tf_op | source)
XLA Modules:
  0.0 273.3 jit_solution(17340260806067079617)
XLA Ops:
  0.6 0.7 divide_reduce_fusion
  1.5 1.3 copy-done
  2.7 1.3 copy-done.2
  4.0 1.7 copy-done.4
  5.7 3.6 %shard_map.59.refs_0_ = bf16[400,1536]{1,0:T(8,128)(2,1)} custom-call(s32[3]{0:T(128)S(1)} %pad_add_fusion.flags, bf16[384,1536]{1,0:T(8,128)(2,1)S(1)} %bitcast.39, bf16[384,1536]{1,0:T(8,128)(2,1)S(1)} %bitcast.34, f32[384,1536]{1,0:T(8,128)S(1)} %bitcast.41, f32[8,1536]{1,0:T(8,128)S(1)} %broadcast_in_dim.19.reciprocal), custom_call_target="tpu_custom_call" | custom-call | tf_op jit(solution)/shard_map/pallas_call | solution.py:103
  9.3 3.6 %collective-permute-start.5 = (bf16[400,1536]{1,0:T(8,128)(2,1)}, bf16[400,1536]{1,0:T(8,128)(2,1)}, u32[]{:S(2)}, u32[]{:S(2)}) collective-permute-start(bf16[400,1536]{1,0:T(8,128)(2,1)} %shard_map.59.refs_0_), channel_id=1, source_target_pairs={{1,0},{2,1},{3,2},{5,4},{6,5},{7,6},{9,8},{10,9},{11,10},{13,12},{... | collective-permute-start | bytes 3686408 | tf_op jit(solution)/shard_map/ppermute | solution.py:325
  12.8 1.3 collective-permute-start
  14.1 5.6 %collective-permute-start.2 = (bf16[384,1536]{1,0:T(8,128)(2,1)S(1)}, bf16[384,1536]{1,0:T(8,128)(2,1)}, u32[]{:S(2)}, u32[]{:S(2)}) collective-permute-start(bf16[384,1536]{1,0:T(8,128)(2,1)S(1)} %bitcast.36), channel_id=1, source_target_pairs={{1,0},{2,1},{3,2},{5,4},{6,5},{7,6},{9,8},{10,9},{11,10},{13,12},{... | collective-permute-start | bytes 3538952 | tf_op jit(solution)/shard_map/ppermute | solution.py:325
  19.7 1.3 collective-permute-start.4
  21.0 18.5 %collective-permute-done.5.refs_2_ = bf16[400,1536]{1,0:T(8,128)(2,1)} collective-permute-done((bf16[400,1536]{1,0:T(8,128)(2,1)}, bf16[400,1536]{1,0:T(8,128)(2,1)}, u32[]{:S(2)}, u32[]{:S(2)}) %collective-permute-start.5) | collective-permute-done | bytes 1228832 | tf_op jit(solution)/shard_map/ppermute | solution.py:325
  39.5 1.7 collective-permute-start.7
  41.2 2.4 collective-permute-done
  43.6 1.3 collective-permute-start.1
  44.9 18.6 %collective-permute-done.2 = bf16[384,1536]{1,0:T(8,128)(2,1)} collective-permute-done((bf16[384,1536]{1,0:T(8,128)(2,1)S(1)}, bf16[384,1536]{1,0:T(8,128)(2,1)}, u32[]{:S(2)}, u32[]{:S(2)}) %collective-permute-start.2) | collective-permute-done | bytes 1179680 | tf_op jit(solution)/shard_map/ppermute | solution.py:325
  63.5 1.7 collective-permute-start.3
  65.2 4.8 %collective-permute-done.4.refs_1_ = bf16[400,1536]{1,0:T(8,128)(2,1)} collective-permute-done((bf16[400,1536]{1,0:T(8,128)(2,1)}, bf16[400,1536]{1,0:T(8,128)(2,1)}, u32[]{:S(2)}, u32[]{:S(2)}) %collective-permute-start.4) | collective-permute-done | bytes 1228832 | tf_op jit(solution)/shard_map/ppermute | solution.py:325
  70.0 1.3 collective-permute-start.6
  71.5 0.7 collective-permute-start.9
  72.3 23.0 %collective-permute-done.1 = bf16[384,1536]{1,0:T(8,128)(2,1)} collective-permute-done((bf16[384,1536]{1,0:T(8,128)(2,1)S(1)}, bf16[384,1536]{1,0:T(8,128)(2,1)}, u32[]{:S(2)}, u32[]{:S(2)}) %collective-permute-start.1) | collective-permute-done | bytes 1179680 | tf_op jit(solution)/shard_map/ppermute | solution.py:325
  95.3 2.2 broadcast_select_fusion.2
  97.6 22.5 %collective-permute-done.6.refs_3_ = bf16[400,1536]{1,0:T(8,128)(2,1)S(1)} collective-permute-done((bf16[400,1536]{1,0:T(8,128)(2,1)}, bf16[400,1536]{1,0:T(8,128)(2,1)S(1)}, u32[]{:S(2)}, u32[]{:S(2)}) %collective-permute-start.6) | collective-permute-done | bytes 1228832 | tf_op jit(solution)/shard_map/ppermute | solution.py:325
  120.1 1.3 collective-permute-start.8
  121.7 1.3 collective-permute-start.12
  123.0 0.7 collective-permute-start.13
  123.8 0.9 slice_select_fusion.1
  124.7 27.2 %collective-permute-done.8.refs_5_ = bf16[400,1536]{1,0:T(8,128)(2,1)S(1)} collective-permute-done((bf16[400,1536]{1,0:T(8,128)(2,1)S(1)}, bf16[400,1536]{1,0:T(8,128)(2,1)S(1)}, u32[]{:S(2)}, u32[]{:S(2)}) %collective-permute-start.8) | collective-permute-done | bytes 1228832 | tf_op jit(solution)/shard_map/ppermute | solution.py:325
  151.9 0.9 slice_select_fusion.2
  153.1 1.3 collective-permute-start.11
  154.4 3.3 %multiply_convert_fusion.prev_whole = bf16[1536,1536]{1,0:T(8,128)(2,1)} fusion(bf16[1536,1536]{1,0:T(8,128)(2,1)S(1)} %pad_maximum_fusion, f32[1536]{0:T(1024)S(1)} %divide_reduce_fusion), kind=kLoop, calls=%fused_computation | loop fusion | flops 7077888 | bytes 9443328 | tf_op jit(solution)/shard_map/convert_element_type | solution.py:34
  157.7 1.5 collective-permute-start.10
  159.2 19.3 %shard_map.60 = (bf16[1536,1536]{1,0:T(8,128)(2,1)}, f32[384,1536]{1,0:T(8,128)S(1)}, f32[384,1536]{1,0:T(8,128)S(1)}, bf16[1536,1536]{1,0:T(8,128)(2,1)S(1)}, bf16[384,1536]{1,0:T(8,128)(2,1)S(1)}) custom-call(s32[3]{0:T(128)S(1)} %pad_add_fusion.flags, bf16[1536,1536]{1,0:T(8,128)(2,1)} %multiply_convert_fusion.prev_whole, bf16[384,1536]{1,0:T(8,128)(2,1)S(1)} %bitcast.37, ...), custom_call_target="tpu_custom_call" | custom-call | tf_op jit(solution)/shard_map/pallas_call | solution.py:150
  178.5 1.4 copy-done.6
  181.2 6.4 %shard_map.61 = (bf16[384,1536]{1,0:T(8,128)(2,1)S(1)}, f32[8,1536]{1,0:T(8,128)S(1)}, f32[8,1536]{1,0:T(8,128)S(1)}) custom-call(s32[3]{0:T(128)S(1)} %pad_add_fusion.flags, bf16[1536,1536]{1,0:T(8,128)(2,1)} %get-tuple-element.21.link, bf16[384,1536]{1,0:T(8,128)(2,1)S(1)} %get-tuple-element.22.mine, bf16[8,1536]{1,0:T(8,128)(2,1)S(1)} %broadcast_in_dim.21.scale, ...), custom_call_target="tpu_custom_call" | custom-call | tf_op jit(solution)/shard_map/pallas_call | solution.py:283
  187.7 5.9 %shard_map.62 = (bf16[384,1536]{1,0:T(8,128)(2,1)S(1)}, bf16[384,384]{1,0:T(8,128)(2,1)S(1)}, bf16[384,384]{1,0:T(8,128)(2,1)S(1)}, f32[8,384]{1,0:T(8,128)S(1)}, f32[8,1536]{1,0:T(8,128)S(1)}) custom-call(s32[3]{0:T(128)S(1)} %pad_add_fusion.flags, f32[8,1536]{1,0:T(8,128)S(1)} %copy-done.9, bf16[384,1536]{1,0:T(8,128)(2,1)S(1)} %bitcast.38, ...), custom_call_target="tpu_custom_call" | custom-call | tf_op jit(solution)/shard_map/pallas_call | solution.py:219
  193.7 1.1 constant_dynamic-update-slice_fusion.2
  194.9 5.2 %collective-permute-start.14 = (bf16[1536,1536]{1,0:T(8,128)(2,1)}, bf16[1536,1536]{1,0:T(8,128)(2,1)}, u32[]{:S(2)}, u32[]{:S(2)}) collective-permute-start(bf16[1536,1536]{1,0:T(8,128)(2,1)} %constant_dynamic-update-slice_fusion.2), channel_id=1, source_target_pairs={{0,4},{8,12},{16,20},{24,28},{1,5},{9,13},{17,21},{25,29},{2,6},{1... | collective-permute-start | bytes 14155784 | tf_op jit(solution)/shard_map/ppermute | solution.py:316
  200.1 0.8 slice_reduce_fusion
  201.2 0.7 collective-permute-start.15
  201.8 1.0 constant_dynamic-update-slice_fusion
  202.8 0.8 add_reduce_fusion
  203.7 1.3 collective-permute-start.18
  205.0 0.6 fusion.42
  205.7 1.5 multiply_convert_fusion.4
  207.2 5.3 %fusion = bf16[384,1536]{1,0:T(8,128)(2,1)} fusion(bf16[384,1536]{1,0:T(8,128)(2,1)S(1)} %multiply_convert_fusion.4, bf16[1536,1536]{1,0:T(8,128)(2,1)} %constant_dynamic-update-slice_fusion.2), kind=kOutput, calls=%fused_computation.10 | convolution fusion | flops 1813118976 | bytes 7077888 | tf_op jit(solution)/shard_map/dot_general | solution.py:46
  212.5 1.7 collective-permute-start.16
  214.2 4.7 %fusion.4 = bf16[384,1536]{1,0:T(8,128)(2,1)S(1)} fusion(bf16[1536,1536]{1,0:T(8,128)(2,1)} %constant_dynamic-update-slice_fusion.2, bf16[384,1536]{1,0:T(8,128)(2,1)} %fusion, f32[1536]{0:T(1024)S(1)} %get-tuple-element.36, f32[1536]{0:T(1024)S(1)} %copy-done.20), kind=kOutput, calls=%fused_computation.14 | convolution fusion | flops 1814888448 | bytes 7090176 | tf_op jit(solution)/shard_map/dot_general | solution.py:42
  219.0 4.4 %fusion.1.refs_1_ = bf16[384,1536]{1,0:T(8,128)(2,1)S(1)} fusion(bf16[384,1536]{1,0:T(8,128)(2,1)S(1)} %fusion.4, bf16[1536,1536]{1,0:T(8,128)(2,1)} %collective-permute-done.14), kind=kOutput, calls=%fused_computation.11 | convolution fusion | flops 1813118976 | bytes 7077888 | tf_op jit(solution)/shard_map/dot_general | solution.py:42
  223.4 1.7 collective-permute-start.21
  225.7 1.3 slice.221
  226.9 0.6 collective-permute-start.17
  228.3 1.1 broadcast_select_fusion
  229.3 1.3 collective-permute-start.20
  230.6 2.4 broadcast_select_fusion.1
  233.1 7.1 %collective-permute-start.19 = (bf16[384,1536]{1,0:T(8,128)(2,1)}, bf16[384,1536]{1,0:T(8,128)(2,1)S(1)}, u32[]{:S(2)}, u32[]{:S(2)}) collective-permute-start(bf16[384,1536]{1,0:T(8,128)(2,1)} %broadcast_select_fusion.1), channel_id=1, source_target_pairs={{0,12},{1,13},{2,14},{3,15}} | collective-permute-start | bytes 3538952 | tf_op jit(solution)/shard_map/ppermute | solution.py:316
  240.2 4.4 %fusion.5 = bf16[384,1536]{1,0:T(8,128)(2,1)S(1)} fusion(bf16[1536,1536]{1,0:T(8,128)(2,1)} %multiply_convert_fusion.prev_whole, pred[]{:T(512)} %bitcast.6, pred[]{:T(512)S(6)} %eq.25, bf16[1,384,1536]{2,1,0:T(8,128)(2,1)S(1)} %copy-done.3), kind=kOutput, calls=%fused_computation.15 | convolution fusion | flops 1814298624 | bytes 7077890 | tf_op jit(solution)/shard_map/dot_general | solution.py:42
  244.6 1.0 copy-done.17
  245.7 0.7 convert_element_type.226
  246.4 1.5 multiply_convert_fusion.2
  247.8 4.4 %fusion.3 = bf16[384,1536]{1,0:T(8,128)(2,1)S(1)} fusion(bf16[384,1536]{1,0:T(8,128)(2,1)S(1)} %multiply_convert_fusion.2, bf16[1536,1536]{1,0:T(8,128)(2,1)} %collective-permute-done.14), kind=kOutput, calls=%fused_computation.13 | convolution fusion | flops 1813118976 | bytes 7077888 | tf_op jit(solution)/shard_map/dot_general | solution.py:42
  252.2 1.7 multiply_convert_fusion.1
  253.9 5.7 %convolution_multiply_fusion = f32[768,1536]{1,0:T(8,128)S(1)} fusion(bf16[768,1536]{1,0:T(8,128)(2,1)S(1)} %multiply_convert_fusion.1, bf16[1536,1536]{1,0:T(8,128)(2,1)} %collective-permute-done.14, f32[1536]{0:T(1024)S(1)} %convert_element_type.226), kind=kOutput, calls=%fused_computation.3 | convolution fusion | flops 3625058304 | bytes 11802624 | tf_op jit(solution)/shard_map/dot_general | solution.py:46
  260.3 5.7 %fusion.48 = f32[768,1536]{1,0:T(8,128)S(1)} fusion(bf16[768,1536]{1,0:T(8,128)(2,1)S(1)} %pad_maximum_fusion.1, bf16[1536,1536]{1,0:T(8,128)(2,1)} %constant_dynamic-update-slice_fusion.2), kind=kOutput, calls=%fused_computation.115 | convolution fusion | flops 3623878656 | bytes 11796480 | tf_op jit(solution)/shard_map/dot_general | solution.py:46
  266.0 2.9 %fusion.11 = bf16[1,384,1536]{2,1,0:T(8,128)(2,1)} fusion(f32[768,1536]{1,0:T(8,128)S(1)} %fusion.48, bf16[384,1536]{1,0:T(8,128)(2,1)} %fusion, bf16[1536,1536]{1,0:T(8,128)(2,1)} %constant_dynamic-update-slice_fusion.2, s32[]{:T(128)S(6)} %select_n.249, pred[]{:T(512)S(6)} %eq.32, pred[]{:T(512)S(6)} %eq.31), kind=kLoop, calls=%fused_computation.29 | loop fusion | flops 1179648 | bytes 4718598 | tf_op jit(solution)/shard_map/broadcast_in_dim | solution.py:437
  268.9 4.4 %fusion.9 = f32[1,384,1536]{2,1,0:T(8,128)} fusion(f32[384,1536]{1,0:T(8,128)S(1)} %copy-done.7, f32[768,1536]{1,0:T(8,128)S(1)} %fusion.48, bf16[384,1536]{1,0:T(8,128)(2,1)} %collective-permute-done.21, bf16[384,1536]{1,0:T(8,128)(2,1)} %collective-permute-done.20, bf16[384,1536]{1,0:T(8,128)(2,1)} %collective-permute-done.18, ...), kind=kLoop, calls=%fused_computation.21 | loop fusion | flops 5308416 | bytes 11796481 | tf_op jit(solution)/shard_map/broadcast_in_dim | solution.py:437
  (85 shorter events, 4.1 us)
Async XLA Ops:
  1.5 1.3 copy-start
  2.7 1.3 copy-start.2
  4.0 1.7 copy-start.4
  5.7 3.6 %copy-start.8 = (f32[8,1536]{1,0:T(8,128)}, f32[8,1536]{1,0:T(8,128)S(1)}, u32[]{:S(2)}) copy-start(f32[8,1536]{1,0:T(8,128)S(1)} %broadcast_in_dim.19.reciprocal) | copy-start | bytes 147460
  5.7 65.7 %copy-start.3 = (bf16[1,384,1536]{2,1,0:T(8,128)(2,1)S(1)}, bf16[1,384,1536]{2,1,0:T(8,128)(2,1)}, u32[]{:S(2)}) copy-start(bf16[1,384,1536]{2,1,0:T(8,128)(2,1)} %param.5) | copy-start | bytes 3538948
  9.3 86.1 %copy-start.1 = (bf16[1,384,1536]{2,1,0:T(8,128)(2,1)S(1)}, bf16[1,384,1536]{2,1,0:T(8,128)(2,1)}, u32[]{:S(2)}) copy-start(bf16[1,384,1536]{2,1,0:T(8,128)(2,1)} %param.6) | copy-start | bytes 3538948
  9.3 30.2 %collective-permute-start.5 = (bf16[400,1536]{1,0:T(8,128)(2,1)}, bf16[400,1536]{1,0:T(8,128)(2,1)}, u32[]{:S(2)}, u32[]{:S(2)}) collective-permute-start(bf16[400,1536]{1,0:T(8,128)(2,1)} %shard_map.59.refs_0_), channel_id=1, source_target_pairs={{1,0},{2,1},{3,2},{5,4},{6,5},{7,6},{9,8},{10,9},{11,10},{13,12},{... | collective-permute-start | bytes 3686408 | tf_op jit(solution)/shard_map/ppermute | solution.py:325
  12.8 30.8 %collective-permute-start = (bf16[384,1536]{1,0:T(8,128)(2,1)S(1)}, bf16[384,1536]{1,0:T(8,128)(2,1)S(1)}, u32[]{:S(2)}, u32[]{:S(2)}) collective-permute-start(bf16[384,1536]{1,0:T(8,128)(2,1)S(1)} %bitcast.35), channel_id=1, source_target_pairs={{0,1},{1,2},{2,3},{4,5},{5,6},{6,7},{8,9},{9,10},{10,11},{12,13},{... | collective-permute-start | bytes 3538952 | tf_op jit(solution)/shard_map/ppermute | solution.py:325
  14.1 49.4 %collective-permute-start.2 = (bf16[384,1536]{1,0:T(8,128)(2,1)S(1)}, bf16[384,1536]{1,0:T(8,128)(2,1)}, u32[]{:S(2)}, u32[]{:S(2)}) collective-permute-start(bf16[384,1536]{1,0:T(8,128)(2,1)S(1)} %bitcast.36), channel_id=1, source_target_pairs={{1,0},{2,1},{3,2},{5,4},{6,5},{7,6},{9,8},{10,9},{11,10},{13,12},{... | collective-permute-start | bytes 3538952 | tf_op jit(solution)/shard_map/ppermute | solution.py:325
  19.7 50.3 %collective-permute-start.4 = (bf16[400,1536]{1,0:T(8,128)(2,1)}, bf16[400,1536]{1,0:T(8,128)(2,1)}, u32[]{:S(2)}, u32[]{:S(2)}) collective-permute-start(bf16[400,1536]{1,0:T(8,128)(2,1)} %shard_map.59.refs_0_), channel_id=1, source_target_pairs={{0,1},{1,2},{2,3},{4,5},{5,6},{6,7},{8,9},{9,10},{10,11},{12,13},{... | collective-permute-start | bytes 3686408 | tf_op jit(solution)/shard_map/ppermute | solution.py:325
  39.5 32.1 %collective-permute-start.7 = (bf16[400,1536]{1,0:T(8,128)(2,1)}, bf16[400,1536]{1,0:T(8,128)(2,1)}, u32[]{:S(2)}, u32[]{:S(2)}) collective-permute-start(bf16[400,1536]{1,0:T(8,128)(2,1)} %collective-permute-done.5.refs_2_), channel_id=1, source_target_pairs={{1,0},{2,1},{5,4},{6,5},{9,8},{10,9},{13,12},{14,13},{17,16},{18,1... | collective-permute-start | bytes 3686408 | tf_op jit(solution)/shard_map/ppermute | solution.py:325
  43.6 51.7 %collective-permute-start.1 = (bf16[384,1536]{1,0:T(8,128)(2,1)S(1)}, bf16[384,1536]{1,0:T(8,128)(2,1)}, u32[]{:S(2)}, u32[]{:S(2)}) collective-permute-start(bf16[384,1536]{1,0:T(8,128)(2,1)S(1)} %collective-permute-done), channel_id=1, source_target_pairs={{1,2},{2,3},{5,6},{6,7},{9,10},{10,11},{13,14},{14,15},{17,18},{18... | collective-permute-start | bytes 3538952 | tf_op jit(solution)/shard_map/ppermute | solution.py:325
  63.5 31.8 %collective-permute-start.3 = (bf16[384,1536]{1,0:T(8,128)(2,1)}, bf16[384,1536]{1,0:T(8,128)(2,1)}, u32[]{:S(2)}, u32[]{:S(2)}) collective-permute-start(bf16[384,1536]{1,0:T(8,128)(2,1)} %collective-permute-done.2), channel_id=1, source_target_pairs={{1,0},{2,1},{5,4},{6,5},{9,8},{10,9},{13,12},{14,13},{17,16},{18,1... | collective-permute-start | bytes 3538952 | tf_op jit(solution)/shard_map/ppermute | solution.py:325
  70.0 50.0 %collective-permute-start.6 = (bf16[400,1536]{1,0:T(8,128)(2,1)}, bf16[400,1536]{1,0:T(8,128)(2,1)S(1)}, u32[]{:S(2)}, u32[]{:S(2)}) collective-permute-start(bf16[400,1536]{1,0:T(8,128)(2,1)} %collective-permute-done.4.refs_1_), channel_id=1, source_target_pairs={{1,2},{2,3},{5,6},{6,7},{9,10},{10,11},{13,14},{14,15},{17,18},{18... | collective-permute-start | bytes 3686408 | tf_op jit(solution)/shard_map/ppermute | solution.py:325
  71.5 52.2 %collective-permute-start.9 = (bf16[400,1536]{1,0:T(8,128)(2,1)}, bf16[400,1536]{1,0:T(8,128)(2,1)S(1)}, u32[]{:S(2)}, u32[]{:S(2)}) collective-permute-start(bf16[400,1536]{1,0:T(8,128)(2,1)} %collective-permute-done.7.refs_4_), channel_id=1, source_target_pairs={{1,0},{5,4},{9,8},{13,12},{17,16},{21,20},{25,24},{29,28}} | collective-permute-start | bytes 3686408 | tf_op jit(solution)/shard_map/ppermute | solution.py:325
  120.1 31.8 %collective-permute-start.8 = (bf16[400,1536]{1,0:T(8,128)(2,1)S(1)}, bf16[400,1536]{1,0:T(8,128)(2,1)S(1)}, u32[]{:S(2)}, u32[]{:S(2)}) collective-permute-start(bf16[400,1536]{1,0:T(8,128)(2,1)S(1)} %collective-permute-done.6.refs_3_), channel_id=1, source_target_pairs={{2,3},{6,7},{10,11},{14,15},{18,19},{22,23},{26,27},{30,31}} | collective-permute-start | bytes 3686408 | tf_op jit(solution)/shard_map/ppermute | solution.py:325
  121.7 66.0 %collective-permute-start.12 = (bf16[384,1536]{1,0:T(8,128)(2,1)}, bf16[384,1536]{1,0:T(8,128)(2,1)S(1)}, u32[]{:S(2)}, u32[]{:S(2)}) collective-permute-start(bf16[384,1536]{1,0:T(8,128)(2,1)} %collective-permute-done.1), channel_id=1, source_target_pairs={{2,3},{6,7},{10,11},{14,15},{18,19},{22,23},{26,27},{30,31}} | collective-permute-start | bytes 3538952 | tf_op jit(solution)/shard_map/ppermute | solution.py:325
  123.0 64.7 %collective-permute-start.13 = (bf16[384,1536]{1,0:T(8,128)(2,1)}, bf16[384,1536]{1,0:T(8,128)(2,1)S(1)}, u32[]{:S(2)}, u32[]{:S(2)}) collective-permute-start(bf16[384,1536]{1,0:T(8,128)(2,1)} %collective-permute-done.3), channel_id=1, source_target_pairs={{1,0},{5,4},{9,8},{13,12},{17,16},{21,20},{25,24},{29,28}} | collective-permute-start | bytes 3538952 | tf_op jit(solution)/shard_map/ppermute | solution.py:325
  153.1 26.8 %collective-permute-start.11 = (f32[1536]{0:T(1024)S(1)}, f32[1536]{0:T(1024)S(1)}, u32[]{:S(2)}, u32[]{:S(2)}) collective-permute-start(f32[1536]{0:T(1024)S(1)} %maximum_subtract_fusion), channel_id=1, source_target_pairs={{0,4},{8,12},{16,20},{24,28},{1,5},{9,13},{17,21},{25,29},{2,6},{1... | collective-permute-start | bytes 18440 | tf_op jit(solution)/shard_map/ppermute | solution.py:316
  154.4 4.8 %copy-start.5 = (f32[1,384,1536]{2,1,0:T(8,128)S(1)}, f32[1,384,1536]{2,1,0:T(8,128)}, u32[]{:S(2)}) copy-start(f32[1,384,1536]{2,1,0:T(8,128)} %param.4) | copy-start | bytes 7077892
  157.7 22.8 %collective-permute-start.10 = (f32[1536]{0:T(1024)S(1)}, f32[1536]{0:T(1024)S(1)}, u32[]{:S(2)}, u32[]{:S(2)}) collective-permute-start(f32[1536]{0:T(1024)S(1)} %pad_maximum_fusion.2), channel_id=1, source_target_pairs={{4,0},{8,4},{12,8},{16,12},{20,16},{24,20},{28,24},{5,1},{9,5},{13... | collective-permute-start | bytes 18440 | tf_op jit(solution)/shard_map/ppermute | solution.py:316
  178.5 1.4 copy-start.6
  180.5 7.1 %copy-start.18 = (bf16[1536]{0:T(1024)(128)(2,1)}, bf16[1536]{0:T(1024)(128)(2,1)S(1)}, u32[]{:S(2)}) copy-start(bf16[1536]{0:T(1024)(128)(2,1)S(1)} %get-tuple-element.41.refs_0_) | copy-start | bytes 9220
  181.2 6.6 %copy-start.9 = (f32[8,1536]{1,0:T(8,128)S(1)}, f32[8,1536]{1,0:T(8,128)}, u32[]{:S(2)}) copy-start(f32[8,1536]{1,0:T(8,128)} %copy-done.8) | copy-start | bytes 147460
  187.6 6.0 %copy-start.13 = (f32[8,1536]{1,0:T(8,128)}, f32[8,1536]{1,0:T(8,128)S(1)}, u32[]{:S(2)}) copy-start(f32[8,1536]{1,0:T(8,128)S(1)} %get-tuple-element.28.ready) | copy-start | bytes 147460
  187.6 6.0 %copy-start.14 = (f32[8,1536]{1,0:T(8,128)}, f32[8,1536]{1,0:T(8,128)S(1)}, u32[]{:S(2)}) copy-start(f32[8,1536]{1,0:T(8,128)S(1)} %get-tuple-element.30) | copy-start | bytes 147460
  193.7 1.2 copy-start.10
  193.7 1.2 copy-start.12
  193.7 1.2 copy-start.15
  193.7 11.3 %copy-start.19 = (f32[1536]{0:T(1024)S(1)}, f32[1536]{0:T(1024)}, u32[]{:S(2)}) copy-start(f32[1536]{0:T(1024)} %get-tuple-element.39) | copy-start | bytes 18436
  193.7 12.0 %copy-start.20 = (f32[1536]{0:T(1024)S(1)}, f32[1536]{0:T(1024)}, u32[]{:S(2)}) copy-start(f32[1536]{0:T(1024)} %get-tuple-element.40) | copy-start | bytes 18436
  194.9 10.9 %collective-permute-start.14 = (bf16[1536,1536]{1,0:T(8,128)(2,1)}, bf16[1536,1536]{1,0:T(8,128)(2,1)}, u32[]{:S(2)}, u32[]{:S(2)}) collective-permute-start(bf16[1536,1536]{1,0:T(8,128)(2,1)} %constant_dynamic-update-slice_fusion.2), channel_id=1, source_target_pairs={{0,4},{8,12},{16,20},{24,28},{1,5},{9,13},{17,21},{25,29},{2,6},{1... | collective-permute-start | bytes 14155784 | tf_op jit(solution)/shard_map/ppermute | solution.py:316
  201.2 3.8 %collective-permute-start.15 = (f32[1536]{0:T(1024)S(1)}, f32[1536]{0:T(1024)S(1)}, u32[]{:S(2)}, u32[]{:S(2)}) collective-permute-start(f32[1536]{0:T(1024)S(1)} %dynamic_update_slice.13), channel_id=1, source_target_pairs={{8,4},{16,12},{24,20},{9,5},{17,13},{25,21},{10,6},{18,14},{26,22}... | collective-permute-start | bytes 18440 | tf_op jit(solution)/shard_map/ppermute | solution.py:316
  203.7 27.0 %collective-permute-start.18 = (bf16[384,1536]{1,0:T(8,128)(2,1)S(1)}, bf16[384,1536]{1,0:T(8,128)(2,1)}, u32[]{:S(2)}, u32[]{:S(2)}) collective-permute-start(bf16[384,1536]{1,0:T(8,128)(2,1)S(1)} %constant_dynamic-update-slice_fusion), channel_id=1, source_target_pairs={{8,4},{24,20},{16,0},{9,5},{25,21},{17,1},{10,6},{26,22},{18,2},{1... | collective-permute-start | bytes 3538952 | tf_op jit(solution)/shard_map/ppermute | solution.py:316
  212.5 33.1 %collective-permute-start.16 = (bf16[384,1536]{1,0:T(8,128)(2,1)}, bf16[384,1536]{1,0:T(8,128)(2,1)}, u32[]{:S(2)}, u32[]{:S(2)}) collective-permute-start(bf16[384,1536]{1,0:T(8,128)(2,1)} %fusion), channel_id=1, source_target_pairs={{20,28},{21,29},{22,30},{23,31}} | collective-permute-start | bytes 3538952 | tf_op jit(solution)/shard_map/ppermute | solution.py:316
  223.3 2.3 copy-start.16
  223.4 45.6 %collective-permute-start.21 = (bf16[384,1536]{1,0:T(8,128)(2,1)S(1)}, bf16[384,1536]{1,0:T(8,128)(2,1)}, u32[]{:S(2)}, u32[]{:S(2)}) collective-permute-start(bf16[384,1536]{1,0:T(8,128)(2,1)S(1)} %fusion.1.refs_1_), channel_id=1, source_target_pairs={{20,12},{21,13},{22,14},{23,15}} | collective-permute-start | bytes 3538952 | tf_op jit(solution)/shard_map/ppermute | solution.py:316
  226.9 18.7 %collective-permute-start.17 = (bf16[1536]{0:T(1024)(128)(2,1)}, bf16[1536]{0:T(1024)(128)(2,1)S(1)}, u32[]{:S(2)}, u32[]{:S(2)}) collective-permute-start(bf16[1536]{0:T(1024)(128)(2,1)} %shard_map.65), channel_id=1, source_target_pairs={{4,12},{20,28},{5,13},{21,29},{6,14},{22,30},{7,15},{23,31}} | collective-permute-start | bytes 9224 | tf_op jit(solution)/shard_map/ppermute | solution.py:316
  229.3 39.6 %collective-permute-start.20 = (bf16[384,1536]{1,0:T(8,128)(2,1)}, bf16[384,1536]{1,0:T(8,128)(2,1)}, u32[]{:S(2)}, u32[]{:S(2)}) collective-permute-start(bf16[384,1536]{1,0:T(8,128)(2,1)} %broadcast_select_fusion), channel_id=1, source_target_pairs={{4,0},{12,8},{20,16},{28,24},{5,1},{13,9},{21,17},{29,25},{6,2},{1... | collective-permute-start | bytes 3538952 | tf_op jit(solution)/shard_map/ppermute | solution.py:316
  233.1 11.5 %copy-start.11 = (bf16[384,384]{1,0:T(8,128)(2,1)S(1)}, bf16[384,384]{1,0:T(8,128)(2,1)}, u32[]{:S(2)}) copy-start(bf16[384,384]{1,0:T(8,128)(2,1)} %copy-done.10) | copy-start | bytes 884740
  233.1 35.8 %collective-permute-start.19 = (bf16[384,1536]{1,0:T(8,128)(2,1)}, bf16[384,1536]{1,0:T(8,128)(2,1)S(1)}, u32[]{:S(2)}, u32[]{:S(2)}) collective-permute-start(bf16[384,1536]{1,0:T(8,128)(2,1)} %broadcast_select_fusion.1), channel_id=1, source_target_pairs={{0,12},{1,13},{2,14},{3,15}} | collective-permute-start | bytes 3538952 | tf_op jit(solution)/shard_map/ppermute | solution.py:316
  244.6 1.0 copy-start.17
  266.0 2.9 %copy-start.7 = (f32[384,1536]{1,0:T(8,128)S(1)}, f32[384,1536]{1,0:T(8,128)}, u32[]{:S(2)}) copy-start(f32[384,1536]{1,0:T(8,128)} %copy-done.6) | copy-start | bytes 7077892

commit v2 on v1

--- a/solution.py
+++ b/solution.py
@@ -175,8 +175,8 @@
 
 
 def late_kernel(
-    size, flags, reciprocal, prev_rows, plain_rows, mine, own, scale, late_scale, from_below, from_above, far,
-    ready, link, corner, across, left_diag, right_diag, raw, scaled, sem,
+    size, flags, reciprocal, prev_rows, mine, own, scale, late_scale, from_below, from_above, far,
+    ready, link, corner, scaled, left_diag, right_diag, raw, sem,
 ):
     del ready
     place = flags[1]
@@ -195,7 +195,6 @@
             pl.when(chosen)(copy.start)
             pl.when(chosen)(copy.wait)
         scaled[...] = (raw[...].astype(F32) * reciprocal[0:1]).astype(BF16)
-        across[...] = jnp.where(flags[0] == 1, 0.0, -dot_nt(plain_rows[...], scaled[...])).astype(BF16)
 
     link[:, here] = jnp.where(flags[0] == 1, 0.0, -dot_nt(scaled[...], own[...])).astype(BF16)
 
@@ -211,7 +210,7 @@
 
 
 def late_forms(
-    flags, reciprocal, prev_rows, plain_rows, mine, own, scale, late_scale, from_below, from_above, far, ready
+    flags, reciprocal, prev_rows, mine, own, scale, late_scale, from_below, from_above, far, ready
 ):
     rows, order = prev_rows.shape
     size = order // rows
@@ -221,7 +220,7 @@
         out_shape=[
             SHAPE((rows, order), BF16),
             SHAPE((rows, rows), BF16),
-            SHAPE((rows, rows), BF16),
+            SHAPE((rows, order), BF16),
             SHAPE((8, rows), F32),
             SHAPE((8, order), F32),
         ],
@@ -230,7 +229,6 @@
             grid=(order // width,),
             in_specs=[
                 whole_spec((8, order)),
-                whole_spec((rows, order)),
                 whole_spec((rows, order)),
                 whole_spec((rows, order)),
                 pl.BlockSpec((width, order), lambda j, f: (j, 0)),
@@ -244,20 +242,15 @@
             out_specs=[
                 whole_spec((rows, order)),
                 whole_spec((rows, rows)),
-                whole_spec((rows, rows)),
+                whole_spec((rows, order)),
                 whole_spec((8, rows)),
                 whole_spec((8, order)),
             ],
-            scratch_shapes=[
-                pltpu.VMEM((rows, order), BF16),
-                pltpu.VMEM((rows, order), BF16),
-                pltpu.SemaphoreType.DMA,
-            ],
+            scratch_shapes=[pltpu.VMEM((rows, order), BF16), pltpu.SemaphoreType.DMA],
         ),
         compiler_params=pltpu.CompilerParams(vmem_limit_bytes=18 * 1024 * 1024),
     )(
-        flags, reciprocal, prev_rows, plain_rows, mine, own, scale, late_scale, from_below, from_above, far,
-        ready,
+        flags, reciprocal, prev_rows, mine, own, scale, late_scale, from_below, from_above, far, ready
     )
 
 
@@ -300,6 +293,107 @@
     )(flags, link, mine, scale, pivot_scale, form)
 
 
+def fetched(early, late, whole, sems, at):
+    rows, order = late.shape
+    size = order // rows
+    place = at[0]
+    low = place < size // 2
+    spans = [pl.ds(spot * rows, rows) for spot in range(size)]
+    copies = []
+    for spot, span in enumerate(spans):
+        plain = pltpu.make_async_copy(early.at[span], whole.at[span], sems.at[spot])
+        if spot not in (0, size - 1):
+            copies.append((True, plain))
+            continue
+        is_late = low if spot else jnp.logical_not(low)
+        copies.append((jnp.logical_not(is_late), plain))
+        copies.append((is_late, pltpu.make_async_copy(late, whole.at[span], sems.at[spot])))
+    for chosen, copy in copies:
+        pl.when(chosen)(copy.start) if chosen is not True else copy.start()
+
+    def wait():
+        for chosen, copy in copies:
+            pl.when(chosen)(copy.wait) if chosen is not True else copy.wait()
+
+    return wait
+
+
+def times(block, factors):
+    return (block.astype(F32) * factors[0:1].astype(F32)).astype(BF16)
+
+
+def next_rows_kernel(flags, pivot_rows, pivot_scale, early, late, *refs):
+    result, link, sems = refs[-3:]
+    wait = fetched(early, late, link, sems, [flags[1]])
+    scaled = times(pivot_rows[...], pivot_scale)
+    wait()
+    result[...] = (-dot_nn(scaled, link[...])).astype(BF16)
+
+
+def level_2_kernel(flags, rows, scale, pivot_scale, early, late, pivot_early, pivot_late, result, link, pivot, sems):
+    wait_link = fetched(early, late, link, sems.at[0], [flags[1]])
+    wait_pivot = fetched(pivot_early, pivot_late, pivot, sems.at[1], [flags[1]])
+    scaled = times(rows[...], scale)
+    wait_link()
+    inner = times(dot_nt(scaled, link[...]), pivot_scale)
+    wait_pivot()
+    result[...] = (-dot_nt(inner, pivot[...])).astype(BF16)
+
+
+def right_kernel(
+    flags, own, pivot_scale, next_scale, prev_early, prev_late, pivot_early, pivot_late, ready,
+    result, prev, pivot, sems,
+):
+    del ready
+    wait_prev = fetched(prev_early, prev_late, prev, sems.at[0], [flags[1]])
+    wait_pivot = fetched(pivot_early, pivot_late, pivot, sems.at[1], [flags[1]])
+    wait_prev()
+    across = jnp.where(flags[0] == 1, 0.0, -dot_nt(own[...], prev[...])).astype(BF16)
+    across = times(across, pivot_scale)
+    wait_pivot()
+    columns = (-dot_nt(across, pivot[...])).astype(BF16)
+    inner = dot_nn(times(columns, next_scale), pivot[...]) * pivot_scale[0:1].astype(F32)
+    keep = jnp.where(flags[3] == 1, 1.0, 0.0)
+    result[...] = (across.astype(F32) - inner * keep).astype(BF16)
+
+
+def last_kernel(
+    flags, rows, right, next_rows, mine, partial, pivot_scale, next_scale,
+    early, late, pivot_early, pivot_late, form, new, link, pivot, sems,
+):
+    wait_pivot = fetched(pivot_early, pivot_late, pivot, sems.at[1], [flags[1]])
+    wait_link = fetched(early, late, link, sems.at[0], [flags[1]])
+    scaled = times(rows[...], next_scale)
+    wait_pivot()
+    inner = times(dot_nn(scaled, pivot[...]), pivot_scale)
+    wait_link()
+    last = dot_nn(inner, link[...]).astype(BF16)
+    odd = jnp.where(flags[2] == 1, 0.0, 1.0)
+    form[...] = partial[...] - odd * dot_nn(right[...], link[...])
+    new[...] = jnp.where(flags[3] == 1, last, jnp.where(flags[2] == 1, mine[...], next_rows[...]))
+
+
+def with_links(kernel, out_shapes, flags, blocks, arrays, links):
+    order = arrays[0].shape[1]
+    rows = arrays[1].shape[0]
+    size = order // rows
+    specs = [spec if spec is not None else whole_spec(block.shape) for block, spec in blocks]
+    sems = (size,) if links == 1 else (links, size)
+    return pl.pallas_call(
+        kernel,
+        out_shape=out_shapes,
+        grid_spec=pltpu.PrefetchScalarGridSpec(
+            num_scalar_prefetch=1,
+            grid=(1,),
+            in_specs=specs + [ANY] * len(arrays),
+            out_specs=[whole_spec(out.shape) for out in out_shapes],
+            scratch_shapes=[pltpu.VMEM((order, order), BF16)] * links + [pltpu.SemaphoreType.DMA(sems)],
+        ),
+        compiler_params=pltpu.CompilerParams(vmem_limit_bytes=32 * 1024 * 1024),
+        cost_estimate=FREE,
+    )(flags, *[block for block, _ in blocks], *arrays)
+
+
 def on_device(sep_block, own_couple, prev_couple, inner_diag):
     separator = sep_block[0]
     own_rows = own_couple[0]
@@ -337,7 +431,9 @@
     is_pivot = partition % 2 == 0
     is_receiver = partition % 2 == 1
     is_last = partition % 4 == 3
-    flags = jnp.stack([is_first.astype(jnp.int32), place, is_pivot.astype(jnp.int32)])
+    flags = jnp.stack(
+        [is_first.astype(jnp.int32), place, is_pivot.astype(jnp.int32), is_last.astype(jnp.int32)]
+    )
     own_long = opening(flags, own_rows, prev_rows, separator, rows_of(reciprocal))
     own_arrived = [(own_long, own_long)]
     prev_arrived = [(prev_rows, prev_rows)]
@@ -384,56 +480,49 @@
     from_below, from_above = prev_arrived[-1]
     late_scale = lax.dynamic_slice_in_dim(pivot_scale, late_start, rows, 0)
     late_scale = jnp.where(is_end, late_scale, jnp.zeros_like(late_scale))
-    late, corner, across_late, left_late, right_late = late_forms(
-        flags, rows_of(reciprocal), prev_rows, own_rows, mine, own_full, scale8, rows_of(late_scale),
+    pivot_early = between(link, [(p, p + 1) for p in even])
+    from_later = between(update, [(p, p - 1) for p in everyone])
+    late, corner, prev_late, left_late, right_late = late_forms(
+        flags, rows_of(reciprocal), prev_rows, mine, own_full, scale8, rows_of(late_scale),
         from_below, from_above, prev_far, right_diag,
     )
-    link = lax.dynamic_update_slice_in_dim(link, late, late_start, 0)
-    pivot_link = between(link, [(p, p + 1) for p in even])
-    update = lax.dynamic_update_slice_in_dim(update, corner, late_start, 1)
     left_diag = lax.dynamic_update_slice_in_dim(left_diag[0], left_late[0], late_start, 0)
-    right_diag = right_diag[0] + right_late[0]
-
     left_diag = between(left_diag, [(p, p - 1) for p in even])
-    from_even = between(
-        update, [(p, p - 1) for p in range(2, parts, 4)] + [(p, p - 4) for p in range(4, parts, 4)]
-    )
-    next_diag = diag - left_diag - right_diag
+    pivot_late = between(late, [(p, p + 1) for p in even])
+    corner = between(corner, [(p, p - 1) for p in everyone])
+
+    own_block = pl.BlockSpec((rows, order), lambda j, f: (f[1], 0), pipeline_mode=pl.Buffered(1))
+    (next_rows,) = with_links(
+        next_rows_kernel, [SHAPE((rows, order), BF16)], flags,
+        [(pivot_early, own_block), (pivot_scale8, None)], [link, late], 1,
+    )
+    pivot_rows = between(next_rows, [(p, p + 2) for p in pivots if p != 1])
+    next_diag = diag - left_diag - right_diag[0] - right_late[0]
     next_scale = (1.0 / jnp.maximum(next_diag, 1.0)).astype(BF16)
-    pivot_rows = lax.dynamic_slice_in_dim(pivot_link, row_start, rows, 0)
-    pivot_rows = lax.optimization_barrier(scaled_by(pivot_rows, pivot_scale))
-    next_rows = (-dot_nn(pivot_rows, link)).astype(BF16)
-    pivot_rows = between(next_rows, [(p, p + 2) for p in pivots if p != 1])
-
-    left_next = scaled_by(dot_nt(scaled_by(next_rows, next_scale), link), pivot_scale)
-    left_next = lax.optimization_barrier(left_next)
-    left_next = (-dot_nt(left_next, pivot_link)).astype(BF16)
+    next_pivot_scale = between(next_scale, [(p, p + 2) for p in pivots])
+
+    links = [link, late, pivot_early, pivot_late]
+    (left_next,) = with_links(
+        level_2_kernel, [SHAPE((rows, order), BF16)], flags,
+        [(next_rows, None), (rows_of(next_scale), None), (pivot_scale8, None)], links, 2,
+    )
     from_pivot = between(left_next, [(p, p - 2) for p in pivots])
-
-    next_pivot_scale = between(after(next_scale, left_next), [(p, p + 2) for p in pivots])
-    go_on = after(jnp.ones((8, 128), jnp.int32), left_next)[0, 0] == 1
-    passed_on = jnp.where(go_on, from_even, jnp.zeros_like(from_even))
-    own_update = jnp.where(go_on, update, jnp.zeros_like(update))
-    from_odd = between(own_update, [(p, p - 1) for p in range(1, parts, 2)])
-    from_far = between(passed_on, [(p - 4, p - 1) for p in range(4, parts, 4)])
-    pivot_scale = after(pivot_scale, left_next, pivot_rows)
-    across = jnp.where(go_on, own_rows, jnp.zeros_like(own_rows))
-    across = (-dot_nt(across, prev_first)).astype(BF16)
-    across = jnp.where(is_first, jnp.zeros_like(across), across)
-    across = lax.dynamic_update_slice_in_dim(across, across_late, late_start, 1)
-    right = lax.optimization_barrier(scaled_by(across, pivot_scale))
-    next_cols = (-dot_nt(right, pivot_link)).astype(BF16)
-    both = jnp.concatenate([next_cols, pivot_rows])
-    both = lax.optimization_barrier(scaled_by(both, next_pivot_scale))
-    both = dot_nn(both, pivot_link) * pivot_scale.astype(F32)[None, :]
-    right = jnp.where(is_last, right.astype(F32) - both[:rows], right.astype(F32))
-    both = lax.optimization_barrier(jnp.concatenate([right, both[rows:]]).astype(BF16))
-    both = lax.optimization_barrier(dot_nn(both, link))
-    link_rows = lax.dynamic_slice_in_dim(link, row_start, rows, 0)
-    out_link = jnp.where(is_last, both[rows:].astype(BF16), jnp.where(is_receiver, next_rows, link_rows))
-    from_even = jnp.where(is_receiver, from_even + from_far, jnp.zeros_like(from_even))
-    from_later = (from_even + from_odd).astype(F32) + from_pivot.astype(F32)
-    schur = partial - jnp.where(is_receiver, both[:rows], 0.0) - from_later
+    next_scale8 = rows_of(next_pivot_scale)
+    (right,) = with_links(
+        right_kernel, [SHAPE((rows, order), BF16)], flags,
+        [(own_rows, None), (pivot_scale8, None), (next_scale8, None)],
+        [prev_first, prev_late, pivot_early, pivot_late, left_next], 2,
+    )
+    form, out_link = with_links(
+        last_kernel, [SHAPE((rows, order), F32), SHAPE((rows, order), BF16)], flags,
+        [
+            (pivot_rows, None), (right, None), (next_rows, None), (mine, None), (partial, None),
+            (pivot_scale8, None), (next_scale8, None),
+        ],
+        links, 2,
+    )
+    from_later = lax.dynamic_update_slice_in_dim(from_later, corner, late_start, 1)
+    schur = form - from_later.astype(F32) - from_pivot.astype(F32)
     return (schur[None], out_link[None])
 
 

time: 275 us -> 300 us (1.091)
  the two profiles are of different devices: /device:TPU:24 before, /device:TPU:7 now
where the time goes in v2:
time: 300 us; the launch traced here: 299 us
  waiting for transfers between devices  145 us (48%)
  Pallas kernels  65 us (22%)
  starting transfers between devices  50.7 us (17%)
  local copies, waits for them, and re-layouts  21.4 us (7%)
  other arithmetic  15.1 us (5%)
    ppermute x12, waiting for transfers between devices, one_step(): return (lax.ppermute(ahead, 'space', up), lax.ppermute(back, 'space', down))  125 us
    ppermute x10, starting transfers between devices, between(): lax.ppermute(block, 'tm', [(a, b) for a, b in route if 0 <= b < parts])  29.8 us
    pallas_call x4, Pallas kernels, with_links(): pl.pallas_call(kernel, out_shape=out_shapes, grid_spec=pltpu.PrefetchScal...  29.1 us
    ppermute x12, starting transfers between devices, one_step(): return (lax.ppermute(ahead, 'space', up), lax.ppermute(back, 'space', down))  20.9 us
    ppermute x10, waiting for transfers between devices, between(): lax.ppermute(block, 'tm', [(a, b) for a, b in route if 0 <= b < parts])  19.9 us
    pallas_call x1, Pallas kernels, early_forms(): pl.pallas_call(functools.partial(early_kernel, size), out_shape=[SHAPE((o...  18.9 us
    unnamed x58, local copies, waits for them, and re-layouts  16.8 us
    pallas_call x1, Pallas kernels, level_forms(): pl.pallas_call(level_kernel, out_shape=[SHAPE((rows, order), BF16), SHAPE...  7.17 us
  transfers between devices with their start and end apart: 22, of which 9 were waited for; matrix products, arithmetic and copies ran while one was open for 6% of the time, Pallas kernels for 22%

profile of v2, /device:TPU:7, one launch (start us, length us, event | category | flops | bytes accessed | tf_op | source)
XLA Modules:
  0.0 298.9 jit_solution(15716598986573940878)
XLA Ops:
  0.6 4.2 %collective-permute-start = (bf16[384,1536]{1,0:T(8,128)(2,1)}, bf16[384,1536]{1,0:T(8,128)(2,1)}, u32[]{:S(2)}, u32[]{:S(2)}) collective-permute-start(bf16[384,1536]{1,0:T(8,128)(2,1)} %bitcast.19), channel_id=1, source_target_pairs={{0,1},{1,2},{2,3},{4,5},{5,6},{6,7},{8,9},{9,10},{10,11},{12,13},{... | collective-permute-start | bytes 3538952 | tf_op jit(solution)/shard_map/ppermute | solution.py:419
  4.9 1.3 collective-permute-start.2
  6.3 0.7 divide_reduce_fusion
  7.0 1.3 copy-done
  8.3 1.3 copy-done.2
  9.6 1.7 copy-done.5
  11.2 3.7 %shard_map.59.refs_0_ = bf16[400,1536]{1,0:T(8,128)(2,1)} custom-call(s32[4]{0:T(128)S(1)} %pad_add_fusion.flags, bf16[384,1536]{1,0:T(8,128)(2,1)S(1)} %bitcast.24, bf16[384,1536]{1,0:T(8,128)(2,1)S(1)} %bitcast.21, f32[384,1536]{1,0:T(8,128)S(1)} %bitcast.26, f32[8,1536]{1,0:T(8,128)S(1)} %broadcast_in_dim.21.reciprocal), custom_call_target="tpu_custom_call" | custom-call | tf_op jit(solution)/shard_map/pallas_call | solution.py:103
  14.9 5.1 %collective-permute-start.4 = (bf16[400,1536]{1,0:T(8,128)(2,1)}, bf16[400,1536]{1,0:T(8,128)(2,1)}, u32[]{:S(2)}, u32[]{:S(2)}) collective-permute-start(bf16[400,1536]{1,0:T(8,128)(2,1)} %shard_map.59.refs_0_), channel_id=1, source_target_pairs={{0,1},{1,2},{2,3},{4,5},{5,6},{6,7},{8,9},{9,10},{10,11},{12,13},{... | collective-permute-start | bytes 3686408 | tf_op jit(solution)/shard_map/ppermute | solution.py:419
  19.9 1.3 collective-permute-start.5
  21.2 7.5 %collective-permute-done = bf16[384,1536]{1,0:T(8,128)(2,1)} collective-permute-done((bf16[384,1536]{1,0:T(8,128)(2,1)}, bf16[384,1536]{1,0:T(8,128)(2,1)}, u32[]{:S(2)}, u32[]{:S(2)}) %collective-permute-start) | collective-permute-done | bytes 1179680 | tf_op jit(solution)/shard_map/ppermute | solution.py:419
  28.8 1.8 collective-permute-start.1
  30.5 3.1 %collective-permute-done.2 = bf16[384,1536]{1,0:T(8,128)(2,1)} collective-permute-done((bf16[384,1536]{1,0:T(8,128)(2,1)}, bf16[384,1536]{1,0:T(8,128)(2,1)}, u32[]{:S(2)}, u32[]{:S(2)}) %collective-permute-start.2) | collective-permute-done | bytes 1179680 | tf_op jit(solution)/shard_map/ppermute | solution.py:419
  33.6 1.3 collective-permute-start.3
  35.1 20.0 %collective-permute-done.4.refs_1_ = bf16[400,1536]{1,0:T(8,128)(2,1)} collective-permute-done((bf16[400,1536]{1,0:T(8,128)(2,1)}, bf16[400,1536]{1,0:T(8,128)(2,1)}, u32[]{:S(2)}, u32[]{:S(2)}) %collective-permute-start.4) | collective-permute-done | bytes 1228832 | tf_op jit(solution)/shard_map/ppermute | solution.py:419
  55.1 0.7 collective-permute-start.6
  55.8 4.1 %collective-permute-done.5.refs_2_ = bf16[400,1536]{1,0:T(8,128)(2,1)} collective-permute-done((bf16[400,1536]{1,0:T(8,128)(2,1)}, bf16[400,1536]{1,0:T(8,128)(2,1)}, u32[]{:S(2)}, u32[]{:S(2)}) %collective-permute-start.5) | collective-permute-done | bytes 1228832 | tf_op jit(solution)/shard_map/ppermute | solution.py:419
  59.9 1.3 collective-permute-start.7
  61.2 24.0 %collective-permute-done.3 = bf16[384,1536]{1,0:T(8,128)(2,1)} collective-permute-done((bf16[384,1536]{1,0:T(8,128)(2,1)}, bf16[384,1536]{1,0:T(8,128)(2,1)}, u32[]{:S(2)}, u32[]{:S(2)}) %collective-permute-start.3) | collective-permute-done | bytes 1179680 | tf_op jit(solution)/shard_map/ppermute | solution.py:419
  85.2 3.5 %broadcast_select_fusion = (bf16[384,1536]{1,0:T(8,128)(2,1)}, bf16[384,1536]{1,0:T(8,128)(2,1)S(1)}, bf16[384,1536]{1,0:T(8,128)(2,1)S(1)}, bf16[384,1536]{1,0:T(8,128)(2,1)S(1)}, bf16[384,1536]{1,0:T(8,128)(2,1)S(1)}) fusion(pred[]{:T(512)S(6)} %lt.20, bf16[384,1536]{1,0:T(8,128)(2,1)} %collective-permute-done.1, ...), kind=kLoop, calls=%fused_computation.8 | loop fusion | flops 7667712 | bytes 11796485 | tf_op jit(solution)/shard_map/jit(_where)/select_n | solution.py:453
  89.0 0.7 collective-permute-start.13
  89.8 1.3 collective-permute-start.14
  91.1 0.7 collective-permute-start.8
  91.8 19.6 %collective-permute-done.7.refs_4_ = bf16[400,1536]{1,0:T(8,128)(2,1)S(1)} collective-permute-done((bf16[400,1536]{1,0:T(8,128)(2,1)}, bf16[400,1536]{1,0:T(8,128)(2,1)S(1)}, u32[]{:S(2)}, u32[]{:S(2)}) %collective-permute-start.7) | collective-permute-done | bytes 1228832 | tf_op jit(solution)/shard_map/ppermute | solution.py:419
  111.4 1.3 collective-permute-start.9
  112.7 3.2 %multiply_convert_fusion.prev_whole.prev_early = bf16[1536,1536]{1,0:T(8,128)(2,1)} fusion(bf16[1536,1536]{1,0:T(8,128)(2,1)S(1)} %pad_maximum_fusion, f32[1536]{0:T(1024)S(1)} %divide_reduce_fusion), kind=kLoop, calls=%fused_computation | loop fusion | flops 7077888 | bytes 9443328 | tf_op jit(solution)/shard_map/convert_element_type | solution.py:34
  115.9 47.1 %collective-permute-done.9.refs_6_ = bf16[400,1536]{1,0:T(8,128)(2,1)S(1)} collective-permute-done((bf16[400,1536]{1,0:T(8,128)(2,1)S(1)}, bf16[400,1536]{1,0:T(8,128)(2,1)S(1)}, u32[]{:S(2)}, u32[]{:S(2)}) %collective-permute-start.9) | collective-permute-done | bytes 1228832 | tf_op jit(solution)/shard_map/ppermute | solution.py:419
  163.0 18.9 %shard_map.60 = (bf16[1536,1536]{1,0:T(8,128)(2,1)}, f32[384,1536]{1,0:T(8,128)S(1)}, f32[384,1536]{1,0:T(8,128)S(1)}, bf16[1536,1536]{1,0:T(8,128)(2,1)S(1)}, bf16[384,1536]{1,0:T(8,128)(2,1)S(1)}) custom-call(s32[4]{0:T(128)S(1)} %pad_add_fusion.flags, bf16[1536,1536]{1,0:T(8,128)(2,1)} %multiply_convert_fusion.prev_whole.prev_early, ...), custom_call_target="tpu_custom_call" | custom-call | tf_op jit(solution)/shard_map/pallas_call | solution.py:150
  181.9 2.1 copy-done.8
  184.1 1.4 copy-done.10
  185.5 1.4 copy-done.12
  186.9 1.3 collective-permute-start.10
  188.1 0.9 slice_select_fusion.1
  189.2 0.8 slice_select_fusion
  190.8 1.3 collective-permute-start.11
  192.1 6.6 %collective-permute-start.12 = (f32[1536]{0:T(1024)}, f32[1536]{0:T(1024)S(1)}, u32[]{:S(2)}, u32[]{:S(2)}) collective-permute-start(f32[1536]{0:T(1024)} %pad_maximum_fusion.1), channel_id=1, source_target_pairs={{4,0},{8,4},{12,8},{16,12},{20,16},{24,20},{28,24},{5,1},{9,5},{13... | collective-permute-start | bytes 18440 | tf_op jit(solution)/shard_map/ppermute | solution.py:410
  198.7 0.7 divide_convert_fusion.2
  200.3 1.7 copy-done.13
  202.0 7.2 %shard_map.61 = (bf16[384,1536]{1,0:T(8,128)(2,1)}, f32[8,1536]{1,0:T(8,128)S(1)}, f32[8,1536]{1,0:T(8,128)S(1)}) custom-call(s32[4]{0:T(128)S(1)} %pad_add_fusion.flags, bf16[1536,1536]{1,0:T(8,128)(2,1)} %get-tuple-element.22.link.early, bf16[384,1536]{1,0:T(8,128)(2,1)S(1)} %get-tuple-element.25.mine, bf16[8,1536]{1,0:T(8,128)(2,1)S(1)} %broadcast_in_dim.23.scale, ...), custom_call_target="tpu_custom_call" | custom-call | tf_op jit(solution)/shard_map/pallas_call | solution.py:276
  209.3 1.0 copy-done.14
  210.3 1.3 copy-done.15
  211.6 6.3 %shard_map.62 = (bf16[384,1536]{1,0:T(8,128)(2,1)S(1)}, bf16[384,384]{1,0:T(8,128)(2,1)S(1)}, bf16[384,1536]{1,0:T(8,128)(2,1)S(1)}, f32[8,384]{1,0:T(8,128)S(1)}, f32[8,1536]{1,0:T(8,128)S(1)}) custom-call(s32[4]{0:T(128)S(1)} %pad_add_fusion.flags, f32[8,1536]{1,0:T(8,128)S(1)} %copy-done.21, bf16[384,1536]{1,0:T(8,128)(2,1)S(1)} %bitcast.23, ...), custom_call_target="tpu_custom_call" | custom-call | tf_op jit(solution)/shard_map/pallas_call | solution.py:218
  217.9 1.0 copy-done.16
  218.9 0.6 copy-done.22
  219.5 0.6 copy-done.23
  220.1 0.7 copy-done.24
  220.8 1.5 collective-permute-start.18
  222.3 4.1 %collective-permute-start.19 = (bf16[384,1536]{1,0:T(8,128)(2,1)}, bf16[384,1536]{1,0:T(8,128)(2,1)}, u32[]{:S(2)}, u32[]{:S(2)}) collective-permute-start(bf16[384,1536]{1,0:T(8,128)(2,1)} %get-tuple-element.37), channel_id=1, source_target_pairs={{4,0},{8,4},{12,8},{16,12},{20,16},{24,20},{28,24},{5,1},{9,5},{13... | collective-permute-start | bytes 3538952 | tf_op jit(solution)/shard_map/ppermute | solution.py:410
  226.4 0.6 slice_reduce_fusion.2
  227.1 1.3 dynamic_update_slice.6
  228.4 0.7 collective-permute-start.16
  229.1 0.8 slice_reduce_fusion.1
  229.9 0.8 slice_reduce_fusion
  230.8 0.7 copy-done.19
  231.5 5.8 %shard_map.63.rows.next_rows = bf16[384,1536]{1,0:T(8,128)(2,1)S(1)} custom-call(s32[4]{0:T(128)S(1)} %pad_add_fusion.flags, bf16[1536,1536]{1,0:T(8,128)(2,1)} %collective-permute-done.10.pivot_rows.pivot_early, bf16[8,1536]{1,0:T(8,128)(2,1)S(1)} %copy-done.19, bf16[1536,1536]{1,0:T(8,128)(2,1)} %get-tuple-element.22.link.early, ...), custom_call_target="tpu_custom_call" | custom-call | tf_op jit(solution)/shard_map/pallas_call | solution.py:382
  237.3 1.3 collective-permute-start.15
  238.7 7.0 %shard_map.64.ready = bf16[384,1536]{1,0:T(8,128)(2,1)S(1)} custom-call(s32[4]{0:T(128)S(1)} %pad_add_fusion.flags, bf16[384,1536]{1,0:T(8,128)(2,1)S(1)} %shard_map.63.rows.next_rows, bf16[8,1536]{1,0:T(8,128)(2,1)S(1)} %broadcast_in_dim.27.scale, bf16[8,1536]{1,0:T(8,128)(2,1)S(1)} %copy-done.19, bf16[1536,1536]{1,0:T(8,128)(2,1)} %get-tuple-element.22.link.early, ...), custom_call_target="tpu_custom_call" | custom-call | tf_op jit(solution)/shard_map/pallas_call | solution.py:382
  245.7 0.7 collective-permute-start.21
  246.4 11.1 %collective-permute-start.20 = (bf16[384,384]{1,0:T(8,128)(2,1)S(1)}, bf16[384,384]{1,0:T(8,128)(2,1)S(1)}, u32[]{:S(2)}, u32[]{:S(2)}) collective-permute-start(bf16[384,384]{1,0:T(8,128)(2,1)S(1)} %copy-done.25), channel_id=1, source_target_pairs={{4,0},{8,4},{12,8},{16,12},{20,16},{24,20},{28,24},{5,1},{9,5},{13... | collective-permute-start | bytes 884744 | tf_op jit(solution)/shard_map/ppermute | solution.py:410
  257.6 1.3 collective-permute-start.17
  258.9 0.8 constant_dynamic-update-slice_fusion
  259.7 19.6 %collective-permute-done.17 = bf16[1536]{0:T(1024)(128)(2,1)S(1)} collective-permute-done((bf16[1536]{0:T(1024)(128)(2,1)S(1)}, bf16[1536]{0:T(1024)(128)(2,1)S(1)}, u32[]{:S(2)}, u32[]{:S(2)}) %collective-permute-start.17) | collective-permute-done | bytes 3104 | tf_op jit(solution)/shard_map/ppermute | solution.py:410
  279.4 7.8 %shard_map.65.right = bf16[384,1536]{1,0:T(8,128)(2,1)S(1)} custom-call(s32[4]{0:T(128)S(1)} %pad_add_fusion.flags, bf16[384,1536]{1,0:T(8,128)(2,1)S(1)} %bitcast.25, bf16[8,1536]{1,0:T(8,128)(2,1)S(1)} %copy-done.19, bf16[8,1536]{1,0:T(8,128)(2,1)S(1)} %broadcast_in_dim.26.next_scale, bf16[1536,1536]{1,0:T(8,128)(2,1)S(1)} %bitcast.18, ...), custom_call_target="tpu_custom_call" | custom-call | tf_op jit(solution)/shard_map/pallas_call | solution.py:382
  287.2 8.5 %shard_map.66 = (f32[384,1536]{1,0:T(8,128)S(1)}, bf16[384,1536]{1,0:T(8,128)(2,1)}) custom-call(s32[4]{0:T(128)S(1)} %pad_add_fusion.flags, bf16[384,1536]{1,0:T(8,128)(2,1)S(1)} %collective-permute-done.15.rows, bf16[384,1536]{1,0:T(8,128)(2,1)S(1)} %shard_map.65.right, bf16[384,1536]{1,0:T(8,128)(2,1)S(1)} %shard_map.63.rows.next_rows, ...), custom_call_target="tpu_custom_call" | custom-call | tf_op jit(solution)/shard_map/pallas_call | solution.py:382
  295.7 3.2 %subtract_bitcast_fusion = f32[1,384,1536]{2,1,0:T(8,128)} fusion(bf16[384,1536]{1,0:T(8,128)(2,1)S(1)} %collective-permute-done.21, f32[384,1536]{1,0:T(8,128)S(1)} %get-tuple-element.36, bf16[384,1536]{1,0:T(8,128)(2,1)} %constant_dynamic-update-slice_fusion), kind=kLoop, calls=%fused_computation.2 | loop fusion | flops 2359296 | bytes 7077888 | tf_op jit(solution)/shard_map/broadcast_in_dim | solution.py:526
  (84 shorter events, 2.7 us)
Async XLA Ops:
  0.6 28.1 %collective-permute-start = (bf16[384,1536]{1,0:T(8,128)(2,1)}, bf16[384,1536]{1,0:T(8,128)(2,1)}, u32[]{:S(2)}, u32[]{:S(2)}) collective-permute-start(bf16[384,1536]{1,0:T(8,128)(2,1)} %bitcast.19), channel_id=1, source_target_pairs={{0,1},{1,2},{2,3},{4,5},{5,6},{6,7},{8,9},{9,10},{10,11},{12,13},{... | collective-permute-start | bytes 3538952 | tf_op jit(solution)/shard_map/ppermute | solution.py:419
  4.9 28.7 %collective-permute-start.2 = (bf16[384,1536]{1,0:T(8,128)(2,1)}, bf16[384,1536]{1,0:T(8,128)(2,1)}, u32[]{:S(2)}, u32[]{:S(2)}) collective-permute-start(bf16[384,1536]{1,0:T(8,128)(2,1)} %bitcast.20), channel_id=1, source_target_pairs={{1,0},{2,1},{3,2},{5,4},{6,5},{7,6},{9,8},{10,9},{11,10},{13,12},{... | collective-permute-start | bytes 3538952 | tf_op jit(solution)/shard_map/ppermute | solution.py:419
  7.0 7.9 %copy-start.20 = (f32[8,1536]{1,0:T(8,128)}, f32[8,1536]{1,0:T(8,128)S(1)}, u32[]{:S(2)}) copy-start(f32[8,1536]{1,0:T(8,128)S(1)} %broadcast_in_dim.21.reciprocal) | copy-start | bytes 147460
  7.0 1.3 copy-start
  8.3 1.3 copy-start.2
  9.6 1.7 copy-start.5
  11.2 23.7 %copy-start.3 = (bf16[1,384,1536]{2,1,0:T(8,128)(2,1)S(1)}, bf16[1,384,1536]{2,1,0:T(8,128)(2,1)}, u32[]{:S(2)}) copy-start(bf16[1,384,1536]{2,1,0:T(8,128)(2,1)} %param.5) | copy-start | bytes 3538948
  14.9 40.2 %collective-permute-start.4 = (bf16[400,1536]{1,0:T(8,128)(2,1)}, bf16[400,1536]{1,0:T(8,128)(2,1)}, u32[]{:S(2)}, u32[]{:S(2)}) collective-permute-start(bf16[400,1536]{1,0:T(8,128)(2,1)} %shard_map.59.refs_0_), channel_id=1, source_target_pairs={{0,1},{1,2},{2,3},{4,5},{5,6},{6,7},{8,9},{9,10},{10,11},{12,13},{... | collective-permute-start | bytes 3686408 | tf_op jit(solution)/shard_map/ppermute | solution.py:419
  19.9 40.0 %collective-permute-start.5 = (bf16[400,1536]{1,0:T(8,128)(2,1)}, bf16[400,1536]{1,0:T(8,128)(2,1)}, u32[]{:S(2)}, u32[]{:S(2)}) collective-permute-start(bf16[400,1536]{1,0:T(8,128)(2,1)} %shard_map.59.refs_0_), channel_id=1, source_target_pairs={{1,0},{2,1},{3,2},{5,4},{6,5},{7,6},{9,8},{10,9},{11,10},{13,12},{... | collective-permute-start | bytes 3686408 | tf_op jit(solution)/shard_map/ppermute | solution.py:419
  28.8 32.4 %collective-permute-start.1 = (bf16[384,1536]{1,0:T(8,128)(2,1)}, bf16[384,1536]{1,0:T(8,128)(2,1)}, u32[]{:S(2)}, u32[]{:S(2)}) collective-permute-start(bf16[384,1536]{1,0:T(8,128)(2,1)} %collective-permute-done), channel_id=1, source_target_pairs={{1,2},{2,3},{5,6},{6,7},{9,10},{10,11},{13,14},{14,15},{17,18},{18... | collective-permute-start | bytes 3538952 | tf_op jit(solution)/shard_map/ppermute | solution.py:419
  33.6 51.6 %collective-permute-start.3 = (bf16[384,1536]{1,0:T(8,128)(2,1)}, bf16[384,1536]{1,0:T(8,128)(2,1)}, u32[]{:S(2)}, u32[]{:S(2)}) collective-permute-start(bf16[384,1536]{1,0:T(8,128)(2,1)} %collective-permute-done.2), channel_id=1, source_target_pairs={{1,0},{2,1},{5,4},{6,5},{9,8},{10,9},{13,12},{14,13},{17,16},{18,1... | collective-permute-start | bytes 3538952 | tf_op jit(solution)/shard_map/ppermute | solution.py:419
  34.9 50.3 %copy-start.1 = (bf16[1,384,1536]{2,1,0:T(8,128)(2,1)S(1)}, bf16[1,384,1536]{2,1,0:T(8,128)(2,1)}, u32[]{:S(2)}) copy-start(bf16[1,384,1536]{2,1,0:T(8,128)(2,1)} %param.6) | copy-start | bytes 3538948
  55.1 36.0 %collective-permute-start.6 = (bf16[400,1536]{1,0:T(8,128)(2,1)}, bf16[400,1536]{1,0:T(8,128)(2,1)S(1)}, u32[]{:S(2)}, u32[]{:S(2)}) collective-permute-start(bf16[400,1536]{1,0:T(8,128)(2,1)} %collective-permute-done.4.refs_1_), channel_id=1, source_target_pairs={{1,2},{2,3},{5,6},{6,7},{9,10},{10,11},{13,14},{14,15},{17,18},{18... | collective-permute-start | bytes 3686408 | tf_op jit(solution)/shard_map/ppermute | solution.py:419
  59.9 51.5 %collective-permute-start.7 = (bf16[400,1536]{1,0:T(8,128)(2,1)}, bf16[400,1536]{1,0:T(8,128)(2,1)S(1)}, u32[]{:S(2)}, u32[]{:S(2)}) collective-permute-start(bf16[400,1536]{1,0:T(8,128)(2,1)} %collective-permute-done.5.refs_2_), channel_id=1, source_target_pairs={{1,0},{2,1},{5,4},{6,5},{9,8},{10,9},{13,12},{14,13},{17,16},{18,1... | collective-permute-start | bytes 3686408 | tf_op jit(solution)/shard_map/ppermute | solution.py:419
  89.0 120.2 %collective-permute-start.13 = (bf16[384,1536]{1,0:T(8,128)(2,1)}, bf16[384,1536]{1,0:T(8,128)(2,1)S(1)}, u32[]{:S(2)}, u32[]{:S(2)}) collective-permute-start(bf16[384,1536]{1,0:T(8,128)(2,1)} %collective-permute-done.1), channel_id=1, source_target_pairs={{2,3},{6,7},{10,11},{14,15},{18,19},{22,23},{26,27},{30,31}} | collective-permute-start | bytes 3538952 | tf_op jit(solution)/shard_map/ppermute | solution.py:419
  89.8 120.5 %collective-permute-start.14 = (bf16[384,1536]{1,0:T(8,128)(2,1)}, bf16[384,1536]{1,0:T(8,128)(2,1)}, u32[]{:S(2)}, u32[]{:S(2)}) collective-permute-start(bf16[384,1536]{1,0:T(8,128)(2,1)} %collective-permute-done.3), channel_id=1, source_target_pairs={{1,0},{5,4},{9,8},{13,12},{17,16},{21,20},{25,24},{29,28}} | collective-permute-start | bytes 3538952 | tf_op jit(solution)/shard_map/ppermute | solution.py:419
  91.1 24.8 %collective-permute-start.8 = (bf16[400,1536]{1,0:T(8,128)(2,1)S(1)}, bf16[400,1536]{1,0:T(8,128)(2,1)S(1)}, u32[]{:S(2)}, u32[]{:S(2)}) collective-permute-start(bf16[400,1536]{1,0:T(8,128)(2,1)S(1)} %collective-permute-done.6.refs_3_), channel_id=1, source_target_pairs={{2,3},{6,7},{10,11},{14,15},{18,19},{22,23},{26,27},{30,31}} | collective-permute-start | bytes 3686408 | tf_op jit(solution)/shard_map/ppermute | solution.py:419
  111.4 51.6 %collective-permute-start.9 = (bf16[400,1536]{1,0:T(8,128)(2,1)S(1)}, bf16[400,1536]{1,0:T(8,128)(2,1)S(1)}, u32[]{:S(2)}, u32[]{:S(2)}) collective-permute-start(bf16[400,1536]{1,0:T(8,128)(2,1)S(1)} %collective-permute-done.7.refs_4_), channel_id=1, source_target_pairs={{1,0},{5,4},{9,8},{13,12},{17,16},{21,20},{25,24},{29,28}} | collective-permute-start | bytes 3686408 | tf_op jit(solution)/shard_map/ppermute | solution.py:419
  112.7 50.3 %copy-start.6 = (f32[1,384,1536]{2,1,0:T(8,128)S(1)}, f32[1,384,1536]{2,1,0:T(8,128)}, u32[]{:S(2)}) copy-start(f32[1,384,1536]{2,1,0:T(8,128)} %param.4) | copy-start | bytes 7077892
  181.9 2.1 copy-start.8
  184.0 1.4 copy-start.10
  185.5 1.4 copy-start.12
  186.9 43.9 %collective-permute-start.10 = (bf16[1536,1536]{1,0:T(8,128)(2,1)}, bf16[1536,1536]{1,0:T(8,128)(2,1)}, u32[]{:S(2)}, u32[]{:S(2)}) collective-permute-start(bf16[1536,1536]{1,0:T(8,128)(2,1)} %get-tuple-element.22.link.early), channel_id=1, source_target_pairs={{0,4},{8,12},{16,20},{24,28},{1,5},{9,13},{17,21},{25,29},{2,6},{1... | collective-permute-start | bytes 14155784 | tf_op jit(solution)/shard_map/ppermute | solution.py:410
  190.8 7.9 %collective-permute-start.11 = (f32[1536]{0:T(1024)S(1)}, f32[1536]{0:T(1024)}, u32[]{:S(2)}, u32[]{:S(2)}) collective-permute-start(f32[1536]{0:T(1024)S(1)} %maximum_subtract_fusion), channel_id=1, source_target_pairs={{0,4},{8,12},{16,20},{24,28},{1,5},{9,13},{17,21},{25,29},{2,6},{1... | collective-permute-start | bytes 18440 | tf_op jit(solution)/shard_map/ppermute | solution.py:410
  192.1 7.6 %collective-permute-start.12 = (f32[1536]{0:T(1024)}, f32[1536]{0:T(1024)S(1)}, u32[]{:S(2)}, u32[]{:S(2)}) collective-permute-start(f32[1536]{0:T(1024)} %pad_maximum_fusion.1), channel_id=1, source_target_pairs={{4,0},{8,4},{12,8},{16,12},{20,16},{24,20},{28,24},{5,1},{9,5},{13... | collective-permute-start | bytes 18440 | tf_op jit(solution)/shard_map/ppermute | solution.py:410
  200.3 8.9 %copy-start.18 = (bf16[8,1536]{1,0:T(8,128)(2,1)}, bf16[8,1536]{1,0:T(8,128)(2,1)S(1)}, u32[]{:S(2)}) copy-start(bf16[8,1536]{1,0:T(8,128)(2,1)S(1)} %broadcast_in_dim.22.pivot_scale) | copy-start | bytes 73732
  200.3 1.7 copy-start.13
  202.0 8.3 %copy-start.7 = (bf16[384,1536]{1,0:T(8,128)(2,1)S(1)}, bf16[384,1536]{1,0:T(8,128)(2,1)}, u32[]{:S(2)}) copy-start(bf16[384,1536]{1,0:T(8,128)(2,1)} %get-tuple-element.27.far) | copy-start | bytes 3538948
  202.0 8.3 %copy-start.9 = (bf16[1536,1536]{1,0:T(8,128)(2,1)S(1)}, bf16[1536,1536]{1,0:T(8,128)(2,1)}, u32[]{:S(2)}) copy-start(bf16[1536,1536]{1,0:T(8,128)(2,1)} %copy-done.8) | copy-start | bytes 14155780
  202.0 8.3 %copy-start.21 = (f32[8,1536]{1,0:T(8,128)S(1)}, f32[8,1536]{1,0:T(8,128)}, u32[]{:S(2)}) copy-start(f32[8,1536]{1,0:T(8,128)} %copy-done.20) | copy-start | bytes 147460
  209.3 1.0 copy-start.14
  210.3 1.3 copy-start.15
  211.6 19.2 %copy-start.26 = (f32[1536]{0:T(1024)S(1)}, f32[1536]{0:T(1024)}, u32[]{:S(2)}) copy-start(f32[1536]{0:T(1024)} %get-tuple-element.41) | copy-start | bytes 18436
  217.9 1.0 copy-start.16
  218.9 0.6 copy-start.22
  219.5 0.6 copy-start.23
  220.1 0.7 copy-start.24
  220.8 17.8 %collective-permute-start.18 = (bf16[384,1536]{1,0:T(8,128)(2,1)S(1)}, bf16[384,1536]{1,0:T(8,128)(2,1)S(1)}, u32[]{:S(2)}, u32[]{:S(2)}) collective-permute-start(bf16[384,1536]{1,0:T(8,128)(2,1)S(1)} %get-tuple-element.30.late), channel_id=1, source_target_pairs={{0,4},{8,12},{16,20},{24,28},{1,5},{9,13},{17,21},{25,29},{2,6},{1... | collective-permute-start | bytes 3538952 | tf_op jit(solution)/shard_map/ppermute | solution.py:410
  222.3 36.6 %collective-permute-start.19 = (bf16[384,1536]{1,0:T(8,128)(2,1)}, bf16[384,1536]{1,0:T(8,128)(2,1)}, u32[]{:S(2)}, u32[]{:S(2)}) collective-permute-start(bf16[384,1536]{1,0:T(8,128)(2,1)} %get-tuple-element.37), channel_id=1, source_target_pairs={{4,0},{8,4},{12,8},{16,12},{20,16},{24,20},{28,24},{5,1},{9,5},{13... | collective-permute-start | bytes 3538952 | tf_op jit(solution)/shard_map/ppermute | solution.py:410
  228.4 2.3 collective-permute-start.16
  230.8 0.7 copy-start.19
  237.3 49.9 %collective-permute-start.15 = (bf16[384,1536]{1,0:T(8,128)(2,1)S(1)}, bf16[384,1536]{1,0:T(8,128)(2,1)S(1)}, u32[]{:S(2)}, u32[]{:S(2)}) collective-permute-start(bf16[384,1536]{1,0:T(8,128)(2,1)S(1)} %shard_map.63.rows.next_rows), channel_id=1, source_target_pairs={{20,28},{21,29},{22,30},{23,31}} | collective-permute-start | bytes 3538952 | tf_op jit(solution)/shard_map/ppermute | solution.py:410
  238.6 40.7 %slice-start = ((s8[4718592]{0:T(1024)(128)(4,1)}), s8[4194304]{0:T(1024)(128)(4,1)S(1)}, s32[]{:S(2)}) async-start(s8[4718592]{0:T(1024)(128)(4,1)} %bitcast.17), calls=%async_computation | async-start | bytes 8388608
  238.7 7.8 %copy-start.25 = (bf16[384,384]{1,0:T(8,128)(2,1)S(1)}, bf16[384,384]{1,0:T(8,128)(2,1)}, u32[]{:S(2)}) copy-start(bf16[384,384]{1,0:T(8,128)(2,1)} %copy-done.24) | copy-start | bytes 884740
  238.7 40.6 %slice-start.1 = ((s8[4718592]{0:T(1024)(128)(4,1)}), s8[524288]{0:T(1024)(128)(4,1)S(1)}, s32[]{:S(2)}) async-start(s8[4718592]{0:T(1024)(128)(4,1)} %bitcast.17), calls=%async_computation.1 | async-start | bytes 1048576
  238.7 40.6 %copy-start.4 = (bf16[1,384,1536]{2,1,0:T(8,128)(2,1)S(1)}, bf16[1,384,1536]{2,1,0:T(8,128)(2,1)}, u32[]{:S(2)}) copy-start(bf16[1,384,1536]{2,1,0:T(8,128)(2,1)} %param.5) | copy-start | bytes 3538948
  238.7 40.6 %copy-start.17 = (bf16[384,1536]{1,0:T(8,128)(2,1)S(1)}, bf16[384,1536]{1,0:T(8,128)(2,1)}, u32[]{:S(2)}) copy-start(bf16[384,1536]{1,0:T(8,128)(2,1)} %copy-done.16) | copy-start | bytes 3538948
  245.7 50.0 %collective-permute-start.21 = (bf16[384,1536]{1,0:T(8,128)(2,1)S(1)}, bf16[384,1536]{1,0:T(8,128)(2,1)S(1)}, u32[]{:S(2)}, u32[]{:S(2)}) collective-permute-start(bf16[384,1536]{1,0:T(8,128)(2,1)S(1)} %shard_map.64.ready), channel_id=1, source_target_pairs={{20,12},{21,13},{22,14},{23,15}} | collective-permute-start | bytes 3538952 | tf_op jit(solution)/shard_map/ppermute | solution.py:410
  246.4 12.4 %collective-permute-start.20 = (bf16[384,384]{1,0:T(8,128)(2,1)S(1)}, bf16[384,384]{1,0:T(8,128)(2,1)S(1)}, u32[]{:S(2)}, u32[]{:S(2)}) collective-permute-start(bf16[384,384]{1,0:T(8,128)(2,1)S(1)} %copy-done.25), channel_id=1, source_target_pairs={{4,0},{8,4},{12,8},{16,12},{20,16},{24,20},{28,24},{5,1},{9,5},{13... | collective-permute-start | bytes 884744 | tf_op jit(solution)/shard_map/ppermute | solution.py:410
  257.6 21.8 %collective-permute-start.17 = (bf16[1536]{0:T(1024)(128)(2,1)S(1)}, bf16[1536]{0:T(1024)(128)(2,1)S(1)}, u32[]{:S(2)}, u32[]{:S(2)}) collective-permute-start(bf16[1536]{0:T(1024)(128)(2,1)S(1)} %divide_convert_fusion), channel_id=1, source_target_pairs={{4,12},{20,28},{5,13},{21,29},{6,14},{22,30},{7,15},{23,31}} | collective-permute-start | bytes 9224 | tf_op jit(solution)/shard_map/ppermute | solution.py:410
  279.4 7.8 %copy-start.11 = (f32[384,1536]{1,0:T(8,128)S(1)}, f32[384,1536]{1,0:T(8,128)}, u32[]{:S(2)}) copy-start(f32[384,1536]{1,0:T(8,128)} %copy-done.10) | copy-start | bytes 7077892

commit v3 on v2

--- a/solution.py
+++ b/solution.py
@@ -116,7 +116,7 @@
 
 def early_kernel(size, flags, prev_whole, prev_rows, own_rows, separator, *refs):
     sources = refs[: 2 * size - 1]
-    link, partial, form, own_out, mine, own, sems = refs[2 * size - 1 :]
+    link, partial, form, own_out, mine, own, sems = refs[2 * size + 1 :]
     rows = separator.shape[0]
     step = pl.program_id(0)
     here = pl.ds(pl.multiple_of(step * WIDTH, WIDTH), WIDTH)
@@ -323,7 +323,8 @@
 
 
 def next_rows_kernel(flags, pivot_rows, pivot_scale, early, late, *refs):
-    result, link, sems = refs[-3:]
+    result, token, link, sems = refs[-4:]
+    token[...] = jnp.ones_like(token)
     wait = fetched(early, late, link, sems, [flags[1]])
     scaled = times(pivot_rows[...], pivot_scale)
     wait()
@@ -373,7 +374,7 @@
     new[...] = jnp.where(flags[3] == 1, last, jnp.where(flags[2] == 1, mine[...], next_rows[...]))
 
 
-def with_links(kernel, out_shapes, flags, blocks, arrays, links):
+def with_links(kernel, out_shapes, flags, blocks, arrays, links, megabytes):
     order = arrays[0].shape[1]
     rows = arrays[1].shape[0]
     size = order // rows
@@ -389,7 +390,7 @@
             out_specs=[whole_spec(out.shape) for out in out_shapes],
             scratch_shapes=[pltpu.VMEM((order, order), BF16)] * links + [pltpu.SemaphoreType.DMA(sems)],
         ),
-        compiler_params=pltpu.CompilerParams(vmem_limit_bytes=32 * 1024 * 1024),
+        compiler_params=pltpu.CompilerParams(vmem_limit_bytes=megabytes * 1024 * 1024),
         cost_estimate=FREE,
     )(flags, *[block for block, _ in blocks], *arrays)
 
@@ -438,8 +439,13 @@
     own_arrived = [(own_long, own_long)]
     prev_arrived = [(prev_rows, prev_rows)]
     for step in range(1, size):
+        blocks = prev_arrived[-1]
+        if step == size - 1:
+            went = [block[rows + EXTRA - 1, 0] == 0 for block in own_arrived[-1]]
+            zero = jnp.zeros_like(prev_rows)
+            blocks = [jnp.where(jnp.logical_and(*went), block, zero) for block in blocks]
         own_arrived.append(one_step(*own_arrived[-1], step))
-        prev_arrived.append(one_step(*prev_arrived[-1], step))
+        prev_arrived.append(one_step(*blocks, step))
     words_arrived = [tuple(block[rows:] for block in pair) for pair in own_arrived]
 
     left_side = place < size // 2
@@ -470,6 +476,7 @@
     sources = [own_long]
     for up, down in own_arrived[1:]:
         sources += [up, down]
+    sources += [scale, pivot_scale]
     prev_first = scaled_by(prev_first, reciprocal)
     link, partial, prev_form, own_full, mine = early_forms(
         flags, prev_first, prev_rows, own_scaled, separator, sources
@@ -481,22 +488,24 @@
     late_scale = lax.dynamic_slice_in_dim(pivot_scale, late_start, rows, 0)
     late_scale = jnp.where(is_end, late_scale, jnp.zeros_like(late_scale))
     pivot_early = between(link, [(p, p + 1) for p in even])
-    from_later = between(update, [(p, p - 1) for p in everyone])
     late, corner, prev_late, left_late, right_late = late_forms(
         flags, rows_of(reciprocal), prev_rows, mine, own_full, scale8, rows_of(late_scale),
         from_below, from_above, prev_far, right_diag,
     )
+    pivot_late = between(late, [(p, p + 1) for p in even])
     left_diag = lax.dynamic_update_slice_in_dim(left_diag[0], left_late[0], late_start, 0)
-    left_diag = between(left_diag, [(p, p - 1) for p in even])
-    pivot_late = between(late, [(p, p + 1) for p in even])
-    corner = between(corner, [(p, p - 1) for p in everyone])
+    high = lax.reduce_precision(left_diag, 8, 7)
+    words = jnp.pad(jnp.stack([high, left_diag - high]).astype(BF16), ((0, EXTRA - 2), (0, 0)))
+    update = jnp.concatenate([lax.dynamic_update_slice_in_dim(update, corner, late_start, 1), words])
+    from_later = between(update, [(p, p - 1) for p in everyone])
 
     own_block = pl.BlockSpec((rows, order), lambda j, f: (f[1], 0), pipeline_mode=pl.Buffered(1))
-    (next_rows,) = with_links(
-        next_rows_kernel, [SHAPE((rows, order), BF16)], flags,
-        [(pivot_early, own_block), (pivot_scale8, None)], [link, late], 1,
+    next_rows, token = with_links(
+        next_rows_kernel, [SHAPE((rows, order), BF16), SHAPE((8, 128), jnp.int32)], flags,
+        [(pivot_early, own_block), (pivot_scale8, None)], [link, late], 1, 14,
     )
     pivot_rows = between(next_rows, [(p, p + 2) for p in pivots if p != 1])
+    left_diag = jnp.where(token[0, 0] == 1, pair_sum(from_later[rows:], 0), 0.0)
     next_diag = diag - left_diag - right_diag[0] - right_late[0]
     next_scale = (1.0 / jnp.maximum(next_diag, 1.0)).astype(BF16)
     next_pivot_scale = between(next_scale, [(p, p + 2) for p in pivots])
@@ -504,14 +513,14 @@
     links = [link, late, pivot_early, pivot_late]
     (left_next,) = with_links(
         level_2_kernel, [SHAPE((rows, order), BF16)], flags,
-        [(next_rows, None), (rows_of(next_scale), None), (pivot_scale8, None)], links, 2,
+        [(next_rows, None), (rows_of(next_scale), None), (pivot_scale8, None)], links, 2, 20,
     )
     from_pivot = between(left_next, [(p, p - 2) for p in pivots])
     next_scale8 = rows_of(next_pivot_scale)
     (right,) = with_links(
         right_kernel, [SHAPE((rows, order), BF16)], flags,
         [(own_rows, None), (pivot_scale8, None), (next_scale8, None)],
-        [prev_first, prev_late, pivot_early, pivot_late, left_next], 2,
+        [prev_first, prev_late, pivot_early, pivot_late, left_next], 2, 22,
     )
     form, out_link = with_links(
         last_kernel, [SHAPE((rows, order), F32), SHAPE((rows, order), BF16)], flags,
@@ -519,10 +528,9 @@
             (pivot_rows, None), (right, None), (next_rows, None), (mine, None), (partial, None),
             (pivot_scale8, None), (next_scale8, None),
         ],
-        links, 2,
-    )
-    from_later = lax.dynamic_update_slice_in_dim(from_later, corner, late_start, 1)
-    schur = form - from_later.astype(F32) - from_pivot.astype(F32)
+        links, 2, 26,
+    )
+    schur = form - from_later[:rows].astype(F32) - from_pivot.astype(F32)
     return (schur[None], out_link[None])
 
 

time: 300 us -> 292 us (0.973)
  starting transfers between devices: 50.7 us -> 38.6 us
  local copies, waits for them, and re-layouts: 21.4 us -> 24.8 us
    ppermute x10 -> x8, starting transfers between devices: 29.8 us -> 17.2 us  [between(): lax.ppermute(block, 'tm', [(a, b) for a, b in route if 0 <= b < parts])]
    ppermute x10 -> x8, waiting for transfers between devices: 19.9 us -> 23.8 us  [between(): lax.ppermute(block, 'tm', [(a, b) for a, b in route if 0 <= b < parts])]
    unnamed x58 -> x62, local copies, waits for them, and re-layouts: 16.8 us -> 18.1 us
  transfers between devices with their start and end apart: 22 -> 20, of which waited for: 9 -> 10; matrix products, arithmetic and copies ran while one was open for 6% -> 6% of each run, Pallas kernels for 22% -> 15%
where the time goes in v3:
time: 292 us; the launch traced here: 291 us
  waiting for transfers between devices  147 us (50%)
  Pallas kernels  63.9 us (22%)
  starting transfers between devices  38.6 us (13%)
  local copies, waits for them, and re-layouts  24.8 us (8%)
  other arithmetic  13.9 us (5%)
  between operations  3.31 us (1%)
    ppermute x12, waiting for transfers between devices, one_step(): return (lax.ppermute(ahead, 'space', up), lax.ppermute(back, 'space', down))  123 us
    pallas_call x4, Pallas kernels, with_links(): pl.pallas_call(kernel, out_shape=out_shapes, grid_spec=pltpu.PrefetchScal...  29.3 us
    ppermute x8, waiting for transfers between devices, between(): lax.ppermute(block, 'tm', [(a, b) for a, b in route if 0 <= b < parts])  23.8 us
    ppermute x12, starting transfers between devices, one_step(): return (lax.ppermute(ahead, 'space', up), lax.ppermute(back, 'space', down))  21.4 us
    pallas_call x1, Pallas kernels, early_forms(): pl.pallas_call(functools.partial(early_kernel, size), out_shape=[SHAPE((o...  19.1 us
    unnamed x62, local copies, waits for them, and re-layouts  18.1 us
    ppermute x8, starting transfers between devices, between(): lax.ppermute(block, 'tm', [(a, b) for a, b in route if 0 <= b < parts])  17.2 us
    pallas_call x1, Pallas kernels, level_forms(): pl.pallas_call(level_kernel, out_shape=[SHAPE((rows, order), BF16), SHAPE...  6.7 us
  transfers between devices with their start and end apart: 20, of which 10 were waited for; matrix products, arithmetic and copies ran while one was open for 6% of the time, Pallas kernels for 15%

profile of v3, /device:TPU:7, one launch (start us, length us, event | category | flops | bytes accessed | tf_op | source)
XLA Modules:
  0.0 291.1 jit_solution(4049928725834080098)
XLA Ops:
  0.7 0.7 divide_reduce_fusion
  1.5 1.3 copy-done
  2.8 1.3 copy-done.2
  4.0 1.7 copy-done.5
  5.7 2.6 shard_map.59.refs_0_
  8.3 4.6 %collective-permute-start.4 = (bf16[400,1536]{1,0:T(8,128)(2,1)S(1)}, bf16[400,1536]{1,0:T(8,128)(2,1)}, u32[]{:S(2)}, u32[]{:S(2)}) collective-permute-start(bf16[400,1536]{1,0:T(8,128)(2,1)S(1)} %shard_map.59.refs_0_), channel_id=1, source_target_pairs={{0,1},{1,2},{2,3},{4,5},{5,6},{6,7},{8,9},{9,10},{10,11},{12,13},{... | collective-permute-start | bytes 3686408 | tf_op jit(solution)/shard_map/ppermute | solution.py:420
  12.9 1.3 collective-permute-start.5
  14.2 4.1 %collective-permute-start = (bf16[384,1536]{1,0:T(8,128)(2,1)S(1)}, bf16[384,1536]{1,0:T(8,128)(2,1)S(1)}, u32[]{:S(2)}, u32[]{:S(2)}) collective-permute-start(bf16[384,1536]{1,0:T(8,128)(2,1)S(1)} %bitcast.22), channel_id=1, source_target_pairs={{0,1},{1,2},{2,3},{4,5},{5,6},{6,7},{8,9},{9,10},{10,11},{12,13},{... | collective-permute-start | bytes 3538952 | tf_op jit(solution)/shard_map/ppermute | solution.py:420
  18.2 1.3 collective-permute-start.2
  19.5 17.9 %collective-permute-done.4.refs_1_ = bf16[400,1536]{1,0:T(8,128)(2,1)} collective-permute-done((bf16[400,1536]{1,0:T(8,128)(2,1)S(1)}, bf16[400,1536]{1,0:T(8,128)(2,1)}, u32[]{:S(2)}, u32[]{:S(2)}) %collective-permute-start.4) | collective-permute-done | bytes 1228832 | tf_op jit(solution)/shard_map/ppermute | solution.py:420
  37.5 1.8 collective-permute-start.6
  39.2 3.2 %collective-permute-done.5.refs_2_ = bf16[400,1536]{1,0:T(8,128)(2,1)} collective-permute-done((bf16[400,1536]{1,0:T(8,128)(2,1)S(1)}, bf16[400,1536]{1,0:T(8,128)(2,1)}, u32[]{:S(2)}, u32[]{:S(2)}) %collective-permute-start.5) | collective-permute-done | bytes 1228832 | tf_op jit(solution)/shard_map/ppermute | solution.py:420
  42.4 1.3 collective-permute-start.7
  43.7 19.0 %collective-permute-done = bf16[384,1536]{1,0:T(8,128)(2,1)S(1)} collective-permute-done((bf16[384,1536]{1,0:T(8,128)(2,1)S(1)}, bf16[384,1536]{1,0:T(8,128)(2,1)S(1)}, u32[]{:S(2)}, u32[]{:S(2)}) %collective-permute-start) | collective-permute-done | bytes 1179680 | tf_op jit(solution)/shard_map/ppermute | solution.py:420
  62.7 1.7 collective-permute-start.1
  64.4 3.3 %collective-permute-done.2 = bf16[384,1536]{1,0:T(8,128)(2,1)} collective-permute-done((bf16[384,1536]{1,0:T(8,128)(2,1)S(1)}, bf16[384,1536]{1,0:T(8,128)(2,1)}, u32[]{:S(2)}, u32[]{:S(2)}) %collective-permute-start.2) | collective-permute-done | bytes 1179680 | tf_op jit(solution)/shard_map/ppermute | solution.py:420
  67.7 1.3 collective-permute-start.3
  69.2 1.2 slice.278
  71.1 23.0 %collective-permute-done.7.refs_4_ = bf16[400,1536]{1,0:T(8,128)(2,1)} collective-permute-done((bf16[400,1536]{1,0:T(8,128)(2,1)}, bf16[400,1536]{1,0:T(8,128)(2,1)}, u32[]{:S(2)}, u32[]{:S(2)}) %collective-permute-start.7) | collective-permute-done | bytes 1228832 | tf_op jit(solution)/shard_map/ppermute | solution.py:420
  94.0 1.2 slice.279
  95.9 0.7 collective-permute-start.8
  96.6 1.3 collective-permute-start.9
  97.9 21.4 %collective-permute-done.3 = bf16[384,1536]{1,0:T(8,128)(2,1)} collective-permute-done((bf16[384,1536]{1,0:T(8,128)(2,1)}, bf16[384,1536]{1,0:T(8,128)(2,1)}, u32[]{:S(2)}, u32[]{:S(2)}) %collective-permute-start.3) | collective-permute-done | bytes 1179680 | tf_op jit(solution)/shard_map/ppermute | solution.py:420
  119.3 3.3 %broadcast_select_fusion.2 = (bf16[384,1536]{1,0:T(8,128)(2,1)}, bf16[384,1536]{1,0:T(8,128)(2,1)S(1)}, bf16[384,1536]{1,0:T(8,128)(2,1)S(1)}, bf16[384,1536]{1,...) fusion(pred[]{:T(512)S(6)} %lt.20, ...), kind=kLoop, calls=%fused_computation.11 | loop fusion | flops 8847360 | bytes 14155782 | tf_op jit(solution)/shard_map/jit(_where)/select_n | solution.py:459
  123.0 0.9 copy-done.8
  124.0 0.9 slice_select_fusion.1
  124.9 20.7 %collective-permute-done.9.refs_6_ = bf16[400,1536]{1,0:T(8,128)(2,1)S(1)} collective-permute-done((bf16[400,1536]{1,0:T(8,128)(2,1)}, bf16[400,1536]{1,0:T(8,128)(2,1)S(1)}, u32[]{:S(2)}, u32[]{:S(2)}) %collective-permute-start.9) | collective-permute-done | bytes 1228832 | tf_op jit(solution)/shard_map/ppermute | solution.py:420
  145.5 0.8 slice_select_fusion
  146.7 1.3 collective-permute-start.11
  148.0 3.3 %multiply_convert_fusion.prev_whole.prev_early = bf16[1536,1536]{1,0:T(8,128)(2,1)} fusion(bf16[1536,1536]{1,0:T(8,128)(2,1)S(1)} %pad_maximum_fusion, f32[1536]{0:T(1024)S(1)} %divide_reduce_fusion), kind=kLoop, calls=%fused_computation | loop fusion | flops 7077888 | bytes 9443328 | tf_op jit(solution)/shard_map/convert_element_type | solution.py:34
  151.3 3.8 %collective-permute-start.10 = (f32[1536]{0:T(1024)S(1)}, f32[1536]{0:T(1024)S(1)}, u32[]{:S(2)}, u32[]{:S(2)}) collective-permute-start(f32[1536]{0:T(1024)S(1)} %pad_maximum_fusion.2), channel_id=1, source_target_pairs={{4,0},{8,4},{12,8},{16,12},{20,16},{24,20},{28,24},{5,1},{9,5},{13... | collective-permute-start | bytes 18440 | tf_op jit(solution)/shard_map/ppermute | solution.py:411
  155.1 0.8 collective-permute-done.10
  156.5 19.1 %shard_map.60 = (bf16[1536,1536]{1,0:T(8,128)(2,1)}, f32[384,1536]{1,0:T(8,128)S(1)}, f32[384,1536]{1,0:T(8,128)S(1)}, bf16[1536,1536]{1,0:T(8,128)(2,1)S(1)}, bf16[384,1536]{1,0:T(8,128)(2,1)S(1)}) custom-call(s32[4]{0:T(128)S(1)} %pad_add_fusion.flags, bf16[1536,1536]{1,0:T(8,128)(2,1)} %multiply_convert_fusion.prev_whole.prev_early, ...), custom_call_target="tpu_custom_call" | custom-call | tf_op jit(solution)/shard_map/pallas_call | solution.py:150
  175.6 2.1 copy-done.10
  177.8 1.4 copy-done.12
  179.2 1.4 copy-done.14
  180.6 1.3 collective-permute-start.12
  181.9 0.7 collective-permute-start.13
  182.6 1.5 collective-permute-start.14
  184.1 1.7 copy-done.15
  185.8 6.7 %shard_map.61 = (bf16[384,1536]{1,0:T(8,128)(2,1)S(1)}, f32[8,1536]{1,0:T(8,128)S(1)}, f32[8,1536]{1,0:T(8,128)S(1)}) custom-call(s32[4]{0:T(128)S(1)} %pad_add_fusion.flags, bf16[1536,1536]{1,0:T(8,128)(2,1)} %get-tuple-element.26.link.early, bf16[384,1536]{1,0:T(8,128)(2,1)S(1)} %get-tuple-element.27.mine, bf16[8,1536]{1,0:T(8,128)(2,1)S(1)} %broadcast_in_dim.23.scale, ...), custom_call_target="tpu_custom_call" | custom-call | tf_op jit(solution)/shard_map/pallas_call | solution.py:276
  192.5 1.0 copy-done.18
  193.6 1.0 copy-done.16
  194.7 14.3 %collective-permute-done.14.from_above = bf16[384,1536]{1,0:T(8,128)(2,1)} collective-permute-done((bf16[384,1536]{1,0:T(8,128)(2,1)}, bf16[384,1536]{1,0:T(8,128)(2,1)}, u32[]{:S(2)}, u32[]{:S(2)}) %collective-permute-start.14) | collective-permute-done | bytes 1179680 | tf_op jit(solution)/shard_map/ppermute | solution.py:420
  209.0 1.3 copy-done.17
  210.2 6.3 %shard_map.62 = (bf16[384,1536]{1,0:T(8,128)(2,1)S(1)}, bf16[384,384]{1,0:T(8,128)(2,1)S(1)}, bf16[384,1536]{1,0:T(8,128)(2,1)S(1)}, f32[8,384]{1,0:T(8,128)S(1)}, f32[8,1536]{1,0:T(8,128)S(1)}) custom-call(s32[4]{0:T(128)S(1)} %pad_add_fusion.flags, f32[8,1536]{1,0:T(8,128)S(1)} %copy-done.24, bf16[384,1536]{1,0:T(8,128)(2,1)S(1)} %bitcast.25, ...), custom_call_target="tpu_custom_call" | custom-call | tf_op jit(solution)/shard_map/pallas_call | solution.py:218
  216.5 1.0 copy-done.19
  217.5 0.7 copy-done.25
  218.9 0.6 copy-done.27
  219.8 1.8 constant_dynamic-update-slice_fusion
  221.6 1.4 pad_maximum_fusion.1
  223.0 6.3 %collective-permute-start.16 = (bf16[400,1536]{1,0:T(8,128)(2,1)S(1)}, bf16[400,1536]{1,0:T(8,128)(2,1)S(1)}, u32[]{:S(2)}, u32[]{:S(2)}) collective-permute-start(bf16[400,1536]{1,0:T(8,128)(2,1)S(1)} %pad_maximum_fusion.1), channel_id=1, source_target_pairs={{4,0},{8,4},{12,8},{16,12},{20,16},{24,20},{28,24},{5,1},{9,5},{13... | collective-permute-start | bytes 3686408 | tf_op jit(solution)/shard_map/ppermute | solution.py:411
  229.2 1.3 collective-permute-start.18
  230.5 0.8 slice_reduce_fusion.1
  231.4 0.8 slice_reduce_fusion
  232.2 5.8 %shard_map.63 = (bf16[384,1536]{1,0:T(8,128)(2,1)S(1)}, s32[8,128]{1,0:T(8,128)S(1)}) custom-call(s32[4]{0:T(128)S(1)} %pad_add_fusion.flags, bf16[1536,1536]{1,0:T(8,128)(2,1)} %collective-permute-done.12.pivot_rows.pivot_early, bf16[8,1536]{1,0:T(8,128)(2,1)S(1)} %copy-done.22, bf16[1536,1536]{1,0:T(8,128)(2,1)} %get-tuple-element.26.link.early, ...), custom_call_target="tpu_custom_call" | custom-call | tf_op jit(solution)/shard_map/pallas_call | solution.py:383
  238.6 1.3 collective-permute-start.15
  240.6 6.9 %shard_map.64.ready = bf16[384,1536]{1,0:T(8,128)(2,1)S(1)} custom-call(s32[4]{0:T(128)S(1)} %pad_add_fusion.flags, bf16[384,1536]{1,0:T(8,128)(2,1)S(1)} %get-tuple-element.33.rows.next_rows, bf16[8,1536]{1,0:T(8,128)(2,1)S(1)} %broadcast_in_dim.29.scale, bf16[8,1536]{1,0:T(8,128)(2,1)S(1)} %copy-done.22, bf16[1536,1536]{1,0:T(8,128)(2,1)} %get-tuple-element.26.link.early, ...), custom_call_target="tpu_custom_call" | custom-call | tf_op jit(solution)/shard_map/pallas_call | solution.py:383
  247.6 0.7 collective-permute-start.19
  248.3 1.3 collective-permute-start.17
  249.6 23.0 %collective-permute-done.17 = bf16[1536]{0:T(1024)(128)(2,1)S(1)} collective-permute-done((bf16[1536]{0:T(1024)(128)(2,1)S(1)}, bf16[1536]{0:T(1024)(128)(2,1)S(1)}, u32[]{:S(2)}, u32[]{:S(2)}) %collective-permute-start.17) | collective-permute-done | bytes 3104 | tf_op jit(solution)/shard_map/ppermute | solution.py:411
  272.7 8.0 %shard_map.65.right = bf16[384,1536]{1,0:T(8,128)(2,1)S(1)} custom-call(s32[4]{0:T(128)S(1)} %pad_add_fusion.flags, bf16[384,1536]{1,0:T(8,128)(2,1)S(1)} %bitcast.27, bf16[8,1536]{1,0:T(8,128)(2,1)S(1)} %copy-done.22, bf16[8,1536]{1,0:T(8,128)(2,1)S(1)} %broadcast_in_dim.28.next_scale, bf16[1536,1536]{1,0:T(8,128)(2,1)S(1)} %bitcast.20, ...), custom_call_target="tpu_custom_call" | custom-call | tf_op jit(solution)/shard_map/pallas_call | solution.py:383
  280.8 8.4 %shard_map.66 = (f32[384,1536]{1,0:T(8,128)S(1)}, bf16[384,1536]{1,0:T(8,128)(2,1)}) custom-call(s32[4]{0:T(128)S(1)} %pad_add_fusion.flags, bf16[384,1536]{1,0:T(8,128)(2,1)S(1)} %collective-permute-done.15.rows, bf16[384,1536]{1,0:T(8,128)(2,1)S(1)} %shard_map.65.right, bf16[384,1536]{1,0:T(8,128)(2,1)S(1)} %get-tuple-element.33.rows.next_rows, ...), custom_call_target="tpu_custom_call" | custom-call | tf_op jit(solution)/shard_map/pallas_call | solution.py:383
  289.3 1.8 subtract_bitcast_fusion
  (93 shorter events, 3.3 us)
Async XLA Ops:
  1.5 6.8 %copy-start.23 = (f32[8,1536]{1,0:T(8,128)}, f32[8,1536]{1,0:T(8,128)S(1)}, u32[]{:S(2)}) copy-start(f32[8,1536]{1,0:T(8,128)S(1)} %broadcast_in_dim.21.reciprocal) | copy-start | bytes 147460
  1.5 1.3 copy-start
  2.8 1.3 copy-start.2
  4.0 1.7 copy-start.5
  5.7 63.3 %copy-start.3 = (bf16[1,384,1536]{2,1,0:T(8,128)(2,1)S(1)}, bf16[1,384,1536]{2,1,0:T(8,128)(2,1)}, u32[]{:S(2)}) copy-start(bf16[1,384,1536]{2,1,0:T(8,128)(2,1)} %param.5) | copy-start | bytes 3538948
  8.3 59.4 %copy-start.7 = (bf16[400,1536]{1,0:T(8,128)(2,1)}, bf16[400,1536]{1,0:T(8,128)(2,1)S(1)}, u32[]{:S(2)}) copy-start(bf16[400,1536]{1,0:T(8,128)(2,1)S(1)} %shard_map.59.refs_0_) | copy-start | bytes 3686404
  8.3 111.0 %copy-start.1 = (bf16[1,384,1536]{2,1,0:T(8,128)(2,1)S(1)}, bf16[1,384,1536]{2,1,0:T(8,128)(2,1)}, u32[]{:S(2)}) copy-start(bf16[1,384,1536]{2,1,0:T(8,128)(2,1)} %param.6) | copy-start | bytes 3538948
  8.3 29.1 %collective-permute-start.4 = (bf16[400,1536]{1,0:T(8,128)(2,1)S(1)}, bf16[400,1536]{1,0:T(8,128)(2,1)}, u32[]{:S(2)}, u32[]{:S(2)}) collective-permute-start(bf16[400,1536]{1,0:T(8,128)(2,1)S(1)} %shard_map.59.refs_0_), channel_id=1, source_target_pairs={{0,1},{1,2},{2,3},{4,5},{5,6},{6,7},{8,9},{9,10},{10,11},{12,13},{... | collective-permute-start | bytes 3686408 | tf_op jit(solution)/shard_map/ppermute | solution.py:420
  12.9 29.6 %collective-permute-start.5 = (bf16[400,1536]{1,0:T(8,128)(2,1)S(1)}, bf16[400,1536]{1,0:T(8,128)(2,1)}, u32[]{:S(2)}, u32[]{:S(2)}) collective-permute-start(bf16[400,1536]{1,0:T(8,128)(2,1)S(1)} %shard_map.59.refs_0_), channel_id=1, source_target_pairs={{1,0},{2,1},{3,2},{5,4},{6,5},{7,6},{9,8},{10,9},{11,10},{13,12},{... | collective-permute-start | bytes 3686408 | tf_op jit(solution)/shard_map/ppermute | solution.py:420
  14.2 48.6 %collective-permute-start = (bf16[384,1536]{1,0:T(8,128)(2,1)S(1)}, bf16[384,1536]{1,0:T(8,128)(2,1)S(1)}, u32[]{:S(2)}, u32[]{:S(2)}) collective-permute-start(bf16[384,1536]{1,0:T(8,128)(2,1)S(1)} %bitcast.22), channel_id=1, source_target_pairs={{0,1},{1,2},{2,3},{4,5},{5,6},{6,7},{8,9},{9,10},{10,11},{12,13},{... | collective-permute-start | bytes 3538952 | tf_op jit(solution)/shard_map/ppermute | solution.py:420
  18.2 49.5 %collective-permute-start.2 = (bf16[384,1536]{1,0:T(8,128)(2,1)S(1)}, bf16[384,1536]{1,0:T(8,128)(2,1)}, u32[]{:S(2)}, u32[]{:S(2)}) collective-permute-start(bf16[384,1536]{1,0:T(8,128)(2,1)S(1)} %bitcast.23), channel_id=1, source_target_pairs={{1,0},{2,1},{3,2},{5,4},{6,5},{7,6},{9,8},{10,9},{11,10},{13,12},{... | collective-permute-start | bytes 3538952 | tf_op jit(solution)/shard_map/ppermute | solution.py:420
  37.5 31.8 %collective-permute-start.6 = (bf16[400,1536]{1,0:T(8,128)(2,1)}, bf16[400,1536]{1,0:T(8,128)(2,1)}, u32[]{:S(2)}, u32[]{:S(2)}) collective-permute-start(bf16[400,1536]{1,0:T(8,128)(2,1)} %collective-permute-done.4.refs_1_), channel_id=1, source_target_pairs={{1,2},{2,3},{5,6},{6,7},{9,10},{10,11},{13,14},{14,15},{17,18},{18... | collective-permute-start | bytes 3686408 | tf_op jit(solution)/shard_map/ppermute | solution.py:420
  42.4 51.6 %collective-permute-start.7 = (bf16[400,1536]{1,0:T(8,128)(2,1)}, bf16[400,1536]{1,0:T(8,128)(2,1)}, u32[]{:S(2)}, u32[]{:S(2)}) collective-permute-start(bf16[400,1536]{1,0:T(8,128)(2,1)} %collective-permute-done.5.refs_2_), channel_id=1, source_target_pairs={{1,0},{2,1},{5,4},{6,5},{9,8},{10,9},{13,12},{14,13},{17,16},{18,1... | collective-permute-start | bytes 3686408 | tf_op jit(solution)/shard_map/ppermute | solution.py:420
  62.7 35.2 %collective-permute-start.1 = (bf16[384,1536]{1,0:T(8,128)(2,1)S(1)}, bf16[384,1536]{1,0:T(8,128)(2,1)}, u32[]{:S(2)}, u32[]{:S(2)}) collective-permute-start(bf16[384,1536]{1,0:T(8,128)(2,1)S(1)} %collective-permute-done), channel_id=1, source_target_pairs={{1,2},{2,3},{5,6},{6,7},{9,10},{10,11},{13,14},{14,15},{17,18},{18... | collective-permute-start | bytes 3538952 | tf_op jit(solution)/shard_map/ppermute | solution.py:420
  67.7 51.6 %collective-permute-start.3 = (bf16[384,1536]{1,0:T(8,128)(2,1)}, bf16[384,1536]{1,0:T(8,128)(2,1)}, u32[]{:S(2)}, u32[]{:S(2)}) collective-permute-start(bf16[384,1536]{1,0:T(8,128)(2,1)} %collective-permute-done.2), channel_id=1, source_target_pairs={{1,0},{2,1},{5,4},{6,5},{9,8},{10,9},{13,12},{14,13},{17,16},{18,1... | collective-permute-start | bytes 3538952 | tf_op jit(solution)/shard_map/ppermute | solution.py:420
  95.9 27.1 %collective-permute-start.8 = (bf16[400,1536]{1,0:T(8,128)(2,1)}, bf16[400,1536]{1,0:T(8,128)(2,1)S(1)}, u32[]{:S(2)}, u32[]{:S(2)}) collective-permute-start(bf16[400,1536]{1,0:T(8,128)(2,1)} %collective-permute-done.6.refs_3_), channel_id=1, source_target_pairs={{2,3},{6,7},{10,11},{14,15},{18,19},{22,23},{26,27},{30,31}} | collective-permute-start | bytes 3686408 | tf_op jit(solution)/shard_map/ppermute | solution.py:420
  96.6 48.9 %collective-permute-start.9 = (bf16[400,1536]{1,0:T(8,128)(2,1)}, bf16[400,1536]{1,0:T(8,128)(2,1)S(1)}, u32[]{:S(2)}, u32[]{:S(2)}) collective-permute-start(bf16[400,1536]{1,0:T(8,128)(2,1)} %collective-permute-done.7.refs_4_), channel_id=1, source_target_pairs={{1,0},{5,4},{9,8},{13,12},{17,16},{21,20},{25,24},{29,28}} | collective-permute-start | bytes 3686408 | tf_op jit(solution)/shard_map/ppermute | solution.py:420
  122.7 1.3 copy-start.8
  146.7 8.4 %collective-permute-start.11 = (f32[1536]{0:T(1024)S(1)}, f32[1536]{0:T(1024)S(1)}, u32[]{:S(2)}, u32[]{:S(2)}) collective-permute-start(f32[1536]{0:T(1024)S(1)} %maximum_subtract_fusion), channel_id=1, source_target_pairs={{0,4},{8,12},{16,20},{24,28},{1,5},{9,13},{17,21},{25,29},{2,6},{1... | collective-permute-start | bytes 18440 | tf_op jit(solution)/shard_map/ppermute | solution.py:411
  148.0 8.5 %copy-start.6 = (f32[1,384,1536]{2,1,0:T(8,128)S(1)}, f32[1,384,1536]{2,1,0:T(8,128)}, u32[]{:S(2)}) copy-start(f32[1,384,1536]{2,1,0:T(8,128)} %param.4) | copy-start | bytes 7077892
  151.3 4.6 %collective-permute-start.10 = (f32[1536]{0:T(1024)S(1)}, f32[1536]{0:T(1024)S(1)}, u32[]{:S(2)}, u32[]{:S(2)}) collective-permute-start(f32[1536]{0:T(1024)S(1)} %pad_maximum_fusion.2), channel_id=1, source_target_pairs={{4,0},{8,4},{12,8},{16,12},{20,16},{24,20},{28,24},{5,1},{9,5},{13... | collective-permute-start | bytes 18440 | tf_op jit(solution)/shard_map/ppermute | solution.py:411
  175.6 2.1 copy-start.10
  177.7 1.4 copy-start.12
  179.2 1.4 copy-start.14
  180.6 51.6 %collective-permute-start.12 = (bf16[1536,1536]{1,0:T(8,128)(2,1)}, bf16[1536,1536]{1,0:T(8,128)(2,1)}, u32[]{:S(2)}, u32[]{:S(2)}) collective-permute-start(bf16[1536,1536]{1,0:T(8,128)(2,1)} %get-tuple-element.26.link.early), channel_id=1, source_target_pairs={{0,4},{8,12},{16,20},{24,28},{1,5},{9,13},{17,21},{25,29},{2,6},{1... | collective-permute-start | bytes 14155784 | tf_op jit(solution)/shard_map/ppermute | solution.py:411
  181.9 11.8 %collective-permute-start.13 = (bf16[384,1536]{1,0:T(8,128)(2,1)}, bf16[384,1536]{1,0:T(8,128)(2,1)S(1)}, u32[]{:S(2)}, u32[]{:S(2)}) collective-permute-start(bf16[384,1536]{1,0:T(8,128)(2,1)} %get-tuple-element.55), channel_id=1, source_target_pairs={{2,3},{6,7},{10,11},{14,15},{18,19},{22,23},{26,27},{30,31}} | collective-permute-start | bytes 3538952 | tf_op jit(solution)/shard_map/ppermute | solution.py:420
  182.6 26.3 %collective-permute-start.14 = (bf16[384,1536]{1,0:T(8,128)(2,1)}, bf16[384,1536]{1,0:T(8,128)(2,1)}, u32[]{:S(2)}, u32[]{:S(2)}) collective-permute-start(bf16[384,1536]{1,0:T(8,128)(2,1)} %get-tuple-element.54), channel_id=1, source_target_pairs={{1,0},{5,4},{9,8},{13,12},{17,16},{21,20},{25,24},{29,28}} | collective-permute-start | bytes 3538952 | tf_op jit(solution)/shard_map/ppermute | solution.py:420
  184.1 8.4 %copy-start.21 = (bf16[8,1536]{1,0:T(8,128)(2,1)}, bf16[8,1536]{1,0:T(8,128)(2,1)S(1)}, u32[]{:S(2)}) copy-start(bf16[8,1536]{1,0:T(8,128)(2,1)S(1)} %broadcast_in_dim.22.pivot_scale) | copy-start | bytes 73732
  184.1 1.7 copy-start.15
  185.8 23.1 %copy-start.9 = (bf16[384,1536]{1,0:T(8,128)(2,1)S(1)}, bf16[384,1536]{1,0:T(8,128)(2,1)}, u32[]{:S(2)}) copy-start(bf16[384,1536]{1,0:T(8,128)(2,1)} %get-tuple-element.29.far) | copy-start | bytes 3538948
  185.8 23.1 %copy-start.11 = (bf16[1536,1536]{1,0:T(8,128)(2,1)S(1)}, bf16[1536,1536]{1,0:T(8,128)(2,1)}, u32[]{:S(2)}) copy-start(bf16[1536,1536]{1,0:T(8,128)(2,1)} %copy-done.10) | copy-start | bytes 14155780
  185.8 23.1 %copy-start.24 = (f32[8,1536]{1,0:T(8,128)S(1)}, f32[8,1536]{1,0:T(8,128)}, u32[]{:S(2)}) copy-start(f32[8,1536]{1,0:T(8,128)} %copy-done.23) | copy-start | bytes 147460
  192.5 1.0 copy-start.18
  193.6 1.0 copy-start.16
  208.9 1.3 copy-start.17
  216.5 1.0 copy-start.19
  217.5 0.7 copy-start.25
  218.2 0.6 copy-start.26
  218.9 0.6 copy-start.27
  221.6 10.6 %copy-start.22 = (bf16[8,1536]{1,0:T(8,128)(2,1)S(1)}, bf16[8,1536]{1,0:T(8,128)(2,1)}, u32[]{:S(2)}) copy-start(bf16[8,1536]{1,0:T(8,128)(2,1)} %copy-done.21) | copy-start | bytes 73732
  223.0 17.5 %collective-permute-start.16 = (bf16[400,1536]{1,0:T(8,128)(2,1)S(1)}, bf16[400,1536]{1,0:T(8,128)(2,1)S(1)}, u32[]{:S(2)}, u32[]{:S(2)}) collective-permute-start(bf16[400,1536]{1,0:T(8,128)(2,1)S(1)} %pad_maximum_fusion.1), channel_id=1, source_target_pairs={{4,0},{8,4},{12,8},{16,12},{20,16},{24,20},{28,24},{5,1},{9,5},{13... | collective-permute-start | bytes 3686408 | tf_op jit(solution)/shard_map/ppermute | solution.py:411
  229.2 11.3 %collective-permute-start.18 = (bf16[384,1536]{1,0:T(8,128)(2,1)S(1)}, bf16[384,1536]{1,0:T(8,128)(2,1)S(1)}, u32[]{:S(2)}, u32[]{:S(2)}) collective-permute-start(bf16[384,1536]{1,0:T(8,128)(2,1)S(1)} %get-tuple-element.32.late), channel_id=1, source_target_pairs={{0,4},{8,12},{16,20},{24,28},{1,5},{9,13},{17,21},{25,29},{2,6},{1... | collective-permute-start | bytes 3538952 | tf_op jit(solution)/shard_map/ppermute | solution.py:411
  232.2 8.4 %copy-start.28 = (f32[1536]{0:T(1024)S(1)}, f32[1536]{0:T(1024)}, u32[]{:S(2)}) copy-start(f32[1536]{0:T(1024)} %get-tuple-element.45) | copy-start | bytes 18436
  238.6 42.2 %collective-permute-start.15 = (bf16[384,1536]{1,0:T(8,128)(2,1)S(1)}, bf16[384,1536]{1,0:T(8,128)(2,1)S(1)}, u32[]{:S(2)}, u32[]{:S(2)}) collective-permute-start(bf16[384,1536]{1,0:T(8,128)(2,1)S(1)} %get-tuple-element.33.rows.next_rows), channel_id=1, source_target_pairs={{20,28},{21,29},{22,30},{23,31}} | collective-permute-start | bytes 3538952 | tf_op jit(solution)/shard_map/ppermute | solution.py:411
  240.6 32.1 %slice-start = ((s8[4718592]{0:T(1024)(128)(4,1)}), s8[4194304]{0:T(1024)(128)(4,1)S(1)}, s32[]{:S(2)}) async-start(s8[4718592]{0:T(1024)(128)(4,1)} %bitcast.19), calls=%async_computation | async-start | bytes 8388608
  240.6 32.1 %slice-start.1 = ((s8[4718592]{0:T(1024)(128)(4,1)}), s8[524288]{0:T(1024)(128)(4,1)S(1)}, s32[]{:S(2)}) async-start(s8[4718592]{0:T(1024)(128)(4,1)} %bitcast.19), calls=%async_computation.1 | async-start | bytes 1048576
  240.6 32.1 %copy-start.4 = (bf16[1,384,1536]{2,1,0:T(8,128)(2,1)S(1)}, bf16[1,384,1536]{2,1,0:T(8,128)(2,1)}, u32[]{:S(2)}) copy-start(bf16[1,384,1536]{2,1,0:T(8,128)(2,1)} %param.5) | copy-start | bytes 3538948
  240.6 32.1 %copy-start.20 = (bf16[384,1536]{1,0:T(8,128)(2,1)S(1)}, bf16[384,1536]{1,0:T(8,128)(2,1)}, u32[]{:S(2)}) copy-start(bf16[384,1536]{1,0:T(8,128)(2,1)} %copy-done.19) | copy-start | bytes 3538948
  247.6 41.7 %collective-permute-start.19 = (bf16[384,1536]{1,0:T(8,128)(2,1)S(1)}, bf16[384,1536]{1,0:T(8,128)(2,1)S(1)}, u32[]{:S(2)}, u32[]{:S(2)}) collective-permute-start(bf16[384,1536]{1,0:T(8,128)(2,1)S(1)} %shard_map.64.ready), channel_id=1, source_target_pairs={{20,12},{21,13},{22,14},{23,15}} | collective-permute-start | bytes 3538952 | tf_op jit(solution)/shard_map/ppermute | solution.py:411
  248.3 24.3 %collective-permute-start.17 = (bf16[1536]{0:T(1024)(128)(2,1)S(1)}, bf16[1536]{0:T(1024)(128)(2,1)S(1)}, u32[]{:S(2)}, u32[]{:S(2)}) collective-permute-start(bf16[1536]{0:T(1024)(128)(2,1)S(1)} %divide_convert_fusion), channel_id=1, source_target_pairs={{4,12},{20,28},{5,13},{21,29},{6,14},{22,30},{7,15},{23,31}} | collective-permute-start | bytes 9224 | tf_op jit(solution)/shard_map/ppermute | solution.py:411
  272.7 8.1 %copy-start.13 = (f32[384,1536]{1,0:T(8,128)S(1)}, f32[384,1536]{1,0:T(8,128)}, u32[]{:S(2)}) copy-start(f32[384,1536]{1,0:T(8,128)} %copy-done.12) | copy-start | bytes 7077892

commit v4 on v2

--- a/solution.py
+++ b/solution.py
@@ -322,76 +322,96 @@
     return (block.astype(F32) * factors[0:1].astype(F32)).astype(BF16)
 
 
-def next_rows_kernel(flags, pivot_rows, pivot_scale, early, late, *refs):
-    result, link, sems = refs[-3:]
-    wait = fetched(early, late, link, sems, [flags[1]])
-    scaled = times(pivot_rows[...], pivot_scale)
-    wait()
-    result[...] = (-dot_nn(scaled, link[...])).astype(BF16)
-
-
-def level_2_kernel(flags, rows, scale, pivot_scale, early, late, pivot_early, pivot_late, result, link, pivot, sems):
-    wait_link = fetched(early, late, link, sems.at[0], [flags[1]])
-    wait_pivot = fetched(pivot_early, pivot_late, pivot, sems.at[1], [flags[1]])
-    scaled = times(rows[...], scale)
-    wait_link()
-    inner = times(dot_nt(scaled, link[...]), pivot_scale)
-    wait_pivot()
-    result[...] = (-dot_nt(inner, pivot[...])).astype(BF16)
-
-
-def right_kernel(
-    flags, own, pivot_scale, next_scale, prev_early, prev_late, pivot_early, pivot_late, ready,
-    result, prev, pivot, sems,
+def columns_kernel(
+    flags, own, pivot_scale, prev_early, prev_late, pivot_whole, update, ready,
+    right, columns, moved, prev, pivot, sems, pivot_sem, move_sem,
 ):
     del ready
-    wait_prev = fetched(prev_early, prev_late, prev, sems.at[0], [flags[1]])
-    wait_pivot = fetched(pivot_early, pivot_late, pivot, sems.at[1], [flags[1]])
+    move = pltpu.make_async_copy(update, moved, move_sem)
+    move.start()
+    wait_prev = fetched(prev_early, prev_late, prev, sems, [flags[1]])
+    copy = pltpu.make_async_copy(pivot_whole, pivot, pivot_sem)
+    copy.start()
     wait_prev()
     across = jnp.where(flags[0] == 1, 0.0, -dot_nt(own[...], prev[...])).astype(BF16)
     across = times(across, pivot_scale)
-    wait_pivot()
-    columns = (-dot_nt(across, pivot[...])).astype(BF16)
-    inner = dot_nn(times(columns, next_scale), pivot[...]) * pivot_scale[0:1].astype(F32)
-    keep = jnp.where(flags[3] == 1, 1.0, 0.0)
-    result[...] = (across.astype(F32) - inner * keep).astype(BF16)
-
-
-def last_kernel(
-    flags, rows, right, next_rows, mine, partial, pivot_scale, next_scale,
-    early, late, pivot_early, pivot_late, form, new, link, pivot, sems,
-):
-    wait_pivot = fetched(pivot_early, pivot_late, pivot, sems.at[1], [flags[1]])
-    wait_link = fetched(early, late, link, sems.at[0], [flags[1]])
-    scaled = times(rows[...], next_scale)
-    wait_pivot()
-    inner = times(dot_nn(scaled, pivot[...]), pivot_scale)
-    wait_link()
-    last = dot_nn(inner, link[...]).astype(BF16)
-    odd = jnp.where(flags[2] == 1, 0.0, 1.0)
-    form[...] = partial[...] - odd * dot_nn(right[...], link[...])
-    new[...] = jnp.where(flags[3] == 1, last, jnp.where(flags[2] == 1, mine[...], next_rows[...]))
-
-
-def with_links(kernel, out_shapes, flags, blocks, arrays, links):
-    order = arrays[0].shape[1]
-    rows = arrays[1].shape[0]
-    size = order // rows
-    specs = [spec if spec is not None else whole_spec(block.shape) for block, spec in blocks]
-    sems = (size,) if links == 1 else (links, size)
-    return pl.pallas_call(
-        kernel,
-        out_shape=out_shapes,
+    right[...] = across
+    copy.wait()
+    columns[...] = (-dot_nt(across, pivot[...])).astype(BF16)
+    move.wait()
+
+
+def columns_forms(flags, own, pivot_scale, prev_early, prev_late, pivot, update, ready):
+    rows, order = own.shape
+    out = SHAPE((rows, order), BF16)
+    return pl.pallas_call(
+        columns_kernel,
+        out_shape=[out, out, out],
         grid_spec=pltpu.PrefetchScalarGridSpec(
             num_scalar_prefetch=1,
             grid=(1,),
-            in_specs=specs + [ANY] * len(arrays),
-            out_specs=[whole_spec(out.shape) for out in out_shapes],
-            scratch_shapes=[pltpu.VMEM((order, order), BF16)] * links + [pltpu.SemaphoreType.DMA(sems)],
+            in_specs=[whole_spec((rows, order)), whole_spec((8, order))] + [ANY] * 5,
+            out_specs=[whole_spec((rows, order)), whole_spec((rows, order)), ANY],
+            scratch_shapes=[
+                pltpu.VMEM((order, order), BF16),
+                pltpu.VMEM((order, order), BF16),
+                pltpu.SemaphoreType.DMA((order // rows,)),
+                pltpu.SemaphoreType.DMA,
+                pltpu.SemaphoreType.DMA,
+            ],
         ),
-        compiler_params=pltpu.CompilerParams(vmem_limit_bytes=32 * 1024 * 1024),
+        compiler_params=pltpu.CompilerParams(vmem_limit_bytes=22 * 1024 * 1024),
         cost_estimate=FREE,
-    )(flags, *[block for block, _ in blocks], *arrays)
+    )(flags, own, pivot_scale, prev_early, prev_late, pivot, update, ready)
+
+
+def last_kernel(
+    flags, pivot_rows, right, columns, next_rows, mine, partial, pivot_scale,
+    link_whole, pivot_whole, form, new, link, pivot, sems,
+):
+    rows = right.shape[0]
+    copies = [
+        pltpu.make_async_copy(pivot_whole, pivot, sems.at[0]),
+        pltpu.make_async_copy(link_whole, link, sems.at[1]),
+    ]
+    for copy in copies:
+        copy.start()
+    scale = pivot_rows[rows : rows + 8, :]
+    both = jnp.concatenate([times(columns[...], scale), times(pivot_rows[0:rows, :], scale)])
+    copies[0].wait()
+    inner = dot_nn(both, pivot[...]) * pivot_scale[0:1].astype(F32)
+    keep = jnp.where(flags[3] == 1, 1.0, 0.0)
+    factor = (right[...].astype(F32) - inner[0:rows] * keep).astype(BF16)
+    both = jnp.concatenate([factor, inner[rows:].astype(BF16)])
+    copies[1].wait()
+    both = dot_nn(both, link[...])
+    odd = jnp.where(flags[2] == 1, 0.0, 1.0)
+    form[...] = partial[...] - odd * both[0:rows]
+    last = both[rows:].astype(BF16)
+    new[...] = jnp.where(flags[3] == 1, last, jnp.where(flags[2] == 1, mine[...], next_rows[...]))
+
+
+def last_forms(flags, pivot_rows, right, columns, next_rows, mine, partial, pivot_scale, link, pivot):
+    rows, order = right.shape
+    return pl.pallas_call(
+        last_kernel,
+        out_shape=[SHAPE((rows, order), F32), SHAPE((rows, order), BF16)],
+        grid_spec=pltpu.PrefetchScalarGridSpec(
+            num_scalar_prefetch=1,
+            grid=(1,),
+            in_specs=[whole_spec(pivot_rows.shape)]
+            + [whole_spec((rows, order))] * 5
+            + [whole_spec((8, order)), ANY, ANY],
+            out_specs=[whole_spec((rows, order)), whole_spec((rows, order))],
+            scratch_shapes=[
+                pltpu.VMEM((order, order), BF16),
+                pltpu.VMEM((order, order), BF16),
+                pltpu.SemaphoreType.DMA((2,)),
+            ],
+        ),
+        compiler_params=pltpu.CompilerParams(vmem_limit_bytes=36 * 1024 * 1024),
+        cost_estimate=FREE,
+    )(flags, pivot_rows, right, columns, next_rows, mine, partial, pivot_scale, link, pivot)
 
 
 def on_device(sep_block, own_couple, prev_couple, inner_diag):
@@ -480,49 +500,38 @@
     from_below, from_above = prev_arrived[-1]
     late_scale = lax.dynamic_slice_in_dim(pivot_scale, late_start, rows, 0)
     late_scale = jnp.where(is_end, late_scale, jnp.zeros_like(late_scale))
-    pivot_early = between(link, [(p, p + 1) for p in even])
-    from_later = between(update, [(p, p - 1) for p in everyone])
     late, corner, prev_late, left_late, right_late = late_forms(
         flags, rows_of(reciprocal), prev_rows, mine, own_full, scale8, rows_of(late_scale),
         from_below, from_above, prev_far, right_diag,
     )
+    link = lax.dynamic_update_slice_in_dim(link, late, late_start, 0)
+    pivot_link = between(link, [(p, p + 1) for p in even])
+    update = lax.dynamic_update_slice_in_dim(update, corner, late_start, 1)
     left_diag = lax.dynamic_update_slice_in_dim(left_diag[0], left_late[0], late_start, 0)
+    right_diag = right_diag[0] + right_late[0]
+
     left_diag = between(left_diag, [(p, p - 1) for p in even])
-    pivot_late = between(late, [(p, p + 1) for p in even])
-    corner = between(corner, [(p, p - 1) for p in everyone])
-
-    own_block = pl.BlockSpec((rows, order), lambda j, f: (f[1], 0), pipeline_mode=pl.Buffered(1))
-    (next_rows,) = with_links(
-        next_rows_kernel, [SHAPE((rows, order), BF16)], flags,
-        [(pivot_early, own_block), (pivot_scale8, None)], [link, late], 1,
-    )
-    pivot_rows = between(next_rows, [(p, p + 2) for p in pivots if p != 1])
-    next_diag = diag - left_diag - right_diag[0] - right_late[0]
+    from_even = between(update, [(p, p - 1) for p in even])
+    next_diag = diag - left_diag - right_diag
     next_scale = (1.0 / jnp.maximum(next_diag, 1.0)).astype(BF16)
-    next_pivot_scale = between(next_scale, [(p, p + 2) for p in pivots])
-
-    links = [link, late, pivot_early, pivot_late]
-    (left_next,) = with_links(
-        level_2_kernel, [SHAPE((rows, order), BF16)], flags,
-        [(next_rows, None), (rows_of(next_scale), None), (pivot_scale8, None)], links, 2,
-    )
+    pivot_rows = lax.dynamic_slice_in_dim(pivot_link, row_start, rows, 0)
+    pivot_rows = lax.optimization_barrier(scaled_by(pivot_rows, pivot_scale))
+    next_rows = (-dot_nn(pivot_rows, link)).astype(BF16)
+    next_long = jnp.concatenate([next_rows, jnp.broadcast_to(next_scale[None, :], (EXTRA, order))])
+    pivot_long = between(next_long, [(p, p + 2) for p in pivots])
+
+    left_next = scaled_by(dot_nt(scaled_by(next_rows, next_scale), link), pivot_scale)
+    left_next = lax.optimization_barrier(left_next)
+    left_next = (-dot_nt(left_next, pivot_link)).astype(BF16)
     from_pivot = between(left_next, [(p, p - 2) for p in pivots])
-    next_scale8 = rows_of(next_pivot_scale)
-    (right,) = with_links(
-        right_kernel, [SHAPE((rows, order), BF16)], flags,
-        [(own_rows, None), (pivot_scale8, None), (next_scale8, None)],
-        [prev_first, prev_late, pivot_early, pivot_late, left_next], 2,
-    )
-    form, out_link = with_links(
-        last_kernel, [SHAPE((rows, order), F32), SHAPE((rows, order), BF16)], flags,
-        [
-            (pivot_rows, None), (right, None), (next_rows, None), (mine, None), (partial, None),
-            (pivot_scale8, None), (next_scale8, None),
-        ],
-        links, 2,
-    )
-    from_later = lax.dynamic_update_slice_in_dim(from_later, corner, late_start, 1)
-    schur = form - from_later.astype(F32) - from_pivot.astype(F32)
+    right, columns, own_update = columns_forms(
+        flags, own_rows, pivot_scale8, prev_first, prev_late, pivot_link, update, left_next
+    )
+    from_odd = between(own_update, [(p, p - 1) for p in range(1, parts, 2)])
+    form, out_link = last_forms(
+        flags, pivot_long, right, columns, next_rows, mine, partial, pivot_scale8, link, pivot_link
+    )
+    schur = form - (from_even + from_odd).astype(F32) - from_pivot.astype(F32)
     return (schur[None], out_link[None])
 
 

time: 300 us -> 251 us (0.84)
  the two profiles are of different devices: /device:TPU:7 before, /device:TPU:27 now
where the time goes in v4:
time: 251 us; the launch traced here: 250 us
  waiting for transfers between devices  119 us (47%)
  Pallas kernels  52.5 us (21%)
  starting transfers between devices  38.3 us (15%)
  other arithmetic  15.4 us (6%)
  matrix products  13.2 us (5%)
  local copies, waits for them, and re-layouts  10.4 us (4%)
    ppermute x12, waiting for transfers between devices, one_step(): return (lax.ppermute(ahead, 'space', up), lax.ppermute(back, 'space', down))  113 us
    ppermute x12, starting transfers between devices, one_step(): return (lax.ppermute(ahead, 'space', up), lax.ppermute(back, 'space', down))  20.9 us
    pallas_call x1, Pallas kernels, early_forms(): pl.pallas_call(functools.partial(early_kernel, size), out_shape=[SHAPE((o...  19.4 us
    ppermute x8, starting transfers between devices, between(): lax.ppermute(block, 'tm', [(a, b) for a, b in route if 0 <= b < parts])  17.5 us
    pallas_call x1, Pallas kernels, last_forms(): pl.pallas_call(last_kernel, out_shape=[SHAPE((rows, order), F32), SHAPE((...  11.6 us
    dot_general x2, matrix products, dot_nt(): lax.dot_general(left, right, (((1,), (1,)), ((), ())), preferred_element_...  8.81 us
    pallas_call x1, Pallas kernels, level_forms(): pl.pallas_call(level_kernel, out_shape=[SHAPE((rows, order), BF16), SHAPE...  6.45 us
    convert_element_type x5, other arithmetic, scaled_by(): return (matrix.astype(F32) * factors.astype(F32)[None, :]).astype(BF16)  6.28 us
  transfers between devices with their start and end apart: 20, of which 10 were waited for; matrix products, arithmetic and copies ran while one was open for 12% of the time, Pallas kernels for 17%

profile of v4, /device:TPU:27, one launch (start us, length us, event | category | flops | bytes accessed | tf_op | source)
XLA Modules:
  0.0 249.8 jit_solution(13777505222009652190)
XLA Ops:
  0.7 0.7 divide_reduce_fusion
  1.4 0.1 pad_add_fusion.flags
  1.5 1.3 copy-done
  2.7 1.3 copy-done.2
  4.0 1.7 copy-done.4
  5.7 3.6 %shard_map.59.refs_0_ = bf16[400,1536]{1,0:T(8,128)(2,1)} custom-call(s32[4]{0:T(128)S(1)} %pad_add_fusion.flags, bf16[384,1536]{1,0:T(8,128)(2,1)S(1)} %bitcast.29, bf16[384,1536]{1,0:T(8,128)(2,1)S(1)} %bitcast.24, f32[384,1536]{1,0:T(8,128)S(1)} %bitcast.31, f32[8,1536]{1,0:T(8,128)S(1)} %broadcast_in_dim.19.reciprocal), custom_call_target="tpu_custom_call" | custom-call | tf_op jit(solution)/shard_map/pallas_call | solution.py:103
  9.3 3.3 %collective-permute-start.5 = (bf16[400,1536]{1,0:T(8,128)(2,1)}, bf16[400,1536]{1,0:T(8,128)(2,1)}, u32[]{:S(2)}, u32[]{:S(2)}) collective-permute-start(bf16[400,1536]{1,0:T(8,128)(2,1)} %shard_map.59.refs_0_), channel_id=1, source_target_pairs={{1,0},{2,1},{3,2},{5,4},{6,5},{7,6},{9,8},{10,9},{11,10},{13,12},{... | collective-permute-start | bytes 3686408 | tf_op jit(solution)/shard_map/ppermute | solution.py:439
  12.6 1.3 collective-permute-start
  13.9 5.0 %collective-permute-start.2 = (bf16[384,1536]{1,0:T(8,128)(2,1)S(1)}, bf16[384,1536]{1,0:T(8,128)(2,1)}, u32[]{:S(2)}, u32[]{:S(2)}) collective-permute-start(bf16[384,1536]{1,0:T(8,128)(2,1)S(1)} %bitcast.26), channel_id=1, source_target_pairs={{1,0},{2,1},{3,2},{5,4},{6,5},{7,6},{9,8},{10,9},{11,10},{13,12},{... | collective-permute-start | bytes 3538952 | tf_op jit(solution)/shard_map/ppermute | solution.py:439
  18.9 1.3 collective-permute-start.4
  20.2 17.3 %collective-permute-done.5.refs_2_ = bf16[400,1536]{1,0:T(8,128)(2,1)} collective-permute-done((bf16[400,1536]{1,0:T(8,128)(2,1)}, bf16[400,1536]{1,0:T(8,128)(2,1)}, u32[]{:S(2)}, u32[]{:S(2)}) %collective-permute-start.5) | collective-permute-done | bytes 1228832 | tf_op jit(solution)/shard_map/ppermute | solution.py:439
  37.5 1.7 collective-permute-start.7
  39.2 1.8 collective-permute-done
  41.0 1.3 collective-permute-start.1
  42.3 20.4 %collective-permute-done.2 = bf16[384,1536]{1,0:T(8,128)(2,1)} collective-permute-done((bf16[384,1536]{1,0:T(8,128)(2,1)S(1)}, bf16[384,1536]{1,0:T(8,128)(2,1)}, u32[]{:S(2)}, u32[]{:S(2)}) %collective-permute-start.2) | collective-permute-done | bytes 1179680 | tf_op jit(solution)/shard_map/ppermute | solution.py:439
  62.6 1.7 collective-permute-start.3
  64.3 3.1 %collective-permute-done.4.refs_1_ = bf16[400,1536]{1,0:T(8,128)(2,1)} collective-permute-done((bf16[400,1536]{1,0:T(8,128)(2,1)}, bf16[400,1536]{1,0:T(8,128)(2,1)}, u32[]{:S(2)}, u32[]{:S(2)}) %collective-permute-start.4) | collective-permute-done | bytes 1228832 | tf_op jit(solution)/shard_map/ppermute | solution.py:439
  67.4 1.3 collective-permute-start.6
  68.7 0.2 multiply_convert_fusion.3.own_rows
  68.9 0.7 collective-permute-start.9
  69.7 23.0 %collective-permute-done.1 = bf16[384,1536]{1,0:T(8,128)(2,1)} collective-permute-done((bf16[384,1536]{1,0:T(8,128)(2,1)S(1)}, bf16[384,1536]{1,0:T(8,128)(2,1)}, u32[]{:S(2)}, u32[]{:S(2)}) %collective-permute-start.1) | collective-permute-done | bytes 1179680 | tf_op jit(solution)/shard_map/ppermute | solution.py:439
  92.7 2.4 broadcast_select_fusion
  95.1 23.9 %collective-permute-done.6.refs_3_ = bf16[400,1536]{1,0:T(8,128)(2,1)S(1)} collective-permute-done((bf16[400,1536]{1,0:T(8,128)(2,1)}, bf16[400,1536]{1,0:T(8,128)(2,1)S(1)}, u32[]{:S(2)}, u32[]{:S(2)}) %collective-permute-start.6) | collective-permute-done | bytes 1228832 | tf_op jit(solution)/shard_map/ppermute | solution.py:439
  118.9 1.3 collective-permute-start.8
  120.2 0.4 pad_maximum_fusion
  120.6 1.3 collective-permute-start.12
  121.9 0.7 collective-permute-start.13
  122.6 0.9 slice_select_fusion
  123.5 23.9 %collective-permute-done.8.refs_5_ = bf16[400,1536]{1,0:T(8,128)(2,1)S(1)} collective-permute-done((bf16[400,1536]{1,0:T(8,128)(2,1)S(1)}, bf16[400,1536]{1,0:T(8,128)(2,1)S(1)}, u32[]{:S(2)}, u32[]{:S(2)}) %collective-permute-start.8) | collective-permute-done | bytes 1228832 | tf_op jit(solution)/shard_map/ppermute | solution.py:439
  147.5 0.9 slice_select_fusion.1
  148.7 7.1 %collective-permute-start.10 = (f32[1536]{0:T(1024)S(1)}, f32[1536]{0:T(1024)S(1)}, u32[]{:S(2)}, u32[]{:S(2)}) collective-permute-start(f32[1536]{0:T(1024)S(1)} %pad_maximum_fusion.2), channel_id=1, source_target_pairs={{4,0},{8,4},{12,8},{16,12},{20,16},{24,20},{28,24},{5,1},{9,5},{13... | collective-permute-start | bytes 18440 | tf_op jit(solution)/shard_map/ppermute | solution.py:430
  155.8 3.2 %multiply_convert_fusion.prev_whole.prev_early = bf16[1536,1536]{1,0:T(8,128)(2,1)} fusion(bf16[1536,1536]{1,0:T(8,128)(2,1)S(1)} %pad_maximum_fusion, f32[1536]{0:T(1024)S(1)} %divide_reduce_fusion), kind=kLoop, calls=%fused_computation | loop fusion | flops 7077888 | bytes 9443328 | tf_op jit(solution)/shard_map/convert_element_type | solution.py:34
  159.0 1.3 collective-permute-start.11
  160.3 19.4 %shard_map.60 = (bf16[1536,1536]{1,0:T(8,128)(2,1)}, f32[384,1536]{1,0:T(8,128)S(1)}, f32[384,1536]{1,0:T(8,128)S(1)}, bf16[1536,1536]{1,0:T(8,128)(2,1)S(1)}, bf16[384,1536]{1,0:T(8,128)(2,1)S(1)}) custom-call(s32[4]{0:T(128)S(1)} %pad_add_fusion.flags, bf16[1536,1536]{1,0:T(8,128)(2,1)} %multiply_convert_fusion.prev_whole.prev_early, ...), custom_call_target="tpu_custom_call" | custom-call | tf_op jit(solution)/shard_map/pallas_call | solution.py:150
  179.7 0.7 divide_convert_fusion.2
  180.4 0.7 fusion.29
  181.1 6.4 %shard_map.61 = (bf16[384,1536]{1,0:T(8,128)(2,1)S(1)}, f32[8,1536]{1,0:T(8,128)S(1)}, f32[8,1536]{1,0:T(8,128)S(1)}) custom-call(s32[4]{0:T(128)S(1)} %pad_add_fusion.flags, bf16[1536,1536]{1,0:T(8,128)(2,1)} %get-tuple-element.25.link, bf16[384,1536]{1,0:T(8,128)(2,1)S(1)} %get-tuple-element.26.mine, bf16[8,1536]{1,0:T(8,128)(2,1)S(1)} %broadcast_in_dim.20.scale, ...), custom_call_target="tpu_custom_call" | custom-call | tf_op jit(solution)/shard_map/pallas_call | solution.py:276
  187.6 0.6 copy-done.18
  188.3 5.3 %shard_map.62 = (bf16[384,1536]{1,0:T(8,128)(2,1)S(1)}, bf16[384,384]{1,0:T(8,128)(2,1)S(1)}, bf16[384,1536]{1,0:T(8,128)(2,1)S(1)}, f32[8,384]{1,0:T(8,128)S(1)}, f32[8,1536]{1,0:T(8,128)S(1)}) custom-call(s32[4]{0:T(128)S(1)} %pad_add_fusion.flags, f32[8,1536]{1,0:T(8,128)S(1)} %copy-done.13, bf16[384,1536]{1,0:T(8,128)(2,1)S(1)} %bitcast.28, ...), custom_call_target="tpu_custom_call" | custom-call | tf_op jit(solution)/shard_map/pallas_call | solution.py:218
  193.6 1.0 copy-done.8
  194.6 1.1 constant_dynamic-update-slice_fusion.1.link_whole
  195.8 1.5 collective-permute-start.14
  197.2 0.6 slice_reduce_fusion.1
  197.8 0.8 slice_reduce_fusion
  198.6 0.9 dynamic_update_slice.10
  199.5 1.3 collective-permute-start.15
  200.8 1.0 constant_dynamic-update-slice_fusion.update
  201.8 0.8 add_reduce_fusion
  202.6 1.3 collective-permute-start.17
  203.9 2.4 collective-permute-done.15
  206.3 0.7 fusion.28
  207.1 1.5 multiply_convert_fusion.2
  208.6 4.3 %fusion.next_rows = bf16[384,1536]{1,0:T(8,128)(2,1)S(1)} fusion(bf16[384,1536]{1,0:T(8,128)(2,1)S(1)} %multiply_convert_fusion.2, bf16[1536,1536]{1,0:T(8,128)(2,1)} %constant_dynamic-update-slice_fusion.1.link_whole), kind=kOutput, calls=%fused_computation.5 | convolution fusion | flops 1813118976 | bytes 7077888 | tf_op jit(solution)/shard_map/dot_general | solution.py:46
  212.9 4.4 %fusion.2 = bf16[384,1536]{1,0:T(8,128)(2,1)S(1)} fusion(bf16[1536,1536]{1,0:T(8,128)(2,1)} %constant_dynamic-update-slice_fusion.1.link_whole, bf16[384,1536]{1,0:T(8,128)(2,1)S(1)} %fusion.next_rows, f32[1536]{0:T(1024)S(1)} %get-tuple-element.46, f32[1536]{0:T(1024)S(1)} %copy-done.20), kind=kOutput, calls=%fused_computation.7 | convolution fusion | flops 1814888448 | bytes 7090176 | tf_op jit(solution)/shard_map/dot_general | solution.py:42
  217.3 0.1 pad_maximum_fusion.1
  217.4 1.6 collective-permute-start.16
  219.0 4.4 %fusion.1.ready = bf16[384,1536]{1,0:T(8,128)(2,1)S(1)} fusion(bf16[384,1536]{1,0:T(8,128)(2,1)S(1)} %fusion.2, bf16[1536,1536]{1,0:T(8,128)(2,1)} %collective-permute-done.14.pivot_whole), kind=kOutput, calls=%fused_computation.6 | convolution fusion | flops 1813118976 | bytes 7077888 | tf_op jit(solution)/shard_map/dot_general | solution.py:42
  223.4 1.3 collective-permute-start.19
  224.8 6.2 %shard_map.63 = (bf16[384,1536]{1,0:T(8,128)(2,1)S(1)}, bf16[384,1536]{1,0:T(8,128)(2,1)S(1)}, bf16[384,1536]{1,0:T(8,128)(2,1)S(1)}) custom-call(s32[4]{0:T(128)S(1)} %pad_add_fusion.flags, bf16[384,1536]{1,0:T(8,128)(2,1)S(1)} %bitcast.30, bf16[8,1536]{1,0:T(8,128)(2,1)S(1)} %copy-done.15, bf16[1536,1536]{1,0:T(8,128)(2,1)S(1)} %bitcast.23, ...), custom_call_target="tpu_custom_call" | custom-call | tf_op jit(solution)/shard_map/pallas_call | solution.py:347
  231.0 2.2 collective-permute-start.18
  233.2 2.0 collective-permute-done.16.pivot_rows
  235.2 11.6 %shard_map.64 = (f32[384,1536]{1,0:T(8,128)S(1)}, bf16[384,1536]{1,0:T(8,128)(2,1)}) custom-call(s32[4]{0:T(128)S(1)} %pad_add_fusion.flags, bf16[400,1536]{1,0:T(8,128)(2,1)S(1)} %collective-permute-done.16.pivot_rows, bf16[384,1536]{1,0:T(8,128)(2,1)S(1)} %get-tuple-element.40.right, bf16[384,1536]{1,0:T(8,128)(2,1)S(1)} %get-tuple-element.41.columns, ...), custom_call_target="tpu_custom_call" | custom-call | tf_op jit(solution)/shard_map/pallas_call | solution.py:396
  246.8 1.1 collective-permute-done.19
  247.9 2.0 subtract_bitcast_fusion
  (70 shorter events, 0.5 us)
Async XLA Ops:
  1.5 1.3 copy-start
  2.7 1.3 copy-start.2
  4.0 1.7 copy-start.4
  5.7 3.6 %copy-start.12 = (f32[8,1536]{1,0:T(8,128)}, f32[8,1536]{1,0:T(8,128)S(1)}, u32[]{:S(2)}) copy-start(f32[8,1536]{1,0:T(8,128)S(1)} %broadcast_in_dim.19.reciprocal) | copy-start | bytes 147460
  5.7 63.0 %copy-start.3 = (bf16[1,384,1536]{2,1,0:T(8,128)(2,1)S(1)}, bf16[1,384,1536]{2,1,0:T(8,128)(2,1)}, u32[]{:S(2)}) copy-start(bf16[1,384,1536]{2,1,0:T(8,128)(2,1)} %param.5) | copy-start | bytes 3538948
  9.3 83.4 %copy-start.1 = (bf16[1,384,1536]{2,1,0:T(8,128)(2,1)S(1)}, bf16[1,384,1536]{2,1,0:T(8,128)(2,1)}, u32[]{:S(2)}) copy-start(bf16[1,384,1536]{2,1,0:T(8,128)(2,1)} %param.6) | copy-start | bytes 3538948
  9.3 28.2 %collective-permute-start.5 = (bf16[400,1536]{1,0:T(8,128)(2,1)}, bf16[400,1536]{1,0:T(8,128)(2,1)}, u32[]{:S(2)}, u32[]{:S(2)}) collective-permute-start(bf16[400,1536]{1,0:T(8,128)(2,1)} %shard_map.59.refs_0_), channel_id=1, source_target_pairs={{1,0},{2,1},{3,2},{5,4},{6,5},{7,6},{9,8},{10,9},{11,10},{13,12},{... | collective-permute-start | bytes 3686408 | tf_op jit(solution)/shard_map/ppermute | solution.py:439
  12.6 28.4 %collective-permute-start = (bf16[384,1536]{1,0:T(8,128)(2,1)S(1)}, bf16[384,1536]{1,0:T(8,128)(2,1)S(1)}, u32[]{:S(2)}, u32[]{:S(2)}) collective-permute-start(bf16[384,1536]{1,0:T(8,128)(2,1)S(1)} %bitcast.25), channel_id=1, source_target_pairs={{0,1},{1,2},{2,3},{4,5},{5,6},{6,7},{8,9},{9,10},{10,11},{12,13},{... | collective-permute-start | bytes 3538952 | tf_op jit(solution)/shard_map/ppermute | solution.py:439
  13.9 48.8 %collective-permute-start.2 = (bf16[384,1536]{1,0:T(8,128)(2,1)S(1)}, bf16[384,1536]{1,0:T(8,128)(2,1)}, u32[]{:S(2)}, u32[]{:S(2)}) collective-permute-start(bf16[384,1536]{1,0:T(8,128)(2,1)S(1)} %bitcast.26), channel_id=1, source_target_pairs={{1,0},{2,1},{3,2},{5,4},{6,5},{7,6},{9,8},{10,9},{11,10},{13,12},{... | collective-permute-start | bytes 3538952 | tf_op jit(solution)/shard_map/ppermute | solution.py:439
  18.9 48.5 %collective-permute-start.4 = (bf16[400,1536]{1,0:T(8,128)(2,1)}, bf16[400,1536]{1,0:T(8,128)(2,1)}, u32[]{:S(2)}, u32[]{:S(2)}) collective-permute-start(bf16[400,1536]{1,0:T(8,128)(2,1)} %shard_map.59.refs_0_), channel_id=1, source_target_pairs={{0,1},{1,2},{2,3},{4,5},{5,6},{6,7},{8,9},{9,10},{10,11},{12,13},{... | collective-permute-start | bytes 3686408 | tf_op jit(solution)/shard_map/ppermute | solution.py:439
  37.5 31.5 %collective-permute-start.7 = (bf16[400,1536]{1,0:T(8,128)(2,1)}, bf16[400,1536]{1,0:T(8,128)(2,1)}, u32[]{:S(2)}, u32[]{:S(2)}) collective-permute-start(bf16[400,1536]{1,0:T(8,128)(2,1)} %collective-permute-done.5.refs_2_), channel_id=1, source_target_pairs={{1,0},{2,1},{5,4},{6,5},{9,8},{10,9},{13,12},{14,13},{17,16},{18,1... | collective-permute-start | bytes 3686408 | tf_op jit(solution)/shard_map/ppermute | solution.py:439
  41.0 51.7 %collective-permute-start.1 = (bf16[384,1536]{1,0:T(8,128)(2,1)S(1)}, bf16[384,1536]{1,0:T(8,128)(2,1)}, u32[]{:S(2)}, u32[]{:S(2)}) collective-permute-start(bf16[384,1536]{1,0:T(8,128)(2,1)S(1)} %collective-permute-done), channel_id=1, source_target_pairs={{1,2},{2,3},{5,6},{6,7},{9,10},{10,11},{13,14},{14,15},{17,18},{18... | collective-permute-start | bytes 3538952 | tf_op jit(solution)/shard_map/ppermute | solution.py:439
  62.6 30.1 %collective-permute-start.3 = (bf16[384,1536]{1,0:T(8,128)(2,1)}, bf16[384,1536]{1,0:T(8,128)(2,1)}, u32[]{:S(2)}, u32[]{:S(2)}) collective-permute-start(bf16[384,1536]{1,0:T(8,128)(2,1)} %collective-permute-done.2), channel_id=1, source_target_pairs={{1,0},{2,1},{5,4},{6,5},{9,8},{10,9},{13,12},{14,13},{17,16},{18,1... | collective-permute-start | bytes 3538952 | tf_op jit(solution)/shard_map/ppermute | solution.py:439
  67.4 51.5 %collective-permute-start.6 = (bf16[400,1536]{1,0:T(8,128)(2,1)}, bf16[400,1536]{1,0:T(8,128)(2,1)S(1)}, u32[]{:S(2)}, u32[]{:S(2)}) collective-permute-start(bf16[400,1536]{1,0:T(8,128)(2,1)} %collective-permute-done.4.refs_1_), channel_id=1, source_target_pairs={{1,2},{2,3},{5,6},{6,7},{9,10},{10,11},{13,14},{14,15},{17,18},{18... | collective-permute-start | bytes 3686408 | tf_op jit(solution)/shard_map/ppermute | solution.py:439
  68.9 53.7 %collective-permute-start.9 = (bf16[400,1536]{1,0:T(8,128)(2,1)}, bf16[400,1536]{1,0:T(8,128)(2,1)S(1)}, u32[]{:S(2)}, u32[]{:S(2)}) collective-permute-start(bf16[400,1536]{1,0:T(8,128)(2,1)} %collective-permute-done.7.refs_4_), channel_id=1, source_target_pairs={{1,0},{5,4},{9,8},{13,12},{17,16},{21,20},{25,24},{29,28}} | collective-permute-start | bytes 3686408 | tf_op jit(solution)/shard_map/ppermute | solution.py:439
  118.9 28.5 %collective-permute-start.8 = (bf16[400,1536]{1,0:T(8,128)(2,1)S(1)}, bf16[400,1536]{1,0:T(8,128)(2,1)S(1)}, u32[]{:S(2)}, u32[]{:S(2)}) collective-permute-start(bf16[400,1536]{1,0:T(8,128)(2,1)S(1)} %collective-permute-done.6.refs_3_), channel_id=1, source_target_pairs={{2,3},{6,7},{10,11},{14,15},{18,19},{22,23},{26,27},{30,31}} | collective-permute-start | bytes 3686408 | tf_op jit(solution)/shard_map/ppermute | solution.py:439
  120.6 67.7 %collective-permute-start.12 = (bf16[384,1536]{1,0:T(8,128)(2,1)}, bf16[384,1536]{1,0:T(8,128)(2,1)S(1)}, u32[]{:S(2)}, u32[]{:S(2)}) collective-permute-start(bf16[384,1536]{1,0:T(8,128)(2,1)} %collective-permute-done.1), channel_id=1, source_target_pairs={{2,3},{6,7},{10,11},{14,15},{18,19},{22,23},{26,27},{30,31}} | collective-permute-start | bytes 3538952 | tf_op jit(solution)/shard_map/ppermute | solution.py:439
  121.9 66.4 %collective-permute-start.13 = (bf16[384,1536]{1,0:T(8,128)(2,1)}, bf16[384,1536]{1,0:T(8,128)(2,1)S(1)}, u32[]{:S(2)}, u32[]{:S(2)}) collective-permute-start(bf16[384,1536]{1,0:T(8,128)(2,1)} %collective-permute-done.3), channel_id=1, source_target_pairs={{1,0},{5,4},{9,8},{13,12},{17,16},{21,20},{25,24},{29,28}} | collective-permute-start | bytes 3538952 | tf_op jit(solution)/shard_map/ppermute | solution.py:439
  148.7 31.0 %collective-permute-start.10 = (f32[1536]{0:T(1024)S(1)}, f32[1536]{0:T(1024)S(1)}, u32[]{:S(2)}, u32[]{:S(2)}) collective-permute-start(f32[1536]{0:T(1024)S(1)} %pad_maximum_fusion.2), channel_id=1, source_target_pairs={{4,0},{8,4},{12,8},{16,12},{20,16},{24,20},{28,24},{5,1},{9,5},{13... | collective-permute-start | bytes 18440 | tf_op jit(solution)/shard_map/ppermute | solution.py:430
  155.8 4.5 %copy-start.5 = (f32[1,384,1536]{2,1,0:T(8,128)S(1)}, f32[1,384,1536]{2,1,0:T(8,128)}, u32[]{:S(2)}) copy-start(f32[1,384,1536]{2,1,0:T(8,128)} %param.4) | copy-start | bytes 7077892
  159.0 21.4 %collective-permute-start.11 = (f32[1536]{0:T(1024)S(1)}, f32[1536]{0:T(1024)S(1)}, u32[]{:S(2)}, u32[]{:S(2)}) collective-permute-start(f32[1536]{0:T(1024)S(1)} %maximum_subtract_fusion), channel_id=1, source_target_pairs={{0,4},{8,12},{16,20},{24,28},{1,5},{9,13},{17,21},{25,29},{2,6},{1... | collective-permute-start | bytes 18440 | tf_op jit(solution)/shard_map/ppermute | solution.py:430
  179.7 7.9 %copy-start.6 = (f32[384,1536]{1,0:T(8,128)}, f32[384,1536]{1,0:T(8,128)S(1)}, u32[]{:S(2)}) copy-start(f32[384,1536]{1,0:T(8,128)S(1)} %get-tuple-element.42.partial) | copy-start | bytes 7077892
  181.1 6.5 %copy-start.14 = (bf16[8,1536]{1,0:T(8,128)(2,1)}, bf16[8,1536]{1,0:T(8,128)(2,1)S(1)}, u32[]{:S(2)}) copy-start(bf16[8,1536]{1,0:T(8,128)(2,1)S(1)} %broadcast_in_dim.23.pivot_scale) | copy-start | bytes 73732
  181.1 7.2 %copy-start.13 = (f32[8,1536]{1,0:T(8,128)S(1)}, f32[8,1536]{1,0:T(8,128)}, u32[]{:S(2)}) copy-start(f32[8,1536]{1,0:T(8,128)} %copy-done.12) | copy-start | bytes 147460
  187.6 0.6 copy-start.18
  188.2 5.4 %copy-start.10 = (bf16[384,1536]{1,0:T(8,128)(2,1)}, bf16[384,1536]{1,0:T(8,128)(2,1)S(1)}, u32[]{:S(2)}) copy-start(bf16[384,1536]{1,0:T(8,128)(2,1)S(1)} %get-tuple-element.38) | copy-start | bytes 3538948
  188.2 5.4 %copy-start.17 = (f32[8,1536]{1,0:T(8,128)}, f32[8,1536]{1,0:T(8,128)S(1)}, u32[]{:S(2)}) copy-start(f32[8,1536]{1,0:T(8,128)S(1)} %get-tuple-element.32.ready) | copy-start | bytes 147460
  193.6 1.0 copy-start.8
  194.6 1.1 copy-start.16
  194.6 1.1 copy-start.19
  194.6 6.1 %copy-start.11 = (bf16[384,1536]{1,0:T(8,128)(2,1)S(1)}, bf16[384,1536]{1,0:T(8,128)(2,1)}, u32[]{:S(2)}) copy-start(bf16[384,1536]{1,0:T(8,128)(2,1)} %copy-done.10) | copy-start | bytes 3538948
  195.8 11.3 %collective-permute-start.14 = (bf16[1536,1536]{1,0:T(8,128)(2,1)}, bf16[1536,1536]{1,0:T(8,128)(2,1)}, u32[]{:S(2)}, u32[]{:S(2)}) collective-permute-start(bf16[1536,1536]{1,0:T(8,128)(2,1)} %constant_dynamic-update-slice_fusion.1.link_whole), channel_id=1, source_target_pairs={{0,4},{8,12},{16,20},{24,28},{1,5},{9,13},{17,21},{25,29},{2,6},{1... | collective-permute-start | bytes 14155784 | tf_op jit(solution)/shard_map/ppermute | solution.py:430
  199.5 6.9 %collective-permute-start.15 = (f32[1536]{0:T(1024)S(1)}, f32[1536]{0:T(1024)S(1)}, u32[]{:S(2)}, u32[]{:S(2)}) collective-permute-start(f32[1536]{0:T(1024)S(1)} %dynamic_update_slice.10), channel_id=1, source_target_pairs={{8,4},{16,12},{24,20},{9,5},{17,13},{25,21},{10,6},{18,14},{26,22}... | collective-permute-start | bytes 18440 | tf_op jit(solution)/shard_map/ppermute | solution.py:430
  202.6 44.2 %collective-permute-start.17 = (bf16[384,1536]{1,0:T(8,128)(2,1)S(1)}, bf16[384,1536]{1,0:T(8,128)(2,1)S(1)}, u32[]{:S(2)}, u32[]{:S(2)}) collective-permute-start(bf16[384,1536]{1,0:T(8,128)(2,1)S(1)} %constant_dynamic-update-slice_fusion.update), channel_id=1, source_target_pairs={{8,4},{16,12},{24,20},{9,5},{17,13},{25,21},{10,6},{18,14},{26,22}... | collective-permute-start | bytes 3538952 | tf_op jit(solution)/shard_map/ppermute | solution.py:430
  208.5 4.4 %copy-start.20 = (f32[1536]{0:T(1024)S(1)}, f32[1536]{0:T(1024)}, u32[]{:S(2)}) copy-start(f32[1536]{0:T(1024)} %get-tuple-element.48) | copy-start | bytes 18436
  217.3 7.4 %slice-start = ((s8[4718592]{0:T(1024)(128)(4,1)}), s8[4194304]{0:T(1024)(128)(4,1)S(1)}, s32[]{:S(2)}) async-start(s8[4718592]{0:T(1024)(128)(4,1)} %bitcast.22), calls=%async_computation | async-start | bytes 8388608
  217.4 7.4 %slice-start.1 = ((s8[4718592]{0:T(1024)(128)(4,1)}), s8[524288]{0:T(1024)(128)(4,1)S(1)}, s32[]{:S(2)}) async-start(s8[4718592]{0:T(1024)(128)(4,1)} %bitcast.22), calls=%async_computation.1 | async-start | bytes 1048576
  217.4 7.4 %copy-start.9 = (bf16[384,1536]{1,0:T(8,128)(2,1)S(1)}, bf16[384,1536]{1,0:T(8,128)(2,1)}, u32[]{:S(2)}) copy-start(bf16[384,1536]{1,0:T(8,128)(2,1)} %copy-done.8) | copy-start | bytes 3538948
  217.4 7.4 %copy-start.15 = (bf16[8,1536]{1,0:T(8,128)(2,1)S(1)}, bf16[8,1536]{1,0:T(8,128)(2,1)}, u32[]{:S(2)}) copy-start(bf16[8,1536]{1,0:T(8,128)(2,1)} %copy-done.14) | copy-start | bytes 73732
  217.4 17.7 %collective-permute-start.16 = (bf16[400,1536]{1,0:T(8,128)(2,1)S(1)}, bf16[400,1536]{1,0:T(8,128)(2,1)S(1)}, u32[]{:S(2)}, u32[]{:S(2)}) collective-permute-start(bf16[400,1536]{1,0:T(8,128)(2,1)S(1)} %pad_maximum_fusion.1), channel_id=1, source_target_pairs={{4,12},{20,28},{5,13},{21,29},{6,14},{22,30},{7,15},{23,31}} | collective-permute-start | bytes 3686408 | tf_op jit(solution)/shard_map/ppermute | solution.py:430
  223.4 24.4 %collective-permute-start.19 = (bf16[384,1536]{1,0:T(8,128)(2,1)S(1)}, bf16[384,1536]{1,0:T(8,128)(2,1)S(1)}, u32[]{:S(2)}, u32[]{:S(2)}) collective-permute-start(bf16[384,1536]{1,0:T(8,128)(2,1)S(1)} %fusion.1.ready), channel_id=1, source_target_pairs={{20,12},{21,13},{22,14},{23,15}} | collective-permute-start | bytes 3538952 | tf_op jit(solution)/shard_map/ppermute | solution.py:430
  224.8 10.4 %copy-start.7 = (f32[384,1536]{1,0:T(8,128)S(1)}, f32[384,1536]{1,0:T(8,128)}, u32[]{:S(2)}) copy-start(f32[384,1536]{1,0:T(8,128)} %copy-done.6) | copy-start | bytes 7077892
  231.0 16.9 %collective-permute-start.18 = (bf16[384,1536]{1,0:T(8,128)(2,1)S(1)}, bf16[384,1536]{1,0:T(8,128)(2,1)S(1)}, u32[]{:S(2)}, u32[]{:S(2)}) collective-permute-start(bf16[384,1536]{1,0:T(8,128)(2,1)S(1)} %get-tuple-element.44), channel_id=1, source_target_pairs={{4,0},{12,8},{20,16},{28,24},{5,1},{13,9},{21,17},{29,25},{6,2},{1... | collective-permute-start | bytes 3538952 | tf_op jit(solution)/shard_map/ppermute | solution.py:430

commit v5 on v4

--- a/solution.py
+++ b/solution.py
@@ -54,6 +54,12 @@
     return jnp.broadcast_to(scale[None, :], (8, scale.shape[0]))
 
 
+def products_cost(rows, order, count):
+    return pl.CostEstimate(
+        flops=2 * count * rows * order * order, bytes_accessed=2 * count * order * order, transcendentals=0
+    )
+
+
 def whole_spec(shape):
     return pl.BlockSpec(shape, lambda j, f: (0,) * len(shape), pipeline_mode=pl.Buffered(1))
 
@@ -68,8 +74,8 @@
 
 def opening_kernel(flags, own, prev, separator, reciprocal, long):
     rows, order = own.shape
-    row_ids = lax.broadcasted_iota(jnp.int32, (rows, order), 0) + flags[1] * rows
-    col_ids = lax.broadcasted_iota(jnp.int32, (rows, order), 1)
+    row_ids = lax.broadcasted_iota(jnp.int32, (rows, rows), 0)
+    col_ids = lax.broadcasted_iota(jnp.int32, (rows, rows), 1)
     on_diagonal = jnp.where(row_ids == col_ids, separator[...], 0.0)
     ones = jnp.ones((8, order), BF16)
 
@@ -90,12 +96,10 @@
         return total.astype(BF16)
 
     long[0:rows, :] = own[...]
-    high, low = split(jnp.sum(on_diagonal, axis=0, keepdims=True))
-    long[rows:, :] = placed({0: high, 1: low}, order)
-    own_high, own_low = split(form_diagonal(own[...]))
+    long[rows:, :] = jnp.zeros((EXTRA, order), BF16)
+    own_high, own_low = split(jnp.sum(on_diagonal, axis=0, keepdims=True) - form_diagonal(own[...]))
     prev_high, prev_low = split(form_diagonal(prev[...]))
-    local = placed({2: own_high, 3: own_low, 4: prev_high, 5: prev_low}, rows)
-    long[rows:, 0:rows] = long[rows:, 0:rows] + local
+    long[rows:, 0:rows] = placed({0: own_high, 1: own_low, 2: prev_high, 3: prev_low}, rows)
 
 
 def opening(flags, own, prev, separator, reciprocal):
@@ -106,7 +110,7 @@
         grid_spec=pltpu.PrefetchScalarGridSpec(
             num_scalar_prefetch=1,
             grid=(1,),
-            in_specs=[whole_spec((rows, order))] * 3 + [whole_spec((8, order))],
+            in_specs=[whole_spec((rows, order))] * 2 + [whole_spec((rows, rows)), whole_spec((8, order))],
             out_specs=whole_spec((rows + EXTRA, order)),
         ),
         compiler_params=pltpu.CompilerParams(vmem_limit_bytes=32 * 1024 * 1024),
@@ -116,7 +120,7 @@
 
 def early_kernel(size, flags, prev_whole, prev_rows, own_rows, separator, *refs):
     sources = refs[: 2 * size - 1]
-    link, partial, form, own_out, mine, own, sems = refs[2 * size - 1 :]
+    link, partial, form, own_out, mine, own, sems = refs[2 * size + 1 :]
     rows = separator.shape[0]
     step = pl.program_id(0)
     here = pl.ds(pl.multiple_of(step * WIDTH, WIDTH), WIDTH)
@@ -175,10 +179,8 @@
 
 
 def late_kernel(
-    size, flags, reciprocal, prev_rows, mine, own, scale, late_scale, from_below, from_above, far,
-    ready, link, corner, scaled, left_diag, right_diag, raw, sem,
+    size, flags, reciprocal, prev_rows, own, from_below, from_above, far, link, corner, scaled, raw, sem
 ):
-    del ready
     place = flags[1]
     step = pl.program_id(0)
     width = own.shape[0]
@@ -195,63 +197,34 @@
             pl.when(chosen)(copy.start)
             pl.when(chosen)(copy.wait)
         scaled[...] = (raw[...].astype(F32) * reciprocal[0:1]).astype(BF16)
+        corner[...] = dot_nt(prev_rows[...], scaled[...])
 
     link[:, here] = jnp.where(flags[0] == 1, 0.0, -dot_nt(scaled[...], own[...])).astype(BF16)
 
-    @pl.when(step == pl.num_programs(0) - 1)
-    def _():
-        late = link[...]
-        square = late * late
-        keep = jnp.where(flags[2] == 1, 1.0, 0.0)
-        ours = mine[...] * scale[0:1]
-        corner[...] = (dot_nt(prev_rows[...], scaled[...]) + keep * dot_nt(ours, late)).astype(BF16)
-        left_diag[...] = dot_nt(scale[...], square)
-        right_diag[...] = dot_nn(late_scale[...], square)
-
-
-def late_forms(
-    flags, reciprocal, prev_rows, mine, own, scale, late_scale, from_below, from_above, far, ready
-):
+
+def late_forms(flags, reciprocal, prev_rows, own, from_below, from_above, far):
     rows, order = prev_rows.shape
     size = order // rows
     width = 512
     return pl.pallas_call(
         functools.partial(late_kernel, size),
-        out_shape=[
-            SHAPE((rows, order), BF16),
-            SHAPE((rows, rows), BF16),
-            SHAPE((rows, order), BF16),
-            SHAPE((8, rows), F32),
-            SHAPE((8, order), F32),
-        ],
+        out_shape=[SHAPE((rows, order), BF16), SHAPE((rows, rows), F32), SHAPE((rows, order), BF16)],
         grid_spec=pltpu.PrefetchScalarGridSpec(
             num_scalar_prefetch=1,
             grid=(order // width,),
             in_specs=[
                 whole_spec((8, order)),
                 whole_spec((rows, order)),
-                whole_spec((rows, order)),
                 pl.BlockSpec((width, order), lambda j, f: (j, 0)),
-                whole_spec((8, order)),
-                whole_spec((8, rows)),
-                ANY,
                 ANY,
                 ANY,
                 ANY,
             ],
-            out_specs=[
-                whole_spec((rows, order)),
-                whole_spec((rows, rows)),
-                whole_spec((rows, order)),
-                whole_spec((8, rows)),
-                whole_spec((8, order)),
-            ],
+            out_specs=[whole_spec((rows, order)), whole_spec((rows, rows)), whole_spec((rows, order))],
             scratch_shapes=[pltpu.VMEM((rows, order), BF16), pltpu.SemaphoreType.DMA],
         ),
         compiler_params=pltpu.CompilerParams(vmem_limit_bytes=18 * 1024 * 1024),
-    )(
-        flags, reciprocal, prev_rows, mine, own, scale, late_scale, from_below, from_above, far, ready
-    )
+    )(flags, reciprocal, prev_rows, own, from_below, from_above, far)
 
 
 def level_kernel(flags, link, mine, scale, pivot_scale, form, update, left_diag, right_diag):
@@ -361,7 +334,7 @@
             ],
         ),
         compiler_params=pltpu.CompilerParams(vmem_limit_bytes=22 * 1024 * 1024),
-        cost_estimate=FREE,
+        cost_estimate=products_cost(rows, order, 2),
     )(flags, own, pivot_scale, prev_early, prev_late, pivot, update, ready)
 
 
@@ -410,7 +383,7 @@
             ],
         ),
         compiler_params=pltpu.CompilerParams(vmem_limit_bytes=36 * 1024 * 1024),
-        cost_estimate=FREE,
+        cost_estimate=products_cost(rows, order, 4),
     )(flags, pivot_rows, right, columns, next_rows, mine, partial, pivot_scale, link, pivot)
 
 
@@ -454,7 +427,8 @@
     flags = jnp.stack(
         [is_first.astype(jnp.int32), place, is_pivot.astype(jnp.int32), is_last.astype(jnp.int32)]
     )
-    own_long = opening(flags, own_rows, prev_rows, separator, rows_of(reciprocal))
+    diagonal_block = lax.dynamic_slice_in_dim(separator, row_start, rows, 1)
+    own_long = opening(flags, own_rows, prev_rows, diagonal_block, rows_of(reciprocal))
     own_arrived = [(own_long, own_long)]
     prev_arrived = [(prev_rows, prev_rows)]
     for step in range(1, size):
@@ -477,9 +451,8 @@
     def pair_sum(block, at):
         return block[at].astype(F32) + block[at + 1].astype(F32)
 
-    part_diag = sum(pair_sum(block, 0) for block in words)
-    part_diag = part_diag - jnp.concatenate([pair_sum(block, 2)[:rows] for block in words])
-    prev_diag = jnp.concatenate([pair_sum(block, 4)[:rows] for block in words])
+    part_diag = jnp.concatenate([pair_sum(block, 0)[:rows] for block in words])
+    prev_diag = jnp.concatenate([pair_sum(block, 2)[:rows] for block in words])
     part_diag, prev_diag = lax.optimization_barrier((part_diag, prev_diag))
     diag = part_diag - between(prev_diag, [(p, p - 1) for p in everyone])
     pivot_diag = between(part_diag, [(p, p + 1) for p in even]) - prev_diag
@@ -490,25 +463,22 @@
     sources = [own_long]
     for up, down in own_arrived[1:]:
         sources += [up, down]
+    sources += [scale, pivot_scale]
     prev_first = scaled_by(prev_first, reciprocal)
     link, partial, prev_form, own_full, mine = early_forms(
         flags, prev_first, prev_rows, own_scaled, separator, sources
     )
     scale8, pivot_scale8 = rows_of(scale), rows_of(pivot_scale)
-    update, left_diag, right_diag = level_forms(flags, link, mine, scale8, pivot_scale8, prev_form)
 
     from_below, from_above = prev_arrived[-1]
-    late_scale = lax.dynamic_slice_in_dim(pivot_scale, late_start, rows, 0)
-    late_scale = jnp.where(is_end, late_scale, jnp.zeros_like(late_scale))
-    late, corner, prev_late, left_late, right_late = late_forms(
-        flags, rows_of(reciprocal), prev_rows, mine, own_full, scale8, rows_of(late_scale),
-        from_below, from_above, prev_far, right_diag,
+    late, corner, prev_late = late_forms(
+        flags, rows_of(reciprocal), prev_rows, own_full, from_below, from_above, prev_far
     )
     link = lax.dynamic_update_slice_in_dim(link, late, late_start, 0)
     pivot_link = between(link, [(p, p + 1) for p in even])
-    update = lax.dynamic_update_slice_in_dim(update, corner, late_start, 1)
-    left_diag = lax.dynamic_update_slice_in_dim(left_diag[0], left_late[0], late_start, 0)
-    right_diag = right_diag[0] + right_late[0]
+    prev_form = lax.dynamic_update_slice_in_dim(prev_form, corner, late_start, 1)
+    update, left_diag, right_diag = level_forms(flags, link, mine, scale8, pivot_scale8, prev_form)
+    left_diag, right_diag = left_diag[0], right_diag[0]
 
     left_diag = between(left_diag, [(p, p - 1) for p in even])
     from_even = between(update, [(p, p - 1) for p in even])

time: 251 us -> 250 us (level)
  the two profiles are of different devices: /device:TPU:27 before, /device:TPU:3 now
where the time goes in v5:
time: 250 us; the launch traced here: 245 us
  waiting for transfers between devices  125 us (50%)
  Pallas kernels  48.2 us (19%)
  starting transfers between devices  39.2 us (16%)
  local copies, waits for them, and re-layouts  14.2 us (6%)
  other arithmetic  11.7 us (5%)
  matrix products  6.04 us (2%)
    ppermute x12, waiting for transfers between devices, one_step(): return (lax.ppermute(ahead, 'space', up), lax.ppermute(back, 'space', down))  116 us
    ppermute x8, starting transfers between devices, between(): lax.ppermute(block, 'tm', [(a, b) for a, b in route if 0 <= b < parts])  20.1 us
    ppermute x12, starting transfers between devices, one_step(): return (lax.ppermute(ahead, 'space', up), lax.ppermute(back, 'space', down))  19.1 us
    pallas_call x1, Pallas kernels, early_forms(): pl.pallas_call(functools.partial(early_kernel, size), out_shape=[SHAPE((o...  18.2 us
    unnamed x42, local copies, waits for them, and re-layouts  12.7 us
    pallas_call x1, Pallas kernels, last_forms(): pl.pallas_call(last_kernel, out_shape=[SHAPE((rows, order), F32), SHAPE((...  11.6 us
    ppermute x8, waiting for transfers between devices, between(): lax.ppermute(block, 'tm', [(a, b) for a, b in route if 0 <= b < parts])  8.56 us
    pallas_call x1, Pallas kernels, columns_forms(): pl.pallas_call(columns_kernel, out_shape=[out, out, out], grid_spec=pltpu...  6.02 us
  transfers between devices with their start and end apart: 20, of which 9 were waited for; matrix products, arithmetic and copies ran while one was open for 6% of the time, Pallas kernels for 17%

profile of v5, /device:TPU:3, one launch (start us, length us, event | category | flops | bytes accessed | tf_op | source)
XLA Modules:
  0.0 245.5 jit_solution(4010745247920487646)
XLA Ops:
  0.7 0.8 divide_reduce_fusion
  1.5 1.1 dynamic-slice_bitcast_fusion.separator
  2.6 0.1 pad_add_fusion.flags
  2.7 0.0 copy-start.1
  2.7 1.3 copy-done.1
  4.0 3.1 %shard_map.59.refs_0_ = bf16[400,1536]{1,0:T(8,128)(2,1)} custom-call(s32[4]{0:T(128)S(1)} %pad_add_fusion.flags, bf16[384,1536]{1,0:T(8,128)(2,1)S(1)} %bitcast.31, bf16[384,1536]{1,0:T(8,128)(2,1)S(1)} %bitcast.26, f32[384,384]{1,0:T(8,128)S(1)} %dynamic-slice_bitcast_fusion.separator, f32[8,1536]{1,0:T(8,128)S(1)} %broadcast_in_dim.15.reciprocal), custom_call_target="tpu_custom_call" | custom-call | tf_op jit(solution)/shard_map/pallas_call | solution.py:107
  7.1 4.3 %collective-permute-start.4 = (bf16[400,1536]{1,0:T(8,128)(2,1)}, bf16[400,1536]{1,0:T(8,128)(2,1)}, u32[]{:S(2)}, u32[]{:S(2)}) collective-permute-start(bf16[400,1536]{1,0:T(8,128)(2,1)} %shard_map.59.refs_0_), channel_id=1, source_target_pairs={{0,1},{1,2},{2,3},{4,5},{5,6},{6,7},{8,9},{9,10},{10,11},{12,13},{... | collective-permute-start | bytes 3686408 | tf_op jit(solution)/shard_map/ppermute | solution.py:412
  11.4 2.2 collective-permute-start
  13.6 1.3 collective-permute-start.2
  14.9 1.3 collective-permute-start.5
  16.2 20.1 %collective-permute-done.4.refs_1_ = bf16[400,1536]{1,0:T(8,128)(2,1)} collective-permute-done((bf16[400,1536]{1,0:T(8,128)(2,1)}, bf16[400,1536]{1,0:T(8,128)(2,1)}, u32[]{:S(2)}, u32[]{:S(2)}) %collective-permute-start.4) | collective-permute-done | bytes 1228832 | tf_op jit(solution)/shard_map/ppermute | solution.py:412
  36.3 1.7 collective-permute-start.6
  38.0 23.5 %collective-permute-done = bf16[384,1536]{1,0:T(8,128)(2,1)S(1)} collective-permute-done((bf16[384,1536]{1,0:T(8,128)(2,1)S(1)}, bf16[384,1536]{1,0:T(8,128)(2,1)S(1)}, u32[]{:S(2)}, u32[]{:S(2)}) %collective-permute-start) | collective-permute-done | bytes 1179680 | tf_op jit(solution)/shard_map/ppermute | solution.py:412
  61.5 1.7 collective-permute-start.1
  63.2 1.3 collective-permute-start.3
  64.5 3.7 %collective-permute-done.5.refs_2_ = bf16[400,1536]{1,0:T(8,128)(2,1)} collective-permute-done((bf16[400,1536]{1,0:T(8,128)(2,1)}, bf16[400,1536]{1,0:T(8,128)(2,1)}, u32[]{:S(2)}, u32[]{:S(2)}) %collective-permute-start.5) | collective-permute-done | bytes 1228832 | tf_op jit(solution)/shard_map/ppermute | solution.py:412
  68.2 1.3 collective-permute-start.7
  69.5 0.2 multiply_convert_fusion.3.own_rows
  69.7 0.7 collective-permute-start.8
  70.4 23.2 %collective-permute-done.3 = bf16[384,1536]{1,0:T(8,128)(2,1)} collective-permute-done((bf16[384,1536]{1,0:T(8,128)(2,1)}, bf16[384,1536]{1,0:T(8,128)(2,1)}, u32[]{:S(2)}, u32[]{:S(2)}) %collective-permute-start.3) | collective-permute-done | bytes 1179680 | tf_op jit(solution)/shard_map/ppermute | solution.py:412
  93.6 2.3 broadcast_select_fusion
  95.9 23.9 %collective-permute-done.7.refs_4_ = bf16[400,1536]{1,0:T(8,128)(2,1)S(1)} collective-permute-done((bf16[400,1536]{1,0:T(8,128)(2,1)}, bf16[400,1536]{1,0:T(8,128)(2,1)S(1)}, u32[]{:S(2)}, u32[]{:S(2)}) %collective-permute-start.7) | collective-permute-done | bytes 1228832 | tf_op jit(solution)/shard_map/ppermute | solution.py:412
  119.9 1.3 collective-permute-start.9
  121.2 0.4 pad_maximum_fusion
  121.5 0.7 collective-permute-start.12
  122.3 1.3 collective-permute-start.13
  123.6 1.1 slice_select_fusion.1
  124.8 22.0 %collective-permute-done.9.refs_6_ = bf16[400,1536]{1,0:T(8,128)(2,1)S(1)} collective-permute-done((bf16[400,1536]{1,0:T(8,128)(2,1)S(1)}, bf16[400,1536]{1,0:T(8,128)(2,1)S(1)}, u32[]{:S(2)}, u32[]{:S(2)}) %collective-permute-start.9) | collective-permute-done | bytes 1228832 | tf_op jit(solution)/shard_map/ppermute | solution.py:412
  146.7 0.8 slice_select_fusion
  147.8 1.3 collective-permute-start.11
  149.1 0.0 copy-start.4
  149.1 3.4 %multiply_convert_fusion.prev_whole.prev_early = bf16[1536,1536]{1,0:T(8,128)(2,1)} fusion(bf16[1536,1536]{1,0:T(8,128)(2,1)S(1)} %pad_maximum_fusion, f32[1536]{0:T(1024)S(1)} %divide_reduce_fusion), kind=kLoop, calls=%fused_computation | loop fusion | flops 7077888 | bytes 9443328 | tf_op jit(solution)/shard_map/convert_element_type | solution.py:34
  152.5 10.4 %collective-permute-start.10 = (f32[1536]{0:T(1024)S(1)}, f32[1536]{0:T(1024)S(1)}, u32[]{:S(2)}, u32[]{:S(2)}) collective-permute-start(f32[1536]{0:T(1024)S(1)} %pad_maximum_fusion.3), channel_id=1, source_target_pairs={{4,0},{8,4},{12,8},{16,12},{20,16},{24,20},{28,24},{5,1},{9,5},{13... | collective-permute-start | bytes 18440 | tf_op jit(solution)/shard_map/ppermute | solution.py:403
  162.9 2.4 collective-permute-done.10
  165.3 1.3 copy-done.6
  166.6 18.2 %shard_map.60 = (bf16[1536,1536]{1,0:T(8,128)(2,1)S(1)}, f32[384,1536]{1,0:T(8,128)S(1)}, f32[384,1536]{1,0:T(8,128)S(1)}, bf16[1536,1536]{1,0:T(8,128)(2,1)S(1)}, bf16[384,1536]{1,0:T(8,128)(2,1)S(1)}) custom-call(s32[4]{0:T(128)S(1)} %pad_add_fusion.flags, bf16[1536,1536]{1,0:T(8,128)(2,1)} %multiply_convert_fusion.prev_whole.prev_early, ...), custom_call_target="tpu_custom_call" | custom-call | tf_op jit(solution)/shard_map/pallas_call | solution.py:154
  184.8 1.4 copy-done.11
  186.2 4.1 %shard_map.61 = (bf16[384,1536]{1,0:T(8,128)(2,1)S(1)}, f32[384,384]{1,0:T(8,128)S(1)}, bf16[384,1536]{1,0:T(8,128)(2,1)S(1)}) custom-call(s32[4]{0:T(128)S(1)} %pad_add_fusion.flags, f32[8,1536]{1,0:T(8,128)S(1)} %copy-done.10, bf16[384,1536]{1,0:T(8,128)(2,1)S(1)} %bitcast.30, bf16[1536,1536]{1,0:T(8,128)(2,1)S(1)} %get-tuple-element.26.own, ...), custom_call_target="tpu_custom_call" | custom-call | tf_op jit(solution)/shard_map/pallas_call | solution.py:209
  190.3 0.1 constant_dynamic-update-slice_fusion.1.link.link_whole
  190.4 1.3 collective-permute-start.14
  191.7 0.1 constant_dynamic-update-slice_fusion.form
  191.8 5.2 %shard_map.62 = (bf16[384,1536]{1,0:T(8,128)(2,1)S(1)}, f32[8,1536]{1,0:T(8,128)S(1)}, f32[8,1536]{1,0:T(8,128)S(1)}) custom-call(s32[4]{0:T(128)S(1)} %pad_add_fusion.flags, bf16[1536,1536]{1,0:T(8,128)(2,1)S(1)} %constant_dynamic-update-slice_fusion.1.link.link_whole, bf16[384,1536]{1,0:T(8,128)(2,1)S(1)} %get-tuple-element.29.mine, ...), custom_call_target="tpu_custom_call" | custom-call | tf_op jit(solution)/shard_map/pallas_call | solution.py:249
  197.1 1.3 collective-permute-start.15
  198.4 1.5 collective-permute-start.17
  199.9 3.1 %collective-permute-done.15 = f32[1536]{0:T(1024)S(1)} collective-permute-done((f32[1536]{0:T(1024)S(1)}, f32[1536]{0:T(1024)S(1)}, u32[]{:S(2)}, u32[]{:S(2)}) %collective-permute-start.15) | collective-permute-done | bytes 6176 | tf_op jit(solution)/shard_map/ppermute | solution.py:403
  203.0 0.2 multiply_convert_fusion.2
  203.2 2.0 fusion.next_rows
  205.2 2.0 fusion.2
  207.2 0.1 pad_maximum_fusion.1
  207.3 1.6 collective-permute-start.16
  208.9 2.0 fusion.1.ready
  211.0 6.0 %shard_map.63 = (bf16[384,1536]{1,0:T(8,128)(2,1)S(1)}, bf16[384,1536]{1,0:T(8,128)(2,1)S(1)}, bf16[384,1536]{1,0:T(8,128)(2,1)}) custom-call(s32[4]{0:T(128)S(1)} %pad_add_fusion.flags, bf16[384,1536]{1,0:T(8,128)(2,1)S(1)} %bitcast.32, bf16[8,1536]{1,0:T(8,128)(2,1)S(1)} %broadcast_in_dim.17.pivot_scale, bf16[1536,1536]{1,0:T(8,128)(2,1)S(1)} %bitcast.25, ...), custom_call_target="tpu_custom_call" | custom-call | flops 3623878656 | bytes 9437184 | tf_op jit(solution)/shard_map/pallas_call | solution.py:320
  217.0 1.0 copy-done.15
  218.0 1.1 copy-done.17
  219.1 1.4 collective-permute-start.18
  220.5 1.5 collective-permute-start.19
  222.0 3.1 %collective-permute-done.16.pivot_rows = bf16[400,1536]{1,0:T(8,128)(2,1)S(1)} collective-permute-done((bf16[400,1536]{1,0:T(8,128)(2,1)S(1)}, bf16[400,1536]{1,0:T(8,128)(2,1)S(1)}, u32[]{:S(2)}, u32[]{:S(2)}) %collective-permute-start.16) | collective-permute-done | bytes 1228832 | tf_op jit(solution)/shard_map/ppermute | solution.py:403
  225.1 1.1 copy-done.13
  226.2 1.7 copy-done.12
  227.9 1.3 copy-done.14
  229.2 1.3 copy-done.16
  230.4 1.3 copy-done.18
  231.7 11.6 %shard_map.64 = (f32[384,1536]{1,0:T(8,128)S(1)}, bf16[384,1536]{1,0:T(8,128)(2,1)}) custom-call(s32[4]{0:T(128)S(1)} %pad_add_fusion.flags, bf16[400,1536]{1,0:T(8,128)(2,1)S(1)} %copy-done.14, bf16[384,1536]{1,0:T(8,128)(2,1)S(1)} %copy-done.16, bf16[384,1536]{1,0:T(8,128)(2,1)S(1)} %copy-done.18, bf16[384,1536]{1,0:T(8,128)(2,1)S(1)} %fusion.next_rows, ...), custom_call_target="tpu_custom_call" | custom-call | flops 7247757312 | bytes 18874368 | tf_op jit(solution)/shard_map/pallas_call | solution.py:369
  243.4 2.1 subtract_bitcast_fusion
  (62 shorter events, 0.4 us)
Async XLA Ops:
  0.6 2.1 copy-start
  2.7 4.4 %copy-start.9 = (f32[8,1536]{1,0:T(8,128)}, f32[8,1536]{1,0:T(8,128)S(1)}, u32[]{:S(2)}) copy-start(f32[8,1536]{1,0:T(8,128)S(1)} %broadcast_in_dim.15.reciprocal) | copy-start | bytes 147460
  2.7 1.3 copy-start.1
  4.0 65.5 %copy-start.2 = (bf16[1,384,1536]{2,1,0:T(8,128)(2,1)S(1)}, bf16[1,384,1536]{2,1,0:T(8,128)(2,1)}, u32[]{:S(2)}) copy-start(bf16[1,384,1536]{2,1,0:T(8,128)(2,1)} %param.5) | copy-start | bytes 3538948
  7.1 29.2 %collective-permute-start.4 = (bf16[400,1536]{1,0:T(8,128)(2,1)}, bf16[400,1536]{1,0:T(8,128)(2,1)}, u32[]{:S(2)}, u32[]{:S(2)}) collective-permute-start(bf16[400,1536]{1,0:T(8,128)(2,1)} %shard_map.59.refs_0_), channel_id=1, source_target_pairs={{0,1},{1,2},{2,3},{4,5},{5,6},{6,7},{8,9},{9,10},{10,11},{12,13},{... | collective-permute-start | bytes 3686408 | tf_op jit(solution)/shard_map/ppermute | solution.py:412
  11.4 50.1 %collective-permute-start = (bf16[384,1536]{1,0:T(8,128)(2,1)S(1)}, bf16[384,1536]{1,0:T(8,128)(2,1)S(1)}, u32[]{:S(2)}, u32[]{:S(2)}) collective-permute-start(bf16[384,1536]{1,0:T(8,128)(2,1)S(1)} %bitcast.27), channel_id=1, source_target_pairs={{0,1},{1,2},{2,3},{4,5},{5,6},{6,7},{8,9},{9,10},{10,11},{12,13},{... | collective-permute-start | bytes 3538952 | tf_op jit(solution)/shard_map/ppermute | solution.py:412
  13.6 49.6 %collective-permute-start.2 = (bf16[384,1536]{1,0:T(8,128)(2,1)S(1)}, bf16[384,1536]{1,0:T(8,128)(2,1)}, u32[]{:S(2)}, u32[]{:S(2)}) collective-permute-start(bf16[384,1536]{1,0:T(8,128)(2,1)S(1)} %bitcast.28), channel_id=1, source_target_pairs={{1,0},{2,1},{3,2},{5,4},{6,5},{7,6},{9,8},{10,9},{11,10},{13,12},{... | collective-permute-start | bytes 3538952 | tf_op jit(solution)/shard_map/ppermute | solution.py:412
  14.9 53.3 %collective-permute-start.5 = (bf16[400,1536]{1,0:T(8,128)(2,1)}, bf16[400,1536]{1,0:T(8,128)(2,1)}, u32[]{:S(2)}, u32[]{:S(2)}) collective-permute-start(bf16[400,1536]{1,0:T(8,128)(2,1)} %shard_map.59.refs_0_), channel_id=1, source_target_pairs={{1,0},{2,1},{3,2},{5,4},{6,5},{7,6},{9,8},{10,9},{11,10},{13,12},{... | collective-permute-start | bytes 3686408 | tf_op jit(solution)/shard_map/ppermute | solution.py:412
  36.3 33.4 %collective-permute-start.6 = (bf16[400,1536]{1,0:T(8,128)(2,1)}, bf16[400,1536]{1,0:T(8,128)(2,1)}, u32[]{:S(2)}, u32[]{:S(2)}) collective-permute-start(bf16[400,1536]{1,0:T(8,128)(2,1)} %collective-permute-done.4.refs_1_), channel_id=1, source_target_pairs={{1,2},{2,3},{5,6},{6,7},{9,10},{10,11},{13,14},{14,15},{17,18},{18... | collective-permute-start | bytes 3686408 | tf_op jit(solution)/shard_map/ppermute | solution.py:412
  61.5 8.9 %collective-permute-start.1 = (bf16[384,1536]{1,0:T(8,128)(2,1)S(1)}, bf16[384,1536]{1,0:T(8,128)(2,1)}, u32[]{:S(2)}, u32[]{:S(2)}) collective-permute-start(bf16[384,1536]{1,0:T(8,128)(2,1)S(1)} %collective-permute-done), channel_id=1, source_target_pairs={{1,2},{2,3},{5,6},{6,7},{9,10},{10,11},{13,14},{14,15},{17,18},{18... | collective-permute-start | bytes 3538952 | tf_op jit(solution)/shard_map/ppermute | solution.py:412
  63.2 30.5 %collective-permute-start.3 = (bf16[384,1536]{1,0:T(8,128)(2,1)}, bf16[384,1536]{1,0:T(8,128)(2,1)}, u32[]{:S(2)}, u32[]{:S(2)}) collective-permute-start(bf16[384,1536]{1,0:T(8,128)(2,1)} %collective-permute-done.2), channel_id=1, source_target_pairs={{1,0},{2,1},{5,4},{6,5},{9,8},{10,9},{13,12},{14,13},{17,16},{18,1... | collective-permute-start | bytes 3538952 | tf_op jit(solution)/shard_map/ppermute | solution.py:412
  68.2 51.7 %collective-permute-start.7 = (bf16[400,1536]{1,0:T(8,128)(2,1)}, bf16[400,1536]{1,0:T(8,128)(2,1)S(1)}, u32[]{:S(2)}, u32[]{:S(2)}) collective-permute-start(bf16[400,1536]{1,0:T(8,128)(2,1)} %collective-permute-done.5.refs_2_), channel_id=1, source_target_pairs={{1,0},{2,1},{5,4},{6,5},{9,8},{10,9},{13,12},{14,13},{17,16},{18,1... | collective-permute-start | bytes 3686408 | tf_op jit(solution)/shard_map/ppermute | solution.py:412
  69.7 53.9 %collective-permute-start.8 = (bf16[400,1536]{1,0:T(8,128)(2,1)}, bf16[400,1536]{1,0:T(8,128)(2,1)S(1)}, u32[]{:S(2)}, u32[]{:S(2)}) collective-permute-start(bf16[400,1536]{1,0:T(8,128)(2,1)} %collective-permute-done.6.refs_3_), channel_id=1, source_target_pairs={{2,3},{6,7},{10,11},{14,15},{18,19},{22,23},{26,27},{30,31}} | collective-permute-start | bytes 3686408 | tf_op jit(solution)/shard_map/ppermute | solution.py:412
  119.9 26.9 %collective-permute-start.9 = (bf16[400,1536]{1,0:T(8,128)(2,1)S(1)}, bf16[400,1536]{1,0:T(8,128)(2,1)S(1)}, u32[]{:S(2)}, u32[]{:S(2)}) collective-permute-start(bf16[400,1536]{1,0:T(8,128)(2,1)S(1)} %collective-permute-done.7.refs_4_), channel_id=1, source_target_pairs={{1,0},{5,4},{9,8},{13,12},{17,16},{21,20},{25,24},{29,28}} | collective-permute-start | bytes 3686408 | tf_op jit(solution)/shard_map/ppermute | solution.py:412
  121.5 64.7 %collective-permute-start.12 = (bf16[384,1536]{1,0:T(8,128)(2,1)}, bf16[384,1536]{1,0:T(8,128)(2,1)S(1)}, u32[]{:S(2)}, u32[]{:S(2)}) collective-permute-start(bf16[384,1536]{1,0:T(8,128)(2,1)} %collective-permute-done.1), channel_id=1, source_target_pairs={{2,3},{6,7},{10,11},{14,15},{18,19},{22,23},{26,27},{30,31}} | collective-permute-start | bytes 3538952 | tf_op jit(solution)/shard_map/ppermute | solution.py:412
  122.3 63.9 %collective-permute-start.13 = (bf16[384,1536]{1,0:T(8,128)(2,1)}, bf16[384,1536]{1,0:T(8,128)(2,1)S(1)}, u32[]{:S(2)}, u32[]{:S(2)}) collective-permute-start(bf16[384,1536]{1,0:T(8,128)(2,1)} %collective-permute-done.3), channel_id=1, source_target_pairs={{1,0},{5,4},{9,8},{13,12},{17,16},{21,20},{25,24},{29,28}} | collective-permute-start | bytes 3538952 | tf_op jit(solution)/shard_map/ppermute | solution.py:412
  123.6 29.0 %copy-start.5 = (bf16[400,1536]{1,0:T(8,128)(2,1)}, bf16[400,1536]{1,0:T(8,128)(2,1)S(1)}, u32[]{:S(2)}) copy-start(bf16[400,1536]{1,0:T(8,128)(2,1)S(1)} %collective-permute-done.8.refs_5_) | copy-start | bytes 3686404
  147.8 15.1 %collective-permute-start.11 = (f32[1536]{0:T(1024)S(1)}, f32[1536]{0:T(1024)S(1)}, u32[]{:S(2)}, u32[]{:S(2)}) collective-permute-start(f32[1536]{0:T(1024)S(1)} %pad_maximum_fusion.2), channel_id=1, source_target_pairs={{0,4},{8,12},{16,20},{24,28},{1,5},{9,13},{17,21},{25,29},{2,6},{1... | collective-permute-start | bytes 18440 | tf_op jit(solution)/shard_map/ppermute | solution.py:403
  149.1 16.2 %copy-start.4 = (f32[1,384,1536]{2,1,0:T(8,128)S(1)}, f32[1,384,1536]{2,1,0:T(8,128)}, u32[]{:S(2)}) copy-start(f32[1,384,1536]{2,1,0:T(8,128)} %param.4) | copy-start | bytes 7077892
  152.5 12.8 %collective-permute-start.10 = (f32[1536]{0:T(1024)S(1)}, f32[1536]{0:T(1024)S(1)}, u32[]{:S(2)}, u32[]{:S(2)}) collective-permute-start(f32[1536]{0:T(1024)S(1)} %pad_maximum_fusion.3), channel_id=1, source_target_pairs={{4,0},{8,4},{12,8},{16,12},{20,16},{24,20},{28,24},{5,1},{9,5},{13... | collective-permute-start | bytes 18440 | tf_op jit(solution)/shard_map/ppermute | solution.py:403
  165.3 1.3 copy-start.6
  166.6 19.6 %copy-start.10 = (f32[8,1536]{1,0:T(8,128)S(1)}, f32[8,1536]{1,0:T(8,128)}, u32[]{:S(2)}) copy-start(f32[8,1536]{1,0:T(8,128)} %copy-done.9) | copy-start | bytes 147460
  184.8 1.4 copy-start.11
  186.2 5.6 %copy-start.7 = (bf16[384,1536]{1,0:T(8,128)(2,1)}, bf16[384,1536]{1,0:T(8,128)(2,1)S(1)}, u32[]{:S(2)}) copy-start(bf16[384,1536]{1,0:T(8,128)(2,1)S(1)} %get-tuple-element.29.mine) | copy-start | bytes 3538948
  190.4 12.5 %collective-permute-start.14 = (bf16[1536,1536]{1,0:T(8,128)(2,1)S(1)}, bf16[1536,1536]{1,0:T(8,128)(2,1)S(1)}, u32[]{:S(2)}, u32[]{:S(2)}) collective-permute-start(bf16[1536,1536]{1,0:T(8,128)(2,1)S(1)} %constant_dynamic-update-slice_fusion.1.link.link_whole), channel_id=1, source_target_pairs={{0,4},{8,12},{16,20},{24,28},{1,5},{9,13},{17,21},{25,29},{2,6},{1... | collective-permute-start | bytes 14155784 | tf_op jit(solution)/shard_map/ppermute | solution.py:403
  197.1 5.9 %collective-permute-start.15 = (f32[1536]{0:T(1024)S(1)}, f32[1536]{0:T(1024)S(1)}, u32[]{:S(2)}, u32[]{:S(2)}) collective-permute-start(f32[1536]{0:T(1024)S(1)} %slice_reduce_fusion.1), channel_id=1, source_target_pairs={{8,4},{16,12},{24,20},{9,5},{17,13},{25,21},{10,6},{18,14},{26,22}... | collective-permute-start | bytes 18440 | tf_op jit(solution)/shard_map/ppermute | solution.py:403
  198.4 44.9 %collective-permute-start.17 = (bf16[384,1536]{1,0:T(8,128)(2,1)S(1)}, bf16[384,1536]{1,0:T(8,128)(2,1)S(1)}, u32[]{:S(2)}, u32[]{:S(2)}) collective-permute-start(bf16[384,1536]{1,0:T(8,128)(2,1)S(1)} %get-tuple-element.35.update), channel_id=1, source_target_pairs={{8,4},{16,12},{24,20},{9,5},{17,13},{25,21},{10,6},{18,14},{26,22}... | collective-permute-start | bytes 3538952 | tf_op jit(solution)/shard_map/ppermute | solution.py:403
  203.0 8.0 %copy-start.3 = (bf16[1536,1536]{1,0:T(8,128)(2,1)}, bf16[1536,1536]{1,0:T(8,128)(2,1)S(1)}, u32[]{:S(2)}) copy-start(bf16[1536,1536]{1,0:T(8,128)(2,1)S(1)} %collective-permute-done.14.pivot_whole) | copy-start | bytes 14155780
  207.2 3.7 %slice-start = ((s8[4718592]{0:T(1024)(128)(4,1)}), s8[4194304]{0:T(1024)(128)(4,1)S(1)}, s32[]{:S(2)}) async-start(s8[4718592]{0:T(1024)(128)(4,1)} %bitcast.24), calls=%async_computation | async-start | bytes 8388608
  207.3 3.6 %slice-start.1 = ((s8[4718592]{0:T(1024)(128)(4,1)}), s8[524288]{0:T(1024)(128)(4,1)S(1)}, s32[]{:S(2)}) async-start(s8[4718592]{0:T(1024)(128)(4,1)} %bitcast.24), calls=%async_computation.1 | async-start | bytes 1048576
  207.3 17.7 %collective-permute-start.16 = (bf16[400,1536]{1,0:T(8,128)(2,1)S(1)}, bf16[400,1536]{1,0:T(8,128)(2,1)S(1)}, u32[]{:S(2)}, u32[]{:S(2)}) collective-permute-start(bf16[400,1536]{1,0:T(8,128)(2,1)S(1)} %pad_maximum_fusion.1), channel_id=1, source_target_pairs={{4,12},{20,28},{5,13},{21,29},{6,14},{22,30},{7,15},{23,31}} | collective-permute-start | bytes 3686408 | tf_op jit(solution)/shard_map/ppermute | solution.py:403
  211.0 15.2 %copy-start.8 = (bf16[384,1536]{1,0:T(8,128)(2,1)S(1)}, bf16[384,1536]{1,0:T(8,128)(2,1)}, u32[]{:S(2)}) copy-start(bf16[384,1536]{1,0:T(8,128)(2,1)} %copy-done.7) | copy-start | bytes 3538948
  217.0 1.0 copy-start.15
  218.0 1.1 copy-start.17
  219.1 24.2 %collective-permute-start.18 = (bf16[384,1536]{1,0:T(8,128)(2,1)}, bf16[384,1536]{1,0:T(8,128)(2,1)S(1)}, u32[]{:S(2)}, u32[]{:S(2)}) collective-permute-start(bf16[384,1536]{1,0:T(8,128)(2,1)} %get-tuple-element.40), channel_id=1, source_target_pairs={{4,0},{12,8},{20,16},{28,24},{5,1},{13,9},{21,17},{29,25},{6,2},{1... | collective-permute-start | bytes 3538952 | tf_op jit(solution)/shard_map/ppermute | solution.py:403
  220.5 22.9 %collective-permute-start.19 = (bf16[384,1536]{1,0:T(8,128)(2,1)S(1)}, bf16[384,1536]{1,0:T(8,128)(2,1)S(1)}, u32[]{:S(2)}, u32[]{:S(2)}) collective-permute-start(bf16[384,1536]{1,0:T(8,128)(2,1)S(1)} %fusion.1.ready), channel_id=1, source_target_pairs={{20,12},{21,13},{22,14},{23,15}} | collective-permute-start | bytes 3538952 | tf_op jit(solution)/shard_map/ppermute | solution.py:403
  225.1 1.1 copy-start.13
  226.2 1.7 copy-start.12
  227.9 1.3 copy-start.14
  229.2 1.3 copy-start.16
  230.4 1.3 copy-start.18

commit v6 on v5

--- a/solution.py
+++ b/solution.py
@@ -296,12 +296,16 @@
 
 
 def columns_kernel(
-    flags, own, pivot_scale, prev_early, prev_late, pivot_whole, update, ready,
-    right, columns, moved, prev, pivot, sems, pivot_sem, move_sem,
+    flags, own, pivot_scale, prev_early, prev_late, pivot_whole, update, received, ready,
+    right, columns, moved, passed, prev, pivot, sems, pivot_sem, move_sems,
 ):
     del ready
-    move = pltpu.make_async_copy(update, moved, move_sem)
-    move.start()
+    moves = [
+        pltpu.make_async_copy(update, moved, move_sems.at[0]),
+        pltpu.make_async_copy(received, passed, move_sems.at[1]),
+    ]
+    for move in moves:
+        move.start()
     wait_prev = fetched(prev_early, prev_late, prev, sems, [flags[1]])
     copy = pltpu.make_async_copy(pivot_whole, pivot, pivot_sem)
     copy.start()
@@ -311,57 +315,68 @@
     right[...] = across
     copy.wait()
     columns[...] = (-dot_nt(across, pivot[...])).astype(BF16)
-    move.wait()
-
-
-def columns_forms(flags, own, pivot_scale, prev_early, prev_late, pivot, update, ready):
+    for move in moves:
+        move.wait()
+
+
+def columns_forms(flags, own, pivot_scale, prev_early, prev_late, pivot, update, received, ready):
     rows, order = own.shape
     out = SHAPE((rows, order), BF16)
     return pl.pallas_call(
         columns_kernel,
-        out_shape=[out, out, out],
+        out_shape=[out, out, out, out],
         grid_spec=pltpu.PrefetchScalarGridSpec(
             num_scalar_prefetch=1,
             grid=(1,),
-            in_specs=[whole_spec((rows, order)), whole_spec((8, order))] + [ANY] * 5,
-            out_specs=[whole_spec((rows, order)), whole_spec((rows, order)), ANY],
+            in_specs=[whole_spec((rows, order)), whole_spec((8, order))] + [ANY] * 6,
+            out_specs=[whole_spec((rows, order)), whole_spec((rows, order)), ANY, ANY],
             scratch_shapes=[
                 pltpu.VMEM((order, order), BF16),
                 pltpu.VMEM((order, order), BF16),
                 pltpu.SemaphoreType.DMA((order // rows,)),
                 pltpu.SemaphoreType.DMA,
-                pltpu.SemaphoreType.DMA,
+                pltpu.SemaphoreType.DMA((2,)),
             ],
         ),
         compiler_params=pltpu.CompilerParams(vmem_limit_bytes=22 * 1024 * 1024),
         cost_estimate=products_cost(rows, order, 2),
-    )(flags, own, pivot_scale, prev_early, prev_late, pivot, update, ready)
+    )(flags, own, pivot_scale, prev_early, prev_late, pivot, update, received, ready)
 
 
 def last_kernel(
-    flags, pivot_rows, right, columns, next_rows, mine, partial, pivot_scale,
-    link_whole, pivot_whole, form, new, link, pivot, sems,
+    flags, pivot_rows, right, columns, pivot_scale, next_rows, mine, partial, link_whole, pivot_whole,
+    form, new, link, pivot, last, sems,
 ):
     rows = right.shape[0]
-    copies = [
+    even, final = flags[2] == 1, flags[3] == 1
+    other = jnp.logical_not(jnp.logical_or(even, final))
+    fetch = [
         pltpu.make_async_copy(pivot_whole, pivot, sems.at[0]),
         pltpu.make_async_copy(link_whole, link, sems.at[1]),
+        pltpu.make_async_copy(partial, form, sems.at[2]),
     ]
-    for copy in copies:
+    for copy in fetch:
         copy.start()
-    scale = pivot_rows[rows : rows + 8, :]
-    both = jnp.concatenate([times(columns[...], scale), times(pivot_rows[0:rows, :], scale)])
-    copies[0].wait()
-    inner = dot_nn(both, pivot[...]) * pivot_scale[0:1].astype(F32)
-    keep = jnp.where(flags[3] == 1, 1.0, 0.0)
-    factor = (right[...].astype(F32) - inner[0:rows] * keep).astype(BF16)
-    both = jnp.concatenate([factor, inner[rows:].astype(BF16)])
-    copies[1].wait()
-    both = dot_nn(both, link[...])
-    odd = jnp.where(flags[2] == 1, 0.0, 1.0)
-    form[...] = partial[...] - odd * both[0:rows]
-    last = both[rows:].astype(BF16)
-    new[...] = jnp.where(flags[3] == 1, last, jnp.where(flags[2] == 1, mine[...], next_rows[...]))
+    plain = [(even, pltpu.make_async_copy(mine, new, sems.at[3]))]
+    plain.append((other, pltpu.make_async_copy(next_rows, new, sems.at[3])))
+    for chosen, copy in plain:
+        pl.when(chosen)(copy.start)
+    scale = pivot_rows[rows : rows + EXTRA, :]
+    wide = pivot_scale[0:1].astype(F32)
+    fetch[0].wait()
+    inner = dot_nn(times(columns[...], scale), pivot[...]) * wide
+    keep = jnp.where(final, 1.0, 0.0)
+    factor = (right[...].astype(F32) - inner * keep).astype(BF16)
+    inner = (dot_nn(times(pivot_rows[0:rows, :], scale), pivot[...]) * wide).astype(BF16)
+    fetch[1].wait()
+    last[...] = dot_nn(inner, link[...]).astype(BF16)
+    store = pltpu.make_async_copy(last, new, sems.at[3])
+    pl.when(final)(store.start)
+    fetch[2].wait()
+    odd = jnp.where(even, 0.0, 1.0)
+    form[...] -= odd * dot_nn(factor, link[...])
+    for chosen, copy in plain + [(final, store)]:
+        pl.when(chosen)(copy.wait)
 
 
 def last_forms(flags, pivot_rows, right, columns, next_rows, mine, partial, pivot_scale, link, pivot):
@@ -372,19 +387,24 @@
         grid_spec=pltpu.PrefetchScalarGridSpec(
             num_scalar_prefetch=1,
             grid=(1,),
-            in_specs=[whole_spec(pivot_rows.shape)]
-            + [whole_spec((rows, order))] * 5
-            + [whole_spec((8, order)), ANY, ANY],
-            out_specs=[whole_spec((rows, order)), whole_spec((rows, order))],
+            in_specs=[
+                whole_spec(pivot_rows.shape),
+                whole_spec((rows, order)),
+                whole_spec((rows, order)),
+                whole_spec((8, order)),
+            ]
+            + [ANY] * 5,
+            out_specs=[whole_spec((rows, order)), ANY],
             scratch_shapes=[
                 pltpu.VMEM((order, order), BF16),
                 pltpu.VMEM((order, order), BF16),
-                pltpu.SemaphoreType.DMA((2,)),
+                pltpu.VMEM((rows, order), BF16),
+                pltpu.SemaphoreType.DMA((4,)),
             ],
         ),
-        compiler_params=pltpu.CompilerParams(vmem_limit_bytes=36 * 1024 * 1024),
+        compiler_params=pltpu.CompilerParams(vmem_limit_bytes=28 * 1024 * 1024),
         cost_estimate=products_cost(rows, order, 4),
-    )(flags, pivot_rows, right, columns, next_rows, mine, partial, pivot_scale, link, pivot)
+    )(flags, pivot_rows, right, columns, pivot_scale, next_rows, mine, partial, link, pivot)
 
 
 def on_device(sep_block, own_couple, prev_couple, inner_diag):
@@ -481,7 +501,9 @@
     left_diag, right_diag = left_diag[0], right_diag[0]
 
     left_diag = between(left_diag, [(p, p - 1) for p in even])
-    from_even = between(update, [(p, p - 1) for p in even])
+    from_even = between(
+        update, [(p, p - 1) for p in range(2, parts, 4)] + [(p, p - 4) for p in range(4, parts, 4)]
+    )
     next_diag = diag - left_diag - right_diag
     next_scale = (1.0 / jnp.maximum(next_diag, 1.0)).astype(BF16)
     pivot_rows = lax.dynamic_slice_in_dim(pivot_link, row_start, rows, 0)
@@ -494,13 +516,15 @@
     left_next = lax.optimization_barrier(left_next)
     left_next = (-dot_nt(left_next, pivot_link)).astype(BF16)
     from_pivot = between(left_next, [(p, p - 2) for p in pivots])
-    right, columns, own_update = columns_forms(
-        flags, own_rows, pivot_scale8, prev_first, prev_late, pivot_link, update, left_next
-    )
+    right, columns, own_update, passed = columns_forms(
+        flags, own_rows, pivot_scale8, prev_first, prev_late, pivot_link, update, from_even, left_next
+    )
+    from_far = between(passed, [(p - 4, p - 1) for p in range(4, parts, 4)])
     from_odd = between(own_update, [(p, p - 1) for p in range(1, parts, 2)])
     form, out_link = last_forms(
         flags, pivot_long, right, columns, next_rows, mine, partial, pivot_scale8, link, pivot_link
     )
+    from_even = jnp.where(is_receiver, from_even + from_far, jnp.zeros_like(from_even))
     schur = form - (from_even + from_odd).astype(F32) - from_pivot.astype(F32)
     return (schur[None], out_link[None])
 

time: 250 us -> 262 us (1.048)
  the two profiles are of different devices: /device:TPU:3 before, /device:TPU:1 now
where the time goes in v6:
time: 262 us; the launch traced here: 261 us
  waiting for transfers between devices  122 us (47%)
  Pallas kernels  49.1 us (19%)
  starting transfers between devices  48.6 us (19%)
  local copies, waits for them, and re-layouts  19.1 us (7%)
  other arithmetic  14.5 us (6%)
  matrix products  6.02 us (2%)
    ppermute x12, waiting for transfers between devices, one_step(): return (lax.ppermute(ahead, 'space', up), lax.ppermute(back, 'space', down))  115 us
    ppermute x9, starting transfers between devices, between(): lax.ppermute(block, 'tm', [(a, b) for a, b in route if 0 <= b < parts])  28.6 us
    ppermute x12, starting transfers between devices, one_step(): return (lax.ppermute(ahead, 'space', up), lax.ppermute(back, 'space', down))  20 us
    pallas_call x1, Pallas kernels, early_forms(): pl.pallas_call(functools.partial(early_kernel, size), out_shape=[SHAPE((o...  18.4 us
    unnamed x56, local copies, waits for them, and re-layouts  17.6 us
    pallas_call x1, Pallas kernels, last_forms(): pl.pallas_call(last_kernel, out_shape=[SHAPE((rows, order), F32), SHAPE((...  10.6 us
    ppermute x9, waiting for transfers between devices, between(): lax.ppermute(block, 'tm', [(a, b) for a, b in route if 0 <= b < parts])  6.89 us
    pallas_call x1, Pallas kernels, columns_forms(): pl.pallas_call(columns_kernel, out_shape=[out, out, out, out], grid_spec=...  6.01 us
  transfers between devices with their start and end apart: 21, of which 9 were waited for; matrix products, arithmetic and copies ran while one was open for 6% of the time, Pallas kernels for 15%

profile of v6, /device:TPU:1, one launch (start us, length us, event | category | flops | bytes accessed | tf_op | source)
XLA Modules:
  0.0 260.8 jit_solution(6274664223914568560)
XLA Ops:
  0.7 0.8 divide_reduce_fusion
  1.5 1.1 dynamic-slice_bitcast_fusion.separator
  2.7 1.3 copy-done.1
  4.0 3.1 %shard_map.59.refs_0_ = bf16[400,1536]{1,0:T(8,128)(2,1)} custom-call(s32[4]{0:T(128)S(1)} %pad_add_fusion.flags, bf16[384,1536]{1,0:T(8,128)(2,1)S(1)} %bitcast.31, bf16[384,1536]{1,0:T(8,128)(2,1)S(1)} %bitcast.26, f32[384,384]{1,0:T(8,128)S(1)} %dynamic-slice_bitcast_fusion.separator, f32[8,1536]{1,0:T(8,128)S(1)} %broadcast_in_dim.12.reciprocal), custom_call_target="tpu_custom_call" | custom-call | tf_op jit(solution)/shard_map/pallas_call | solution.py:107
  7.1 5.1 %collective-permute-start.4 = (bf16[400,1536]{1,0:T(8,128)(2,1)}, bf16[400,1536]{1,0:T(8,128)(2,1)}, u32[]{:S(2)}, u32[]{:S(2)}) collective-permute-start(bf16[400,1536]{1,0:T(8,128)(2,1)} %shard_map.59.refs_0_), channel_id=1, source_target_pairs={{0,1},{1,2},{2,3},{4,5},{5,6},{6,7},{8,9},{9,10},{10,11},{12,13},{... | collective-permute-start | bytes 3686408 | tf_op jit(solution)/shard_map/ppermute | solution.py:432
  12.2 2.2 collective-permute-start
  14.5 1.3 collective-permute-start.2
  15.8 1.3 collective-permute-start.5
  17.1 20.1 %collective-permute-done.4.refs_1_ = bf16[400,1536]{1,0:T(8,128)(2,1)} collective-permute-done((bf16[400,1536]{1,0:T(8,128)(2,1)}, bf16[400,1536]{1,0:T(8,128)(2,1)}, u32[]{:S(2)}, u32[]{:S(2)}) %collective-permute-start.4) | collective-permute-done | bytes 1228832 | tf_op jit(solution)/shard_map/ppermute | solution.py:432
  37.2 1.8 collective-permute-start.6
  38.9 23.4 %collective-permute-done = bf16[384,1536]{1,0:T(8,128)(2,1)S(1)} collective-permute-done((bf16[384,1536]{1,0:T(8,128)(2,1)S(1)}, bf16[384,1536]{1,0:T(8,128)(2,1)S(1)}, u32[]{:S(2)}, u32[]{:S(2)}) %collective-permute-start) | collective-permute-done | bytes 1179680 | tf_op jit(solution)/shard_map/ppermute | solution.py:432
  62.3 1.7 collective-permute-start.1
  64.0 1.3 collective-permute-start.3
  65.3 3.7 %collective-permute-done.5.refs_2_ = bf16[400,1536]{1,0:T(8,128)(2,1)} collective-permute-done((bf16[400,1536]{1,0:T(8,128)(2,1)}, bf16[400,1536]{1,0:T(8,128)(2,1)}, u32[]{:S(2)}, u32[]{:S(2)}) %collective-permute-start.5) | collective-permute-done | bytes 1228832 | tf_op jit(solution)/shard_map/ppermute | solution.py:432
  69.0 1.3 collective-permute-start.7
  70.3 0.2 multiply_convert_fusion.3.own_rows
  70.5 0.7 collective-permute-start.8
  71.3 23.2 %collective-permute-done.3 = bf16[384,1536]{1,0:T(8,128)(2,1)} collective-permute-done((bf16[384,1536]{1,0:T(8,128)(2,1)}, bf16[384,1536]{1,0:T(8,128)(2,1)}, u32[]{:S(2)}, u32[]{:S(2)}) %collective-permute-start.3) | collective-permute-done | bytes 1179680 | tf_op jit(solution)/shard_map/ppermute | solution.py:432
  94.5 2.4 broadcast_select_fusion
  96.8 23.9 %collective-permute-done.7.refs_4_ = bf16[400,1536]{1,0:T(8,128)(2,1)S(1)} collective-permute-done((bf16[400,1536]{1,0:T(8,128)(2,1)}, bf16[400,1536]{1,0:T(8,128)(2,1)S(1)}, u32[]{:S(2)}, u32[]{:S(2)}) %collective-permute-start.7) | collective-permute-done | bytes 1228832 | tf_op jit(solution)/shard_map/ppermute | solution.py:432
  120.7 1.3 collective-permute-start.9
  122.0 0.4 pad_maximum_fusion
  122.4 0.7 collective-permute-start.12
  123.1 1.3 collective-permute-start.13
  124.4 0.9 slice_select_fusion.1
  125.3 1.0 copy-done.8
  126.4 21.2 %collective-permute-done.9.refs_6_ = bf16[400,1536]{1,0:T(8,128)(2,1)S(1)} collective-permute-done((bf16[400,1536]{1,0:T(8,128)(2,1)S(1)}, bf16[400,1536]{1,0:T(8,128)(2,1)S(1)}, u32[]{:S(2)}, u32[]{:S(2)}) %collective-permute-start.9) | collective-permute-done | bytes 1228832 | tf_op jit(solution)/shard_map/ppermute | solution.py:432
  147.6 0.8 slice_select_fusion
  148.4 1.0 copy-done.10
  149.7 1.4 collective-permute-start.11
  151.2 3.1 %multiply_convert_fusion.prev_whole.prev_early = bf16[1536,1536]{1,0:T(8,128)(2,1)} fusion(bf16[1536,1536]{1,0:T(8,128)(2,1)S(1)} %pad_maximum_fusion, f32[1536]{0:T(1024)S(1)} %divide_reduce_fusion), kind=kLoop, calls=%fused_computation | loop fusion | flops 7077888 | bytes 9443328 | tf_op jit(solution)/shard_map/convert_element_type | solution.py:34
  154.3 10.4 %collective-permute-start.10 = (f32[1536]{0:T(1024)S(1)}, f32[1536]{0:T(1024)S(1)}, u32[]{:S(2)}, u32[]{:S(2)}) collective-permute-start(f32[1536]{0:T(1024)S(1)} %pad_maximum_fusion.3), channel_id=1, source_target_pairs={{4,0},{8,4},{12,8},{16,12},{20,16},{24,20},{28,24},{5,1},{9,5},{13... | collective-permute-start | bytes 18440 | tf_op jit(solution)/shard_map/ppermute | solution.py:423
  164.7 2.8 %collective-permute-done.10 = f32[1536]{0:T(1024)S(1)} collective-permute-done((f32[1536]{0:T(1024)S(1)}, f32[1536]{0:T(1024)S(1)}, u32[]{:S(2)}, u32[]{:S(2)}) %collective-permute-start.10) | collective-permute-done | bytes 6176 | tf_op jit(solution)/shard_map/ppermute | solution.py:423
  167.5 18.4 %shard_map.60 = (bf16[1536,1536]{1,0:T(8,128)(2,1)S(1)}, f32[384,1536]{1,0:T(8,128)S(1)}, f32[384,1536]{1,0:T(8,128)S(1)}, bf16[1536,1536]{1,0:T(8,128)(2,1)S(1)}, bf16[384,1536]{1,0:T(8,128)(2,1)S(1)}) custom-call(s32[4]{0:T(128)S(1)} %pad_add_fusion.flags, bf16[1536,1536]{1,0:T(8,128)(2,1)} %multiply_convert_fusion.prev_whole.prev_early, ...), custom_call_target="tpu_custom_call" | custom-call | tf_op jit(solution)/shard_map/pallas_call | solution.py:154
  186.0 5.7 %shard_map.61 = (bf16[384,1536]{1,0:T(8,128)(2,1)S(1)}, f32[384,384]{1,0:T(8,128)S(1)}, bf16[384,1536]{1,0:T(8,128)(2,1)S(1)}) custom-call(s32[4]{0:T(128)S(1)} %pad_add_fusion.flags, f32[8,1536]{1,0:T(8,128)S(1)} %copy-done.17, bf16[384,1536]{1,0:T(8,128)(2,1)S(1)} %bitcast.30, bf16[1536,1536]{1,0:T(8,128)(2,1)S(1)} %get-tuple-element.27.own, ...), custom_call_target="tpu_custom_call" | custom-call | tf_op jit(solution)/shard_map/pallas_call | solution.py:209
  191.7 0.1 constant_dynamic-update-slice_fusion.1.link.link_whole
  191.9 1.3 collective-permute-start.14
  193.3 5.2 %shard_map.62 = (bf16[384,1536]{1,0:T(8,128)(2,1)S(1)}, f32[8,1536]{1,0:T(8,128)S(1)}, f32[8,1536]{1,0:T(8,128)S(1)}) custom-call(s32[4]{0:T(128)S(1)} %pad_add_fusion.flags, bf16[1536,1536]{1,0:T(8,128)(2,1)S(1)} %constant_dynamic-update-slice_fusion.1.link.link_whole, bf16[384,1536]{1,0:T(8,128)(2,1)S(1)} %get-tuple-element.30.mine, ...), custom_call_target="tpu_custom_call" | custom-call | tf_op jit(solution)/shard_map/pallas_call | solution.py:249
  198.5 1.3 collective-permute-start.15
  199.8 1.5 collective-permute-start.17
  201.3 2.2 collective-permute-done.15
  203.5 0.2 multiply_convert_fusion.2
  203.7 2.0 fusion.next_rows
  205.7 2.0 fusion.2
  207.8 1.1 pad_maximum_fusion.1
  208.9 4.8 %collective-permute-start.16 = (bf16[400,1536]{1,0:T(8,128)(2,1)}, bf16[400,1536]{1,0:T(8,128)(2,1)}, u32[]{:S(2)}, u32[]{:S(2)}) collective-permute-start(bf16[400,1536]{1,0:T(8,128)(2,1)} %pad_maximum_fusion.1), channel_id=1, source_target_pairs={{4,12},{20,28},{5,13},{21,29},{6,14},{22,30},{7,15},{23,31}} | collective-permute-start | bytes 3686408 | tf_op jit(solution)/shard_map/ppermute | solution.py:423
  213.7 2.0 fusion.1.ready
  215.7 1.9 collective-permute-done.17.received
  217.7 6.0 %shard_map.63 = (bf16[384,1536]{1,0:T(8,128)(2,1)S(1)}, bf16[384,1536]{1,0:T(8,128)(2,1)S(1)}, bf16[384,1536]{1,0:T(8,128)(2,1)}, bf16[384,1536]{1,0:T(8,128)(2,1)}) custom-call(s32[4]{0:T(128)S(1)} %pad_add_fusion.flags, bf16[384,1536]{1,0:T(8,128)(2,1)S(1)} %bitcast.32, bf16[8,1536]{1,0:T(8,128)(2,1)S(1)} %broadcast_in_dim.14.pivot_scale, ...), custom_call_target="tpu_custom_call" | custom-call | flops 3623878656 | bytes 9437184 | tf_op jit(solution)/shard_map/pallas_call | solution.py:325
  223.7 1.0 copy-done.22
  224.7 1.0 copy-done.24
  225.8 1.7 collective-permute-start.18
  227.4 4.6 %collective-permute-start.19 = (bf16[384,1536]{1,0:T(8,128)(2,1)}, bf16[384,1536]{1,0:T(8,128)(2,1)}, u32[]{:S(2)}, u32[]{:S(2)}) collective-permute-start(bf16[384,1536]{1,0:T(8,128)(2,1)} %get-tuple-element.42), channel_id=1, source_target_pairs={{4,0},{12,8},{20,16},{28,24},{5,1},{13,9},{21,17},{29,25},{6,2},{1... | collective-permute-start | bytes 3538952 | tf_op jit(solution)/shard_map/ppermute | solution.py:423
  232.1 1.7 collective-permute-start.20
  233.7 2.3 copy-done.4
  236.1 2.3 copy-done.6
  238.4 1.3 copy-done.13
  239.7 1.3 copy-done.15
  241.0 0.7 copy-done.19
  241.7 1.7 copy-done.21
  243.4 1.3 copy-done.23
  244.6 1.3 copy-done.25
  245.9 10.6 %shard_map.64 = (f32[384,1536]{1,0:T(8,128)S(1)}, bf16[384,1536]{1,0:T(8,128)(2,1)}) custom-call(s32[4]{0:T(128)S(1)} %pad_add_fusion.flags, bf16[400,1536]{1,0:T(8,128)(2,1)} %collective-permute-done.16.pivot_rows, bf16[384,1536]{1,0:T(8,128)(2,1)S(1)} %copy-done.23, bf16[384,1536]{1,0:T(8,128)(2,1)S(1)} %copy-done.25, bf16[8,1536]{1,0:T(8,128)(2,1)S(1)} %copy-done.19, ...), custom_call_target="tpu_custom_call" | custom-call | flops 7247757312 | bytes 18874368 | tf_op jit(solution)/shard_map/pallas_call | solution.py:384
  256.5 4.3 %subtract_bitcast_fusion = f32[1,384,1536]{2,1,0:T(8,128)} fusion(bf16[384,1536]{1,0:T(8,128)(2,1)} %collective-permute-done.20, f32[384,1536]{1,0:T(8,128)S(1)} %get-tuple-element.40, bf16[384,1536]{1,0:T(8,128)(2,1)} %collective-permute-done.19, bf16[384,1536]{1,0:T(8,128)(2,1)S(1)} %collective-permute-done.17.received, ...), kind=kLoop, calls=%fused_computation.8 | loop fusion | flops 4128768 | bytes 9437185 | tf_op jit(solution)/shard_map/broadcast_in_dim | solution.py:529
  (78 shorter events, 0.6 us)
Async XLA Ops:
  0.6 2.1 copy-start
  2.7 4.5 %copy-start.16 = (f32[8,1536]{1,0:T(8,128)}, f32[8,1536]{1,0:T(8,128)S(1)}, u32[]{:S(2)}) copy-start(f32[8,1536]{1,0:T(8,128)S(1)} %broadcast_in_dim.12.reciprocal) | copy-start | bytes 147460
  2.7 1.3 copy-start.1
  4.0 66.3 %copy-start.2 = (bf16[1,384,1536]{2,1,0:T(8,128)(2,1)S(1)}, bf16[1,384,1536]{2,1,0:T(8,128)(2,1)}, u32[]{:S(2)}) copy-start(bf16[1,384,1536]{2,1,0:T(8,128)(2,1)} %param.5) | copy-start | bytes 3538948
  7.1 30.0 %collective-permute-start.4 = (bf16[400,1536]{1,0:T(8,128)(2,1)}, bf16[400,1536]{1,0:T(8,128)(2,1)}, u32[]{:S(2)}, u32[]{:S(2)}) collective-permute-start(bf16[400,1536]{1,0:T(8,128)(2,1)} %shard_map.59.refs_0_), channel_id=1, source_target_pairs={{0,1},{1,2},{2,3},{4,5},{5,6},{6,7},{8,9},{9,10},{10,11},{12,13},{... | collective-permute-start | bytes 3686408 | tf_op jit(solution)/shard_map/ppermute | solution.py:432
  12.2 50.1 %collective-permute-start = (bf16[384,1536]{1,0:T(8,128)(2,1)S(1)}, bf16[384,1536]{1,0:T(8,128)(2,1)S(1)}, u32[]{:S(2)}, u32[]{:S(2)}) collective-permute-start(bf16[384,1536]{1,0:T(8,128)(2,1)S(1)} %bitcast.27), channel_id=1, source_target_pairs={{0,1},{1,2},{2,3},{4,5},{5,6},{6,7},{8,9},{9,10},{10,11},{12,13},{... | collective-permute-start | bytes 3538952 | tf_op jit(solution)/shard_map/ppermute | solution.py:432
  14.5 49.6 %collective-permute-start.2 = (bf16[384,1536]{1,0:T(8,128)(2,1)S(1)}, bf16[384,1536]{1,0:T(8,128)(2,1)}, u32[]{:S(2)}, u32[]{:S(2)}) collective-permute-start(bf16[384,1536]{1,0:T(8,128)(2,1)S(1)} %bitcast.28), channel_id=1, source_target_pairs={{1,0},{2,1},{3,2},{5,4},{6,5},{7,6},{9,8},{10,9},{11,10},{13,12},{... | collective-permute-start | bytes 3538952 | tf_op jit(solution)/shard_map/ppermute | solution.py:432
  15.8 53.3 %collective-permute-start.5 = (bf16[400,1536]{1,0:T(8,128)(2,1)}, bf16[400,1536]{1,0:T(8,128)(2,1)}, u32[]{:S(2)}, u32[]{:S(2)}) collective-permute-start(bf16[400,1536]{1,0:T(8,128)(2,1)} %shard_map.59.refs_0_), channel_id=1, source_target_pairs={{1,0},{2,1},{3,2},{5,4},{6,5},{7,6},{9,8},{10,9},{11,10},{13,12},{... | collective-permute-start | bytes 3686408 | tf_op jit(solution)/shard_map/ppermute | solution.py:432
  37.2 33.4 %collective-permute-start.6 = (bf16[400,1536]{1,0:T(8,128)(2,1)}, bf16[400,1536]{1,0:T(8,128)(2,1)}, u32[]{:S(2)}, u32[]{:S(2)}) collective-permute-start(bf16[400,1536]{1,0:T(8,128)(2,1)} %collective-permute-done.4.refs_1_), channel_id=1, source_target_pairs={{1,2},{2,3},{5,6},{6,7},{9,10},{10,11},{13,14},{14,15},{17,18},{18... | collective-permute-start | bytes 3686408 | tf_op jit(solution)/shard_map/ppermute | solution.py:432
  62.3 8.9 %collective-permute-start.1 = (bf16[384,1536]{1,0:T(8,128)(2,1)S(1)}, bf16[384,1536]{1,0:T(8,128)(2,1)}, u32[]{:S(2)}, u32[]{:S(2)}) collective-permute-start(bf16[384,1536]{1,0:T(8,128)(2,1)S(1)} %collective-permute-done), channel_id=1, source_target_pairs={{1,2},{2,3},{5,6},{6,7},{9,10},{10,11},{13,14},{14,15},{17,18},{18... | collective-permute-start | bytes 3538952 | tf_op jit(solution)/shard_map/ppermute | solution.py:432
  64.0 30.5 %collective-permute-start.3 = (bf16[384,1536]{1,0:T(8,128)(2,1)}, bf16[384,1536]{1,0:T(8,128)(2,1)}, u32[]{:S(2)}, u32[]{:S(2)}) collective-permute-start(bf16[384,1536]{1,0:T(8,128)(2,1)} %collective-permute-done.2), channel_id=1, source_target_pairs={{1,0},{2,1},{5,4},{6,5},{9,8},{10,9},{13,12},{14,13},{17,16},{18,1... | collective-permute-start | bytes 3538952 | tf_op jit(solution)/shard_map/ppermute | solution.py:432
  69.0 51.7 %collective-permute-start.7 = (bf16[400,1536]{1,0:T(8,128)(2,1)}, bf16[400,1536]{1,0:T(8,128)(2,1)S(1)}, u32[]{:S(2)}, u32[]{:S(2)}) collective-permute-start(bf16[400,1536]{1,0:T(8,128)(2,1)} %collective-permute-done.5.refs_2_), channel_id=1, source_target_pairs={{1,0},{2,1},{5,4},{6,5},{9,8},{10,9},{13,12},{14,13},{17,16},{18,1... | collective-permute-start | bytes 3686408 | tf_op jit(solution)/shard_map/ppermute | solution.py:432
  70.5 53.9 %collective-permute-start.8 = (bf16[400,1536]{1,0:T(8,128)(2,1)}, bf16[400,1536]{1,0:T(8,128)(2,1)S(1)}, u32[]{:S(2)}, u32[]{:S(2)}) collective-permute-start(bf16[400,1536]{1,0:T(8,128)(2,1)} %collective-permute-done.6.refs_3_), channel_id=1, source_target_pairs={{2,3},{6,7},{10,11},{14,15},{18,19},{22,23},{26,27},{30,31}} | collective-permute-start | bytes 3686408 | tf_op jit(solution)/shard_map/ppermute | solution.py:432
  120.7 26.9 %collective-permute-start.9 = (bf16[400,1536]{1,0:T(8,128)(2,1)S(1)}, bf16[400,1536]{1,0:T(8,128)(2,1)S(1)}, u32[]{:S(2)}, u32[]{:S(2)}) collective-permute-start(bf16[400,1536]{1,0:T(8,128)(2,1)S(1)} %collective-permute-done.7.refs_4_), channel_id=1, source_target_pairs={{1,0},{5,4},{9,8},{13,12},{17,16},{21,20},{25,24},{29,28}} | collective-permute-start | bytes 3686408 | tf_op jit(solution)/shard_map/ppermute | solution.py:432
  122.4 63.6 %collective-permute-start.12 = (bf16[384,1536]{1,0:T(8,128)(2,1)}, bf16[384,1536]{1,0:T(8,128)(2,1)S(1)}, u32[]{:S(2)}, u32[]{:S(2)}) collective-permute-start(bf16[384,1536]{1,0:T(8,128)(2,1)} %collective-permute-done.1), channel_id=1, source_target_pairs={{2,3},{6,7},{10,11},{14,15},{18,19},{22,23},{26,27},{30,31}} | collective-permute-start | bytes 3538952 | tf_op jit(solution)/shard_map/ppermute | solution.py:432
  123.1 62.9 %collective-permute-start.13 = (bf16[384,1536]{1,0:T(8,128)(2,1)}, bf16[384,1536]{1,0:T(8,128)(2,1)}, u32[]{:S(2)}, u32[]{:S(2)}) collective-permute-start(bf16[384,1536]{1,0:T(8,128)(2,1)} %collective-permute-done.3), channel_id=1, source_target_pairs={{1,0},{5,4},{9,8},{13,12},{17,16},{21,20},{25,24},{29,28}} | collective-permute-start | bytes 3538952 | tf_op jit(solution)/shard_map/ppermute | solution.py:432
  125.3 1.0 copy-start.8
  148.4 1.0 copy-start.10
  149.7 17.8 %copy-start.9 = (bf16[400,1536]{1,0:T(8,128)(2,1)S(1)}, bf16[400,1536]{1,0:T(8,128)(2,1)}, u32[]{:S(2)}) copy-start(bf16[400,1536]{1,0:T(8,128)(2,1)} %copy-done.8) | copy-start | bytes 3686404
  149.7 17.8 %copy-start.11 = (bf16[400,1536]{1,0:T(8,128)(2,1)S(1)}, bf16[400,1536]{1,0:T(8,128)(2,1)}, u32[]{:S(2)}) copy-start(bf16[400,1536]{1,0:T(8,128)(2,1)} %copy-done.10) | copy-start | bytes 3686404
  149.7 14.9 %collective-permute-start.11 = (f32[1536]{0:T(1024)S(1)}, f32[1536]{0:T(1024)S(1)}, u32[]{:S(2)}, u32[]{:S(2)}) collective-permute-start(f32[1536]{0:T(1024)S(1)} %pad_maximum_fusion.2), channel_id=1, source_target_pairs={{0,4},{8,12},{16,20},{24,28},{1,5},{9,13},{17,21},{25,29},{2,6},{1... | collective-permute-start | bytes 18440 | tf_op jit(solution)/shard_map/ppermute | solution.py:423
  151.1 16.3 %copy-start.7 = (f32[1,384,1536]{2,1,0:T(8,128)S(1)}, f32[1,384,1536]{2,1,0:T(8,128)}, u32[]{:S(2)}) copy-start(f32[1,384,1536]{2,1,0:T(8,128)} %param.4) | copy-start | bytes 7077892
  154.3 13.2 %collective-permute-start.10 = (f32[1536]{0:T(1024)S(1)}, f32[1536]{0:T(1024)S(1)}, u32[]{:S(2)}, u32[]{:S(2)}) collective-permute-start(f32[1536]{0:T(1024)S(1)} %pad_maximum_fusion.3), channel_id=1, source_target_pairs={{4,0},{8,4},{12,8},{16,12},{20,16},{24,20},{28,24},{5,1},{9,5},{13... | collective-permute-start | bytes 18440 | tf_op jit(solution)/shard_map/ppermute | solution.py:423
  167.5 18.5 %copy-start.17 = (f32[8,1536]{1,0:T(8,128)S(1)}, f32[8,1536]{1,0:T(8,128)}, u32[]{:S(2)}) copy-start(f32[8,1536]{1,0:T(8,128)} %copy-done.16) | copy-start | bytes 147460
  185.9 5.8 %copy-start.20 = (f32[384,1536]{1,0:T(8,128)}, f32[384,1536]{1,0:T(8,128)S(1)}, u32[]{:S(2)}) copy-start(f32[384,1536]{1,0:T(8,128)S(1)} %get-tuple-element.39.partial) | copy-start | bytes 7077892
  185.9 7.3 %copy-start.14 = (bf16[384,1536]{1,0:T(8,128)(2,1)}, bf16[384,1536]{1,0:T(8,128)(2,1)S(1)}, u32[]{:S(2)}) copy-start(bf16[384,1536]{1,0:T(8,128)(2,1)S(1)} %get-tuple-element.30.mine) | copy-start | bytes 3538948
  191.9 13.9 %copy-start.5 = (bf16[1536,1536]{1,0:T(8,128)(2,1)}, bf16[1536,1536]{1,0:T(8,128)(2,1)S(1)}, u32[]{:S(2)}) copy-start(bf16[1536,1536]{1,0:T(8,128)(2,1)S(1)} %constant_dynamic-update-slice_fusion.1.link.link_whole) | copy-start | bytes 14155780
  191.9 11.6 %collective-permute-start.14 = (bf16[1536,1536]{1,0:T(8,128)(2,1)S(1)}, bf16[1536,1536]{1,0:T(8,128)(2,1)S(1)}, u32[]{:S(2)}, u32[]{:S(2)}) collective-permute-start(bf16[1536,1536]{1,0:T(8,128)(2,1)S(1)} %constant_dynamic-update-slice_fusion.1.link.link_whole), channel_id=1, source_target_pairs={{0,4},{8,12},{16,20},{24,28},{1,5},{9,13},{17,21},{25,29},{2,6},{1... | collective-permute-start | bytes 14155784 | tf_op jit(solution)/shard_map/ppermute | solution.py:423
  193.3 24.4 %copy-start.18 = (bf16[8,1536]{1,0:T(8,128)(2,1)}, bf16[8,1536]{1,0:T(8,128)(2,1)S(1)}, u32[]{:S(2)}) copy-start(bf16[8,1536]{1,0:T(8,128)(2,1)S(1)} %broadcast_in_dim.14.pivot_scale) | copy-start | bytes 73732
  198.5 5.0 %collective-permute-start.15 = (f32[1536]{0:T(1024)S(1)}, f32[1536]{0:T(1024)S(1)}, u32[]{:S(2)}, u32[]{:S(2)}) collective-permute-start(f32[1536]{0:T(1024)S(1)} %slice_reduce_fusion.1), channel_id=1, source_target_pairs={{8,4},{16,12},{24,20},{9,5},{17,13},{25,21},{10,6},{18,14},{26,22}... | collective-permute-start | bytes 18440 | tf_op jit(solution)/shard_map/ppermute | solution.py:423
  199.8 17.8 %collective-permute-start.17 = (bf16[384,1536]{1,0:T(8,128)(2,1)S(1)}, bf16[384,1536]{1,0:T(8,128)(2,1)S(1)}, u32[]{:S(2)}, u32[]{:S(2)}) collective-permute-start(bf16[384,1536]{1,0:T(8,128)(2,1)S(1)} %get-tuple-element.36.update), channel_id=1, source_target_pairs={{8,4},{24,20},{16,0},{9,5},{25,21},{17,1},{10,6},{26,22},{18,2},{1... | collective-permute-start | bytes 3538952 | tf_op jit(solution)/shard_map/ppermute | solution.py:423
  203.5 14.2 %copy-start.3 = (bf16[1536,1536]{1,0:T(8,128)(2,1)}, bf16[1536,1536]{1,0:T(8,128)(2,1)S(1)}, u32[]{:S(2)}) copy-start(bf16[1536,1536]{1,0:T(8,128)(2,1)S(1)} %collective-permute-done.14.pivot_whole) | copy-start | bytes 14155780
  205.7 2.1 copy-start.12
  207.8 9.9 %slice-start = ((s8[4718592]{0:T(1024)(128)(4,1)}), s8[4194304]{0:T(1024)(128)(4,1)S(1)}, s32[]{:S(2)}) async-start(s8[4718592]{0:T(1024)(128)(4,1)} %bitcast.24), calls=%async_computation | async-start | bytes 8388608
  208.9 8.8 %slice-start.1 = ((s8[4718592]{0:T(1024)(128)(4,1)}), s8[524288]{0:T(1024)(128)(4,1)S(1)}, s32[]{:S(2)}) async-start(s8[4718592]{0:T(1024)(128)(4,1)} %bitcast.24), calls=%async_computation.1 | async-start | bytes 1048576
  208.9 24.8 %collective-permute-start.16 = (bf16[400,1536]{1,0:T(8,128)(2,1)}, bf16[400,1536]{1,0:T(8,128)(2,1)}, u32[]{:S(2)}, u32[]{:S(2)}) collective-permute-start(bf16[400,1536]{1,0:T(8,128)(2,1)} %pad_maximum_fusion.1), channel_id=1, source_target_pairs={{4,12},{20,28},{5,13},{21,29},{6,14},{22,30},{7,15},{23,31}} | collective-permute-start | bytes 3686408 | tf_op jit(solution)/shard_map/ppermute | solution.py:423
  223.7 1.0 copy-start.22
  224.7 1.0 copy-start.24
  225.8 30.7 %collective-permute-start.18 = (bf16[384,1536]{1,0:T(8,128)(2,1)}, bf16[384,1536]{1,0:T(8,128)(2,1)}, u32[]{:S(2)}, u32[]{:S(2)}) collective-permute-start(bf16[384,1536]{1,0:T(8,128)(2,1)} %get-tuple-element.41), channel_id=1, source_target_pairs={{0,12},{1,13},{2,14},{3,15}} | collective-permute-start | bytes 3538952 | tf_op jit(solution)/shard_map/ppermute | solution.py:423
  227.4 29.0 %collective-permute-start.19 = (bf16[384,1536]{1,0:T(8,128)(2,1)}, bf16[384,1536]{1,0:T(8,128)(2,1)}, u32[]{:S(2)}, u32[]{:S(2)}) collective-permute-start(bf16[384,1536]{1,0:T(8,128)(2,1)} %get-tuple-element.42), channel_id=1, source_target_pairs={{4,0},{12,8},{20,16},{28,24},{5,1},{13,9},{21,17},{29,25},{6,2},{1... | collective-permute-start | bytes 3538952 | tf_op jit(solution)/shard_map/ppermute | solution.py:423
  232.1 24.4 %collective-permute-start.20 = (bf16[384,1536]{1,0:T(8,128)(2,1)S(1)}, bf16[384,1536]{1,0:T(8,128)(2,1)}, u32[]{:S(2)}, u32[]{:S(2)}) collective-permute-start(bf16[384,1536]{1,0:T(8,128)(2,1)S(1)} %fusion.1.ready), channel_id=1, source_target_pairs={{20,12},{21,13},{22,14},{23,15}} | collective-permute-start | bytes 3538952 | tf_op jit(solution)/shard_map/ppermute | solution.py:423
  233.7 2.3 copy-start.4
  236.1 2.3 copy-start.6
  238.4 1.3 copy-start.13
  239.7 1.3 copy-start.15
  241.0 0.7 copy-start.19
  241.7 1.7 copy-start.21
  243.4 1.3 copy-start.23
  244.6 1.3 copy-start.25

commit v7 on v6

--- a/solution.py
+++ b/solution.py
@@ -13,6 +13,7 @@
 WIDTH = 256
 
 ANY = pl.BlockSpec(memory_space=pl.ANY)
+HBM = pl.BlockSpec(memory_space=pltpu.HBM)
 SHAPE = jax.ShapeDtypeStruct
 FREE = pl.CostEstimate(flops=0, bytes_accessed=0, transcendentals=0)
 
@@ -296,58 +297,65 @@
 
 
 def columns_kernel(
-    flags, own, pivot_scale, prev_early, prev_late, pivot_whole, update, received, ready,
-    right, columns, moved, passed, prev, pivot, sems, pivot_sem, move_sems,
+    flags, own, pivot_scale, prev_early, prev_late, pivot_whole, update, ready,
+    right, columns, moved, prev, pivot, results, sems, more_sems,
 ):
     del ready
-    moves = [
-        pltpu.make_async_copy(update, moved, move_sems.at[0]),
-        pltpu.make_async_copy(received, passed, move_sems.at[1]),
-    ]
-    for move in moves:
-        move.start()
+    move = pltpu.make_async_copy(update, moved, more_sems.at[0])
+    move.start()
     wait_prev = fetched(prev_early, prev_late, prev, sems, [flags[1]])
-    copy = pltpu.make_async_copy(pivot_whole, pivot, pivot_sem)
+    copy = pltpu.make_async_copy(pivot_whole, pivot, more_sems.at[1])
     copy.start()
     wait_prev()
     across = jnp.where(flags[0] == 1, 0.0, -dot_nt(own[...], prev[...])).astype(BF16)
     across = times(across, pivot_scale)
-    right[...] = across
+    results[0] = across
+    store = pltpu.make_async_copy(results.at[0], right, more_sems.at[2])
+    store.start()
     copy.wait()
-    columns[...] = (-dot_nt(across, pivot[...])).astype(BF16)
-    for move in moves:
-        move.wait()
-
-
-def columns_forms(flags, own, pivot_scale, prev_early, prev_late, pivot, update, received, ready):
+    results[1] = (-dot_nt(across, pivot[...])).astype(BF16)
+    last = pltpu.make_async_copy(results.at[1], columns, more_sems.at[3])
+    last.start()
+    for copy in (move, store, last):
+        copy.wait()
+
+
+def columns_forms(flags, own, pivot_scale, prev_early, prev_late, pivot, update, ready):
     rows, order = own.shape
     out = SHAPE((rows, order), BF16)
     return pl.pallas_call(
         columns_kernel,
-        out_shape=[out, out, out, out],
+        out_shape=[out, out, out],
         grid_spec=pltpu.PrefetchScalarGridSpec(
             num_scalar_prefetch=1,
             grid=(1,),
-            in_specs=[whole_spec((rows, order)), whole_spec((8, order))] + [ANY] * 6,
-            out_specs=[whole_spec((rows, order)), whole_spec((rows, order)), ANY, ANY],
+            in_specs=[whole_spec((rows, order)), whole_spec((8, order))] + [ANY] * 5,
+            out_specs=[HBM, HBM, HBM],
             scratch_shapes=[
                 pltpu.VMEM((order, order), BF16),
                 pltpu.VMEM((order, order), BF16),
+                pltpu.VMEM((2, rows, order), BF16),
                 pltpu.SemaphoreType.DMA((order // rows,)),
-                pltpu.SemaphoreType.DMA,
-                pltpu.SemaphoreType.DMA((2,)),
+                pltpu.SemaphoreType.DMA((4,)),
             ],
         ),
         compiler_params=pltpu.CompilerParams(vmem_limit_bytes=22 * 1024 * 1024),
         cost_estimate=products_cost(rows, order, 2),
-    )(flags, own, pivot_scale, prev_early, prev_late, pivot, update, received, ready)
+    )(flags, own, pivot_scale, prev_early, prev_late, pivot, update, ready)
 
 
 def last_kernel(
-    flags, pivot_rows, right, columns, pivot_scale, next_rows, mine, partial, link_whole, pivot_whole,
-    form, new, link, pivot, last, sems,
+    flags, pivot_scale, pivot_rows, right_whole, columns_whole, next_rows, mine, partial, link_whole, pivot_whole,
+    form, new, link, pivot, last, long, right, columns, sems,
 ):
     rows = right.shape[0]
+    small = [
+        pltpu.make_async_copy(pivot_rows, long, sems.at[4]),
+        pltpu.make_async_copy(columns_whole, columns, sems.at[5]),
+        pltpu.make_async_copy(right_whole, right, sems.at[6]),
+    ]
+    for copy in small:
+        copy.start()
     even, final = flags[2] == 1, flags[3] == 1
     other = jnp.logical_not(jnp.logical_or(even, final))
     fetch = [
@@ -361,13 +369,15 @@
     plain.append((other, pltpu.make_async_copy(next_rows, new, sems.at[3])))
     for chosen, copy in plain:
         pl.when(chosen)(copy.start)
-    scale = pivot_rows[rows : rows + EXTRA, :]
     wide = pivot_scale[0:1].astype(F32)
+    for copy in small:
+        copy.wait()
+    scale = long[rows : rows + EXTRA, :]
     fetch[0].wait()
     inner = dot_nn(times(columns[...], scale), pivot[...]) * wide
     keep = jnp.where(final, 1.0, 0.0)
     factor = (right[...].astype(F32) - inner * keep).astype(BF16)
-    inner = (dot_nn(times(pivot_rows[0:rows, :], scale), pivot[...]) * wide).astype(BF16)
+    inner = (dot_nn(times(long[0:rows, :], scale), pivot[...]) * wide).astype(BF16)
     fetch[1].wait()
     last[...] = dot_nn(inner, link[...]).astype(BF16)
     store = pltpu.make_async_copy(last, new, sems.at[3])
@@ -387,24 +397,21 @@
         grid_spec=pltpu.PrefetchScalarGridSpec(
             num_scalar_prefetch=1,
             grid=(1,),
-            in_specs=[
-                whole_spec(pivot_rows.shape),
-                whole_spec((rows, order)),
-                whole_spec((rows, order)),
-                whole_spec((8, order)),
-            ]
-            + [ANY] * 5,
+            in_specs=[whole_spec((8, order))] + [HBM] * 8,
             out_specs=[whole_spec((rows, order)), ANY],
             scratch_shapes=[
                 pltpu.VMEM((order, order), BF16),
                 pltpu.VMEM((order, order), BF16),
                 pltpu.VMEM((rows, order), BF16),
-                pltpu.SemaphoreType.DMA((4,)),
+                pltpu.VMEM(pivot_rows.shape, BF16),
+                pltpu.VMEM((rows, order), BF16),
+                pltpu.VMEM((rows, order), BF16),
+                pltpu.SemaphoreType.DMA((7,)),
             ],
         ),
         compiler_params=pltpu.CompilerParams(vmem_limit_bytes=28 * 1024 * 1024),
         cost_estimate=products_cost(rows, order, 4),
-    )(flags, pivot_rows, right, columns, pivot_scale, next_rows, mine, partial, link, pivot)
+    )(flags, pivot_scale, pivot_rows, right, columns, next_rows, mine, partial, link, pivot)
 
 
 def on_device(sep_block, own_couple, prev_couple, inner_diag):
@@ -501,9 +508,7 @@
     left_diag, right_diag = left_diag[0], right_diag[0]
 
     left_diag = between(left_diag, [(p, p - 1) for p in even])
-    from_even = between(
-        update, [(p, p - 1) for p in range(2, parts, 4)] + [(p, p - 4) for p in range(4, parts, 4)]
-    )
+    from_even = between(update, [(p, p - 1) for p in even])
     next_diag = diag - left_diag - right_diag
     next_scale = (1.0 / jnp.maximum(next_diag, 1.0)).astype(BF16)
     pivot_rows = lax.dynamic_slice_in_dim(pivot_link, row_start, rows, 0)
@@ -516,15 +521,13 @@
     left_next = lax.optimization_barrier(left_next)
     left_next = (-dot_nt(left_next, pivot_link)).astype(BF16)
     from_pivot = between(left_next, [(p, p - 2) for p in pivots])
-    right, columns, own_update, passed = columns_forms(
-        flags, own_rows, pivot_scale8, prev_first, prev_late, pivot_link, update, from_even, left_next
-    )
-    from_far = between(passed, [(p - 4, p - 1) for p in range(4, parts, 4)])
+    right, columns, own_update = columns_forms(
+        flags, own_rows, pivot_scale8, prev_first, prev_late, pivot_link, update, left_next
+    )
     from_odd = between(own_update, [(p, p - 1) for p in range(1, parts, 2)])
     form, out_link = last_forms(
         flags, pivot_long, right, columns, next_rows, mine, partial, pivot_scale8, link, pivot_link
     )
-    from_even = jnp.where(is_receiver, from_even + from_far, jnp.zeros_like(from_even))
     schur = form - (from_even + from_odd).astype(F32) - from_pivot.astype(F32)
     return (schur[None], out_link[None])
 

time: 262 us -> 242 us (0.924)
  the two profiles are of different devices: /device:TPU:1 before, /device:TPU:3 now
where the time goes in v7:
time: 242 us; the launch traced here: 241 us
  waiting for transfers between devices  130 us (54%)
  Pallas kernels  47.4 us (20%)
  starting transfers between devices  39 us (16%)
  other arithmetic  11.4 us (5%)
  matrix products  6.06 us (3%)
  local copies, waits for them, and re-layouts  5.6 us (2%)
    ppermute x12, waiting for transfers between devices, one_step(): return (lax.ppermute(ahead, 'space', up), lax.ppermute(back, 'space', down))  113 us
    ppermute x12, starting transfers between devices, one_step(): return (lax.ppermute(ahead, 'space', up), lax.ppermute(back, 'space', down))  22 us
    pallas_call x1, Pallas kernels, early_forms(): pl.pallas_call(functools.partial(early_kernel, size), out_shape=[SHAPE((o...  18.1 us
    ppermute x8, waiting for transfers between devices, between(): lax.ppermute(block, 'tm', [(a, b) for a, b in route if 0 <= b < parts])  17.4 us
    ppermute x8, starting transfers between devices, between(): lax.ppermute(block, 'tm', [(a, b) for a, b in route if 0 <= b < parts])  17 us
    pallas_call x1, Pallas kernels, last_forms(): pl.pallas_call(last_kernel, out_shape=[SHAPE((rows, order), F32), SHAPE((...  10 us
    pallas_call x1, Pallas kernels, columns_forms(): pl.pallas_call(columns_kernel, out_shape=[out, out, out], grid_spec=pltpu...  6.78 us
    pallas_call x1, Pallas kernels, level_forms(): pl.pallas_call(level_kernel, out_shape=[SHAPE((rows, order), BF16), SHAPE...  5.19 us
  transfers between devices with their start and end apart: 20, of which 11 were waited for; matrix products, arithmetic and copies ran while one was open for 6% of the time, Pallas kernels for 17%

profile of v7, /device:TPU:3, one launch (start us, length us, event | category | flops | bytes accessed | tf_op | source)
XLA Modules:
  0.0 241.0 jit_solution(4110446428164272990)
XLA Ops:
  0.7 0.8 divide_reduce_fusion
  1.5 1.1 dynamic-slice_bitcast_fusion.separator
  2.6 0.1 pad_add_fusion.flags
  2.7 0.0 copy-start.1
  2.7 1.3 copy-done.1
  4.0 3.1 %shard_map.59.refs_0_ = bf16[400,1536]{1,0:T(8,128)(2,1)} custom-call(s32[4]{0:T(128)S(1)} %pad_add_fusion.flags, bf16[384,1536]{1,0:T(8,128)(2,1)S(1)} %bitcast.31, bf16[384,1536]{1,0:T(8,128)(2,1)S(1)} %bitcast.26, f32[384,384]{1,0:T(8,128)S(1)} %dynamic-slice_bitcast_fusion.separator, f32[8,1536]{1,0:T(8,128)S(1)} %broadcast_in_dim.17.reciprocal), custom_call_target="tpu_custom_call" | custom-call | tf_op jit(solution)/shard_map/pallas_call | solution.py:108
  7.1 4.3 %collective-permute-start = (bf16[400,1536]{1,0:T(8,128)(2,1)}, bf16[400,1536]{1,0:T(8,128)(2,1)}, u32[]{:S(2)}, u32[]{:S(2)}) collective-permute-start(bf16[400,1536]{1,0:T(8,128)(2,1)} %shard_map.59.refs_0_), channel_id=1, source_target_pairs={{0,1},{1,2},{2,3},{4,5},{5,6},{6,7},{8,9},{9,10},{10,11},{12,13},{... | collective-permute-start | bytes 3686408 | tf_op jit(solution)/shard_map/ppermute | solution.py:439
  11.4 1.3 collective-permute-start.9
  12.7 5.1 %collective-permute-start.7 = (bf16[384,1536]{1,0:T(8,128)(2,1)S(1)}, bf16[384,1536]{1,0:T(8,128)(2,1)}, u32[]{:S(2)}, u32[]{:S(2)}) collective-permute-start(bf16[384,1536]{1,0:T(8,128)(2,1)S(1)} %bitcast.28), channel_id=1, source_target_pairs={{0,1},{1,2},{2,3},{4,5},{5,6},{6,7},{8,9},{9,10},{10,11},{12,13},{... | collective-permute-start | bytes 3538952 | tf_op jit(solution)/shard_map/ppermute | solution.py:439
  17.8 1.3 collective-permute-start.3
  19.1 17.2 %collective-permute-done.refs_1_ = bf16[400,1536]{1,0:T(8,128)(2,1)} collective-permute-done((bf16[400,1536]{1,0:T(8,128)(2,1)}, bf16[400,1536]{1,0:T(8,128)(2,1)}, u32[]{:S(2)}, u32[]{:S(2)}) %collective-permute-start) | collective-permute-done | bytes 1228832 | tf_op jit(solution)/shard_map/ppermute | solution.py:439
  36.3 1.8 collective-permute-start.1
  38.1 1.7 collective-permute-done.9
  39.8 1.3 collective-permute-start.10
  41.1 20.4 %collective-permute-done.7 = bf16[384,1536]{1,0:T(8,128)(2,1)} collective-permute-done((bf16[384,1536]{1,0:T(8,128)(2,1)S(1)}, bf16[384,1536]{1,0:T(8,128)(2,1)}, u32[]{:S(2)}, u32[]{:S(2)}) %collective-permute-start.7) | collective-permute-done | bytes 1179680 | tf_op jit(solution)/shard_map/ppermute | solution.py:439
  61.5 1.7 collective-permute-start.8
  63.2 3.1 %collective-permute-done.3.refs_2_ = bf16[400,1536]{1,0:T(8,128)(2,1)} collective-permute-done((bf16[400,1536]{1,0:T(8,128)(2,1)}, bf16[400,1536]{1,0:T(8,128)(2,1)}, u32[]{:S(2)}, u32[]{:S(2)}) %collective-permute-start.3) | collective-permute-done | bytes 1228832 | tf_op jit(solution)/shard_map/ppermute | solution.py:439
  66.2 1.3 collective-permute-start.4
  67.5 0.2 multiply_convert_fusion.3.own_rows
  67.7 0.0 collective-permute-done.1.refs_3_
  67.7 0.7 collective-permute-start.2
  68.5 23.0 %collective-permute-done.10 = bf16[384,1536]{1,0:T(8,128)(2,1)} collective-permute-done((bf16[384,1536]{1,0:T(8,128)(2,1)S(1)}, bf16[384,1536]{1,0:T(8,128)(2,1)}, u32[]{:S(2)}, u32[]{:S(2)}) %collective-permute-start.10) | collective-permute-done | bytes 1179680 | tf_op jit(solution)/shard_map/ppermute | solution.py:439
  91.5 0.0 collective-permute-done.8
  91.5 2.2 broadcast_select_fusion
  93.8 24.0 %collective-permute-done.4.refs_4_ = bf16[400,1536]{1,0:T(8,128)(2,1)S(1)} collective-permute-done((bf16[400,1536]{1,0:T(8,128)(2,1)}, bf16[400,1536]{1,0:T(8,128)(2,1)S(1)}, u32[]{:S(2)}, u32[]{:S(2)}) %collective-permute-start.4) | collective-permute-done | bytes 1228832 | tf_op jit(solution)/shard_map/ppermute | solution.py:439
  117.7 1.3 collective-permute-start.5
  119.0 0.4 pad_maximum_fusion
  119.4 0.7 collective-permute-start.12
  120.1 1.3 collective-permute-start.13
  121.4 0.0 collective-permute-done.2.refs_5_
  121.5 1.1 slice_select_fusion.1
  122.6 23.6 %collective-permute-done.5.refs_6_ = bf16[400,1536]{1,0:T(8,128)(2,1)S(1)} collective-permute-done((bf16[400,1536]{1,0:T(8,128)(2,1)S(1)}, bf16[400,1536]{1,0:T(8,128)(2,1)S(1)}, u32[]{:S(2)}, u32[]{:S(2)}) %collective-permute-start.5) | collective-permute-done | bytes 1228832 | tf_op jit(solution)/shard_map/ppermute | solution.py:439
  146.3 0.8 slice_select_fusion
  147.3 1.3 collective-permute-start.6
  148.6 0.0 copy-start.3
  148.7 3.3 %multiply_convert_fusion.prev_whole.prev_early = bf16[1536,1536]{1,0:T(8,128)(2,1)} fusion(bf16[1536,1536]{1,0:T(8,128)(2,1)S(1)} %pad_maximum_fusion, f32[1536]{0:T(1024)S(1)} %divide_reduce_fusion), kind=kLoop, calls=%fused_computation | loop fusion | flops 7077888 | bytes 9443328 | tf_op jit(solution)/shard_map/convert_element_type | solution.py:35
  151.9 7.1 %collective-permute-start.11 = (f32[1536]{0:T(1024)S(1)}, f32[1536]{0:T(1024)S(1)}, u32[]{:S(2)}, u32[]{:S(2)}) collective-permute-start(f32[1536]{0:T(1024)S(1)} %pad_maximum_fusion.3), channel_id=1, source_target_pairs={{4,0},{8,4},{12,8},{16,12},{20,16},{24,20},{28,24},{5,1},{9,5},{13... | collective-permute-start | bytes 18440 | tf_op jit(solution)/shard_map/ppermute | solution.py:430
  159.0 2.4 collective-permute-done.11
  161.5 1.3 copy-done.7
  162.7 18.1 %shard_map.60 = (bf16[1536,1536]{1,0:T(8,128)(2,1)S(1)}, f32[384,1536]{1,0:T(8,128)S(1)}, f32[384,1536]{1,0:T(8,128)S(1)}, bf16[1536,1536]{1,0:T(8,128)(2,1)S(1)}, bf16[384,1536]{1,0:T(8,128)(2,1)S(1)}) custom-call(s32[4]{0:T(128)S(1)} %pad_add_fusion.flags, bf16[1536,1536]{1,0:T(8,128)(2,1)} %multiply_convert_fusion.prev_whole.prev_early, ...), custom_call_target="tpu_custom_call" | custom-call | tf_op jit(solution)/shard_map/pallas_call | solution.py:155
  180.9 1.4 copy-done.10
  182.4 4.1 %shard_map.61 = (bf16[384,1536]{1,0:T(8,128)(2,1)S(1)}, f32[384,384]{1,0:T(8,128)S(1)}, bf16[384,1536]{1,0:T(8,128)(2,1)S(1)}) custom-call(s32[4]{0:T(128)S(1)} %pad_add_fusion.flags, f32[8,1536]{1,0:T(8,128)S(1)} %copy-done.9, bf16[384,1536]{1,0:T(8,128)(2,1)S(1)} %bitcast.30, bf16[1536,1536]{1,0:T(8,128)(2,1)S(1)} %get-tuple-element.26.own, ...), custom_call_target="tpu_custom_call" | custom-call | tf_op jit(solution)/shard_map/pallas_call | solution.py:210
  186.5 0.0 copy-start.5
  186.5 0.1 constant_dynamic-update-slice_fusion.1.link.link_whole
  186.6 1.4 collective-permute-start.14
  188.0 0.1 copy-done.5
  188.1 0.1 constant_dynamic-update-slice_fusion.form
  188.2 5.2 %shard_map.62 = (bf16[384,1536]{1,0:T(8,128)(2,1)S(1)}, f32[8,1536]{1,0:T(8,128)S(1)}, f32[8,1536]{1,0:T(8,128)S(1)}) custom-call(s32[4]{0:T(128)S(1)} %pad_add_fusion.flags, bf16[1536,1536]{1,0:T(8,128)(2,1)S(1)} %constant_dynamic-update-slice_fusion.1.link.link_whole, bf16[384,1536]{1,0:T(8,128)(2,1)S(1)} %get-tuple-element.29.mine, ...), custom_call_target="tpu_custom_call" | custom-call | tf_op jit(solution)/shard_map/pallas_call | solution.py:250
  193.5 1.3 collective-permute-start.15
  194.8 1.5 collective-permute-start.17
  196.3 3.1 %collective-permute-done.15 = f32[1536]{0:T(1024)S(1)} collective-permute-done((f32[1536]{0:T(1024)S(1)}, f32[1536]{0:T(1024)S(1)}, u32[]{:S(2)}, u32[]{:S(2)}) %collective-permute-start.15) | collective-permute-done | bytes 6176 | tf_op jit(solution)/shard_map/ppermute | solution.py:430
  199.3 0.2 multiply_convert_fusion.2
  199.6 2.0 fusion.next_rows
  201.6 2.0 fusion.2
  203.6 0.1 pad_maximum_fusion.1
  203.7 1.6 collective-permute-start.16
  205.3 2.0 fusion.1.ready
  207.4 6.8 %shard_map.63 = (bf16[384,1536]{1,0:T(8,128)(2,1)S(1)}, bf16[384,1536]{1,0:T(8,128)(2,1)S(1)}, bf16[384,1536]{1,0:T(8,128)(2,1)S(1)}) custom-call(s32[4]{0:T(128)S(1)} %pad_add_fusion.flags, bf16[384,1536]{1,0:T(8,128)(2,1)S(1)} %bitcast.32, bf16[8,1536]{1,0:T(8,128)(2,1)S(1)} %broadcast_in_dim.18.pivot_scale, bf16[1536,1536]{1,0:T(8,128)(2,1)S(1)} %bitcast.25, ...), custom_call_target="tpu_custom_call" | custom-call | flops 3623878656 | bytes 9437184 | tf_op jit(solution)/shard_map/pallas_call | solution.py:326
  214.1 1.4 collective-permute-start.18
  215.5 1.5 collective-permute-start.19
  217.0 4.4 %collective-permute-done.16.pivot_rows = bf16[400,1536]{1,0:T(8,128)(2,1)S(1)} collective-permute-done((bf16[400,1536]{1,0:T(8,128)(2,1)S(1)}, bf16[400,1536]{1,0:T(8,128)(2,1)S(1)}, u32[]{:S(2)}, u32[]{:S(2)}) %collective-permute-start.16) | collective-permute-done | bytes 1228832 | tf_op jit(solution)/shard_map/ppermute | solution.py:430
  221.5 10.0 %shard_map.64 = (f32[384,1536]{1,0:T(8,128)S(1)}, bf16[384,1536]{1,0:T(8,128)(2,1)}) custom-call(s32[4]{0:T(128)S(1)} %pad_add_fusion.flags, bf16[8,1536]{1,0:T(8,128)(2,1)S(1)} %broadcast_in_dim.18.pivot_scale, bf16[400,1536]{1,0:T(8,128)(2,1)S(1)} %collective-permute-done.16.pivot_rows, bf16[384,1536]{1,0:T(8,128)(2,1)S(1)} %get-tuple-element.36.right_whole, ...), custom_call_target="tpu_custom_call" | custom-call | flops 7247757312 | bytes 18874368 | tf_op jit(solution)/shard_map/pallas_call | solution.py:394
  231.5 7.5 %collective-permute-done.19 = bf16[384,1536]{1,0:T(8,128)(2,1)S(1)} collective-permute-done((bf16[384,1536]{1,0:T(8,128)(2,1)S(1)}, bf16[384,1536]{1,0:T(8,128)(2,1)S(1)}, u32[]{:S(2)}, u32[]{:S(2)}) %collective-permute-start.19) | collective-permute-done | bytes 1179680 | tf_op jit(solution)/shard_map/ppermute | solution.py:430
  239.0 2.0 subtract_bitcast_fusion
  (48 shorter events, 0.4 us)
Async XLA Ops:
  0.6 2.1 copy-start
  2.7 4.4 %copy-start.8 = (f32[8,1536]{1,0:T(8,128)}, f32[8,1536]{1,0:T(8,128)S(1)}, u32[]{:S(2)}) copy-start(f32[8,1536]{1,0:T(8,128)S(1)} %broadcast_in_dim.17.reciprocal) | copy-start | bytes 147460
  2.7 1.3 copy-start.1
  4.0 63.5 %copy-start.2 = (bf16[1,384,1536]{2,1,0:T(8,128)(2,1)S(1)}, bf16[1,384,1536]{2,1,0:T(8,128)(2,1)}, u32[]{:S(2)}) copy-start(bf16[1,384,1536]{2,1,0:T(8,128)(2,1)} %param.5) | copy-start | bytes 3538948
  7.1 29.2 %collective-permute-start = (bf16[400,1536]{1,0:T(8,128)(2,1)}, bf16[400,1536]{1,0:T(8,128)(2,1)}, u32[]{:S(2)}, u32[]{:S(2)}) collective-permute-start(bf16[400,1536]{1,0:T(8,128)(2,1)} %shard_map.59.refs_0_), channel_id=1, source_target_pairs={{0,1},{1,2},{2,3},{4,5},{5,6},{6,7},{8,9},{9,10},{10,11},{12,13},{... | collective-permute-start | bytes 3686408 | tf_op jit(solution)/shard_map/ppermute | solution.py:439
  11.4 28.4 %collective-permute-start.9 = (bf16[384,1536]{1,0:T(8,128)(2,1)S(1)}, bf16[384,1536]{1,0:T(8,128)(2,1)S(1)}, u32[]{:S(2)}, u32[]{:S(2)}) collective-permute-start(bf16[384,1536]{1,0:T(8,128)(2,1)S(1)} %bitcast.27), channel_id=1, source_target_pairs={{1,0},{2,1},{3,2},{5,4},{6,5},{7,6},{9,8},{10,9},{11,10},{13,12},{... | collective-permute-start | bytes 3538952 | tf_op jit(solution)/shard_map/ppermute | solution.py:439
  12.7 48.8 %collective-permute-start.7 = (bf16[384,1536]{1,0:T(8,128)(2,1)S(1)}, bf16[384,1536]{1,0:T(8,128)(2,1)}, u32[]{:S(2)}, u32[]{:S(2)}) collective-permute-start(bf16[384,1536]{1,0:T(8,128)(2,1)S(1)} %bitcast.28), channel_id=1, source_target_pairs={{0,1},{1,2},{2,3},{4,5},{5,6},{6,7},{8,9},{9,10},{10,11},{12,13},{... | collective-permute-start | bytes 3538952 | tf_op jit(solution)/shard_map/ppermute | solution.py:439
  17.8 48.4 %collective-permute-start.3 = (bf16[400,1536]{1,0:T(8,128)(2,1)}, bf16[400,1536]{1,0:T(8,128)(2,1)}, u32[]{:S(2)}, u32[]{:S(2)}) collective-permute-start(bf16[400,1536]{1,0:T(8,128)(2,1)} %shard_map.59.refs_0_), channel_id=1, source_target_pairs={{1,0},{2,1},{3,2},{5,4},{6,5},{7,6},{9,8},{10,9},{11,10},{13,12},{... | collective-permute-start | bytes 3686408 | tf_op jit(solution)/shard_map/ppermute | solution.py:439
  36.3 31.4 %collective-permute-start.1 = (bf16[400,1536]{1,0:T(8,128)(2,1)}, bf16[400,1536]{1,0:T(8,128)(2,1)}, u32[]{:S(2)}, u32[]{:S(2)}) collective-permute-start(bf16[400,1536]{1,0:T(8,128)(2,1)} %collective-permute-done.refs_1_), channel_id=1, source_target_pairs={{1,2},{2,3},{5,6},{6,7},{9,10},{10,11},{13,14},{14,15},{17,18},{18... | collective-permute-start | bytes 3686408 | tf_op jit(solution)/shard_map/ppermute | solution.py:439
  39.8 51.7 %collective-permute-start.10 = (bf16[384,1536]{1,0:T(8,128)(2,1)S(1)}, bf16[384,1536]{1,0:T(8,128)(2,1)}, u32[]{:S(2)}, u32[]{:S(2)}) collective-permute-start(bf16[384,1536]{1,0:T(8,128)(2,1)S(1)} %collective-permute-done.9), channel_id=1, source_target_pairs={{1,0},{2,1},{5,4},{6,5},{9,8},{10,9},{13,12},{14,13},{17,16},{18,1... | collective-permute-start | bytes 3538952 | tf_op jit(solution)/shard_map/ppermute | solution.py:439
  61.5 30.0 %collective-permute-start.8 = (bf16[384,1536]{1,0:T(8,128)(2,1)}, bf16[384,1536]{1,0:T(8,128)(2,1)}, u32[]{:S(2)}, u32[]{:S(2)}) collective-permute-start(bf16[384,1536]{1,0:T(8,128)(2,1)} %collective-permute-done.7), channel_id=1, source_target_pairs={{1,2},{2,3},{5,6},{6,7},{9,10},{10,11},{13,14},{14,15},{17,18},{18... | collective-permute-start | bytes 3538952 | tf_op jit(solution)/shard_map/ppermute | solution.py:439
  66.2 51.5 %collective-permute-start.4 = (bf16[400,1536]{1,0:T(8,128)(2,1)}, bf16[400,1536]{1,0:T(8,128)(2,1)S(1)}, u32[]{:S(2)}, u32[]{:S(2)}) collective-permute-start(bf16[400,1536]{1,0:T(8,128)(2,1)} %collective-permute-done.3.refs_2_), channel_id=1, source_target_pairs={{1,0},{2,1},{5,4},{6,5},{9,8},{10,9},{13,12},{14,13},{17,16},{18,1... | collective-permute-start | bytes 3686408 | tf_op jit(solution)/shard_map/ppermute | solution.py:439
  67.7 53.7 %collective-permute-start.2 = (bf16[400,1536]{1,0:T(8,128)(2,1)}, bf16[400,1536]{1,0:T(8,128)(2,1)S(1)}, u32[]{:S(2)}, u32[]{:S(2)}) collective-permute-start(bf16[400,1536]{1,0:T(8,128)(2,1)} %collective-permute-done.1.refs_3_), channel_id=1, source_target_pairs={{2,3},{6,7},{10,11},{14,15},{18,19},{22,23},{26,27},{30,31}} | collective-permute-start | bytes 3686408 | tf_op jit(solution)/shard_map/ppermute | solution.py:439
  117.7 28.5 %collective-permute-start.5 = (bf16[400,1536]{1,0:T(8,128)(2,1)S(1)}, bf16[400,1536]{1,0:T(8,128)(2,1)S(1)}, u32[]{:S(2)}, u32[]{:S(2)}) collective-permute-start(bf16[400,1536]{1,0:T(8,128)(2,1)S(1)} %collective-permute-done.4.refs_4_), channel_id=1, source_target_pairs={{1,0},{5,4},{9,8},{13,12},{17,16},{21,20},{25,24},{29,28}} | collective-permute-start | bytes 3686408 | tf_op jit(solution)/shard_map/ppermute | solution.py:439
  119.4 63.0 %collective-permute-start.12 = (bf16[384,1536]{1,0:T(8,128)(2,1)}, bf16[384,1536]{1,0:T(8,128)(2,1)S(1)}, u32[]{:S(2)}, u32[]{:S(2)}) collective-permute-start(bf16[384,1536]{1,0:T(8,128)(2,1)} %collective-permute-done.8), channel_id=1, source_target_pairs={{2,3},{6,7},{10,11},{14,15},{18,19},{22,23},{26,27},{30,31}} | collective-permute-start | bytes 3538952 | tf_op jit(solution)/shard_map/ppermute | solution.py:439
  120.1 62.2 %collective-permute-start.13 = (bf16[384,1536]{1,0:T(8,128)(2,1)}, bf16[384,1536]{1,0:T(8,128)(2,1)S(1)}, u32[]{:S(2)}, u32[]{:S(2)}) collective-permute-start(bf16[384,1536]{1,0:T(8,128)(2,1)} %collective-permute-done.10), channel_id=1, source_target_pairs={{1,0},{5,4},{9,8},{13,12},{17,16},{21,20},{25,24},{29,28}} | collective-permute-start | bytes 3538952 | tf_op jit(solution)/shard_map/ppermute | solution.py:439
  121.4 30.5 %copy-start.6 = (bf16[400,1536]{1,0:T(8,128)(2,1)}, bf16[400,1536]{1,0:T(8,128)(2,1)S(1)}, u32[]{:S(2)}) copy-start(bf16[400,1536]{1,0:T(8,128)(2,1)S(1)} %collective-permute-done.2.refs_5_) | copy-start | bytes 3686404
  147.3 11.7 %collective-permute-start.6 = (f32[1536]{0:T(1024)S(1)}, f32[1536]{0:T(1024)S(1)}, u32[]{:S(2)}, u32[]{:S(2)}) collective-permute-start(f32[1536]{0:T(1024)S(1)} %pad_maximum_fusion.2), channel_id=1, source_target_pairs={{0,4},{8,12},{16,20},{24,28},{1,5},{9,13},{17,21},{25,29},{2,6},{1... | collective-permute-start | bytes 18440 | tf_op jit(solution)/shard_map/ppermute | solution.py:430
  148.6 12.8 %copy-start.3 = (f32[1,384,1536]{2,1,0:T(8,128)S(1)}, f32[1,384,1536]{2,1,0:T(8,128)}, u32[]{:S(2)}) copy-start(f32[1,384,1536]{2,1,0:T(8,128)} %param.4) | copy-start | bytes 7077892
  151.9 9.5 %collective-permute-start.11 = (f32[1536]{0:T(1024)S(1)}, f32[1536]{0:T(1024)S(1)}, u32[]{:S(2)}, u32[]{:S(2)}) collective-permute-start(f32[1536]{0:T(1024)S(1)} %pad_maximum_fusion.3), channel_id=1, source_target_pairs={{4,0},{8,4},{12,8},{16,12},{20,16},{24,20},{28,24},{5,1},{9,5},{13... | collective-permute-start | bytes 18440 | tf_op jit(solution)/shard_map/ppermute | solution.py:430
  161.4 1.3 copy-start.7
  162.7 19.6 %copy-start.9 = (f32[8,1536]{1,0:T(8,128)S(1)}, f32[8,1536]{1,0:T(8,128)}, u32[]{:S(2)}) copy-start(f32[8,1536]{1,0:T(8,128)} %copy-done.8) | copy-start | bytes 147460
  180.9 1.4 copy-start.10
  182.3 4.1 %copy-start.4 = (f32[384,1536]{1,0:T(8,128)}, f32[384,1536]{1,0:T(8,128)S(1)}, u32[]{:S(2)}) copy-start(f32[384,1536]{1,0:T(8,128)S(1)} %get-tuple-element.30) | copy-start | bytes 7077892
  186.5 1.7 copy-start.5
  186.6 12.7 %collective-permute-start.14 = (bf16[1536,1536]{1,0:T(8,128)(2,1)S(1)}, bf16[1536,1536]{1,0:T(8,128)(2,1)S(1)}, u32[]{:S(2)}, u32[]{:S(2)}) collective-permute-start(bf16[1536,1536]{1,0:T(8,128)(2,1)S(1)} %constant_dynamic-update-slice_fusion.1.link.link_whole), channel_id=1, source_target_pairs={{0,4},{8,12},{16,20},{24,28},{1,5},{9,13},{17,21},{25,29},{2,6},{1... | collective-permute-start | bytes 14155784 | tf_op jit(solution)/shard_map/ppermute | solution.py:430
  193.5 5.9 %collective-permute-start.15 = (f32[1536]{0:T(1024)S(1)}, f32[1536]{0:T(1024)S(1)}, u32[]{:S(2)}, u32[]{:S(2)}) collective-permute-start(f32[1536]{0:T(1024)S(1)} %slice_reduce_fusion.1), channel_id=1, source_target_pairs={{8,4},{16,12},{24,20},{9,5},{17,13},{25,21},{10,6},{18,14},{26,22}... | collective-permute-start | bytes 18440 | tf_op jit(solution)/shard_map/ppermute | solution.py:430
  194.8 36.7 %collective-permute-start.17 = (bf16[384,1536]{1,0:T(8,128)(2,1)S(1)}, bf16[384,1536]{1,0:T(8,128)(2,1)S(1)}, u32[]{:S(2)}, u32[]{:S(2)}) collective-permute-start(bf16[384,1536]{1,0:T(8,128)(2,1)S(1)} %get-tuple-element.35.update), channel_id=1, source_target_pairs={{8,4},{16,12},{24,20},{9,5},{17,13},{25,21},{10,6},{18,14},{26,22}... | collective-permute-start | bytes 3538952 | tf_op jit(solution)/shard_map/ppermute | solution.py:430
  203.6 3.7 %slice-start = ((s8[4718592]{0:T(1024)(128)(4,1)}), s8[4194304]{0:T(1024)(128)(4,1)S(1)}, s32[]{:S(2)}) async-start(s8[4718592]{0:T(1024)(128)(4,1)} %bitcast.24), calls=%async_computation | async-start | bytes 8388608
  203.7 3.6 %slice-start.1 = ((s8[4718592]{0:T(1024)(128)(4,1)}), s8[524288]{0:T(1024)(128)(4,1)S(1)}, s32[]{:S(2)}) async-start(s8[4718592]{0:T(1024)(128)(4,1)} %bitcast.24), calls=%async_computation.1 | async-start | bytes 1048576
  203.7 17.7 %collective-permute-start.16 = (bf16[400,1536]{1,0:T(8,128)(2,1)S(1)}, bf16[400,1536]{1,0:T(8,128)(2,1)S(1)}, u32[]{:S(2)}, u32[]{:S(2)}) collective-permute-start(bf16[400,1536]{1,0:T(8,128)(2,1)S(1)} %pad_maximum_fusion.1), channel_id=1, source_target_pairs={{4,12},{20,28},{5,13},{21,29},{6,14},{22,30},{7,15},{23,31}} | collective-permute-start | bytes 3686408 | tf_op jit(solution)/shard_map/ppermute | solution.py:430
  207.4 14.1 %copy-start.11 = (f32[384,1536]{1,0:T(8,128)S(1)}, f32[384,1536]{1,0:T(8,128)}, u32[]{:S(2)}) copy-start(f32[384,1536]{1,0:T(8,128)} %copy-done.10) | copy-start | bytes 7077892
  214.1 17.4 %collective-permute-start.18 = (bf16[384,1536]{1,0:T(8,128)(2,1)S(1)}, bf16[384,1536]{1,0:T(8,128)(2,1)S(1)}, u32[]{:S(2)}, u32[]{:S(2)}) collective-permute-start(bf16[384,1536]{1,0:T(8,128)(2,1)S(1)} %get-tuple-element.40), channel_id=1, source_target_pairs={{4,0},{12,8},{20,16},{28,24},{5,1},{13,9},{21,17},{29,25},{6,2},{1... | collective-permute-start | bytes 3538952 | tf_op jit(solution)/shard_map/ppermute | solution.py:430
  215.5 23.5 %collective-permute-start.19 = (bf16[384,1536]{1,0:T(8,128)(2,1)S(1)}, bf16[384,1536]{1,0:T(8,128)(2,1)S(1)}, u32[]{:S(2)}, u32[]{:S(2)}) collective-permute-start(bf16[384,1536]{1,0:T(8,128)(2,1)S(1)} %fusion.1.ready), channel_id=1, source_target_pairs={{20,12},{21,13},{22,14},{23,15}} | collective-permute-start | bytes 3538952 | tf_op jit(solution)/shard_map/ppermute | solution.py:430

commit v8 on v7

--- a/solution.py
+++ b/solution.py
@@ -53,12 +53,6 @@
 
 def rows_of(scale):
     return jnp.broadcast_to(scale[None, :], (8, scale.shape[0]))
-
-
-def products_cost(rows, order, count):
-    return pl.CostEstimate(
-        flops=2 * count * rows * order * order, bytes_accessed=2 * count * order * order, transcendentals=0
-    )
 
 
 def whole_spec(shape):
@@ -340,7 +334,7 @@
             ],
         ),
         compiler_params=pltpu.CompilerParams(vmem_limit_bytes=22 * 1024 * 1024),
-        cost_estimate=products_cost(rows, order, 2),
+        cost_estimate=FREE,
     )(flags, own, pivot_scale, prev_early, prev_late, pivot, update, ready)
 
 
@@ -410,7 +404,7 @@
             ],
         ),
         compiler_params=pltpu.CompilerParams(vmem_limit_bytes=28 * 1024 * 1024),
-        cost_estimate=products_cost(rows, order, 4),
+        cost_estimate=FREE,
     )(flags, pivot_scale, pivot_rows, right, columns, next_rows, mine, partial, link, pivot)
 
 

time: 242 us -> 241 us (level)
  local copies, waits for them, and re-layouts: 5.6 us -> 2.89 us
    unnamed x28 -> x24, local copies, waits for them, and re-layouts: 4.15 us -> 1.44 us
where the time goes in v8:
time: 241 us; the launch traced here: 240 us
  waiting for transfers between devices  131 us (54%)
  Pallas kernels  49.3 us (20%)
  starting transfers between devices  38.9 us (16%)
  other arithmetic  11.2 us (5%)
  matrix products  6.06 us (3%)
  local copies, waits for them, and re-layouts  2.89 us (1%)
    ppermute x12, waiting for transfers between devices, one_step(): return (lax.ppermute(ahead, 'space', up), lax.ppermute(back, 'space', down))  113 us
    ppermute x12, starting transfers between devices, one_step(): return (lax.ppermute(ahead, 'space', up), lax.ppermute(back, 'space', down))  21.9 us
    pallas_call x1, Pallas kernels, early_forms(): pl.pallas_call(functools.partial(early_kernel, size), out_shape=[SHAPE((o...  18.1 us
    ppermute x8, waiting for transfers between devices, between(): lax.ppermute(block, 'tm', [(a, b) for a, b in route if 0 <= b < parts])  17.4 us
    ppermute x8, starting transfers between devices, between(): lax.ppermute(block, 'tm', [(a, b) for a, b in route if 0 <= b < parts])  17 us
    pallas_call x1, Pallas kernels, last_forms(): pl.pallas_call(last_kernel, out_shape=[SHAPE((rows, order), F32), SHAPE((...  10 us
    pallas_call x1, Pallas kernels, columns_forms(): pl.pallas_call(columns_kernel, out_shape=[out, out, out], grid_spec=pltpu...  6.78 us
    pallas_call x1, Pallas kernels, late_forms(): pl.pallas_call(functools.partial(late_kernel, size), out_shape=[SHAPE((ro...  5.99 us
  transfers between devices with their start and end apart: 20, of which 11 were waited for; matrix products, arithmetic and copies ran while one was open for 6% of the time, Pallas kernels for 17%

profile of v8, /device:TPU:3, one launch (start us, length us, event | category | flops | bytes accessed | tf_op | source)
XLA Modules:
  0.0 240.2 jit_solution(9616456011885253671)
XLA Ops:
  0.7 0.8 divide_reduce_fusion
  1.5 1.1 dynamic-slice_bitcast_fusion.separator
  2.6 0.1 pad_add_fusion.flags
  2.7 0.0 copy-start.1
  2.7 1.3 copy-done.1
  4.0 3.1 %shard_map.59.refs_0_ = bf16[400,1536]{1,0:T(8,128)(2,1)} custom-call(s32[4]{0:T(128)S(1)} %pad_add_fusion.flags, bf16[384,1536]{1,0:T(8,128)(2,1)S(1)} %bitcast.31, bf16[384,1536]{1,0:T(8,128)(2,1)S(1)} %bitcast.26, f32[384,384]{1,0:T(8,128)S(1)} %dynamic-slice_bitcast_fusion.separator, f32[8,1536]{1,0:T(8,128)S(1)} %broadcast_in_dim.17.reciprocal), custom_call_target="tpu_custom_call" | custom-call | tf_op jit(solution)/shard_map/pallas_call | solution.py:102
  7.1 4.3 %collective-permute-start = (bf16[400,1536]{1,0:T(8,128)(2,1)}, bf16[400,1536]{1,0:T(8,128)(2,1)}, u32[]{:S(2)}, u32[]{:S(2)}) collective-permute-start(bf16[400,1536]{1,0:T(8,128)(2,1)} %shard_map.59.refs_0_), channel_id=1, source_target_pairs={{0,1},{1,2},{2,3},{4,5},{5,6},{6,7},{8,9},{9,10},{10,11},{12,13},{... | collective-permute-start | bytes 3686408 | tf_op jit(solution)/shard_map/ppermute | solution.py:433
  11.4 1.3 collective-permute-start.9
  12.7 5.0 %collective-permute-start.7 = (bf16[384,1536]{1,0:T(8,128)(2,1)S(1)}, bf16[384,1536]{1,0:T(8,128)(2,1)}, u32[]{:S(2)}, u32[]{:S(2)}) collective-permute-start(bf16[384,1536]{1,0:T(8,128)(2,1)S(1)} %bitcast.28), channel_id=1, source_target_pairs={{0,1},{1,2},{2,3},{4,5},{5,6},{6,7},{8,9},{9,10},{10,11},{12,13},{... | collective-permute-start | bytes 3538952 | tf_op jit(solution)/shard_map/ppermute | solution.py:433
  17.7 1.3 collective-permute-start.3
  19.0 17.3 %collective-permute-done.refs_1_ = bf16[400,1536]{1,0:T(8,128)(2,1)} collective-permute-done((bf16[400,1536]{1,0:T(8,128)(2,1)}, bf16[400,1536]{1,0:T(8,128)(2,1)}, u32[]{:S(2)}, u32[]{:S(2)}) %collective-permute-start) | collective-permute-done | bytes 1228832 | tf_op jit(solution)/shard_map/ppermute | solution.py:433
  36.3 1.7 collective-permute-start.1
  38.1 1.7 collective-permute-done.9
  39.8 1.3 collective-permute-start.10
  41.1 20.4 %collective-permute-done.7 = bf16[384,1536]{1,0:T(8,128)(2,1)} collective-permute-done((bf16[384,1536]{1,0:T(8,128)(2,1)S(1)}, bf16[384,1536]{1,0:T(8,128)(2,1)}, u32[]{:S(2)}, u32[]{:S(2)}) %collective-permute-start.7) | collective-permute-done | bytes 1179680 | tf_op jit(solution)/shard_map/ppermute | solution.py:433
  61.5 1.7 collective-permute-start.8
  63.2 3.0 %collective-permute-done.3.refs_2_ = bf16[400,1536]{1,0:T(8,128)(2,1)} collective-permute-done((bf16[400,1536]{1,0:T(8,128)(2,1)}, bf16[400,1536]{1,0:T(8,128)(2,1)}, u32[]{:S(2)}, u32[]{:S(2)}) %collective-permute-start.3) | collective-permute-done | bytes 1228832 | tf_op jit(solution)/shard_map/ppermute | solution.py:433
  66.2 1.3 collective-permute-start.4
  67.5 0.2 multiply_convert_fusion.3.own_rows
  67.7 0.0 collective-permute-done.1.refs_3_
  67.7 0.7 collective-permute-start.2
  68.5 23.0 %collective-permute-done.10 = bf16[384,1536]{1,0:T(8,128)(2,1)} collective-permute-done((bf16[384,1536]{1,0:T(8,128)(2,1)S(1)}, bf16[384,1536]{1,0:T(8,128)(2,1)}, u32[]{:S(2)}, u32[]{:S(2)}) %collective-permute-start.10) | collective-permute-done | bytes 1179680 | tf_op jit(solution)/shard_map/ppermute | solution.py:433
  91.5 0.0 collective-permute-done.8
  91.5 2.2 broadcast_select_fusion
  93.8 24.0 %collective-permute-done.4.refs_4_ = bf16[400,1536]{1,0:T(8,128)(2,1)S(1)} collective-permute-done((bf16[400,1536]{1,0:T(8,128)(2,1)}, bf16[400,1536]{1,0:T(8,128)(2,1)S(1)}, u32[]{:S(2)}, u32[]{:S(2)}) %collective-permute-start.4) | collective-permute-done | bytes 1228832 | tf_op jit(solution)/shard_map/ppermute | solution.py:433
  117.7 1.3 collective-permute-start.5
  119.0 0.4 pad_maximum_fusion
  119.4 0.7 collective-permute-start.12
  120.1 1.3 collective-permute-start.13
  121.4 0.0 collective-permute-done.2.refs_5_
  121.4 0.9 slice_select_fusion.1
  122.4 23.9 %collective-permute-done.5.refs_6_ = bf16[400,1536]{1,0:T(8,128)(2,1)S(1)} collective-permute-done((bf16[400,1536]{1,0:T(8,128)(2,1)S(1)}, bf16[400,1536]{1,0:T(8,128)(2,1)S(1)}, u32[]{:S(2)}, u32[]{:S(2)}) %collective-permute-start.5) | collective-permute-done | bytes 1228832 | tf_op jit(solution)/shard_map/ppermute | solution.py:433
  146.3 0.8 slice_select_fusion
  147.3 1.3 collective-permute-start.6
  148.6 0.0 copy-start.3
  148.7 3.3 %multiply_convert_fusion.prev_whole.prev_early = bf16[1536,1536]{1,0:T(8,128)(2,1)} fusion(bf16[1536,1536]{1,0:T(8,128)(2,1)S(1)} %pad_maximum_fusion, f32[1536]{0:T(1024)S(1)} %divide_reduce_fusion), kind=kLoop, calls=%fused_computation | loop fusion | flops 7077888 | bytes 9443328 | tf_op jit(solution)/shard_map/convert_element_type | solution.py:35
  151.9 7.1 %collective-permute-start.11 = (f32[1536]{0:T(1024)S(1)}, f32[1536]{0:T(1024)S(1)}, u32[]{:S(2)}, u32[]{:S(2)}) collective-permute-start(f32[1536]{0:T(1024)S(1)} %pad_maximum_fusion.3), channel_id=1, source_target_pairs={{4,0},{8,4},{12,8},{16,12},{20,16},{24,20},{28,24},{5,1},{9,5},{13... | collective-permute-start | bytes 18440 | tf_op jit(solution)/shard_map/ppermute | solution.py:424
  159.0 2.4 collective-permute-done.11
  161.4 0.0 copy-start.9
  161.5 18.1 %shard_map.60 = (bf16[1536,1536]{1,0:T(8,128)(2,1)S(1)}, f32[384,1536]{1,0:T(8,128)S(1)}, f32[384,1536]{1,0:T(8,128)S(1)}, bf16[1536,1536]{1,0:T(8,128)(2,1)S(1)}, bf16[384,1536]{1,0:T(8,128)(2,1)S(1)}) custom-call(s32[4]{0:T(128)S(1)} %pad_add_fusion.flags, bf16[1536,1536]{1,0:T(8,128)(2,1)} %multiply_convert_fusion.prev_whole.prev_early, ...), custom_call_target="tpu_custom_call" | custom-call | tf_op jit(solution)/shard_map/pallas_call | solution.py:149
  179.6 0.0 copy-start.6
  179.7 6.0 %shard_map.61 = (bf16[384,1536]{1,0:T(8,128)(2,1)S(1)}, f32[384,384]{1,0:T(8,128)S(1)}, bf16[384,1536]{1,0:T(8,128)(2,1)S(1)}) custom-call(s32[4]{0:T(128)S(1)} %pad_add_fusion.flags, f32[8,1536]{1,0:T(8,128)S(1)} %copy-done.9, bf16[384,1536]{1,0:T(8,128)(2,1)S(1)} %bitcast.30, bf16[1536,1536]{1,0:T(8,128)(2,1)S(1)} %get-tuple-element.26.own, ...), custom_call_target="tpu_custom_call" | custom-call | tf_op jit(solution)/shard_map/pallas_call | solution.py:204
  185.7 0.0 copy-start.7
  185.7 0.1 constant_dynamic-update-slice_fusion.1.link.link_whole
  185.8 1.4 collective-permute-start.14
  187.2 0.1 copy-done.7
  187.4 0.1 constant_dynamic-update-slice_fusion.form
  187.5 5.2 %shard_map.62 = (bf16[384,1536]{1,0:T(8,128)(2,1)S(1)}, f32[8,1536]{1,0:T(8,128)S(1)}, f32[8,1536]{1,0:T(8,128)S(1)}) custom-call(s32[4]{0:T(128)S(1)} %pad_add_fusion.flags, bf16[1536,1536]{1,0:T(8,128)(2,1)S(1)} %constant_dynamic-update-slice_fusion.1.link.link_whole, bf16[384,1536]{1,0:T(8,128)(2,1)S(1)} %get-tuple-element.29.mine, ...), custom_call_target="tpu_custom_call" | custom-call | tf_op jit(solution)/shard_map/pallas_call | solution.py:244
  192.7 1.3 collective-permute-start.15
  194.0 1.5 collective-permute-start.17
  195.5 3.1 %collective-permute-done.15 = f32[1536]{0:T(1024)S(1)} collective-permute-done((f32[1536]{0:T(1024)S(1)}, f32[1536]{0:T(1024)S(1)}, u32[]{:S(2)}, u32[]{:S(2)}) %collective-permute-start.15) | collective-permute-done | bytes 6176 | tf_op jit(solution)/shard_map/ppermute | solution.py:424
  198.6 0.2 multiply_convert_fusion.2
  198.8 2.0 fusion.next_rows
  200.8 2.0 fusion.2
  202.9 0.1 pad_maximum_fusion.1
  203.0 1.6 collective-permute-start.16
  204.5 2.0 fusion.1.ready
  206.6 6.8 %shard_map.63 = (bf16[384,1536]{1,0:T(8,128)(2,1)S(1)}, bf16[384,1536]{1,0:T(8,128)(2,1)S(1)}, bf16[384,1536]{1,0:T(8,128)(2,1)S(1)}) custom-call(s32[4]{0:T(128)S(1)} %pad_add_fusion.flags, bf16[384,1536]{1,0:T(8,128)(2,1)S(1)} %bitcast.32, bf16[8,1536]{1,0:T(8,128)(2,1)S(1)} %broadcast_in_dim.18.pivot_scale, bf16[1536,1536]{1,0:T(8,128)(2,1)S(1)} %bitcast.25, ...), custom_call_target="tpu_custom_call" | custom-call | tf_op jit(solution)/shard_map/pallas_call | solution.py:320
  213.4 1.4 collective-permute-start.18
  214.7 1.5 collective-permute-start.19
  216.3 4.4 %collective-permute-done.16.pivot_rows = bf16[400,1536]{1,0:T(8,128)(2,1)S(1)} collective-permute-done((bf16[400,1536]{1,0:T(8,128)(2,1)S(1)}, bf16[400,1536]{1,0:T(8,128)(2,1)S(1)}, u32[]{:S(2)}, u32[]{:S(2)}) %collective-permute-start.16) | collective-permute-done | bytes 1228832 | tf_op jit(solution)/shard_map/ppermute | solution.py:424
  220.7 10.0 %shard_map.64 = (f32[384,1536]{1,0:T(8,128)S(1)}, bf16[384,1536]{1,0:T(8,128)(2,1)}) custom-call(s32[4]{0:T(128)S(1)} %pad_add_fusion.flags, bf16[8,1536]{1,0:T(8,128)(2,1)S(1)} %broadcast_in_dim.18.pivot_scale, bf16[400,1536]{1,0:T(8,128)(2,1)S(1)} %collective-permute-done.16.pivot_rows, bf16[384,1536]{1,0:T(8,128)(2,1)S(1)} %get-tuple-element.36.right_whole, ...), custom_call_target="tpu_custom_call" | custom-call | tf_op jit(solution)/shard_map/pallas_call | solution.py:388
  230.8 7.5 %collective-permute-done.19 = bf16[384,1536]{1,0:T(8,128)(2,1)S(1)} collective-permute-done((bf16[384,1536]{1,0:T(8,128)(2,1)S(1)}, bf16[384,1536]{1,0:T(8,128)(2,1)S(1)}, u32[]{:S(2)}, u32[]{:S(2)}) %collective-permute-start.19) | collective-permute-done | bytes 1179680 | tf_op jit(solution)/shard_map/ppermute | solution.py:424
  238.2 2.0 subtract_bitcast_fusion
  (44 shorter events, 0.4 us)
Async XLA Ops:
  0.6 2.1 copy-start
  2.7 4.4 %copy-start.8 = (f32[8,1536]{1,0:T(8,128)}, f32[8,1536]{1,0:T(8,128)S(1)}, u32[]{:S(2)}) copy-start(f32[8,1536]{1,0:T(8,128)S(1)} %broadcast_in_dim.17.reciprocal) | copy-start | bytes 147460
  2.7 1.3 copy-start.1
  4.0 63.5 %copy-start.2 = (bf16[1,384,1536]{2,1,0:T(8,128)(2,1)S(1)}, bf16[1,384,1536]{2,1,0:T(8,128)(2,1)}, u32[]{:S(2)}) copy-start(bf16[1,384,1536]{2,1,0:T(8,128)(2,1)} %param.5) | copy-start | bytes 3538948
  7.1 29.2 %collective-permute-start = (bf16[400,1536]{1,0:T(8,128)(2,1)}, bf16[400,1536]{1,0:T(8,128)(2,1)}, u32[]{:S(2)}, u32[]{:S(2)}) collective-permute-start(bf16[400,1536]{1,0:T(8,128)(2,1)} %shard_map.59.refs_0_), channel_id=1, source_target_pairs={{0,1},{1,2},{2,3},{4,5},{5,6},{6,7},{8,9},{9,10},{10,11},{12,13},{... | collective-permute-start | bytes 3686408 | tf_op jit(solution)/shard_map/ppermute | solution.py:433
  11.4 28.4 %collective-permute-start.9 = (bf16[384,1536]{1,0:T(8,128)(2,1)S(1)}, bf16[384,1536]{1,0:T(8,128)(2,1)S(1)}, u32[]{:S(2)}, u32[]{:S(2)}) collective-permute-start(bf16[384,1536]{1,0:T(8,128)(2,1)S(1)} %bitcast.27), channel_id=1, source_target_pairs={{1,0},{2,1},{3,2},{5,4},{6,5},{7,6},{9,8},{10,9},{11,10},{13,12},{... | collective-permute-start | bytes 3538952 | tf_op jit(solution)/shard_map/ppermute | solution.py:433
  12.7 48.8 %collective-permute-start.7 = (bf16[384,1536]{1,0:T(8,128)(2,1)S(1)}, bf16[384,1536]{1,0:T(8,128)(2,1)}, u32[]{:S(2)}, u32[]{:S(2)}) collective-permute-start(bf16[384,1536]{1,0:T(8,128)(2,1)S(1)} %bitcast.28), channel_id=1, source_target_pairs={{0,1},{1,2},{2,3},{4,5},{5,6},{6,7},{8,9},{9,10},{10,11},{12,13},{... | collective-permute-start | bytes 3538952 | tf_op jit(solution)/shard_map/ppermute | solution.py:433
  17.7 48.5 %collective-permute-start.3 = (bf16[400,1536]{1,0:T(8,128)(2,1)}, bf16[400,1536]{1,0:T(8,128)(2,1)}, u32[]{:S(2)}, u32[]{:S(2)}) collective-permute-start(bf16[400,1536]{1,0:T(8,128)(2,1)} %shard_map.59.refs_0_), channel_id=1, source_target_pairs={{1,0},{2,1},{3,2},{5,4},{6,5},{7,6},{9,8},{10,9},{11,10},{13,12},{... | collective-permute-start | bytes 3686408 | tf_op jit(solution)/shard_map/ppermute | solution.py:433
  36.3 31.4 %collective-permute-start.1 = (bf16[400,1536]{1,0:T(8,128)(2,1)}, bf16[400,1536]{1,0:T(8,128)(2,1)}, u32[]{:S(2)}, u32[]{:S(2)}) collective-permute-start(bf16[400,1536]{1,0:T(8,128)(2,1)} %collective-permute-done.refs_1_), channel_id=1, source_target_pairs={{1,2},{2,3},{5,6},{6,7},{9,10},{10,11},{13,14},{14,15},{17,18},{18... | collective-permute-start | bytes 3686408 | tf_op jit(solution)/shard_map/ppermute | solution.py:433
  39.8 51.7 %collective-permute-start.10 = (bf16[384,1536]{1,0:T(8,128)(2,1)S(1)}, bf16[384,1536]{1,0:T(8,128)(2,1)}, u32[]{:S(2)}, u32[]{:S(2)}) collective-permute-start(bf16[384,1536]{1,0:T(8,128)(2,1)S(1)} %collective-permute-done.9), channel_id=1, source_target_pairs={{1,0},{2,1},{5,4},{6,5},{9,8},{10,9},{13,12},{14,13},{17,16},{18,1... | collective-permute-start | bytes 3538952 | tf_op jit(solution)/shard_map/ppermute | solution.py:433
  61.5 30.0 %collective-permute-start.8 = (bf16[384,1536]{1,0:T(8,128)(2,1)}, bf16[384,1536]{1,0:T(8,128)(2,1)}, u32[]{:S(2)}, u32[]{:S(2)}) collective-permute-start(bf16[384,1536]{1,0:T(8,128)(2,1)} %collective-permute-done.7), channel_id=1, source_target_pairs={{1,2},{2,3},{5,6},{6,7},{9,10},{10,11},{13,14},{14,15},{17,18},{18... | collective-permute-start | bytes 3538952 | tf_op jit(solution)/shard_map/ppermute | solution.py:433
  66.2 51.5 %collective-permute-start.4 = (bf16[400,1536]{1,0:T(8,128)(2,1)}, bf16[400,1536]{1,0:T(8,128)(2,1)S(1)}, u32[]{:S(2)}, u32[]{:S(2)}) collective-permute-start(bf16[400,1536]{1,0:T(8,128)(2,1)} %collective-permute-done.3.refs_2_), channel_id=1, source_target_pairs={{1,0},{2,1},{5,4},{6,5},{9,8},{10,9},{13,12},{14,13},{17,16},{18,1... | collective-permute-start | bytes 3686408 | tf_op jit(solution)/shard_map/ppermute | solution.py:433
  67.7 53.7 %collective-permute-start.2 = (bf16[400,1536]{1,0:T(8,128)(2,1)}, bf16[400,1536]{1,0:T(8,128)(2,1)S(1)}, u32[]{:S(2)}, u32[]{:S(2)}) collective-permute-start(bf16[400,1536]{1,0:T(8,128)(2,1)} %collective-permute-done.1.refs_3_), channel_id=1, source_target_pairs={{2,3},{6,7},{10,11},{14,15},{18,19},{22,23},{26,27},{30,31}} | collective-permute-start | bytes 3686408 | tf_op jit(solution)/shard_map/ppermute | solution.py:433
  117.7 28.5 %collective-permute-start.5 = (bf16[400,1536]{1,0:T(8,128)(2,1)S(1)}, bf16[400,1536]{1,0:T(8,128)(2,1)S(1)}, u32[]{:S(2)}, u32[]{:S(2)}) collective-permute-start(bf16[400,1536]{1,0:T(8,128)(2,1)S(1)} %collective-permute-done.4.refs_4_), channel_id=1, source_target_pairs={{1,0},{5,4},{9,8},{13,12},{17,16},{21,20},{25,24},{29,28}} | collective-permute-start | bytes 3686408 | tf_op jit(solution)/shard_map/ppermute | solution.py:433
  119.4 60.3 %collective-permute-start.12 = (bf16[384,1536]{1,0:T(8,128)(2,1)}, bf16[384,1536]{1,0:T(8,128)(2,1)S(1)}, u32[]{:S(2)}, u32[]{:S(2)}) collective-permute-start(bf16[384,1536]{1,0:T(8,128)(2,1)} %collective-permute-done.8), channel_id=1, source_target_pairs={{2,3},{6,7},{10,11},{14,15},{18,19},{22,23},{26,27},{30,31}} | collective-permute-start | bytes 3538952 | tf_op jit(solution)/shard_map/ppermute | solution.py:433
  120.1 59.5 %collective-permute-start.13 = (bf16[384,1536]{1,0:T(8,128)(2,1)}, bf16[384,1536]{1,0:T(8,128)(2,1)}, u32[]{:S(2)}, u32[]{:S(2)}) collective-permute-start(bf16[384,1536]{1,0:T(8,128)(2,1)} %collective-permute-done.10), channel_id=1, source_target_pairs={{1,0},{5,4},{9,8},{13,12},{17,16},{21,20},{25,24},{29,28}} | collective-permute-start | bytes 3538952 | tf_op jit(solution)/shard_map/ppermute | solution.py:433
  147.3 11.7 %collective-permute-start.6 = (f32[1536]{0:T(1024)S(1)}, f32[1536]{0:T(1024)S(1)}, u32[]{:S(2)}, u32[]{:S(2)}) collective-permute-start(f32[1536]{0:T(1024)S(1)} %pad_maximum_fusion.2), channel_id=1, source_target_pairs={{0,4},{8,12},{16,20},{24,28},{1,5},{9,13},{17,21},{25,29},{2,6},{1... | collective-permute-start | bytes 18440 | tf_op jit(solution)/shard_map/ppermute | solution.py:424
  148.6 12.8 %copy-start.3 = (f32[1,384,1536]{2,1,0:T(8,128)S(1)}, f32[1,384,1536]{2,1,0:T(8,128)}, u32[]{:S(2)}) copy-start(f32[1,384,1536]{2,1,0:T(8,128)} %param.4) | copy-start | bytes 7077892
  151.9 9.5 %collective-permute-start.11 = (f32[1536]{0:T(1024)S(1)}, f32[1536]{0:T(1024)S(1)}, u32[]{:S(2)}, u32[]{:S(2)}) collective-permute-start(f32[1536]{0:T(1024)S(1)} %pad_maximum_fusion.3), channel_id=1, source_target_pairs={{4,0},{8,4},{12,8},{16,12},{20,16},{24,20},{28,24},{5,1},{9,5},{13... | collective-permute-start | bytes 18440 | tf_op jit(solution)/shard_map/ppermute | solution.py:424
  161.4 18.2 %copy-start.9 = (f32[8,1536]{1,0:T(8,128)S(1)}, f32[8,1536]{1,0:T(8,128)}, u32[]{:S(2)}) copy-start(f32[8,1536]{1,0:T(8,128)} %copy-done.8) | copy-start | bytes 147460
  179.6 6.0 %copy-start.4 = (f32[384,1536]{1,0:T(8,128)}, f32[384,1536]{1,0:T(8,128)S(1)}, u32[]{:S(2)}) copy-start(f32[384,1536]{1,0:T(8,128)S(1)} %get-tuple-element.38.partial) | copy-start | bytes 7077892
  179.6 6.0 %copy-start.6 = (f32[384,1536]{1,0:T(8,128)}, f32[384,1536]{1,0:T(8,128)S(1)}, u32[]{:S(2)}) copy-start(f32[384,1536]{1,0:T(8,128)S(1)} %get-tuple-element.30) | copy-start | bytes 7077892
  185.7 1.7 copy-start.7
  185.8 12.7 %collective-permute-start.14 = (bf16[1536,1536]{1,0:T(8,128)(2,1)S(1)}, bf16[1536,1536]{1,0:T(8,128)(2,1)S(1)}, u32[]{:S(2)}, u32[]{:S(2)}) collective-permute-start(bf16[1536,1536]{1,0:T(8,128)(2,1)S(1)} %constant_dynamic-update-slice_fusion.1.link.link_whole), channel_id=1, source_target_pairs={{0,4},{8,12},{16,20},{24,28},{1,5},{9,13},{17,21},{25,29},{2,6},{1... | collective-permute-start | bytes 14155784 | tf_op jit(solution)/shard_map/ppermute | solution.py:424
  192.7 5.9 %collective-permute-start.15 = (f32[1536]{0:T(1024)S(1)}, f32[1536]{0:T(1024)S(1)}, u32[]{:S(2)}, u32[]{:S(2)}) collective-permute-start(f32[1536]{0:T(1024)S(1)} %slice_reduce_fusion.1), channel_id=1, source_target_pairs={{8,4},{16,12},{24,20},{9,5},{17,13},{25,21},{10,6},{18,14},{26,22}... | collective-permute-start | bytes 18440 | tf_op jit(solution)/shard_map/ppermute | solution.py:424
  194.0 36.7 %collective-permute-start.17 = (bf16[384,1536]{1,0:T(8,128)(2,1)S(1)}, bf16[384,1536]{1,0:T(8,128)(2,1)S(1)}, u32[]{:S(2)}, u32[]{:S(2)}) collective-permute-start(bf16[384,1536]{1,0:T(8,128)(2,1)S(1)} %get-tuple-element.35.update), channel_id=1, source_target_pairs={{8,4},{16,12},{24,20},{9,5},{17,13},{25,21},{10,6},{18,14},{26,22}... | collective-permute-start | bytes 3538952 | tf_op jit(solution)/shard_map/ppermute | solution.py:424
  202.9 3.7 %slice-start = ((s8[4718592]{0:T(1024)(128)(4,1)}), s8[4194304]{0:T(1024)(128)(4,1)S(1)}, s32[]{:S(2)}) async-start(s8[4718592]{0:T(1024)(128)(4,1)} %bitcast.24), calls=%async_computation | async-start | bytes 8388608
  203.0 3.6 %slice-start.1 = ((s8[4718592]{0:T(1024)(128)(4,1)}), s8[524288]{0:T(1024)(128)(4,1)S(1)}, s32[]{:S(2)}) async-start(s8[4718592]{0:T(1024)(128)(4,1)} %bitcast.24), calls=%async_computation.1 | async-start | bytes 1048576
  203.0 17.7 %collective-permute-start.16 = (bf16[400,1536]{1,0:T(8,128)(2,1)S(1)}, bf16[400,1536]{1,0:T(8,128)(2,1)S(1)}, u32[]{:S(2)}, u32[]{:S(2)}) collective-permute-start(bf16[400,1536]{1,0:T(8,128)(2,1)S(1)} %pad_maximum_fusion.1), channel_id=1, source_target_pairs={{4,12},{20,28},{5,13},{21,29},{6,14},{22,30},{7,15},{23,31}} | collective-permute-start | bytes 3686408 | tf_op jit(solution)/shard_map/ppermute | solution.py:424
  206.6 14.1 %copy-start.5 = (f32[384,1536]{1,0:T(8,128)S(1)}, f32[384,1536]{1,0:T(8,128)}, u32[]{:S(2)}) copy-start(f32[384,1536]{1,0:T(8,128)} %copy-done.4) | copy-start | bytes 7077892
  213.4 17.4 %collective-permute-start.18 = (bf16[384,1536]{1,0:T(8,128)(2,1)S(1)}, bf16[384,1536]{1,0:T(8,128)(2,1)S(1)}, u32[]{:S(2)}, u32[]{:S(2)}) collective-permute-start(bf16[384,1536]{1,0:T(8,128)(2,1)S(1)} %get-tuple-element.40), channel_id=1, source_target_pairs={{4,0},{12,8},{20,16},{28,24},{5,1},{13,9},{21,17},{29,25},{6,2},{1... | collective-permute-start | bytes 3538952 | tf_op jit(solution)/shard_map/ppermute | solution.py:424
  214.7 23.5 %collective-permute-start.19 = (bf16[384,1536]{1,0:T(8,128)(2,1)S(1)}, bf16[384,1536]{1,0:T(8,128)(2,1)S(1)}, u32[]{:S(2)}, u32[]{:S(2)}) collective-permute-start(bf16[384,1536]{1,0:T(8,128)(2,1)S(1)} %fusion.1.ready), channel_id=1, source_target_pairs={{20,12},{21,13},{22,14},{23,15}} | collective-permute-start | bytes 3538952 | tf_op jit(solution)/shard_map/ppermute | solution.py:424

commit v9 on v8

--- a/solution.py
+++ b/solution.py
@@ -10,7 +10,7 @@
 BF16 = jnp.bfloat16
 F32 = jnp.float32
 EXTRA = 16
-WIDTH = 256
+WIDTH = 384
 
 ANY = pl.BlockSpec(memory_space=pl.ANY)
 HBM = pl.BlockSpec(memory_space=pltpu.HBM)
@@ -168,7 +168,7 @@
             out_specs=[along_spec(order), along_spec(rows), along_spec(rows), down_spec(order), along_spec(rows)],
             scratch_shapes=[pltpu.VMEM((order, order), BF16), pltpu.SemaphoreType.DMA((size,))],
         ),
-        compiler_params=pltpu.CompilerParams(vmem_limit_bytes=26 * 1024 * 1024),
+        compiler_params=pltpu.CompilerParams(vmem_limit_bytes=30 * 1024 * 1024),
         cost_estimate=FREE,
     )(flags, prev_whole, prev_rows, own_rows, separator, *sources)
 

time: 241 us -> 249 us (1.033)
  local copies, waits for them, and re-layouts: 2.89 us -> 6.77 us
    pallas_call x1, Pallas kernels: 18.1 us -> 22.2 us  [early_forms(): pl.pallas_call(functools.partial(early_kernel, size), out_shape=[SHAPE((o...]
    unnamed x24 -> x22, local copies, waits for them, and re-layouts: 1.44 us -> 5.32 us
  transfers between devices with their start and end apart: 20 -> 20, of which waited for: 11 -> 11; matrix products, arithmetic and copies ran while one was open for 6% -> 6% of each run, Pallas kernels for 17% -> 18%
where the time goes in v9:
time: 249 us; the launch traced here: 248 us
  waiting for transfers between devices  131 us (53%)
  Pallas kernels  51.4 us (21%)
  starting transfers between devices  38.9 us (16%)
  other arithmetic  12.8 us (5%)
  local copies, waits for them, and re-layouts  6.77 us (3%)
  matrix products  6.03 us (2%)
    ppermute x12, waiting for transfers between devices, one_step(): return (lax.ppermute(ahead, 'space', up), lax.ppermute(back, 'space', down))  113 us
    pallas_call x1, Pallas kernels, early_forms(): pl.pallas_call(functools.partial(early_kernel, size), out_shape=[SHAPE((o...  22.2 us
    ppermute x12, starting transfers between devices, one_step(): return (lax.ppermute(ahead, 'space', up), lax.ppermute(back, 'space', down))  21.9 us
    ppermute x8, waiting for transfers between devices, between(): lax.ppermute(block, 'tm', [(a, b) for a, b in route if 0 <= b < parts])  17.6 us
    ppermute x8, starting transfers between devices, between(): lax.ppermute(block, 'tm', [(a, b) for a, b in route if 0 <= b < parts])  17 us
    pallas_call x1, Pallas kernels, last_forms(): pl.pallas_call(last_kernel, out_shape=[SHAPE((rows, order), F32), SHAPE((...  10 us
    pallas_call x1, Pallas kernels, columns_forms(): pl.pallas_call(columns_kernel, out_shape=[out, out, out], grid_spec=pltpu...  6.75 us
    unnamed x22, local copies, waits for them, and re-layouts  5.32 us
  transfers between devices with their start and end apart: 20, of which 11 were waited for; matrix products, arithmetic and copies ran while one was open for 6% of the time, Pallas kernels for 18%

profile of v9, /device:TPU:3, one launch (start us, length us, event | category | flops | bytes accessed | tf_op | source)
XLA Modules:
  0.0 247.7 jit_solution(10282960829580803693)
XLA Ops:
  0.7 0.8 divide_reduce_fusion
  1.5 1.1 dynamic-slice_bitcast_fusion.separator
  2.6 0.1 pad_add_fusion.flags
  2.7 0.0 copy-start.1
  2.7 1.3 copy-done.1
  4.0 3.1 %shard_map.59.refs_0_ = bf16[400,1536]{1,0:T(8,128)(2,1)} custom-call(s32[4]{0:T(128)S(1)} %pad_add_fusion.flags, bf16[384,1536]{1,0:T(8,128)(2,1)S(1)} %bitcast.31, bf16[384,1536]{1,0:T(8,128)(2,1)S(1)} %bitcast.26, f32[384,384]{1,0:T(8,128)S(1)} %dynamic-slice_bitcast_fusion.separator, f32[8,1536]{1,0:T(8,128)S(1)} %broadcast_in_dim.17.reciprocal), custom_call_target="tpu_custom_call" | custom-call | tf_op jit(solution)/shard_map/pallas_call | solution.py:102
  7.1 4.3 %collective-permute-start = (bf16[400,1536]{1,0:T(8,128)(2,1)}, bf16[400,1536]{1,0:T(8,128)(2,1)}, u32[]{:S(2)}, u32[]{:S(2)}) collective-permute-start(bf16[400,1536]{1,0:T(8,128)(2,1)} %shard_map.59.refs_0_), channel_id=1, source_target_pairs={{0,1},{1,2},{2,3},{4,5},{5,6},{6,7},{8,9},{9,10},{10,11},{12,13},{... | collective-permute-start | bytes 3686408 | tf_op jit(solution)/shard_map/ppermute | solution.py:433
  11.4 1.3 collective-permute-start.9
  12.6 5.0 %collective-permute-start.7 = (bf16[384,1536]{1,0:T(8,128)(2,1)S(1)}, bf16[384,1536]{1,0:T(8,128)(2,1)}, u32[]{:S(2)}, u32[]{:S(2)}) collective-permute-start(bf16[384,1536]{1,0:T(8,128)(2,1)S(1)} %bitcast.28), channel_id=1, source_target_pairs={{0,1},{1,2},{2,3},{4,5},{5,6},{6,7},{8,9},{9,10},{10,11},{12,13},{... | collective-permute-start | bytes 3538952 | tf_op jit(solution)/shard_map/ppermute | solution.py:433
  17.7 1.3 collective-permute-start.3
  19.0 17.3 %collective-permute-done.refs_1_ = bf16[400,1536]{1,0:T(8,128)(2,1)} collective-permute-done((bf16[400,1536]{1,0:T(8,128)(2,1)}, bf16[400,1536]{1,0:T(8,128)(2,1)}, u32[]{:S(2)}, u32[]{:S(2)}) %collective-permute-start) | collective-permute-done | bytes 1228832 | tf_op jit(solution)/shard_map/ppermute | solution.py:433
  36.3 1.8 collective-permute-start.1
  38.0 1.8 collective-permute-done.9
  39.9 1.3 collective-permute-start.10
  41.1 20.3 %collective-permute-done.7 = bf16[384,1536]{1,0:T(8,128)(2,1)} collective-permute-done((bf16[384,1536]{1,0:T(8,128)(2,1)S(1)}, bf16[384,1536]{1,0:T(8,128)(2,1)}, u32[]{:S(2)}, u32[]{:S(2)}) %collective-permute-start.7) | collective-permute-done | bytes 1179680 | tf_op jit(solution)/shard_map/ppermute | solution.py:433
  61.5 1.7 collective-permute-start.8
  63.1 3.0 %collective-permute-done.3.refs_2_ = bf16[400,1536]{1,0:T(8,128)(2,1)} collective-permute-done((bf16[400,1536]{1,0:T(8,128)(2,1)}, bf16[400,1536]{1,0:T(8,128)(2,1)}, u32[]{:S(2)}, u32[]{:S(2)}) %collective-permute-start.3) | collective-permute-done | bytes 1228832 | tf_op jit(solution)/shard_map/ppermute | solution.py:433
  66.2 1.3 collective-permute-start.4
  67.5 0.2 multiply_convert_fusion.3.own_rows
  67.7 0.0 collective-permute-done.1.refs_3_
  67.7 0.7 collective-permute-start.2
  68.5 23.0 %collective-permute-done.10 = bf16[384,1536]{1,0:T(8,128)(2,1)} collective-permute-done((bf16[384,1536]{1,0:T(8,128)(2,1)}, bf16[384,1536]{1,0:T(8,128)(2,1)}, u32[]{:S(2)}, u32[]{:S(2)}) %collective-permute-start.10) | collective-permute-done | bytes 1179680 | tf_op jit(solution)/shard_map/ppermute | solution.py:433
  91.5 2.6 %broadcast_select_fusion = (bf16[384,1536]{1,0:T(8,128)(2,1)S(1)}, bf16[384,1536]{1,0:T(8,128)(2,1)S(1)}, bf16[384,1536]{1,0:T(8,128)(2,1)S(1)}, bf16[384,1536]{1,0:T(8,128)(2,1)S(1)}, bf16[384,1536]{1,0:T(8,128)(2,1)S(1)}) fusion(pred[]{:T(512)S(6)} %lt.24, bf16[384,1536]{1,0:T(8,128)(2,1)} %collective-permute-done.8, ...), kind=kLoop, calls=%fused_computation.18 | loop fusion | flops 7667712 | bytes 11796485 | tf_op jit(solution)/shard_map/jit(_where)/select_n | solution.py:468
  94.1 23.6 %collective-permute-done.4.refs_4_ = bf16[400,1536]{1,0:T(8,128)(2,1)S(1)} collective-permute-done((bf16[400,1536]{1,0:T(8,128)(2,1)}, bf16[400,1536]{1,0:T(8,128)(2,1)S(1)}, u32[]{:S(2)}, u32[]{:S(2)}) %collective-permute-start.4) | collective-permute-done | bytes 1228832 | tf_op jit(solution)/shard_map/ppermute | solution.py:433
  117.7 1.3 collective-permute-start.5
  119.0 0.4 pad_maximum_fusion
  119.4 0.7 collective-permute-start.12
  120.1 1.3 collective-permute-start.13
  121.4 0.0 collective-permute-done.2.refs_5_
  121.4 0.9 slice_select_fusion.1
  122.3 23.9 %collective-permute-done.5.refs_6_ = bf16[400,1536]{1,0:T(8,128)(2,1)S(1)} collective-permute-done((bf16[400,1536]{1,0:T(8,128)(2,1)S(1)}, bf16[400,1536]{1,0:T(8,128)(2,1)S(1)}, u32[]{:S(2)}, u32[]{:S(2)}) %collective-permute-start.5) | collective-permute-done | bytes 1228832 | tf_op jit(solution)/shard_map/ppermute | solution.py:433
  146.2 0.8 slice_select_fusion
  147.3 1.3 collective-permute-start.6
  148.6 0.0 copy-start.4
  148.6 3.3 %multiply_convert_fusion.prev_whole.prev_early = bf16[1536,1536]{1,0:T(8,128)(2,1)} fusion(bf16[1536,1536]{1,0:T(8,128)(2,1)S(1)} %pad_maximum_fusion, f32[1536]{0:T(1024)S(1)} %divide_reduce_fusion), kind=kLoop, calls=%fused_computation | loop fusion | flops 7077888 | bytes 9443328 | tf_op jit(solution)/shard_map/convert_element_type | solution.py:35
  151.9 7.1 %collective-permute-start.11 = (f32[1536]{0:T(1024)S(1)}, f32[1536]{0:T(1024)S(1)}, u32[]{:S(2)}, u32[]{:S(2)}) collective-permute-start(f32[1536]{0:T(1024)S(1)} %pad_maximum_fusion.3), channel_id=1, source_target_pairs={{4,0},{8,4},{12,8},{16,12},{20,16},{24,20},{28,24},{5,1},{9,5},{13... | collective-permute-start | bytes 18440 | tf_op jit(solution)/shard_map/ppermute | solution.py:424
  159.0 0.0 collective-permute-done.6
  159.0 2.4 collective-permute-done.11
  161.4 22.2 %shard_map.60 = (bf16[1536,1536]{1,0:T(8,128)(2,1)S(1)}, f32[384,1536]{1,0:T(8,128)S(1)}, f32[384,1536]{1,0:T(8,128)S(1)}, bf16[1536,1536]{1,0:T(8,128)(2,1)}, bf16[384,1536]{1,0:T(8,128)(2,1)S(1)}) custom-call(s32[4]{0:T(128)S(1)} %pad_add_fusion.flags, bf16[1536,1536]{1,0:T(8,128)(2,1)} %multiply_convert_fusion.prev_whole.prev_early, ...), custom_call_target="tpu_custom_call" | custom-call | tf_op jit(solution)/shard_map/pallas_call | solution.py:149
  183.7 0.0 copy-start.7
  183.7 4.0 %copy-done.3 = bf16[1536,1536]{1,0:T(8,128)(2,1)S(1)} copy-done((bf16[1536,1536]{1,0:T(8,128)(2,1)S(1)}, bf16[1536,1536]{1,0:T(8,128)(2,1)}, u32[]{:S(2)}) %copy-start.3) | copy-done | bytes 4718616
  187.7 4.1 %shard_map.61 = (bf16[384,1536]{1,0:T(8,128)(2,1)S(1)}, f32[384,384]{1,0:T(8,128)S(1)}, bf16[384,1536]{1,0:T(8,128)(2,1)S(1)}) custom-call(s32[4]{0:T(128)S(1)} %pad_add_fusion.flags, f32[8,1536]{1,0:T(8,128)S(1)} %broadcast_in_dim.17.reciprocal, bf16[384,1536]{1,0:T(8,128)(2,1)S(1)} %bitcast.30, bf16[1536,1536]{1,0:T(8,128)(2,1)S(1)} %copy-done.3, ...), custom_call_target="tpu_custom_call" | custom-call | tf_op jit(solution)/shard_map/pallas_call | solution.py:204
  191.8 0.0 copy-start.8
  191.8 0.1 constant_dynamic-update-slice_fusion.1.link.link_whole
  191.9 1.6 collective-permute-start.14
  193.6 0.1 constant_dynamic-update-slice_fusion.form
  193.7 5.2 %shard_map.62 = (bf16[384,1536]{1,0:T(8,128)(2,1)S(1)}, f32[8,1536]{1,0:T(8,128)S(1)}, f32[8,1536]{1,0:T(8,128)S(1)}) custom-call(s32[4]{0:T(128)S(1)} %pad_add_fusion.flags, bf16[1536,1536]{1,0:T(8,128)(2,1)S(1)} %constant_dynamic-update-slice_fusion.1.link.link_whole, bf16[384,1536]{1,0:T(8,128)(2,1)S(1)} %get-tuple-element.29.mine, ...), custom_call_target="tpu_custom_call" | custom-call | tf_op jit(solution)/shard_map/pallas_call | solution.py:244
  198.9 1.3 collective-permute-start.15
  200.2 1.3 collective-permute-start.17
  201.5 3.2 %collective-permute-done.15 = f32[1536]{0:T(1024)S(1)} collective-permute-done((f32[1536]{0:T(1024)S(1)}, f32[1536]{0:T(1024)S(1)}, u32[]{:S(2)}, u32[]{:S(2)}) %collective-permute-start.15) | collective-permute-done | bytes 6176 | tf_op jit(solution)/shard_map/ppermute | solution.py:424
  204.8 0.0 collective-permute-done.14.pivot_whole
  204.8 0.2 multiply_convert_fusion.2
  205.0 2.0 fusion.next_rows
  207.0 2.0 fusion.2
  209.1 0.1 pad_maximum_fusion.1
  209.2 1.6 collective-permute-start.16
  210.7 2.0 fusion.1.ready
  212.8 6.8 %shard_map.63 = (bf16[384,1536]{1,0:T(8,128)(2,1)S(1)}, bf16[384,1536]{1,0:T(8,128)(2,1)S(1)}, bf16[384,1536]{1,0:T(8,128)(2,1)S(1)}) custom-call(s32[4]{0:T(128)S(1)} %pad_add_fusion.flags, bf16[384,1536]{1,0:T(8,128)(2,1)S(1)} %bitcast.32, bf16[8,1536]{1,0:T(8,128)(2,1)S(1)} %broadcast_in_dim.18.pivot_scale, bf16[1536,1536]{1,0:T(8,128)(2,1)S(1)} %bitcast.25, ...), custom_call_target="tpu_custom_call" | custom-call | tf_op jit(solution)/shard_map/pallas_call | solution.py:320
  219.5 1.4 collective-permute-start.18
  220.9 1.5 collective-permute-start.19
  222.4 4.5 %collective-permute-done.16.pivot_rows = bf16[400,1536]{1,0:T(8,128)(2,1)S(1)} collective-permute-done((bf16[400,1536]{1,0:T(8,128)(2,1)S(1)}, bf16[400,1536]{1,0:T(8,128)(2,1)S(1)}, u32[]{:S(2)}, u32[]{:S(2)}) %collective-permute-start.16) | collective-permute-done | bytes 1228832 | tf_op jit(solution)/shard_map/ppermute | solution.py:424
  226.9 10.0 %shard_map.64 = (f32[384,1536]{1,0:T(8,128)S(1)}, bf16[384,1536]{1,0:T(8,128)(2,1)}) custom-call(s32[4]{0:T(128)S(1)} %pad_add_fusion.flags, bf16[8,1536]{1,0:T(8,128)(2,1)S(1)} %broadcast_in_dim.18.pivot_scale, bf16[400,1536]{1,0:T(8,128)(2,1)S(1)} %collective-permute-done.16.pivot_rows, bf16[384,1536]{1,0:T(8,128)(2,1)S(1)} %get-tuple-element.36.right_whole, ...), custom_call_target="tpu_custom_call" | custom-call | tf_op jit(solution)/shard_map/pallas_call | solution.py:388
  237.0 7.5 %collective-permute-done.19 = bf16[384,1536]{1,0:T(8,128)(2,1)S(1)} collective-permute-done((bf16[384,1536]{1,0:T(8,128)(2,1)S(1)}, bf16[384,1536]{1,0:T(8,128)(2,1)S(1)}, u32[]{:S(2)}, u32[]{:S(2)}) %collective-permute-start.19) | collective-permute-done | bytes 1179680 | tf_op jit(solution)/shard_map/ppermute | solution.py:424
  244.5 3.3 %subtract_bitcast_fusion = f32[1,384,1536]{2,1,0:T(8,128)} fusion(bf16[384,1536]{1,0:T(8,128)(2,1)S(1)} %collective-permute-done.19, f32[384,1536]{1,0:T(8,128)S(1)} %get-tuple-element.39, bf16[384,1536]{1,0:T(8,128)(2,1)} %collective-permute-done.17, bf16[384,1536]{1,0:T(8,128)(2,1)S(1)} %collective-permute-done.18), kind=kLoop, calls=%fused_computation.8 | loop fusion | flops 2949120 | bytes 8257536 | tf_op jit(solution)/shard_map/broadcast_in_dim | solution.py:526
  (42 shorter events, 0.4 us)
Async XLA Ops:
  0.6 2.0 copy-start
  2.7 1.3 copy-start.1
  4.0 63.5 %copy-start.2 = (bf16[1,384,1536]{2,1,0:T(8,128)(2,1)S(1)}, bf16[1,384,1536]{2,1,0:T(8,128)(2,1)}, u32[]{:S(2)}) copy-start(bf16[1,384,1536]{2,1,0:T(8,128)(2,1)} %param.5) | copy-start | bytes 3538948
  7.1 29.2 %collective-permute-start = (bf16[400,1536]{1,0:T(8,128)(2,1)}, bf16[400,1536]{1,0:T(8,128)(2,1)}, u32[]{:S(2)}, u32[]{:S(2)}) collective-permute-start(bf16[400,1536]{1,0:T(8,128)(2,1)} %shard_map.59.refs_0_), channel_id=1, source_target_pairs={{0,1},{1,2},{2,3},{4,5},{5,6},{6,7},{8,9},{9,10},{10,11},{12,13},{... | collective-permute-start | bytes 3686408 | tf_op jit(solution)/shard_map/ppermute | solution.py:433
  11.4 28.5 %collective-permute-start.9 = (bf16[384,1536]{1,0:T(8,128)(2,1)S(1)}, bf16[384,1536]{1,0:T(8,128)(2,1)}, u32[]{:S(2)}, u32[]{:S(2)}) collective-permute-start(bf16[384,1536]{1,0:T(8,128)(2,1)S(1)} %bitcast.27), channel_id=1, source_target_pairs={{1,0},{2,1},{3,2},{5,4},{6,5},{7,6},{9,8},{10,9},{11,10},{13,12},{... | collective-permute-start | bytes 3538952 | tf_op jit(solution)/shard_map/ppermute | solution.py:433
  12.6 48.8 %collective-permute-start.7 = (bf16[384,1536]{1,0:T(8,128)(2,1)S(1)}, bf16[384,1536]{1,0:T(8,128)(2,1)}, u32[]{:S(2)}, u32[]{:S(2)}) collective-permute-start(bf16[384,1536]{1,0:T(8,128)(2,1)S(1)} %bitcast.28), channel_id=1, source_target_pairs={{0,1},{1,2},{2,3},{4,5},{5,6},{6,7},{8,9},{9,10},{10,11},{12,13},{... | collective-permute-start | bytes 3538952 | tf_op jit(solution)/shard_map/ppermute | solution.py:433
  17.7 48.5 %collective-permute-start.3 = (bf16[400,1536]{1,0:T(8,128)(2,1)}, bf16[400,1536]{1,0:T(8,128)(2,1)}, u32[]{:S(2)}, u32[]{:S(2)}) collective-permute-start(bf16[400,1536]{1,0:T(8,128)(2,1)} %shard_map.59.refs_0_), channel_id=1, source_target_pairs={{1,0},{2,1},{3,2},{5,4},{6,5},{7,6},{9,8},{10,9},{11,10},{13,12},{... | collective-permute-start | bytes 3686408 | tf_op jit(solution)/shard_map/ppermute | solution.py:433
  36.3 31.4 %collective-permute-start.1 = (bf16[400,1536]{1,0:T(8,128)(2,1)}, bf16[400,1536]{1,0:T(8,128)(2,1)}, u32[]{:S(2)}, u32[]{:S(2)}) collective-permute-start(bf16[400,1536]{1,0:T(8,128)(2,1)} %collective-permute-done.refs_1_), channel_id=1, source_target_pairs={{1,2},{2,3},{5,6},{6,7},{9,10},{10,11},{13,14},{14,15},{17,18},{18... | collective-permute-start | bytes 3686408 | tf_op jit(solution)/shard_map/ppermute | solution.py:433
  39.9 51.6 %collective-permute-start.10 = (bf16[384,1536]{1,0:T(8,128)(2,1)}, bf16[384,1536]{1,0:T(8,128)(2,1)}, u32[]{:S(2)}, u32[]{:S(2)}) collective-permute-start(bf16[384,1536]{1,0:T(8,128)(2,1)} %collective-permute-done.9), channel_id=1, source_target_pairs={{1,0},{2,1},{5,4},{6,5},{9,8},{10,9},{13,12},{14,13},{17,16},{18,1... | collective-permute-start | bytes 3538952 | tf_op jit(solution)/shard_map/ppermute | solution.py:433
  61.5 30.0 %collective-permute-start.8 = (bf16[384,1536]{1,0:T(8,128)(2,1)}, bf16[384,1536]{1,0:T(8,128)(2,1)}, u32[]{:S(2)}, u32[]{:S(2)}) collective-permute-start(bf16[384,1536]{1,0:T(8,128)(2,1)} %collective-permute-done.7), channel_id=1, source_target_pairs={{1,2},{2,3},{5,6},{6,7},{9,10},{10,11},{13,14},{14,15},{17,18},{18... | collective-permute-start | bytes 3538952 | tf_op jit(solution)/shard_map/ppermute | solution.py:433
  66.2 51.5 %collective-permute-start.4 = (bf16[400,1536]{1,0:T(8,128)(2,1)}, bf16[400,1536]{1,0:T(8,128)(2,1)S(1)}, u32[]{:S(2)}, u32[]{:S(2)}) collective-permute-start(bf16[400,1536]{1,0:T(8,128)(2,1)} %collective-permute-done.3.refs_2_), channel_id=1, source_target_pairs={{1,0},{2,1},{5,4},{6,5},{9,8},{10,9},{13,12},{14,13},{17,16},{18,1... | collective-permute-start | bytes 3686408 | tf_op jit(solution)/shard_map/ppermute | solution.py:433
  67.7 53.7 %collective-permute-start.2 = (bf16[400,1536]{1,0:T(8,128)(2,1)}, bf16[400,1536]{1,0:T(8,128)(2,1)S(1)}, u32[]{:S(2)}, u32[]{:S(2)}) collective-permute-start(bf16[400,1536]{1,0:T(8,128)(2,1)} %collective-permute-done.1.refs_3_), channel_id=1, source_target_pairs={{2,3},{6,7},{10,11},{14,15},{18,19},{22,23},{26,27},{30,31}} | collective-permute-start | bytes 3686408 | tf_op jit(solution)/shard_map/ppermute | solution.py:433
  117.7 28.5 %collective-permute-start.5 = (bf16[400,1536]{1,0:T(8,128)(2,1)S(1)}, bf16[400,1536]{1,0:T(8,128)(2,1)S(1)}, u32[]{:S(2)}, u32[]{:S(2)}) collective-permute-start(bf16[400,1536]{1,0:T(8,128)(2,1)S(1)} %collective-permute-done.4.refs_4_), channel_id=1, source_target_pairs={{1,0},{5,4},{9,8},{13,12},{17,16},{21,20},{25,24},{29,28}} | collective-permute-start | bytes 3686408 | tf_op jit(solution)/shard_map/ppermute | solution.py:433
  119.4 64.3 %collective-permute-start.12 = (bf16[384,1536]{1,0:T(8,128)(2,1)}, bf16[384,1536]{1,0:T(8,128)(2,1)S(1)}, u32[]{:S(2)}, u32[]{:S(2)}) collective-permute-start(bf16[384,1536]{1,0:T(8,128)(2,1)} %collective-permute-done.8), channel_id=1, source_target_pairs={{2,3},{6,7},{10,11},{14,15},{18,19},{22,23},{26,27},{30,31}} | collective-permute-start | bytes 3538952 | tf_op jit(solution)/shard_map/ppermute | solution.py:433
  120.1 63.6 %collective-permute-start.13 = (bf16[384,1536]{1,0:T(8,128)(2,1)}, bf16[384,1536]{1,0:T(8,128)(2,1)S(1)}, u32[]{:S(2)}, u32[]{:S(2)}) collective-permute-start(bf16[384,1536]{1,0:T(8,128)(2,1)} %collective-permute-done.10), channel_id=1, source_target_pairs={{1,0},{5,4},{9,8},{13,12},{17,16},{21,20},{25,24},{29,28}} | collective-permute-start | bytes 3538952 | tf_op jit(solution)/shard_map/ppermute | solution.py:433
  147.3 11.7 %collective-permute-start.6 = (f32[1536]{0:T(1024)S(1)}, f32[1536]{0:T(1024)S(1)}, u32[]{:S(2)}, u32[]{:S(2)}) collective-permute-start(f32[1536]{0:T(1024)S(1)} %pad_maximum_fusion.2), channel_id=1, source_target_pairs={{0,4},{8,12},{16,20},{24,28},{1,5},{9,13},{17,21},{25,29},{2,6},{1... | collective-permute-start | bytes 18440 | tf_op jit(solution)/shard_map/ppermute | solution.py:424
  148.6 12.8 %copy-start.4 = (f32[1,384,1536]{2,1,0:T(8,128)S(1)}, f32[1,384,1536]{2,1,0:T(8,128)}, u32[]{:S(2)}) copy-start(f32[1,384,1536]{2,1,0:T(8,128)} %param.4) | copy-start | bytes 7077892
  151.9 9.5 %collective-permute-start.11 = (f32[1536]{0:T(1024)S(1)}, f32[1536]{0:T(1024)S(1)}, u32[]{:S(2)}, u32[]{:S(2)}) collective-permute-start(f32[1536]{0:T(1024)S(1)} %pad_maximum_fusion.3), channel_id=1, source_target_pairs={{4,0},{8,4},{12,8},{16,12},{20,16},{24,20},{28,24},{5,1},{9,5},{13... | collective-permute-start | bytes 18440 | tf_op jit(solution)/shard_map/ppermute | solution.py:424
  183.7 8.1 %copy-start.5 = (f32[384,1536]{1,0:T(8,128)}, f32[384,1536]{1,0:T(8,128)S(1)}, u32[]{:S(2)}) copy-start(f32[384,1536]{1,0:T(8,128)S(1)} %get-tuple-element.38.partial) | copy-start | bytes 7077892
  183.7 8.1 %copy-start.7 = (f32[384,1536]{1,0:T(8,128)}, f32[384,1536]{1,0:T(8,128)S(1)}, u32[]{:S(2)}) copy-start(f32[384,1536]{1,0:T(8,128)S(1)} %get-tuple-element.30) | copy-start | bytes 7077892
  183.7 4.0 %copy-start.3 = (bf16[1536,1536]{1,0:T(8,128)(2,1)S(1)}, bf16[1536,1536]{1,0:T(8,128)(2,1)}, u32[]{:S(2)}) copy-start(bf16[1536,1536]{1,0:T(8,128)(2,1)} %get-tuple-element.26.own) | copy-start | bytes 14155780
  191.8 1.7 copy-start.8
  191.9 12.8 %collective-permute-start.14 = (bf16[1536,1536]{1,0:T(8,128)(2,1)S(1)}, bf16[1536,1536]{1,0:T(8,128)(2,1)S(1)}, u32[]{:S(2)}, u32[]{:S(2)}) collective-permute-start(bf16[1536,1536]{1,0:T(8,128)(2,1)S(1)} %constant_dynamic-update-slice_fusion.1.link.link_whole), channel_id=1, source_target_pairs={{0,4},{8,12},{16,20},{24,28},{1,5},{9,13},{17,21},{25,29},{2,6},{1... | collective-permute-start | bytes 14155784 | tf_op jit(solution)/shard_map/ppermute | solution.py:424
  198.9 5.9 %collective-permute-start.15 = (f32[1536]{0:T(1024)S(1)}, f32[1536]{0:T(1024)S(1)}, u32[]{:S(2)}, u32[]{:S(2)}) collective-permute-start(f32[1536]{0:T(1024)S(1)} %slice_reduce_fusion.1), channel_id=1, source_target_pairs={{8,4},{16,12},{24,20},{9,5},{17,13},{25,21},{10,6},{18,14},{26,22}... | collective-permute-start | bytes 18440 | tf_op jit(solution)/shard_map/ppermute | solution.py:424
  200.2 36.7 %collective-permute-start.17 = (bf16[384,1536]{1,0:T(8,128)(2,1)S(1)}, bf16[384,1536]{1,0:T(8,128)(2,1)}, u32[]{:S(2)}, u32[]{:S(2)}) collective-permute-start(bf16[384,1536]{1,0:T(8,128)(2,1)S(1)} %get-tuple-element.35.update), channel_id=1, source_target_pairs={{8,4},{16,12},{24,20},{9,5},{17,13},{25,21},{10,6},{18,14},{26,22}... | collective-permute-start | bytes 3538952 | tf_op jit(solution)/shard_map/ppermute | solution.py:424
  209.0 3.7 %slice-start = ((s8[4718592]{0:T(1024)(128)(4,1)}), s8[4194304]{0:T(1024)(128)(4,1)S(1)}, s32[]{:S(2)}) async-start(s8[4718592]{0:T(1024)(128)(4,1)} %bitcast.24), calls=%async_computation | async-start | bytes 8388608
  209.1 3.6 %slice-start.1 = ((s8[4718592]{0:T(1024)(128)(4,1)}), s8[524288]{0:T(1024)(128)(4,1)S(1)}, s32[]{:S(2)}) async-start(s8[4718592]{0:T(1024)(128)(4,1)} %bitcast.24), calls=%async_computation.1 | async-start | bytes 1048576
  209.2 17.7 %collective-permute-start.16 = (bf16[400,1536]{1,0:T(8,128)(2,1)S(1)}, bf16[400,1536]{1,0:T(8,128)(2,1)S(1)}, u32[]{:S(2)}, u32[]{:S(2)}) collective-permute-start(bf16[400,1536]{1,0:T(8,128)(2,1)S(1)} %pad_maximum_fusion.1), channel_id=1, source_target_pairs={{4,12},{20,28},{5,13},{21,29},{6,14},{22,30},{7,15},{23,31}} | collective-permute-start | bytes 3686408 | tf_op jit(solution)/shard_map/ppermute | solution.py:424
  212.8 14.1 %copy-start.6 = (f32[384,1536]{1,0:T(8,128)S(1)}, f32[384,1536]{1,0:T(8,128)}, u32[]{:S(2)}) copy-start(f32[384,1536]{1,0:T(8,128)} %copy-done.5) | copy-start | bytes 7077892
  219.5 17.4 %collective-permute-start.18 = (bf16[384,1536]{1,0:T(8,128)(2,1)S(1)}, bf16[384,1536]{1,0:T(8,128)(2,1)S(1)}, u32[]{:S(2)}, u32[]{:S(2)}) collective-permute-start(bf16[384,1536]{1,0:T(8,128)(2,1)S(1)} %get-tuple-element.40), channel_id=1, source_target_pairs={{4,0},{12,8},{20,16},{28,24},{5,1},{13,9},{21,17},{29,25},{6,2},{1... | collective-permute-start | bytes 3538952 | tf_op jit(solution)/shard_map/ppermute | solution.py:424
  220.9 23.5 %collective-permute-start.19 = (bf16[384,1536]{1,0:T(8,128)(2,1)S(1)}, bf16[384,1536]{1,0:T(8,128)(2,1)S(1)}, u32[]{:S(2)}, u32[]{:S(2)}) collective-permute-start(bf16[384,1536]{1,0:T(8,128)(2,1)S(1)} %fusion.1.ready), channel_id=1, source_target_pairs={{20,12},{21,13},{22,14},{23,15}} | collective-permute-start | bytes 3538952 | tf_op jit(solution)/shard_map/ppermute | solution.py:424
